TPU v7x, 128 devices: a whole 4x4x4 slice. The times are simulated.
128 devices in a mesh: rows: 4 (over x), wide: 32 (over y, z, core).
Axes of the slice: x: 4, y: 4, z: 4, core: 2. Of those that a mesh axis runs over, the one named last changes fastest.
Arguments:
- hidden: bfloat16 [64, 5120], P(None, 'rows'), may hold values from -6 to 6
- attn_gain: bfloat16 [5120], P('rows'), may hold values from 0.099609375 to 1.8984375
- w_query: bfloat16 [5120, 8192], P('rows', 'wide'), may hold values from -1 to 1
- w_keyval: bfloat16 [5120, 2048], P('rows', 'wide'), may hold values from -1 to 1
- query_gain: bfloat16 [128], replicated, may hold values from 0.099609375 to 1.8984375
- key_norm_gain: bfloat16 [128], replicated, may hold values from 1 to 3
- keys_cache: bfloat16 [64, 8192, 1024], P('rows', 'wide'), may hold values from -600 to 600
- physical_values_cache: bfloat16 [64, 8192, 1024], P('rows', 'wide'), may hold values from -18 to 18
- lengths: int32 [64], P('rows'), may hold values from 4096 to 8191
- block_index: int32 [64, 32], P('rows', 'wide'), may hold values from 0 to 31, each once within a row
- w_out: bfloat16 [8192, 5120], P('wide', 'rows'), may hold values from -0.0625 to 0.0625
- mlp_gain: bfloat16 [5120], P('rows'), may hold values from 0.099609375 to 1.8984375
- w_gate: bfloat16 [5120, 25600], P('rows', 'wide'), may hold values from -0.078125 to 0.078125
- w_up: bfloat16 [5120, 25600], P('rows', 'wide'), may hold values from -0.078125 to 0.078125
- w_down: bfloat16 [25600, 5120], P('wide', 'rows'), may hold values from -0.0390625 to 0.0390625
Outputs:
- layer_out: bfloat16 [64, 5120], P(None, 'rows')
- attention_heads: bfloat16 [64, 8192], P('rows', 'wide')
Inputs may be any that keep to these rules, and one draw needn't show every extreme that they name: Each row of block_index is a permutation of the 32 block numbers.
All inputs are finite; a program needn't handle non-finite values.
Results may differ from a plain program's by a relative error of at most 0.0173.
Values may be sent and summed in bfloat16 or wider, within the bound.
No kernel may reach another device: no remote copies, remote signals or barrier semaphores. Data moves between devices by JAX's collectives and lax.ppermute only.
A program may use at most 128 MiB of HBM per device.

v0:
```python
import jax
import jax.numpy as jnp
from jax import lax
from jax.sharding import PartitionSpec as P

MODEL_WIDTH = 5120
QUERY_HEADS = 64
KEY_VALUE_HEADS = 8
HEAD_WIDTH = 128


EPSILON = 1e-06
ROPE_BASE = 1000000.0
MASKED = -1e30


def joined(part, axis, combine):
    gathered = jax.tree.map(lambda a: lax.all_gather(a, axis), part)

    def take(source):
        return jax.tree.map(lambda a: lax.dynamic_index_in_dim(a, source, 0, False), gathered)

    return lax.fori_loop(
        1, lax.axis_size(axis), lambda source, state: combine(state, take(source)), take(0)
    )


def head_rms_norm(values, gain):
    return (
        values
        * lax.rsqrt(jnp.mean(values * values, axis=-1, keepdims=True) + EPSILON)
        * gain.astype(jnp.float32)
    )


def rotary_apply(values, positions):
    half_dim = values.shape[-1] // 2
    inverse_freq = ROPE_BASE ** (
        -(jnp.arange(half_dim, dtype=jnp.float32) * 2.0 / values.shape[-1])
    )
    angles = positions.astype(jnp.float32)[:, None] * inverse_freq[None, :]
    cosine = jnp.cos(angles)[:, None, :]
    sine = jnp.sin(angles)[:, None, :]
    first_half = values[..., :half_dim]
    second_half = values[..., half_dim:]
    return jnp.concatenate(
        [first_half * cosine - second_half * sine, second_half * cosine + first_half * sine],
        axis=-1,
    )


def join(earlier, latter):
    highest = jnp.maximum(earlier[1], latter[1])
    early_factor = jnp.exp(earlier[1] - highest)
    late_factor = jnp.exp(latter[1] - highest)
    numer_sum = earlier[0] * early_factor[..., None] + latter[0] * late_factor[..., None]
    return (numer_sum, highest, earlier[2] * early_factor + latter[2] * late_factor)


def body(
    hidden,
    attn_gain,
    w_query,
    w_keyval,
    query_gain,
    key_norm_gain,
    keys_cache,
    physical_values_cache,
    lengths,
    block_index,
    w_out,
    mlp_gain,
    w_gate,
    w_up,
    w_down,
):
    hidden_f = hidden.astype(jnp.float32)
    square_sum = jnp.sum(hidden_f * hidden_f, axis=1)
    scaled = (hidden_f * attn_gain.astype(jnp.float32)).astype(jnp.bfloat16)
    query_part = jnp.dot(scaled, w_query, preferred_element_type=jnp.float32)
    keyval_part = jnp.dot(scaled, w_keyval, preferred_element_type=jnp.float32)
    query_own, keyval_own, square_own = (
        lax.psum_scatter(query_part, "rows", scatter_dimension=0, tiled=True),
        lax.psum_scatter(keyval_part, "rows", scatter_dimension=0, tiled=True),
        lax.psum_scatter(square_sum, "rows", scatter_dimension=0, tiled=True),
    )
    inverse = lax.rsqrt(square_own / MODEL_WIDTH + EPSILON)
    count_of_rows = query_own.shape[0]
    head_count = query_own.shape[1] // HEAD_WIDTH
    query_local = rotary_apply(
        head_rms_norm(
            (query_own * inverse[:, None]).reshape(count_of_rows, head_count, HEAD_WIDTH),
            query_gain,
        ),
        lengths,
    )
    query_local = query_local.astype(jnp.bfloat16).reshape(count_of_rows, head_count * HEAD_WIDTH)
    keyval_local = (keyval_own * inverse[:, None]).astype(jnp.bfloat16)
    query_vector, key_value_proj = (
        lax.all_gather(query_local, "wide", axis=1, tiled=True),
        lax.all_gather(keyval_local, "wide", axis=1, tiled=True),
    )
    key_unnormed = (
        key_value_proj[:, : KEY_VALUE_HEADS * HEAD_WIDTH]
        .astype(jnp.float32)
        .reshape(count_of_rows, KEY_VALUE_HEADS, HEAD_WIDTH)
    )
    fresh_key = (
        rotary_apply(head_rms_norm(key_unnormed, key_norm_gain), lengths)
        .astype(jnp.bfloat16)
        .reshape(count_of_rows, KEY_VALUE_HEADS * HEAD_WIDTH)
    )
    fresh_value = key_value_proj[:, KEY_VALUE_HEADS * HEAD_WIDTH :]
    block_length = keys_cache.shape[1]
    position = block_index * block_length + jnp.arange(block_length, dtype=jnp.int32)[None, :]
    fresh_slot = (position == lengths[:, None])[:, :, None]
    key_batch_rows = jnp.where(fresh_slot, fresh_key[:, None, :], keys_cache).reshape(
        count_of_rows, block_length, KEY_VALUE_HEADS, HEAD_WIDTH
    )
    value_batch_rows = jnp.where(
        fresh_slot, fresh_value[:, None, :], physical_values_cache
    ).reshape(count_of_rows, block_length, KEY_VALUE_HEADS, HEAD_WIDTH)
    visible = (position <= lengths[:, None])[:, None, None, :]
    grouped_queries = query_vector.reshape(
        count_of_rows, KEY_VALUE_HEADS, QUERY_HEADS // KEY_VALUE_HEADS, HEAD_WIDTH
    )
    scores = jnp.einsum(
        "bkgd,btkd->bkgt", grouped_queries, key_batch_rows, preferred_element_type=jnp.float32
    ) * HEAD_WIDTH ** (-0.5)
    scores = jnp.where(visible, scores, MASKED)
    local_max = jnp.max(scores, axis=-1)
    weights = jnp.where(visible, jnp.exp(scores - local_max[..., None]), 0.0)
    local_total = jnp.sum(weights, axis=-1).reshape(count_of_rows, QUERY_HEADS)
    numer_local = jnp.einsum(
        "bkgt,btkd->bkgd",
        weights.astype(jnp.bfloat16),
        value_batch_rows,
        preferred_element_type=jnp.float32,
    )
    numer_local = numer_local.reshape(count_of_rows, QUERY_HEADS, HEAD_WIDTH)
    local_max = local_max.reshape(count_of_rows, QUERY_HEADS)
    numer_all, max_all, total_all = joined((numer_local, local_max, local_total), "wide", join)
    first_head = lax.axis_index("wide") * head_count
    numer_sel = lax.dynamic_slice_in_dim(numer_all, first_head, head_count, 1)
    total_sel = lax.dynamic_slice_in_dim(total_all, first_head, head_count, 1)
    heads_out = (
        (numer_sel / total_sel[..., None])
        .astype(jnp.bfloat16)
        .reshape(count_of_rows, head_count * HEAD_WIDTH)
    )
    out_part = jnp.dot(
        lax.all_gather(heads_out, "rows", axis=0, tiled=True),
        w_out,
        preferred_element_type=jnp.float32,
    )
    attended = lax.psum(out_part.astype(jnp.bfloat16), "wide").astype(jnp.float32)
    stream = hidden_f + attended
    stream_square = jnp.sum(stream * stream, axis=1)
    mlp_scaled = (stream * mlp_gain.astype(jnp.float32)).astype(jnp.bfloat16)
    gate_part = jnp.dot(mlp_scaled, w_gate, preferred_element_type=jnp.float32)
    up_part = jnp.dot(mlp_scaled, w_up, preferred_element_type=jnp.float32)
    gate_sum, up_sum, norm_sum = (
        lax.psum(gate_part.astype(jnp.bfloat16), "rows").astype(jnp.float32),
        lax.psum(up_part.astype(jnp.bfloat16), "rows").astype(jnp.float32),
        lax.psum(stream_square.astype(jnp.bfloat16), "rows").astype(jnp.float32),
    )
    mlp_inverse = lax.rsqrt(norm_sum / MODEL_WIDTH + EPSILON)
    activated = (
        jax.nn.silu(gate_sum * mlp_inverse[:, None]) * (up_sum * mlp_inverse[:, None])
    ).astype(jnp.bfloat16)
    down_part = jnp.dot(activated, w_down, preferred_element_type=jnp.float32)
    down_total = lax.psum(down_part.astype(jnp.bfloat16), "wide").astype(jnp.float32)
    layer_out = (stream + down_total).astype(jnp.bfloat16)
    return (layer_out, heads_out)


def solution(mesh):
    in_specs = (
        P(None, "rows"),
        P("rows"),
        P("rows", "wide"),
        P("rows", "wide"),
        P(),
        P(),
        P("rows", "wide", None),
        P("rows", "wide", None),
        P("rows"),
        P("rows", "wide"),
        P("wide", "rows"),
        P("rows"),
        P("rows", "wide"),
        P("rows", "wide"),
        P("wide", "rows"),
    )
    out_specs = (P(None, "rows"), P("rows", "wide"))
    return jax.shard_map(body, mesh=mesh, in_specs=in_specs, out_specs=out_specs, check_vma=False)
```

profile of v0, /device:TPU:1, one launch (start us, length us, event | category | flops | bytes accessed | tf_op | source)
XLA Modules:
  0.0 525.0 jit_solution(13852389422838894220)
XLA Ops:
  8.1 1.8 fusion.26
  9.9 2.1 fusion.28
  15.8 9.3 %all-reduce = f32[64]{0:T(128)S(1)} all-reduce(f32[64]{0:T(128)S(1)} %fusion.25), channel_id=3, replica_groups=mesh['rows'=4,'wide'=32] {'rows'}, use_global_device_ids=true, to_apply=%region_2.0.clone | all-reduce | flops 64 | bytes 512
  27.9 3.7 reduce-scatter.5.cloned.1.call-done
  32.3 27.5 %all-gather = bf16[32,64,16]{1,2,0:T(8,128)(2,1)S(1)} all-gather(bf16[1,64,16]{1,2,0:T(8,128)(2,1)S(1)} %fusion.35), channel_id=1, replica_groups=mesh['rows'=4,'wide'=32] {'wide'}, dimensions={0}, use_global_device_ids=true | all-gather | bytes 67584 | tf_op jit(solution)/shard_map/all_gather | solution.py:101
  60.5 11.5 %select_bitcast_fusion.1 = (bf16[16,32,8,8,128]{4,3,2,1,0:T(8,128)(2,1)}, bf16[16,32,8,8,128]{4,3,2,1,0:T(8,128)(2,1)}) fusion(bf16[16,256,1024]{2,1,0:T(8,128)(2,1)} %param.23, pred[16,256]{1,0:T(8,128)(4,1)S(1)} %get-tuple-element.217, bf16[16,1024]{1,0:T(8,128)(2,1)S(1)} %bitcast.91, bf16[16,256,1024]{2,1,0:T(8,128)(2,1)} %param.24, ...), kind=kLoop, calls=%fused_computation.15 | loop fusion | flops 8388608 | bytes 33624064
  73.2 24.3 %all_gather.18 = bf16[16,8192]{1,0:T(8,128)(2,1)S(1)} all-gather(bf16[16,256]{1,0:T(8,128)(2,1)S(1)} %bitcast.95), channel_id=1, replica_groups=mesh['rows'=4,'wide'=32] {'wide'}, dimensions={1}, use_global_device_ids=true | all-gather | bytes 270336 | tf_op jit(solution)/shard_map/all_gather | solution.py:100
  97.6 5.7 %fusion.41 = (f32[16,8,8]{2,1,0:T(8,128)S(1)}, f32[16,8,8,256]{3,2,1,0:T(8,128)S(1)}) fusion(bf16[16,8,8,128]{3,2,1,0:T(8,128)(2,1)S(1)} %bitcast.84, bf16[16,32,8,8,128]{4,3,2,1,0:T(8,128)(2,1)} %get-tuple-element.214, pred[16,256]{1,0:T(8,128)(4,1)S(1)} %get-tuple-element.216), kind=kOutput, calls=%fused_computation.80 | convolution fusion | flops 67894272 | bytes 9707520 | tf_op jit(solution)/shard_map/bkgd,btkd->bkgt/dot_general | solution.py:127
  103.3 2.1 fusion.15
  106.2 22.5 %all_gather.21 = f32[32,16,64]{2,1,0:T(8,128)S(1)} all-gather(f32[1,16,64]{2,1,0:T(8,128)S(1)} %copy.31), channel_id=1, replica_groups=mesh['rows'=4,'wide'=32] {'wide'}, dimensions={0}, use_global_device_ids=true | all-gather | bytes 135168 | tf_op jit(solution)/shard_map/all_gather | solution.py:18
  128.7 24.2 %all_gather.22 = f32[32,16,64]{2,1,0:T(8,128)S(1)} all-gather(f32[1,16,64]{2,1,0:T(8,128)S(1)} %copy.33), channel_id=1, replica_groups=mesh['rows'=4,'wide'=32] {'wide'}, dimensions={0}, use_global_device_ids=true | all-gather | bytes 135168 | tf_op jit(solution)/shard_map/all_gather | solution.py:18
  153.7 22.2 %all-gather.3.cloned.1.call-done = f32[32,16,64,128]{3,2,1,0:T(8,128)} async-done(((f32[1,16,64,128]{3,2,1,0:T(8,128)}), f32[32,16,64,128]{3,2,1,0:T(8,128)}) %all-gather.3.cloned.1.call-update) | async-done | bytes 16777232 | tf_op jit(solution)/shard_map/all_gather | solution.py:18
  177.0 71.5 %while.19 = (s32[]{:T(128)}, f32[16,64,128]{2,1,0:T(8,128)S(1)}, f32[16,64]{1,0:T(8,128)S(1)}, f32[16,64]{1,0:T(8,128)S(1)}, f32[32,16,64]{2,1,0:T(8,128)}, /*in...) while((s32[]{:T(128)}, f32[16,64,128]{2,1,0:T(8,128)S(1)}, ...), condition=%wide.region_9.10_spmd, body=%wide.region_8.9_spmd.sunk | while | flops 399365 | bytes 1613967 | solution.py:23
  177.7 1.5 fusion.53
  196.2 1.5 fusion.53
  248.7 9.6 %all_gather.23 = bf16[64,256]{1,0:T(8,128)(2,1)S(1)} all-gather(bf16[16,256]{1,0:T(8,128)(2,1)S(1)} %bitcast.92), channel_id=1, replica_groups=mesh['rows'=4,'wide'=32] {'rows'}, dimensions={0}, use_global_device_ids=true | all-gather | bytes 40960 | tf_op jit(solution)/shard_map/all_gather | solution.py:152
  259.3 99.7 %all-reduce.6.cloned.1.call-done = bf16[64,1280]{1,0:T(8,128)(2,1)} async-done(((bf16[64,1280]{1,0:T(8,128)(2,1)}), bf16[64,1280]{1,0:T(8,128)(2,1)}) %all-reduce.6.cloned.1.call-update) | async-done | bytes 163856 | tf_op jit(solution)/shard_map/psum | solution.py:156
  360.1 8.4 %psum.37 = bf16[64]{0:T(256)(128)(2,1)S(1)} all-reduce(bf16[64]{0:T(256)(128)(2,1)S(1)} %multiply_reduce_fusion), channel_id=1, replica_groups=mesh['rows'=4,'wide'=32] {'rows'}, use_global_device_ids=true, to_apply=%region_13.14 | all-reduce | flops 64 | bytes 256 | tf_op jit(solution)/shard_map/psum | solution.py:165
  368.5 3.1 convolution_convert_fusion.2
  371.6 3.1 convolution_convert_fusion.3
  374.7 36.8 %all-reduce.10.cloned.1.call-done = (bf16[64,800]{1,0:T(8,128)(2,1)}, bf16[64,800]{1,0:T(8,128)(2,1)}) async-done(((bf16[64,800]{1,0:T(8,128)(2,1)}, bf16[64,800]{1,0:T(8,128)(2,1)}), (bf16[64,800]{1,0:T(8,128)(2,1)}, bf16[64,800]{1,0:T(8,128)(2,1)})) %all-reduce.10.cloned.1.call-update) | async-done | bytes 204816 | tf_op jit(solution)/shard_map/psum | solution.py:164
  411.5 2.2 convolution_convert_fusion
  413.7 102.8 %all-reduce.8.cloned.1.call-done = bf16[64,1280]{1,0:T(8,128)(2,1)} async-done(((bf16[64,1280]{1,0:T(8,128)(2,1)}), bf16[64,1280]{1,0:T(8,128)(2,1)}) %all-reduce.8.cloned.1.call-update) | async-done | bytes 163856 | tf_op jit(solution)/shard_map/psum | solution.py:172
  516.5 1.6 add_convert_fusion
  (137 shorter events, 82.0 us)
Async XLA Ops:
  7.2 404.3 %copy-start = (bf16[800,1280]{1,0:T(8,128)(2,1)S(1)}, bf16[800,1280]{1,0:T(8,128)(2,1)}, u32[]{:S(2)}) copy-start(bf16[800,1280]{1,0:T(8,128)(2,1)} %param.31) | copy-start | bytes 6144004
  7.2 24.4 %reduce-scatter.5.cloned.1.call-start = ((), (), s32[]{:S(2)}) async-start(), calls=%async_computation.3 | async-start | bytes 40960 | tf_op jit(solution)/shard_map/reduce_scatter | solution.py:84
  9.9 62.1 %reduce-scatter.3.cloned.1.call-start = ((), (), s32[]{:S(2)}) async-start(), calls=%async_computation.2 | async-start | bytes 81920 | tf_op jit(solution)/shard_map/reduce_scatter | solution.py:83
  12.0 163.9 %all-gather.3.cloned.1.call-start = ((), (), s32[]{:S(2)}) async-start(), calls=%async_computation.4 | async-start | bytes 17301504 | tf_op jit(solution)/shard_map/all_gather | solution.py:18
  72.8 30.5 %copy-start.1 = (bf16[16,32,8,8,128]{4,3,2,1,0:T(8,128)(2,1)S(1)}, bf16[16,32,8,8,128]{4,3,2,1,0:T(8,128)(2,1)}, u32[]{:S(2)}) copy-start(bf16[16,32,8,8,128]{4,3,2,1,0:T(8,128)(2,1)} %get-tuple-element.215) | copy-start | bytes 25165828
  105.4 153.9 %copy-start.8 = (bf16[1280]{0:T(1024)(128)(2,1)S(1)}, bf16[1280]{0:T(1024)(128)(2,1)}, u32[]{:S(2)}) copy-start(bf16[1280]{0:T(1024)(128)(2,1)} %param.28) | copy-start | bytes 7684
  105.4 253.5 %copy-start.2 = (bf16[64,1280]{1,0:T(8,128)(2,1)S(1)}, bf16[64,1280]{1,0:T(8,128)(2,1)}, u32[]{:S(2)}) copy-start(bf16[64,1280]{1,0:T(8,128)(2,1)} %param.17) | copy-start | bytes 491524
  105.4 253.5 %all-reduce.6.cloned.1.call-start = ((), (), s32[]{:S(2)}) async-start(), calls=%async_computation.5 | async-start | bytes 327680 | tf_op jit(solution)/shard_map/psum | solution.py:156
  106.0 152.3 %copy-start.4 = (bf16[256,1280]{1,0:T(8,128)(2,1)S(1)}, bf16[256,1280]{1,0:T(8,128)(2,1)}, u32[]{:S(2)}) copy-start(bf16[256,1280]{1,0:T(8,128)(2,1)} %param.27) | copy-start | bytes 1966084
  128.7 24.2 %copy-start.5 = (f32[32,16,64]{2,1,0:T(8,128)}, f32[32,16,64]{2,1,0:T(8,128)S(1)}, u32[]{:S(2)}) copy-start(f32[32,16,64]{2,1,0:T(8,128)S(1)} %all_gather.21) | copy-start | bytes 393220
  153.0 0.7 copy-start.6
  248.7 269.5 %copy-start.7 = (bf16[2,8,2,128]{3,1,2,0:T(8,128)(2,1)}, bf16[2,8,2,128]{3,1,2,0:T(8,128)(2,1)S(1)}, u32[]{:S(2)}) copy-start(bf16[2,8,2,128]{3,1,2,0:T(8,128)(2,1)S(1)} %copy.61) | copy-start | bytes 24580
  259.2 152.3 %all-reduce.10.cloned.1.call-start = ((), (), s32[]{:S(2)}) async-start(), calls=%async_computation.7 | async-start | bytes 458752 | tf_op jit(solution)/shard_map/psum | solution.py:164
  358.9 157.6 %copy-start.3 = (bf16[64,1280]{1,0:T(8,128)(2,1)S(1)}, bf16[64,1280]{1,0:T(8,128)(2,1)}, u32[]{:S(2)}) copy-start(bf16[64,1280]{1,0:T(8,128)(2,1)} %all-reduce.6.cloned.1.call-done) | copy-start | bytes 491524
  374.7 141.8 %all-reduce.8.cloned.1.call-start = ((), (), s32[]{:S(2)}) async-start(), calls=%async_computation.6 | async-start | bytes 327680 | tf_op jit(solution)/shard_map/psum | solution.py:172
Sparse Core Ops, SparseCore 0:
  10.4 21.1 reduce-scatter.4
  34.6 20.0 reduce-scatter.2
  105.6 70.2 all-gather.2
  259.3 99.5 all-reduce.5
  374.8 36.6 all-reduce.9
  415.2 101.2 all-reduce.7
where the time goes:
time: 529 us; the launch traced here: 525 us
  waiting for transfers between devices  265 us (50%)
  blocking collectives  126 us (24%)
  other arithmetic  93.2 us (18%)
  matrix products  20.9 us (4%)
  between operations  15 us (3%)
    psum x1, waiting for transfers between devices, body(): lax.psum(down_part.astype(jnp.bfloat16), 'wide').astype(jnp.float32)  103 us
    psum x1, waiting for transfers between devices, body(): lax.psum(out_part.astype(jnp.bfloat16), 'wide').astype(jnp.float32)  99.7 us
    add x31, other arithmetic, join(): earlier[0] * early_factor[..., None] + latter[0] * late_factor[..., None]  48 us
    all_gather x2, blocking collectives, joined(): gathered = jax.tree.map(lambda a: lax.all_gather(a, axis), part)  46.7 us
    psum x1, waiting for transfers between devices, body(): lax.psum(up_part.astype(jnp.bfloat16), 'rows').astype(jnp.float32)  36.8 us
    all_gather x1, blocking collectives, body(): lax.all_gather(keyval_local, 'wide', axis=1, tiled=True)  27.5 us
    all_gather x1, blocking collectives, body(): lax.all_gather(query_local, 'wide', axis=1, tiled=True)  24.3 us
    add x31, other arithmetic, join(): earlier[2] * early_factor + latter[2] * late_factor  22.7 us
  transfers between devices with their start and end apart: 6, of which 5 were waited for; matrix products, arithmetic and copies ran while one was open for 4% of the time, Pallas kernels for 0%

commit v1 on v0

v1 whole, which is shorter than its diff:
```python
import jax
import jax.numpy as jnp
import numpy as np
from jax import lax
from jax.experimental import pallas as pl
from jax.experimental.pallas import tpu as pltpu
from jax.sharding import PartitionSpec as P

MODEL_WIDTH = 5120
QUERY_HEADS = 64
KEY_VALUE_HEADS = 8
HEAD_WIDTH = 128
EPSILON = 1e-06
ROPE_BASE = 1000000.0
MASKED = -1e30
SCALE = HEAD_WIDTH ** (-0.5)

ROWS = 4
WIDE = 32
WIDE_AXES = ("y", "z", "core")
PLANE = ("z", "core")
OWN = 16
BLOCK = 256
HIDDEN_UNITS = 800
AT_ONCE = 4
HALF = 896

f32 = jnp.float32
bf16 = jnp.bfloat16
VMEM = pl.BlockSpec(memory_space=pltpu.VMEM)
HBM = pl.BlockSpec(memory_space=pltpu.HBM)
SMEM = pl.BlockSpec(memory_space=pltpu.SMEM)
NT = (((1,), (1,)), ((), ()))


def call(kernel, out_shape, in_specs, scratch_shapes=(), limit=24, name=None):
    many = isinstance(out_shape, (tuple, list))
    return pl.pallas_call(
        kernel,
        out_shape=out_shape,
        in_specs=in_specs,
        out_specs=[VMEM] * len(out_shape) if many else VMEM,
        scratch_shapes=list(scratch_shapes),
        compiler_params=pltpu.CompilerParams(vmem_limit_bytes=limit << 20),
        name=name,
    )


def three_terms(value):
    high = value.astype(bf16).astype(f32)
    rest = value - high
    middle = rest.astype(bf16).astype(f32)
    return high, middle, rest - middle


def swap_halves(value):
    half = HEAD_WIDTH // 2
    return jnp.concatenate([value[:, half:], value[:, :half]], axis=1)


def norm_rope(value, gain, cosine, sine):
    value = value * lax.rsqrt(jnp.mean(value * value, axis=-1, keepdims=True) + EPSILON) * gain
    return value * cosine + swap_halves(value) * sine


def project_kernel(hidden_hbm, gain_ref, wq_hbm, wkv_hbm, out_ref, hidden_ref, wq_ref, wkv_ref, sems):
    moves = [
        pltpu.make_async_copy(source, target, sems.at[at])
        for at, (source, target) in enumerate(
            ((hidden_hbm, hidden_ref), (wkv_hbm, wkv_ref), (wq_hbm, wq_ref))
        )
    ]
    for move in moves:
        move.start()
    moves[0].wait()
    hidden = hidden_ref[...].astype(f32)
    square = jnp.sum(hidden * hidden, axis=1, keepdims=True)
    scaled = (hidden * gain_ref[...].astype(f32)).astype(bf16)
    moves[1].wait()
    keyval = lax.dot_general(scaled, wkv_ref[...], NT, preferred_element_type=f32)
    tail = jnp.concatenate([keyval, jnp.broadcast_to(square, keyval.shape)], axis=1)
    moves[2].wait()
    query = jnp.dot(scaled, wq_ref[...], preferred_element_type=f32)
    out_ref[...] = jnp.concatenate([query, tail], axis=1).reshape(out_ref.shape)


def heads_kernel(got_ref, cos_ref, sin_ref, gain_ref, out_ref):
    total = (got_ref[0] + got_ref[1]) + (got_ref[2] + got_ref[3])
    inverse = lax.rsqrt(total[:, 320:321] / MODEL_WIDTH + EPSILON)
    scaled = total * inverse
    gain = gain_ref[...].astype(f32)
    cosine, sine = cos_ref[...], sin_ref[...]
    parts = [
        norm_rope(scaled[:, j * 128 : (j + 1) * 128], gain, cosine, sine).astype(bf16)
        for j in range(2)
    ]
    parts.append(scaled[:, 256:].astype(bf16))
    out = jnp.concatenate(parts, axis=1)
    out_ref[...] = jnp.broadcast_to(out[None], out_ref.shape)


def attend_kernel(length_ref, block_ref, g_ref, k_ref, v_ref, o_ref, q_scr, n_scr, s_scr):
    step = pl.program_id(0)

    @pl.when(step == 0)
    def _():
        for head in range(QUERY_HEADS):
            w, j = divmod(head, 2)
            q_scr[pl.ds(head, OWN, stride=QUERY_HEADS), :] = g_ref[
                w, :, j * 128 : (j + 1) * 128
            ].astype(f32)

    row = lax.broadcasted_iota(jnp.int32, (16, 256), 0)
    lane = lax.broadcasted_iota(jnp.int32, (16, 256), 1)
    own_half = (row < 8) == (lane < 128)
    place = lax.rem(lax.broadcasted_iota(jnp.int32, (QUERY_HEADS, 128), 1), 8)
    for u in range(AT_ONCE):
        b = step * AT_ONCE + u
        here = pl.ds(pl.multiple_of(b * QUERY_HEADS, QUERY_HEADS), QUERY_HEADS)
        query = q_scr[here, :]
        limit = length_ref[b] - block_ref[b] * BLOCK
        scores = []
        for p in range(4):
            pair = query[16 * p : 16 * p + 16]
            wide_query = jnp.where(own_half, jnp.concatenate([pair, pair], axis=1), 0.0)
            scores.append(
                lax.dot_general(
                    wide_query.astype(bf16),
                    k_ref[u, :, 256 * p : 256 * p + 256],
                    NT,
                    preferred_element_type=f32,
                )
            )
        scores = jnp.concatenate(scores, axis=0) * SCALE
        visible = lax.broadcasted_iota(jnp.int32, scores.shape, 1) < limit
        scores = jnp.where(visible, scores, MASKED)
        highest = jnp.max(scores, axis=1, keepdims=True)
        weights = jnp.where(visible, jnp.exp(scores - highest), 0.0)
        total = jnp.sum(weights, axis=1, keepdims=True)
        weights = weights.astype(bf16)
        sums = []
        for p in range(4):
            both = jnp.dot(
                weights[16 * p : 16 * p + 16],
                v_ref[u, :, 256 * p : 256 * p + 256],
                preferred_element_type=f32,
            )
            sums += [both[:8, :128], both[8:, 128:]]
        n_scr[here, :] = jnp.concatenate(sums, axis=0) / jnp.maximum(total, 1.0)
        stats = jnp.zeros((QUERY_HEADS, 128), f32)
        for at, term in enumerate(three_terms(highest) + three_terms(total)):
            stats = jnp.where(place == at, term, stats)
        s_scr[here, :] = stats

    @pl.when(step == OWN // AT_ONCE - 1)
    def _():
        low = lax.broadcasted_iota(jnp.int32, (OWN, 128), 1) < 8
        for w in range(WIDE):
            rows = [pl.ds(2 * w + j, OWN, stride=QUERY_HEADS) for j in range(2)]
            for j in range(2):
                o_ref[w, :, j * 128 : (j + 1) * 128] = n_scr[rows[j], :].astype(bf16)
            o_ref[w, :, 256:] = jnp.where(low, s_scr[rows[0], :], s_scr[rows[1], :]).astype(bf16)


def combine_kernel(wide_ref, r_ref, g_ref, cos_ref, sin_ref, gain_ref, out_ref):
    wide = wide_ref[0]
    group = wide // 4
    key = jnp.concatenate(
        [g_ref[2 * group, :, 256:320], g_ref[2 * group + 1, :, 256:320]], axis=1
    ).astype(f32)
    value = jnp.concatenate(
        [g_ref[16 + 2 * group, :, 256:320], g_ref[17 + 2 * group, :, 256:320]], axis=1
    ).astype(f32)
    key = norm_rope(key, gain_ref[...].astype(f32), cos_ref[...], sin_ref[...])
    key = key.astype(bf16).astype(f32)
    for j in range(2):
        lanes = slice(j * 128, (j + 1) * 128)
        query = g_ref[wide, :, lanes].astype(f32)
        fresh = jnp.sum(query * key, axis=1, keepdims=True) * SCALE
        stats = r_ref[:, :, 256:].astype(f32)
        base = 8 * j
        tops = (
            stats[:, :, base : base + 1]
            + stats[:, :, base + 1 : base + 2]
            + stats[:, :, base + 2 : base + 3]
        )
        totals = (
            stats[:, :, base + 3 : base + 4]
            + stats[:, :, base + 4 : base + 5]
            + stats[:, :, base + 5 : base + 6]
        )
        highest = jnp.maximum(jnp.max(tops, axis=0), fresh)
        factors = jnp.exp(tops - highest[None]) * totals
        fresh_weight = jnp.exp(fresh - highest)
        weight_sum = jnp.sum(factors, axis=0) + fresh_weight
        numer = jnp.sum(r_ref[:, :, lanes].astype(f32) * factors, axis=0)
        numer = numer + fresh_weight.astype(bf16).astype(f32) * value
        out_ref[:, lanes] = (numer / weight_sum).astype(bf16)


def output_kernel(got_ref, w_ref, out_ref):
    heads = got_ref[...].reshape(-1, got_ref.shape[-1])
    out_ref[...] = jnp.dot(heads, w_ref[...], preferred_element_type=f32).astype(bf16)


def gate_up_kernel(hidden_ref, attended_ref, gain_ref, wg_ref, wu_ref, stream_ref, out_ref):
    stream = hidden_ref[...].astype(f32) + attended_ref[...].astype(f32)
    stream_ref[...] = stream
    square = jnp.sum(stream * stream, axis=1, keepdims=True)
    scaled = (stream * gain_ref[...].astype(f32)).astype(bf16)
    gate = lax.dot_general(scaled, wg_ref[...], NT, preferred_element_type=f32).astype(bf16)
    up = lax.dot_general(scaled, wu_ref[...], NT, preferred_element_type=f32).astype(bf16)
    pad = HALF - HIDDEN_UNITS
    place = lax.broadcasted_iota(jnp.int32, (stream.shape[0], pad), 1)
    norm = jnp.zeros(place.shape, f32)
    for at, term in enumerate(three_terms(square)):
        norm = jnp.where(place == at, term, norm)
    norm = norm.astype(bf16)
    out_ref[...] = jnp.concatenate([gate, norm, up, norm], axis=1).reshape(out_ref.shape)


def activate_kernel(got_ref, out_ref):
    total = jnp.sum(got_ref[...].astype(f32), axis=0)
    square = (
        total[:, HIDDEN_UNITS : HIDDEN_UNITS + 1]
        + total[:, HIDDEN_UNITS + 1 : HIDDEN_UNITS + 2]
        + total[:, HIDDEN_UNITS + 2 : HIDDEN_UNITS + 3]
    )
    inverse = lax.rsqrt(square / MODEL_WIDTH + EPSILON)
    gate = total[:, :HALF] * inverse
    up = total[:, HALF:] * inverse
    activated = (gate / (1.0 + jnp.exp(-gate)) * up).astype(bf16)
    out_ref[...] = jnp.broadcast_to(activated[None], out_ref.shape)


def down_kernel(got_ref, w_ref, out_ref):
    units = got_ref[...].reshape(-1, HALF)
    out_ref[...] = jnp.dot(
        units[:, :HIDDEN_UNITS], w_ref[...], preferred_element_type=f32
    ).astype(bf16)


def final_kernel(stream_ref, down_ref, out_ref):
    out_ref[...] = (stream_ref[...] + down_ref[...].astype(f32)).astype(bf16)


def sum_spread_kernel(got_ref, out_ref):
    total = jnp.sum(got_ref[...].astype(f32), axis=0).astype(bf16)
    out_ref[...] = jnp.broadcast_to(total[None], out_ref.shape)


def exchange(blocks, axes):
    return lax.all_to_all(blocks, axes, split_axis=0, concat_axis=0, tiled=True)


def spread(own, axes, count):
    return exchange(jnp.broadcast_to(own[None], (count, *own.shape)), axes)


def sum_wide(part):
    height, width = part.shape
    piece = (height // 8, width)

    def stage(blocks, axes, count):
        return call(
            sum_spread_kernel,
            jax.ShapeDtypeStruct((count, *piece), bf16),
            [VMEM],
            name="sum_spread",
        )(exchange(blocks, axes))

    over_plane = stage(part.reshape(8, *piece), PLANE, 4)
    total = stage(over_plane, "y", 8)
    return exchange(total, PLANE).reshape(height, width)


def body(
    hidden,
    attn_gain,
    w_query,
    w_keyval,
    query_gain,
    key_norm_gain,
    keys_cache,
    values_cache,
    lengths,
    block_index,
    w_out,
    mlp_gain,
    w_gate,
    w_up,
    w_down,
):
    wide = lax.axis_index(WIDE_AXES).astype(jnp.int32).reshape(1)
    sds = jax.ShapeDtypeStruct

    half = HEAD_WIDTH // 2
    frequency = np.power(ROPE_BASE, -(np.arange(half) * 2.0 / HEAD_WIDTH)).astype(np.float32)
    angles = lengths.astype(f32)[:, None] * jnp.asarray(frequency)[None, :]
    cosine, sine = jnp.cos(angles), jnp.sin(angles)
    cosine = jnp.concatenate([cosine, cosine], axis=1)
    sine = jnp.concatenate([-sine, sine], axis=1)

    blocks = call(
        project_kernel,
        sds((ROWS, OWN, 384), f32),
        [HBM, VMEM, HBM, HBM],
        [
            pltpu.VMEM(hidden.shape, bf16),
            pltpu.VMEM(w_query.shape, bf16),
            pltpu.VMEM(w_keyval.shape[::-1], bf16),
            pltpu.SemaphoreType.DMA((3,)),
        ],
        name="project",
    )(hidden, attn_gain[None], w_query, w_keyval.T)
    payload = call(
        heads_kernel, sds((8, OWN, 384), bf16), [VMEM] * 4, name="heads"
    )(exchange(blocks, "rows"), cosine, sine, query_gain[None])
    gathered = spread(exchange(payload, PLANE), "y", 4).reshape(WIDE, OWN, 384)

    parts = pl.pallas_call(
        attend_kernel,
        out_shape=sds((WIDE, OWN, 384), bf16),
        grid_spec=pltpu.PrefetchScalarGridSpec(
            num_scalar_prefetch=2,
            grid=(OWN // AT_ONCE,),
            in_specs=[
                pl.BlockSpec((WIDE, OWN, 384), lambda b, *_: (0, 0, 0)),
                pl.BlockSpec((AT_ONCE, BLOCK, 1024), lambda b, *_: (b, 0, 0)),
                pl.BlockSpec((AT_ONCE, BLOCK, 1024), lambda b, *_: (b, 0, 0)),
            ],
            out_specs=pl.BlockSpec((WIDE, OWN, 384), lambda b, *_: (0, 0, 0)),
            scratch_shapes=[pltpu.VMEM((OWN * QUERY_HEADS, 128), f32)] * 3,
        ),
        compiler_params=pltpu.CompilerParams(
            dimension_semantics=("arbitrary",), vmem_limit_bytes=56 << 20
        ),
        name="attend",
    )(lengths, block_index.reshape(OWN), gathered, keys_cache, values_cache)
    heads_out = call(
        combine_kernel, sds((OWN, 256), bf16), [SMEM] + [VMEM] * 5, name="combine"
    )(wide, exchange(parts, WIDE_AXES), gathered, cosine, sine, key_norm_gain[None])

    out_part = call(output_kernel, sds((64, 1280), bf16), [VMEM] * 2, name="output")(
        spread(heads_out, "rows", ROWS), w_out
    )
    stream, blocks = call(
        gate_up_kernel,
        [sds((64, 1280), f32), sds((ROWS, OWN, 2 * HALF), bf16)],
        [VMEM] * 5,
        name="gate_up",
    )(hidden, sum_wide(out_part), mlp_gain[None], w_gate.T, w_up.T)
    activated = call(
        activate_kernel, sds((ROWS, OWN, HALF), bf16), [VMEM], name="activate"
    )(exchange(blocks, "rows"))
    down_part = call(down_kernel, sds((64, 1280), bf16), [VMEM] * 2, name="down")(
        exchange(activated, "rows"), w_down
    )
    layer_out = call(final_kernel, sds((64, 1280), bf16), [VMEM] * 2, name="final")(
        stream, sum_wide(down_part)
    )
    return (layer_out, heads_out)


def solution(mesh):
    mesh = jax.sharding.Mesh(
        mesh.devices.reshape(4, 4, 4, 2), ("rows", "y", "z", "core")
    )
    in_specs = (
        P(None, "rows"),
        P("rows"),
        P("rows", WIDE_AXES),
        P("rows", WIDE_AXES),
        P(),
        P(),
        P("rows", WIDE_AXES, None),
        P("rows", WIDE_AXES, None),
        P("rows"),
        P("rows", WIDE_AXES),
        P(WIDE_AXES, "rows"),
        P("rows"),
        P("rows", WIDE_AXES),
        P("rows", WIDE_AXES),
        P(WIDE_AXES, "rows"),
    )
    out_specs = (P(None, "rows"), P("rows", WIDE_AXES))
    return jax.shard_map(body, mesh=mesh, in_specs=in_specs, out_specs=out_specs, check_vma=False)
```

time: 529 us -> 155 us (0.29)
  waiting for transfers between devices: 265 us -> 19.1 us
  other arithmetic: 93.2 us -> 1.51 us
  blocking collectives: 126 us -> 89.2 us
  matrix products: 20.9 us -> 0 us
  Pallas kernels: 0 us -> 19.8 us
  starting transfers between devices: 0.25 us -> 15.9 us
  between operations: 15 us -> 0.72 us
    psum x3 -> x0, waiting for transfers between devices: 239 us -> none  [the longest x1 103 us: body(): lax.psum(down_part.astype(jnp.bfloat16), 'wide').astype(jnp.float32)]
    all_gather x5 -> x0, blocking collectives: 108 us -> none  [the longest x2 46.7 us: joined(): gathered = jax.tree.map(lambda a: lax.all_gather(a, axis), part)]
    all_to_all x0 -> x10, blocking collectives: none -> 89.2 us  [exchange(): return lax.all_to_all(blocks, axes, split_axis=0, concat_axis=0, tiled=True)]
    add x63 -> x0, other arithmetic: 71.4 us -> none  [the longest x31 48 us: join(): earlier[0] * early_factor[..., None] + latter[0] * late_factor[..., None]]
    all_gather x1 -> x0, waiting for transfers between devices: 22.2 us -> none  [joined(): gathered = jax.tree.map(lambda a: lax.all_gather(a, axis), part)]
    dot_general x8 -> x0, matrix products: 20.9 us -> none  [the longest x1 5.73 us: body(): jnp.einsum('bkgd,btkd->bkgt', grouped_queries, key_batch_rows, preferred_...]
    pallas_call x0 -> x13, Pallas kernels: none -> 19.8 us  [the longest x1 12.7 us: body(): pl.pallas_call(attend_kernel, out_shape=sds((WIDE, OWN, 384), bf16), grid...]
    all_to_all x0 -> x3, waiting for transfers between devices: none -> 19.1 us  [exchange(): return lax.all_to_all(blocks, axes, split_axis=0, concat_axis=0, tiled=True)]
  transfers between devices with their start and end apart: 6 -> 3, of which waited for: 5 -> 3; matrix products, arithmetic and copies ran while one was open for 4% -> 1% of each run, Pallas kernels for 0% -> 0%
where the time goes in v1:
time: 155 us; the launch traced here: 154 us
  blocking collectives  89.2 us (58%)
  Pallas kernels  19.8 us (13%)
  waiting for transfers between devices  19.1 us (12%)
  starting transfers between devices  15.9 us (10%)
  local copies, waits for them, and re-layouts  7.69 us (5%)
    all_to_all x10, blocking collectives, exchange(): return lax.all_to_all(blocks, axes, split_axis=0, concat_axis=0, tiled=True)  89.2 us
    all_to_all x3, waiting for transfers between devices, exchange(): return lax.all_to_all(blocks, axes, split_axis=0, concat_axis=0, tiled=True)  19.1 us
    all_to_all x3, starting transfers between devices, exchange(): return lax.all_to_all(blocks, axes, split_axis=0, concat_axis=0, tiled=True)  15.9 us
    pallas_call x1, Pallas kernels, body(): pl.pallas_call(attend_kernel, out_shape=sds((WIDE, OWN, 384), bf16), grid...  12.7 us
    unnamed x24, local copies, waits for them, and re-layouts  6.26 us
  transfers between devices with their start and end apart: 3, of which 3 were waited for; matrix products, arithmetic and copies ran while one was open for 1% of the time, Pallas kernels for 0%

profile of v1, /device:TPU:1, one launch (start us, length us, event | category | flops | bytes accessed | tf_op | source)
XLA Modules:
  0.0 153.9 jit_solution(6705278099476074759)
XLA Ops:
  2.2 1.1 copy-done.6
  3.3 0.9 copy-done.8
  4.2 1.9 %project.1 = f32[4,16,384]{2,1,0:T(8,128)} custom-call(bf16[64,1280]{1,0:T(8,128)(2,1)S(1)} %copy-done.4, bf16[1,1280]{1,0:T(2,128)(2,1)S(1)} %broadcast_in_dim.12.gain_ref, bf16[1280,256]{1,0:T(8,128)(2,1)S(1)} %copy-done.6, bf16[64,1280]{1,0:T(8,128)(2,1)S(1)} %bitcast.20), custom_call_target="tpu_custom_call" | custom-call | tf_op jit(solution)/shard_map/project/pallas_call | solution.py:304
  6.1 4.9 %all-to-all-start = ((f32[4,16,384]{2,1,0:T(8,128)}), f32[4,16,384]{2,1,0:T(8,128)S(1)}, u32[]{:S(2)}, u32[]{:S(2)}) async-start(f32[4,16,384]{2,1,0:T(8,128)} %project.1), calls=%async_computation | async-start | bytes 196608 | tf_op jit(solution)/shard_map/all_to_all | solution.py:253
  12.5 3.1 %all-to-all-done.got_ref = f32[4,16,384]{2,1,0:T(8,128)S(1)} async-done(((f32[4,16,384]{2,1,0:T(8,128)}), f32[4,16,384]{2,1,0:T(8,128)S(1)}, u32[]{:S(2)}, u32[]{:S(2)}) %all-to-all-start) | async-done | bytes 98336 | tf_op jit(solution)/shard_map/all_to_all | solution.py:253
  16.5 12.2 %all_to_all.65 = bf16[8,16,384]{2,1,0:T(8,128)(2,1)S(1)} all-to-all(bf16[8,16,384]{2,1,0:T(8,128)(2,1)S(1)} %heads.1), channel_id=1, replica_groups=mesh['rows'=4,'y'=4,'z'=4,'core'=2] {'z','core'}, dimensions={0} | all-to-all | bytes 196608 | tf_op jit(solution)/shard_map/all_to_all | solution.py:253
  28.8 11.1 %all_to_all.66 = bf16[4,8,16,384]{3,2,1,0:T(8,128)(2,1)} all-to-all(bf16[4,8,16,384]{3,2,1,0:T(8,128)(2,1)S(1)} %broadcast_in_dim.28), channel_id=1, replica_groups=mesh['rows'=4,'y'=4,'z'=4,'core'=2] {'y'}, dimensions={0} | all-to-all | bytes 786432 | tf_op jit(solution)/shard_map/all_to_all | solution.py:253
  39.9 12.7 %attend.1 = bf16[32,16,384]{2,1,0:T(8,128)(2,1)} custom-call(s32[16]{0:T(128)} %length_ref.1, s32[16]{0:T(128)} %bitcast.23, bf16[32,16,384]{2,1,0:T(8,128)(2,1)} %bitcast.12, bf16[16,256,1024]{2,1,0:T(8,128)(2,1)} %k_ref.1, bf16[16,256,1024]{2,1,0:T(8,128)(2,1)} %v_ref.1), custom_call_target="tpu_custom_call" | custom-call | tf_op jit(solution)/shard_map/attend/pallas_call | solution.py:321
  52.6 5.7 %all-to-all-start.3 = ((bf16[32,16,384]{2,1,0:T(8,128)(2,1)}), bf16[32,16,384]{2,1,0:T(8,128)(2,1)S(1)}, u32[]{:S(2)}, u32[]{:S(2)}) async-start(bf16[32,16,384]{2,1,0:T(8,128)(2,1)} %attend.1), calls=%async_computation.3 | async-start | bytes 786432 | tf_op jit(solution)/shard_map/all_to_all | solution.py:253
  58.3 10.4 %all-to-all-done.3.r_ref = bf16[32,16,384]{2,1,0:T(8,128)(2,1)S(1)} async-done(((bf16[32,16,384]{2,1,0:T(8,128)(2,1)}), bf16[32,16,384]{2,1,0:T(8,128)(2,1)S(1)}, u32[]{:S(2)}, u32[]{:S(2)}) %all-to-all-start.3) | async-done | bytes 393248 | tf_op jit(solution)/shard_map/all_to_all | solution.py:253
  68.7 1.3 combine.1
  70.7 6.7 %all_to_all.67.got_ref = bf16[4,16,256]{2,1,0:T(8,128)(2,1)S(1)} all-to-all(bf16[4,16,256]{2,1,0:T(8,128)(2,1)S(1)} %broadcast_in_dim.30), channel_id=1, replica_groups=mesh['rows'=4,'y'=4,'z'=4,'core'=2] {'rows'}, dimensions={0} | all-to-all | bytes 65536 | tf_op jit(solution)/shard_map/all_to_all | solution.py:253
  77.4 1.1 copy-done.7
  78.7 9.3 %all_to_all.68.got_ref = bf16[8,8,1280]{2,1,0:T(8,128)(2,1)S(1)} all-to-all(bf16[8,8,1280]{2,1,0:T(8,128)(2,1)S(1)} %bitcast.19), channel_id=1, replica_groups=mesh['rows'=4,'y'=4,'z'=4,'core'=2] {'z','core'}, dimensions={0} | all-to-all | bytes 327680 | tf_op jit(solution)/shard_map/all_to_all | solution.py:253
  88.0 6.9 %all_to_all.69.got_ref = bf16[4,8,1280]{2,1,0:T(8,128)(2,1)S(1)} all-to-all(bf16[4,8,1280]{2,1,0:T(8,128)(2,1)S(1)} %sum_spread.4), channel_id=1, replica_groups=mesh['rows'=4,'y'=4,'z'=4,'core'=2] {'y'}, dimensions={0} | all-to-all | bytes 163840 | tf_op jit(solution)/shard_map/all_to_all | solution.py:253
  95.7 5.4 %all-to-all-start.7 = ((bf16[8,8,1280]{2,1,0:T(8,128)(2,1)}), bf16[8,8,1280]{2,1,0:T(8,128)(2,1)S(1)}, u32[]{:S(2)}, u32[]{:S(2)}) async-start(bf16[8,8,1280]{2,1,0:T(8,128)(2,1)} %sum_spread.5), calls=%async_computation.7 | async-start | bytes 327680 | tf_op jit(solution)/shard_map/all_to_all | solution.py:253
  101.0 5.6 %all-to-all-done.7 = bf16[8,8,1280]{2,1,0:T(8,128)(2,1)S(1)} async-done(((bf16[8,8,1280]{2,1,0:T(8,128)(2,1)}), bf16[8,8,1280]{2,1,0:T(8,128)(2,1)S(1)}, u32[]{:S(2)}, u32[]{:S(2)}) %all-to-all-start.7) | async-done | bytes 163872 | tf_op jit(solution)/shard_map/all_to_all | solution.py:253
  106.6 1.6 %copy-done.2 = bf16[1280,800]{0,1:T(8,128)(2,1)S(1)} copy-done((bf16[1280,800]{0,1:T(8,128)(2,1)S(1)}, bf16[1280,800]{0,1:T(8,128)(2,1)}, u32[]{:S(2)}) %copy-start.2) | copy-done | bytes 2048024
  108.2 1.3 gate_up.1
  109.5 7.7 %all_to_all.70.got_ref = bf16[4,16,1792]{2,1,0:T(8,128)(2,1)S(1)} all-to-all(bf16[4,16,1792]{2,1,0:T(8,128)(2,1)S(1)} %get-tuple-element.5), channel_id=1, replica_groups=mesh['rows'=4,'y'=4,'z'=4,'core'=2] {'rows'}, dimensions={0} | all-to-all | bytes 458752 | tf_op jit(solution)/shard_map/all_to_all | solution.py:253
  117.4 7.1 %all_to_all.71.got_ref = bf16[4,16,896]{2,1,0:T(8,128)(2,1)S(1)} all-to-all(bf16[4,16,896]{2,1,0:T(8,128)(2,1)S(1)} %activate.1), channel_id=1, replica_groups=mesh['rows'=4,'y'=4,'z'=4,'core'=2] {'rows'}, dimensions={0} | all-to-all | bytes 229376 | tf_op jit(solution)/shard_map/all_to_all | solution.py:253
  125.0 11.2 %all_to_all.72.got_ref = bf16[8,8,1280]{2,1,0:T(8,128)(2,1)S(1)} all-to-all(bf16[8,8,1280]{2,1,0:T(8,128)(2,1)S(1)} %bitcast.17), channel_id=1, replica_groups=mesh['rows'=4,'y'=4,'z'=4,'core'=2] {'z','core'}, dimensions={0} | all-to-all | bytes 327680 | tf_op jit(solution)/shard_map/all_to_all | solution.py:253
  136.2 6.9 %all_to_all.73.got_ref = bf16[4,8,1280]{2,1,0:T(8,128)(2,1)S(1)} all-to-all(bf16[4,8,1280]{2,1,0:T(8,128)(2,1)S(1)} %sum_spread.6), channel_id=1, replica_groups=mesh['rows'=4,'y'=4,'z'=4,'core'=2] {'y'}, dimensions={0} | all-to-all | bytes 163840 | tf_op jit(solution)/shard_map/all_to_all | solution.py:253
  143.2 10.0 %all_to_all.74 = bf16[8,8,1280]{2,1,0:T(8,128)(2,1)S(1)} all-to-all(bf16[8,8,1280]{2,1,0:T(8,128)(2,1)S(1)} %sum_spread.7), channel_id=1, replica_groups=mesh['rows'=4,'y'=4,'z'=4,'core'=2] {'z','core'}, dimensions={0} | all-to-all | bytes 327680 | tf_op jit(solution)/shard_map/all_to_all | solution.py:253
  (36 shorter events, 7.1 us)
Async XLA Ops:
  1.3 0.9 copy-start.4
  2.2 1.1 copy-start.6
  3.3 0.9 copy-start.8
  6.1 9.5 %all-to-all-start = ((f32[4,16,384]{2,1,0:T(8,128)}), f32[4,16,384]{2,1,0:T(8,128)S(1)}, u32[]{:S(2)}, u32[]{:S(2)}) async-start(f32[4,16,384]{2,1,0:T(8,128)} %project.1), calls=%async_computation | async-start | bytes 196608 | tf_op jit(solution)/shard_map/all_to_all | solution.py:253
  15.6 0.7 copy-start.9
  39.9 28.8 %copy-start = (bf16[4,8,16,384]{3,2,1,0:T(8,128)(2,1)S(1)}, bf16[4,8,16,384]{3,2,1,0:T(8,128)(2,1)}, u32[]{:S(2)}) copy-start(bf16[4,8,16,384]{3,2,1,0:T(8,128)(2,1)} %all_to_all.66) | copy-start | bytes 1179652
  39.9 28.8 %copy-start.10 = (bf16[128]{0:T(256)(128)(2,1)S(1)}, bf16[128]{0:T(256)(128)(2,1)}, u32[]{:S(2)}) copy-start(bf16[128]{0:T(256)(128)(2,1)} %param.21) | copy-start | bytes 772
  39.9 61.1 %copy-start.11 = (bf16[1280]{0:T(1024)(128)(2,1)S(1)}, bf16[1280]{0:T(1024)(128)(2,1)}, u32[]{:S(2)}) copy-start(bf16[1280]{0:T(1024)(128)(2,1)} %param.27) | copy-start | bytes 7684
  52.6 54.0 %copy-start.1 = (bf16[1280,800]{0,1:T(8,128)(2,1)S(1)}, bf16[1280,800]{0,1:T(8,128)(2,1)}, u32[]{:S(2)}) copy-start(bf16[1280,800]{0,1:T(8,128)(2,1)} %param.28) | copy-start | bytes 6144004
  52.6 54.0 %copy-start.5 = (bf16[64,1280]{1,0:T(8,128)(2,1)S(1)}, bf16[64,1280]{1,0:T(8,128)(2,1)}, u32[]{:S(2)}) copy-start(bf16[64,1280]{1,0:T(8,128)(2,1)} %hidden_ref.1) | copy-start | bytes 491524
  52.6 16.1 %all-to-all-start.3 = ((bf16[32,16,384]{2,1,0:T(8,128)(2,1)}), bf16[32,16,384]{2,1,0:T(8,128)(2,1)S(1)}, u32[]{:S(2)}, u32[]{:S(2)}) async-start(bf16[32,16,384]{2,1,0:T(8,128)(2,1)} %attend.1), calls=%async_computation.3 | async-start | bytes 786432 | tf_op jit(solution)/shard_map/all_to_all | solution.py:253
  77.4 1.1 copy-start.7
  95.7 11.0 %all-to-all-start.7 = ((bf16[8,8,1280]{2,1,0:T(8,128)(2,1)}), bf16[8,8,1280]{2,1,0:T(8,128)(2,1)S(1)}, u32[]{:S(2)}, u32[]{:S(2)}) async-start(bf16[8,8,1280]{2,1,0:T(8,128)(2,1)} %sum_spread.5), calls=%async_computation.7 | async-start | bytes 327680 | tf_op jit(solution)/shard_map/all_to_all | solution.py:253
  106.6 1.6 %copy-start.2 = (bf16[1280,800]{0,1:T(8,128)(2,1)S(1)}, bf16[1280,800]{0,1:T(8,128)(2,1)}, u32[]{:S(2)}) copy-start(bf16[1280,800]{0,1:T(8,128)(2,1)} %param.29) | copy-start | bytes 6144004
  108.2 16.4 %copy-start.3 = (bf16[800,1280]{1,0:T(8,128)(2,1)S(1)}, bf16[800,1280]{1,0:T(8,128)(2,1)}, u32[]{:S(2)}) copy-start(bf16[800,1280]{1,0:T(8,128)(2,1)} %w_ref.3) | copy-start | bytes 6144004

commit v2 on v1

v2 whole, which is shorter than its diff:
```python
import jax
import jax.numpy as jnp
import numpy as np
from jax import lax
from jax.experimental import pallas as pl
from jax.experimental.pallas import tpu as pltpu
from jax.sharding import PartitionSpec as P

MODEL_WIDTH = 5120
QUERY_HEADS = 64
KEY_VALUE_HEADS = 8
HEAD_WIDTH = 128
EPSILON = 1e-06
ROPE_BASE = 1000000.0
MASKED = -1e30
SCALE = HEAD_WIDTH ** (-0.5)

ROWS = 4
WIDE = 32
PACKED = 40
AT_ONCE = 4
OWN = 16
BLOCK = 256
HIDDEN_UNITS = 800
HALF = 896

f32 = jnp.float32
bf16 = jnp.bfloat16
VMEM = pl.BlockSpec(memory_space=pltpu.VMEM)
HBM = pl.BlockSpec(memory_space=pltpu.HBM)
SMEM = pl.BlockSpec(memory_space=pltpu.SMEM)
NT = (((1,), (1,)), ((), ()))


def call(kernel, out_shape, in_specs, scratch_shapes=(), limit=24, name=None):
    many = isinstance(out_shape, (tuple, list))
    return pl.pallas_call(
        kernel,
        out_shape=out_shape,
        in_specs=in_specs,
        out_specs=[VMEM] * len(out_shape) if many else VMEM,
        scratch_shapes=list(scratch_shapes),
        compiler_params=pltpu.CompilerParams(vmem_limit_bytes=limit << 20),
        name=name,
    )


def row_block(mine, k):
    return pl.ds(pl.multiple_of(lax.rem(mine + k, ROWS) * OWN, OWN), OWN)


def terms(value, count):
    out = []
    for _ in range(count):
        out.append(value.astype(bf16).astype(f32))
        value = value - out[-1]
    return out


def swap_halves(value):
    half = HEAD_WIDTH // 2
    return jnp.concatenate([value[..., half:], value[..., :half]], axis=-1)


def norm_rope(value, straight, swapped):
    value = value * lax.rsqrt(jnp.mean(value * value, axis=-1, keepdims=True) + EPSILON)
    return value * straight + swap_halves(value) * swapped


def pack(value):
    return jnp.concatenate([value[:8], value[8:]], axis=1)


def unpack(value):
    return jnp.concatenate([value[:, :64], value[:, 64:]], axis=0)


def project_kernel(mine_ref, hidden_hbm, gain_ref, wq_hbm, wkv_hbm, *rest):
    outs, (whole, hidden_ref, wq_ref, wkv_ref, sems) = rest[:ROWS], rest[ROWS:]
    moves = [
        pltpu.make_async_copy(source, target, sems.at[at])
        for at, (source, target) in enumerate(
            ((hidden_hbm, hidden_ref), (wkv_hbm, wkv_ref), (wq_hbm, wq_ref))
        )
    ]
    for move in moves:
        move.start()
    moves[0].wait()
    hidden = hidden_ref[...].astype(f32)
    square = jnp.sum(hidden * hidden, axis=1, keepdims=True)
    scaled = (hidden * gain_ref[...].astype(f32)).astype(bf16)
    moves[1].wait()
    keyval = lax.dot_general(scaled, wkv_ref[...], NT, preferred_element_type=f32)
    whole[:, 256:] = jnp.concatenate([keyval, jnp.broadcast_to(square, keyval.shape)], axis=1)
    moves[2].wait()
    whole[:, :256] = jnp.dot(scaled, wq_ref[...], preferred_element_type=f32)
    mine = mine_ref[0]
    for k in range(ROWS):
        outs[k][...] = whole[row_block(mine, k), :]


def heads_kernel(a_ref, b_ref, c_ref, d_ref, straight_ref, swapped_ref, out_ref):
    total = (a_ref[...] + b_ref[...]) + (c_ref[...] + d_ref[...])
    inverse = lax.rsqrt(total[:, 320:321] / MODEL_WIDTH + EPSILON)
    scaled = total * inverse
    straight, swapped = straight_ref[0], swapped_ref[0]
    parts = [
        norm_rope(scaled[:, j * 128 : (j + 1) * 128], straight, swapped) for j in range(2)
    ]
    parts.append(pack(scaled[:, 256:320]))
    out = jnp.concatenate(parts, axis=0).astype(bf16)
    out_ref[...] = jnp.broadcast_to(out[None], out_ref.shape)


def attend_kernel(
    length_ref,
    block_ref,
    g_ref,
    k_hbm,
    v_hbm,
    o_ref,
    k_scr,
    v_scr,
    q_scr,
    p_scr,
    w_scr,
    n_scr,
    s_scr,
    k_sems,
    v_sems,
):
    def k_move(b):
        return pltpu.make_async_copy(k_hbm.at[b], k_scr.at[b], k_sems.at[b])

    def v_move(b):
        return pltpu.make_async_copy(v_hbm.at[b], v_scr.at[b], v_sems.at[b])

    for b in range(OWN):
        k_move(b).start()
    for b in range(OWN):
        v_move(b).start()

    for head in range(QUERY_HEADS):
        w, j = divmod(head, 2)
        q_scr[pl.ds(head, OWN, stride=QUERY_HEADS), :] = g_ref[
            w, j * OWN : (j + 1) * OWN, :
        ].astype(f32)

    def rows_of(b, start, size):
        return pl.ds(pl.multiple_of(b * QUERY_HEADS + start, 16), size)

    def limit(b):
        return length_ref[b] - block_ref[b] * BLOCK

    row = lax.broadcasted_iota(jnp.int32, (16, 256), 0)
    lane = lax.broadcasted_iota(jnp.int32, (16, 256), 1)
    own_half = (row < 8) == (lane < 128)
    slot = lax.broadcasted_iota(jnp.int32, (QUERY_HEADS, 256), 1)
    place = lax.rem(lax.broadcasted_iota(jnp.int32, (QUERY_HEADS, 128), 1), 8)

    @pl.loop(0, OWN // AT_ONCE)
    def _(step):
        for u in range(AT_ONCE):
            k_move(step * AT_ONCE + u).wait()
        for u in range(AT_ONCE):
            b = step * AT_ONCE + u
            for p in range(4):
                here = rows_of(b, 16 * p, 16)
                pair = q_scr[here, :]
                query = jnp.where(own_half, jnp.concatenate([pair, pair], axis=1), 0.0)
                p_scr[here, :] = lax.dot_general(
                    query.astype(bf16),
                    k_scr[b, :, 256 * p : 256 * p + 256],
                    NT,
                    preferred_element_type=f32,
                )

    @pl.loop(0, OWN // AT_ONCE)
    def _(step):
        for u in range(AT_ONCE):
            b = step * AT_ONCE + u
            here = rows_of(b, 0, QUERY_HEADS)
            visible = slot < limit(b)
            scores = jnp.where(visible, p_scr[here, :] * SCALE, MASKED)
            shift = jnp.max(scores, axis=1, keepdims=True).astype(bf16).astype(f32)
            weights = jnp.where(visible, jnp.exp(scores - shift), 0.0)
            total = jnp.sum(weights, axis=1, keepdims=True)
            w_scr[here, :] = weights.astype(bf16)
            stats = jnp.where(place == 0, shift, 0.0)
            for at, term in enumerate(terms(total, 2)):
                stats = jnp.where(place == at + 1, term, stats)
            s_scr[here, :] = stats

    @pl.loop(0, OWN // AT_ONCE)
    def _(step):
        for u in range(AT_ONCE):
            v_move(step * AT_ONCE + u).wait()
        for u in range(AT_ONCE):
            b = step * AT_ONCE + u
            for p in range(4):
                here = rows_of(b, 16 * p, 16)
                both = jnp.dot(
                    w_scr[here, :],
                    v_scr[b, :, 256 * p : 256 * p + 256],
                    preferred_element_type=f32,
                )
                n_scr[here, :] = jnp.concatenate([both[:8, :128], both[8:, 128:]], axis=0)

    lane = lax.broadcasted_iota(jnp.int32, (OWN, 128), 1)
    first = lax.rem(lane, 64) < 8
    for w in range(WIDE):
        rows = [pl.ds(2 * w + j, OWN, stride=QUERY_HEADS) for j in range(2)]
        for j in range(2):
            o_ref[w, j * OWN : (j + 1) * OWN, :] = n_scr[rows[j], :].astype(bf16)
        stats = jnp.where(first, s_scr[rows[0], :], s_scr[rows[1], :])
        o_ref[w, 2 * OWN :, :] = jnp.where(lane[:8] < 64, stats[:8], stats[8:]).astype(bf16)


def combine_kernel(wide_ref, r_ref, g_ref, straight_ref, swapped_ref, out_ref, again_ref):
    wide = wide_ref[0]
    group = wide // 4

    def half(source):
        return unpack(g_ref[source, 2 * OWN :, :].astype(f32))

    key = jnp.concatenate([half(2 * group), half(2 * group + 1)], axis=1)
    value = jnp.concatenate([half(16 + 2 * group), half(17 + 2 * group)], axis=1)
    key = norm_rope(key, straight_ref[1], swapped_ref[1]).astype(bf16).astype(f32)
    stats = r_ref[:, 2 * OWN :, :].astype(f32)

    def stat(at):
        return jnp.concatenate(
            [stats[:, :, at : at + 1], stats[:, :, 64 + at : 65 + at]], axis=1
        )

    for j in range(2):
        lanes = slice(j * 128, (j + 1) * 128)
        here = slice(j * OWN, (j + 1) * OWN)
        query = g_ref[wide, here, :].astype(f32)
        fresh = jnp.sum(query * key, axis=1, keepdims=True) * SCALE
        shifts = stat(8 * j)
        totals = stat(8 * j + 1) + stat(8 * j + 2)
        highest = jnp.maximum(jnp.max(shifts, axis=0), fresh)
        factors = jnp.exp(shifts - highest[None])
        fresh_weight = jnp.exp(fresh - highest)
        weight_sum = jnp.sum(factors * totals, axis=0) + fresh_weight
        numer = jnp.sum(r_ref[:, here, :].astype(f32) * factors, axis=0)
        numer = numer + fresh_weight.astype(bf16).astype(f32) * value
        heads = (numer / weight_sum).astype(bf16)
        out_ref[:, lanes] = heads
        again_ref[:, lanes] = heads


def output_kernel(a_ref, b_ref, c_ref, d_ref, w_ref, out_ref):
    heads = jnp.concatenate([a_ref[...], b_ref[...], c_ref[...], d_ref[...]], axis=0)
    out_ref[...] = jnp.dot(heads, w_ref[...], preferred_element_type=f32).astype(bf16)


def gate_up_kernel(mine_ref, hidden_ref, attended_ref, gain_ref, wg_ref, wu_ref, stream_ref, *outs):
    mine = mine_ref[0]
    for k in range(ROWS):
        at = slice(k * OWN, (k + 1) * OWN)
        stream_ref[at, :] = hidden_ref[row_block(mine, k), :].astype(f32) + attended_ref[
            at, :
        ].astype(f32)
    stream = stream_ref[...]
    square = jnp.sum(stream * stream, axis=1, keepdims=True)
    scaled = (stream * gain_ref[...].astype(f32)).astype(bf16)
    gate = lax.dot_general(scaled, wg_ref[...], NT, preferred_element_type=f32).astype(bf16)
    up = lax.dot_general(scaled, wu_ref[...], NT, preferred_element_type=f32).astype(bf16)
    pad = HALF - HIDDEN_UNITS
    place = lax.broadcasted_iota(jnp.int32, (stream.shape[0], pad), 1)
    norm = jnp.zeros(place.shape, f32)
    for at, term in enumerate(terms(square, 3)):
        norm = jnp.where(place == at, term, norm)
    norm = norm.astype(bf16)
    for k in range(ROWS):
        at = slice(k * OWN, (k + 1) * OWN)
        outs[k][...] = jnp.concatenate([gate[at], norm[at], up[at], norm[at]], axis=1)


def activate_kernel(a_ref, b_ref, c_ref, d_ref, out_ref):
    total = (a_ref[...].astype(f32) + b_ref[...].astype(f32)) + (
        c_ref[...].astype(f32) + d_ref[...].astype(f32)
    )
    square = (
        total[:, HIDDEN_UNITS : HIDDEN_UNITS + 1]
        + total[:, HIDDEN_UNITS + 1 : HIDDEN_UNITS + 2]
        + total[:, HIDDEN_UNITS + 2 : HIDDEN_UNITS + 3]
    )
    inverse = lax.rsqrt(square / MODEL_WIDTH + EPSILON)
    gate = total[:, :HALF] * inverse
    up = total[:, HALF:] * inverse
    out_ref[...] = (gate / (1.0 + jnp.exp(-gate)) * up).astype(bf16)


def down_kernel(a_ref, b_ref, c_ref, d_ref, w_ref, out_ref):
    units = jnp.concatenate([a_ref[...], b_ref[...], c_ref[...], d_ref[...]], axis=0)
    out_ref[...] = jnp.dot(
        units[:, :HIDDEN_UNITS], w_ref[...], preferred_element_type=f32
    ).astype(bf16)


def final_kernel(mine_ref, stream_ref, down_ref, out_ref):
    mine = mine_ref[0]
    for k in range(ROWS):
        at = slice(k * OWN, (k + 1) * OWN)
        out_ref[row_block(mine, k), :] = (stream_ref[at, :] + down_ref[at, :].astype(f32)).astype(
            bf16
        )


def to_rows(blocks):
    got = [blocks[0]]
    for k in range(1, ROWS):
        got.append(lax.ppermute(blocks[k], "rows", [(i, (i + k) % ROWS) for i in range(ROWS)]))
    return got


def from_rows(own):
    got = [own]
    for k in range(1, ROWS):
        got.append(lax.ppermute(own, "rows", [((i + k) % ROWS, i) for i in range(ROWS)]))
    return got


def exchange(blocks):
    return lax.all_to_all(blocks, "wide", split_axis=0, concat_axis=0, tiled=True)


def sum_wide(part):
    height, width = part.shape
    got = exchange(part.reshape(WIDE, height // WIDE, width))
    total = jnp.sum(got.astype(f32), axis=0).astype(bf16)
    return exchange(jnp.broadcast_to(total[None], got.shape)).reshape(height, width)


def body(
    hidden,
    attn_gain,
    w_query,
    w_keyval,
    query_gain,
    key_norm_gain,
    keys_cache,
    values_cache,
    lengths,
    block_index,
    w_out,
    mlp_gain,
    w_gate,
    w_up,
    w_down,
):
    mine = lax.axis_index("rows").astype(jnp.int32).reshape(1)
    wide = lax.axis_index("wide").astype(jnp.int32).reshape(1)
    sds = jax.ShapeDtypeStruct

    half = HEAD_WIDTH // 2
    frequency = np.power(ROPE_BASE, -(np.arange(half) * 2.0 / HEAD_WIDTH)).astype(np.float32)
    angles = lengths.astype(f32)[:, None] * jnp.asarray(frequency)[None, :]
    cosine, sine = jnp.cos(angles), jnp.sin(angles)
    gains = jnp.stack([query_gain, key_norm_gain]).astype(f32)[:, None, :]
    straight = gains * jnp.concatenate([cosine, cosine], axis=1)
    swapped = swap_halves(gains) * jnp.concatenate([-sine, sine], axis=1)

    blocks = call(
        project_kernel,
        [sds((OWN, 384), f32)] * ROWS,
        [SMEM, HBM, VMEM, HBM, HBM],
        [
            pltpu.VMEM((64, 384), f32),
            pltpu.VMEM(hidden.shape, bf16),
            pltpu.VMEM(w_query.shape, bf16),
            pltpu.VMEM(w_keyval.shape[::-1], bf16),
            pltpu.SemaphoreType.DMA((3,)),
        ],
        limit=60,
        name="project",
    )(mine, hidden, attn_gain[None], w_query, w_keyval.T)
    payload = call(
        heads_kernel, sds((WIDE, PACKED, 128), bf16), [VMEM] * 6, limit=8, name="heads"
    )(*to_rows(blocks), straight, swapped)
    gathered = exchange(payload)

    parts = call(
        attend_kernel,
        sds((WIDE, PACKED, 128), bf16),
        [SMEM, SMEM, VMEM, HBM, HBM],
        [
            pltpu.VMEM(keys_cache.shape, bf16),
            pltpu.VMEM(values_cache.shape, bf16),
            pltpu.VMEM((OWN * QUERY_HEADS, 128), f32),
            pltpu.VMEM((OWN * QUERY_HEADS, 256), f32),
            pltpu.VMEM((OWN * QUERY_HEADS, 256), bf16),
            pltpu.VMEM((OWN * QUERY_HEADS, 128), f32),
            pltpu.VMEM((OWN * QUERY_HEADS, 128), f32),
            pltpu.SemaphoreType.DMA((OWN,)),
            pltpu.SemaphoreType.DMA((OWN,)),
        ],
        limit=57,
        name="attend",
    )(lengths, block_index.reshape(OWN), gathered, keys_cache, values_cache)
    heads_out, heads_own = call(
        combine_kernel, [sds((OWN, 256), bf16)] * 2, [SMEM] + [VMEM] * 4, limit=8, name="combine"
    )(wide, exchange(parts), gathered, straight, swapped)

    out_part = call(output_kernel, sds((64, 1280), bf16), [VMEM] * 5, limit=8, name="output")(
        *from_rows(heads_own), w_out
    )
    attended = sum_wide(out_part)

    stream, *blocks = call(
        gate_up_kernel,
        [sds((64, 1280), f32)] + [sds((OWN, 2 * HALF), bf16)] * ROWS,
        [SMEM] + [VMEM] * 5,
        limit=16,
        name="gate_up",
    )(mine, hidden, attended, mlp_gain[None], w_gate.T, w_up.T)
    activated = call(
        activate_kernel, sds((OWN, HALF), bf16), [VMEM] * 4, limit=8, name="activate"
    )(*to_rows(blocks))
    down_part = call(down_kernel, sds((64, 1280), bf16), [VMEM] * 5, limit=8, name="down")(
        *from_rows(activated), w_down
    )
    layer_out = call(final_kernel, sds((64, 1280), bf16), [SMEM] + [VMEM] * 2, limit=8, name="final")(
        mine, stream, sum_wide(down_part)
    )
    return (layer_out, heads_out)


def solution(mesh):
    in_specs = (
        P(None, "rows"),
        P("rows"),
        P("rows", "wide"),
        P("rows", "wide"),
        P(),
        P(),
        P("rows", "wide", None),
        P("rows", "wide", None),
        P("rows"),
        P("rows", "wide"),
        P("wide", "rows"),
        P("rows"),
        P("rows", "wide"),
        P("rows", "wide"),
        P("wide", "rows"),
    )
    out_specs = (P(None, "rows"), P("rows", "wide"))
    return jax.shard_map(body, mesh=mesh, in_specs=in_specs, out_specs=out_specs, check_vma=False)
```

time: 155 us -> 135 us (0.87)
  blocking collectives: 89.2 us -> 58 us
  starting transfers between devices: 15.9 us -> 23.8 us
  waiting for transfers between devices: 19.1 us -> 25.2 us
  local copies, waits for them, and re-layouts: 7.69 us -> 4.8 us
  other arithmetic: 1.51 us -> 3.26 us
    all_to_all x10 -> x4, blocking collectives: 89.2 us -> 58 us  [exchange(): lax.all_to_all(blocks, 'wide', split_axis=0, concat_axis=0, tiled=True)]
    ppermute x0 -> x12, starting transfers between devices: none -> 16.1 us  [the longest x6 9.41 us: to_rows(): lax.ppermute(blocks[k], 'rows', [(i, (i + k) % ROWS) for i in range(ROWS)])]
    all_to_all x3 -> x2, starting transfers between devices: 15.9 us -> 7.68 us  [exchange(): lax.all_to_all(blocks, 'wide', split_axis=0, concat_axis=0, tiled=True)]
    ppermute x0 -> x12, waiting for transfers between devices: none -> 7.51 us  [the longest x6 5.23 us: from_rows(): lax.ppermute(own, 'rows', [((i + k) % ROWS, i) for i in range(ROWS)])]
    unnamed x24 -> x16, local copies, waits for them, and re-layouts: 6.26 us -> 2.33 us
    all_to_all x3 -> x2, waiting for transfers between devices: 19.1 us -> 17.7 us  [exchange(): lax.all_to_all(blocks, 'wide', split_axis=0, concat_axis=0, tiled=True)]
    pallas_call x13 -> x9, Pallas kernels: 19.8 us -> 18.9 us  [the longest x1 11.5 us: body(): call(attend_kernel, sds((WIDE, PACKED, 128), bf16), [SMEM, SMEM, VMEM, HB...]
  transfers between devices with their start and end apart: 3 -> 14, of which waited for: 3 -> 7; matrix products, arithmetic and copies ran while one was open for 1% -> 2% of each run, Pallas kernels for 0% -> 0%
where the time goes in v2:
time: 135 us
  blocking collectives  58 us (43%)
  waiting for transfers between devices  25.2 us (19%)
  starting transfers between devices  23.8 us (18%)
  Pallas kernels  18.9 us (14%)
  local copies, waits for them, and re-layouts  4.8 us (4%)
  other arithmetic  3.26 us (2%)
    all_to_all x4, blocking collectives, exchange(): lax.all_to_all(blocks, 'wide', split_axis=0, concat_axis=0, tiled=True)  58 us
    all_to_all x2, waiting for transfers between devices, exchange(): lax.all_to_all(blocks, 'wide', split_axis=0, concat_axis=0, tiled=True)  17.7 us
    pallas_call x1, Pallas kernels, body(): call(attend_kernel, sds((WIDE, PACKED, 128), bf16), [SMEM, SMEM, VMEM, HB...  11.5 us
    ppermute x6, starting transfers between devices, to_rows(): lax.ppermute(blocks[k], 'rows', [(i, (i + k) % ROWS) for i in range(ROWS)])  9.41 us
    all_to_all x2, starting transfers between devices, exchange(): lax.all_to_all(blocks, 'wide', split_axis=0, concat_axis=0, tiled=True)  7.68 us
    ppermute x6, starting transfers between devices, from_rows(): lax.ppermute(own, 'rows', [((i + k) % ROWS, i) for i in range(ROWS)])  6.73 us
    ppermute x6, waiting for transfers between devices, from_rows(): lax.ppermute(own, 'rows', [((i + k) % ROWS, i) for i in range(ROWS)])  5.23 us
    pallas_call x1, Pallas kernels, body(): call(project_kernel, [sds((OWN, 384), f32)] * ROWS, [SMEM, HBM, VMEM, HBM...  2.89 us
  transfers between devices with their start and end apart: 14, of which 7 were waited for; matrix products, arithmetic and copies ran while one was open for 2% of the time, Pallas kernels for 0%

profile of v2, /device:TPU:1, one launch (start us, length us, event | category | flops | bytes accessed | tf_op | source)
XLA Modules:
  0.0 134.8 jit_solution(5666353067206297438)
XLA Ops:
  0.6 1.3 broadcast_in_dim.8.gain_ref
  1.9 2.9 %project.1 = (f32[16,384]{1,0:T(8,128)}, f32[16,384]{1,0:T(8,128)}, f32[16,384]{1,0:T(8,128)}, f32[16,384]{1,0:T(8,128)}) custom-call(s32[1]{0:T(128)} %bitcast.mine_ref, bf16[64,1280]{1,0:T(8,128)(2,1)} %hidden_ref.1, bf16[1,1280]{1,0:T(2,128)(2,1)} %broadcast_in_dim.8.gain_ref, bf16[1280,256]{1,0:T(8,128)(2,1)} %wq_hbm.1, bf16[64,1280]{1,0:T(8,128)(2,1)} %bitcast.13), custom_call_target="tpu_custom_call" | custom-call | tf_op jit(solution)/shard_map/project/pallas_call | solution.py:367
  4.8 2.1 %collective-permute-start = (f32[16,384]{1,0:T(8,128)}, f32[16,384]{1,0:T(8,128)S(1)}, u32[]{:S(2)}, u32[]{:S(2)}) collective-permute-start(f32[16,384]{1,0:T(8,128)} %get-tuple-element.14), channel_id=1, source_target_pairs={{0,32},{32,64},{64,96},{96,0},{1,33},{33,65},{65,97},{97,1},{2,34}... | collective-permute-start | bytes 73736 | tf_op jit(solution)/shard_map/ppermute | solution.py:316
  6.9 2.5 %collective-permute-start.1 = (f32[16,384]{1,0:T(8,128)}, f32[16,384]{1,0:T(8,128)S(1)}, u32[]{:S(2)}, u32[]{:S(2)}) collective-permute-start(f32[16,384]{1,0:T(8,128)} %get-tuple-element.15), channel_id=1, source_target_pairs={{0,64},{32,96},{64,0},{96,32},{1,65},{33,97},{65,1},{97,33},{2,66}... | collective-permute-start | bytes 73736 | tf_op jit(solution)/shard_map/ppermute | solution.py:316
  14.6 19.2 %all_to_all.30.g_ref = bf16[32,40,128]{2,1,0:T(8,128)(2,1)} all-to-all(bf16[32,40,128]{2,1,0:T(8,128)(2,1)S(1)} %heads.1), channel_id=1, replica_groups=mesh['rows'=4,'wide'=32] {'wide'}, dimensions={0} | all-to-all | bytes 655360 | tf_op jit(solution)/shard_map/all_to_all | solution.py:328
  33.8 11.5 %attend.1 = bf16[32,40,128]{2,1,0:T(8,128)(2,1)} custom-call(s32[16]{0:T(128)} %length_ref.1, s32[16]{0:T(128)} %bitcast.19, bf16[32,40,128]{2,1,0:T(8,128)(2,1)} %all_to_all.30.g_ref, bf16[16,256,1024]{2,1,0:T(8,128)(2,1)} %k_hbm.1, bf16[16,256,1024]{2,1,0:T(8,128)(2,1)} %v_hbm.1), custom_call_target="tpu_custom_call" | custom-call | tf_op jit(solution)/shard_map/attend/pallas_call | solution.py:386
  45.3 3.8 %all-to-all-start.1 = ((bf16[32,40,128]{2,1,0:T(8,128)(2,1)}), bf16[32,40,128]{2,1,0:T(8,128)(2,1)S(1)}, u32[]{:S(2)}, u32[]{:S(2)}) async-start(bf16[32,40,128]{2,1,0:T(8,128)(2,1)} %attend.1), calls=%async_computation.1 | async-start | bytes 655360 | tf_op jit(solution)/shard_map/all_to_all | solution.py:328
  49.1 9.6 %all-to-all-done.1.r_ref = bf16[32,40,128]{2,1,0:T(8,128)(2,1)S(1)} async-done(((bf16[32,40,128]{2,1,0:T(8,128)(2,1)}), bf16[32,40,128]{2,1,0:T(8,128)(2,1)S(1)}, u32[]{:S(2)}, u32[]{:S(2)}) %all-to-all-start.1) | async-done | bytes 327712 | tf_op jit(solution)/shard_map/all_to_all | solution.py:328
  58.7 1.4 %combine.1 = (bf16[16,256]{1,0:T(8,128)(2,1)}, bf16[16,256]{1,0:T(8,128)(2,1)S(1)}) custom-call(s32[1]{0:T(128)} %bitcast.1.wide_ref, bf16[32,40,128]{2,1,0:T(8,128)(2,1)S(1)} %all-to-all-done.1.r_ref, bf16[32,40,128]{2,1,0:T(8,128)(2,1)S(1)} %copy-done, f32[2,16,128]{2,1,0:T(8,128)S(1)} %broadcast_multiply_fusion.1.straight_ref, ...), custom_call_target="tpu_custom_call" | custom-call | tf_op jit(solution)/shard_map/combine/pallas_call | solution.py:404
  60.1 1.9 %collective-permute-start.3 = (bf16[16,256]{1,0:T(8,128)(2,1)S(1)}, bf16[16,256]{1,0:T(8,128)(2,1)S(1)}, u32[]{:S(2)}, u32[]{:S(2)}) collective-permute-start(bf16[16,256]{1,0:T(8,128)(2,1)S(1)} %get-tuple-element.17.a_ref), channel_id=1, source_target_pairs={{32,0},{64,32},{96,64},{0,96},{33,1},{65,33},{97,65},{1,97},{34,2}... | collective-permute-start | bytes 24584 | tf_op jit(solution)/shard_map/ppermute | solution.py:323
  62.8 3.2 %collective-permute-done.4.c_ref = bf16[16,256]{1,0:T(8,128)(2,1)S(1)} collective-permute-done((bf16[16,256]{1,0:T(8,128)(2,1)S(1)}, bf16[16,256]{1,0:T(8,128)(2,1)S(1)}, u32[]{:S(2)}, u32[]{:S(2)}) %collective-permute-start.4) | collective-permute-done | bytes 8224 | tf_op jit(solution)/shard_map/ppermute | solution.py:323
  66.4 13.0 %all_to_all.31 = bf16[32,2,1280]{2,1,0:T(2,128)(2,1)S(1)} all-to-all(bf16[32,2,1280]{2,1,0:T(2,128)(2,1)S(1)} %reshape.69), channel_id=1, replica_groups=mesh['rows'=4,'wide'=32] {'wide'}, dimensions={0} | all-to-all | bytes 327680 | tf_op jit(solution)/shard_map/all_to_all | solution.py:328
  80.2 3.9 %all-to-all-start.3 = ((bf16[32,2,1280]{2,1,0:T(2,128)(2,1)}), bf16[32,2,1280]{2,1,0:T(2,128)(2,1)S(1)}, u32[]{:S(2)}, u32[]{:S(2)}) async-start(bf16[32,2,1280]{2,1,0:T(2,128)(2,1)} %broadcast_in_dim.9), calls=%async_computation.3 | async-start | bytes 327680 | tf_op jit(solution)/shard_map/all_to_all | solution.py:328
  84.1 8.1 %all-to-all-done.3 = bf16[32,2,1280]{2,1,0:T(2,128)(2,1)S(1)} async-done(((bf16[32,2,1280]{2,1,0:T(2,128)(2,1)}), bf16[32,2,1280]{2,1,0:T(2,128)(2,1)S(1)}, u32[]{:S(2)}, u32[]{:S(2)}) %all-to-all-start.3) | async-done | bytes 163872 | tf_op jit(solution)/shard_map/all_to_all | solution.py:328
  92.3 1.6 %copy-done.2 = bf16[1280,800]{0,1:T(8,128)(2,1)S(1)} copy-done((bf16[1280,800]{0,1:T(8,128)(2,1)S(1)}, bf16[1280,800]{0,1:T(8,128)(2,1)}, u32[]{:S(2)}) %copy-start.2) | copy-done | bytes 2048024
  93.9 1.3 gate_up.1
  95.3 1.7 %collective-permute-start.7 = (bf16[16,1792]{1,0:T(8,128)(2,1)S(1)}, bf16[16,1792]{1,0:T(8,128)(2,1)S(1)}, u32[]{:S(2)}, u32[]{:S(2)}) collective-permute-start(bf16[16,1792]{1,0:T(8,128)(2,1)S(1)} %get-tuple-element.21), channel_id=1, source_target_pairs={{0,64},{32,96},{64,0},{96,32},{1,65},{33,97},{65,1},{97,33},{2,66}... | collective-permute-start | bytes 172040 | tf_op jit(solution)/shard_map/ppermute | solution.py:316
  97.0 1.9 %collective-permute-start.8 = (bf16[16,1792]{1,0:T(8,128)(2,1)S(1)}, bf16[16,1792]{1,0:T(8,128)(2,1)S(1)}, u32[]{:S(2)}, u32[]{:S(2)}) collective-permute-start(bf16[16,1792]{1,0:T(8,128)(2,1)S(1)} %get-tuple-element.22), channel_id=1, source_target_pairs={{0,96},{32,0},{64,32},{96,64},{1,97},{33,1},{65,33},{97,65},{2,98}... | collective-permute-start | bytes 172040 | tf_op jit(solution)/shard_map/ppermute | solution.py:316
  98.9 2.3 %collective-permute-done.6.b_ref = bf16[16,1792]{1,0:T(8,128)(2,1)S(1)} collective-permute-done((bf16[16,1792]{1,0:T(8,128)(2,1)S(1)}, bf16[16,1792]{1,0:T(8,128)(2,1)S(1)}, u32[]{:S(2)}, u32[]{:S(2)}) %collective-permute-start.6) | collective-permute-done | bytes 57376 | tf_op jit(solution)/shard_map/ppermute | solution.py:316
  101.4 1.6 %collective-permute-start.10 = (bf16[16,896]{1,0:T(8,128)(2,1)S(1)}, bf16[16,896]{1,0:T(8,128)(2,1)S(1)}, u32[]{:S(2)}, u32[]{:S(2)}) collective-permute-start(bf16[16,896]{1,0:T(8,128)(2,1)S(1)} %activate.1.a_ref), channel_id=1, source_target_pairs={{64,0},{96,32},{0,64},{32,96},{65,1},{97,33},{1,65},{33,97},{66,2}... | collective-permute-start | bytes 86024 | tf_op jit(solution)/shard_map/ppermute | solution.py:323
  102.9 1.5 %collective-permute-start.11 = (bf16[16,896]{1,0:T(8,128)(2,1)S(1)}, bf16[16,896]{1,0:T(8,128)(2,1)S(1)}, u32[]{:S(2)}, u32[]{:S(2)}) collective-permute-start(bf16[16,896]{1,0:T(8,128)(2,1)S(1)} %activate.1.a_ref), channel_id=1, source_target_pairs={{96,0},{0,32},{32,64},{64,96},{97,1},{1,33},{33,65},{65,97},{98,2}... | collective-permute-start | bytes 86024 | tf_op jit(solution)/shard_map/ppermute | solution.py:323
  104.4 1.2 collective-permute-start.9
  108.0 14.3 %all_to_all.32 = bf16[32,2,1280]{2,1,0:T(2,128)(2,1)S(1)} all-to-all(bf16[32,2,1280]{2,1,0:T(2,128)(2,1)S(1)} %reshape.71), channel_id=1, replica_groups=mesh['rows'=4,'wide'=32] {'wide'}, dimensions={0} | all-to-all | bytes 327680 | tf_op jit(solution)/shard_map/all_to_all | solution.py:328
  122.5 11.6 %all_to_all.33 = bf16[32,2,1280]{2,1,0:T(2,128)(2,1)S(1)} all-to-all(bf16[32,2,1280]{2,1,0:T(2,128)(2,1)S(1)} %broadcast_in_dim.11), channel_id=1, replica_groups=mesh['rows'=4,'wide'=32] {'wide'}, dimensions={0} | all-to-all | bytes 327680 | tf_op jit(solution)/shard_map/all_to_all | solution.py:328
  (52 shorter events, 10.9 us)
Async XLA Ops:
  4.8 8.8 %collective-permute-start = (f32[16,384]{1,0:T(8,128)}, f32[16,384]{1,0:T(8,128)S(1)}, u32[]{:S(2)}, u32[]{:S(2)}) collective-permute-start(f32[16,384]{1,0:T(8,128)} %get-tuple-element.14), channel_id=1, source_target_pairs={{0,32},{32,64},{64,96},{96,0},{1,33},{33,65},{65,97},{97,1},{2,34}... | collective-permute-start | bytes 73736 | tf_op jit(solution)/shard_map/ppermute | solution.py:316
  6.9 6.7 %collective-permute-start.1 = (f32[16,384]{1,0:T(8,128)}, f32[16,384]{1,0:T(8,128)S(1)}, u32[]{:S(2)}, u32[]{:S(2)}) collective-permute-start(f32[16,384]{1,0:T(8,128)} %get-tuple-element.15), channel_id=1, source_target_pairs={{0,64},{32,96},{64,0},{96,32},{1,65},{33,97},{65,1},{97,33},{2,66}... | collective-permute-start | bytes 73736 | tf_op jit(solution)/shard_map/ppermute | solution.py:316
  9.4 4.2 %collective-permute-start.2 = (f32[16,384]{1,0:T(8,128)}, f32[16,384]{1,0:T(8,128)S(1)}, u32[]{:S(2)}, u32[]{:S(2)}) collective-permute-start(f32[16,384]{1,0:T(8,128)} %get-tuple-element.16), channel_id=1, source_target_pairs={{0,96},{32,0},{64,32},{96,64},{1,97},{33,1},{65,33},{97,65},{2,98}... | collective-permute-start | bytes 73736 | tf_op jit(solution)/shard_map/ppermute | solution.py:316
  13.6 0.7 copy-start.6
  33.8 25.0 %copy-start = (bf16[32,40,128]{2,1,0:T(8,128)(2,1)S(1)}, bf16[32,40,128]{2,1,0:T(8,128)(2,1)}, u32[]{:S(2)}) copy-start(bf16[32,40,128]{2,1,0:T(8,128)(2,1)} %all_to_all.30.g_ref) | copy-start | bytes 983044
  33.8 32.3 %copy-start.5 = (bf16[256,1280]{1,0:T(8,128)(2,1)S(1)}, bf16[256,1280]{1,0:T(8,128)(2,1)}, u32[]{:S(2)}) copy-start(bf16[256,1280]{1,0:T(8,128)(2,1)} %w_ref.2) | copy-start | bytes 1966084
  45.3 47.0 %copy-start.1 = (bf16[1280,800]{0,1:T(8,128)(2,1)S(1)}, bf16[1280,800]{0,1:T(8,128)(2,1)}, u32[]{:S(2)}) copy-start(bf16[1280,800]{0,1:T(8,128)(2,1)} %param.28) | copy-start | bytes 6144004
  45.3 47.0 %copy-start.4 = (bf16[64,1280]{1,0:T(8,128)(2,1)S(1)}, bf16[64,1280]{1,0:T(8,128)(2,1)}, u32[]{:S(2)}) copy-start(bf16[64,1280]{1,0:T(8,128)(2,1)} %hidden_ref.1) | copy-start | bytes 491524
  45.3 13.4 %all-to-all-start.1 = ((bf16[32,40,128]{2,1,0:T(8,128)(2,1)}), bf16[32,40,128]{2,1,0:T(8,128)(2,1)S(1)}, u32[]{:S(2)}, u32[]{:S(2)}) async-start(bf16[32,40,128]{2,1,0:T(8,128)(2,1)} %attend.1), calls=%async_computation.1 | async-start | bytes 655360 | tf_op jit(solution)/shard_map/all_to_all | solution.py:328
  60.1 24.0 %copy-start.7 = (bf16[1280]{0:T(1024)(128)(2,1)S(1)}, bf16[1280]{0:T(1024)(128)(2,1)}, u32[]{:S(2)}) copy-start(bf16[1280]{0:T(1024)(128)(2,1)} %param.27) | copy-start | bytes 7684
  60.1 2.7 %collective-permute-start.3 = (bf16[16,256]{1,0:T(8,128)(2,1)S(1)}, bf16[16,256]{1,0:T(8,128)(2,1)S(1)}, u32[]{:S(2)}, u32[]{:S(2)}) collective-permute-start(bf16[16,256]{1,0:T(8,128)(2,1)S(1)} %get-tuple-element.17.a_ref), channel_id=1, source_target_pairs={{32,0},{64,32},{96,64},{0,96},{33,1},{65,33},{97,65},{1,97},{34,2}... | collective-permute-start | bytes 24584 | tf_op jit(solution)/shard_map/ppermute | solution.py:323
  62.0 4.0 %collective-permute-start.4 = (bf16[16,256]{1,0:T(8,128)(2,1)S(1)}, bf16[16,256]{1,0:T(8,128)(2,1)S(1)}, u32[]{:S(2)}, u32[]{:S(2)}) collective-permute-start(bf16[16,256]{1,0:T(8,128)(2,1)S(1)} %get-tuple-element.17.a_ref), channel_id=1, source_target_pairs={{64,0},{96,32},{0,64},{32,96},{65,1},{97,33},{1,65},{33,97},{66,2}... | collective-permute-start | bytes 24584 | tf_op jit(solution)/shard_map/ppermute | solution.py:323
  62.2 3.8 %collective-permute-start.5 = (bf16[16,256]{1,0:T(8,128)(2,1)S(1)}, bf16[16,256]{1,0:T(8,128)(2,1)S(1)}, u32[]{:S(2)}, u32[]{:S(2)}) collective-permute-start(bf16[16,256]{1,0:T(8,128)(2,1)S(1)} %get-tuple-element.17.a_ref), channel_id=1, source_target_pairs={{96,0},{0,32},{32,64},{64,96},{97,1},{1,33},{33,65},{65,97},{98,2}... | collective-permute-start | bytes 24584 | tf_op jit(solution)/shard_map/ppermute | solution.py:323
  80.2 12.0 %all-to-all-start.3 = ((bf16[32,2,1280]{2,1,0:T(2,128)(2,1)}), bf16[32,2,1280]{2,1,0:T(2,128)(2,1)S(1)}, u32[]{:S(2)}, u32[]{:S(2)}) async-start(bf16[32,2,1280]{2,1,0:T(2,128)(2,1)} %broadcast_in_dim.9), calls=%async_computation.3 | async-start | bytes 327680 | tf_op jit(solution)/shard_map/all_to_all | solution.py:328
  92.3 1.6 %copy-start.2 = (bf16[1280,800]{0,1:T(8,128)(2,1)S(1)}, bf16[1280,800]{0,1:T(8,128)(2,1)}, u32[]{:S(2)}) copy-start(bf16[1280,800]{0,1:T(8,128)(2,1)} %param.29) | copy-start | bytes 6144004
  93.9 13.5 %copy-start.3 = (bf16[800,1280]{1,0:T(8,128)(2,1)S(1)}, bf16[800,1280]{1,0:T(8,128)(2,1)}, u32[]{:S(2)}) copy-start(bf16[800,1280]{1,0:T(8,128)(2,1)} %w_ref.3) | copy-start | bytes 6144004
  95.2 6.0 %collective-permute-start.6 = (bf16[16,1792]{1,0:T(8,128)(2,1)S(1)}, bf16[16,1792]{1,0:T(8,128)(2,1)S(1)}, u32[]{:S(2)}, u32[]{:S(2)}) collective-permute-start(bf16[16,1792]{1,0:T(8,128)(2,1)S(1)} %get-tuple-element.20), channel_id=1, source_target_pairs={{0,32},{32,64},{64,96},{96,0},{1,33},{33,65},{65,97},{97,1},{2,34}... | collective-permute-start | bytes 172040 | tf_op jit(solution)/shard_map/ppermute | solution.py:316
  95.3 5.9 %collective-permute-start.7 = (bf16[16,1792]{1,0:T(8,128)(2,1)S(1)}, bf16[16,1792]{1,0:T(8,128)(2,1)S(1)}, u32[]{:S(2)}, u32[]{:S(2)}) collective-permute-start(bf16[16,1792]{1,0:T(8,128)(2,1)S(1)} %get-tuple-element.21), channel_id=1, source_target_pairs={{0,64},{32,96},{64,0},{96,32},{1,65},{33,97},{65,1},{97,33},{2,66}... | collective-permute-start | bytes 172040 | tf_op jit(solution)/shard_map/ppermute | solution.py:316
  97.0 4.2 %collective-permute-start.8 = (bf16[16,1792]{1,0:T(8,128)(2,1)S(1)}, bf16[16,1792]{1,0:T(8,128)(2,1)S(1)}, u32[]{:S(2)}, u32[]{:S(2)}) collective-permute-start(bf16[16,1792]{1,0:T(8,128)(2,1)S(1)} %get-tuple-element.22), channel_id=1, source_target_pairs={{0,96},{32,0},{64,32},{96,64},{1,97},{33,1},{65,33},{97,65},{2,98}... | collective-permute-start | bytes 172040 | tf_op jit(solution)/shard_map/ppermute | solution.py:316
  101.4 4.3 %collective-permute-start.10 = (bf16[16,896]{1,0:T(8,128)(2,1)S(1)}, bf16[16,896]{1,0:T(8,128)(2,1)S(1)}, u32[]{:S(2)}, u32[]{:S(2)}) collective-permute-start(bf16[16,896]{1,0:T(8,128)(2,1)S(1)} %activate.1.a_ref), channel_id=1, source_target_pairs={{64,0},{96,32},{0,64},{32,96},{65,1},{97,33},{1,65},{33,97},{66,2}... | collective-permute-start | bytes 86024 | tf_op jit(solution)/shard_map/ppermute | solution.py:323
  102.9 3.9 %collective-permute-start.11 = (bf16[16,896]{1,0:T(8,128)(2,1)S(1)}, bf16[16,896]{1,0:T(8,128)(2,1)S(1)}, u32[]{:S(2)}, u32[]{:S(2)}) collective-permute-start(bf16[16,896]{1,0:T(8,128)(2,1)S(1)} %activate.1.a_ref), channel_id=1, source_target_pairs={{96,0},{0,32},{32,64},{64,96},{97,1},{1,33},{33,65},{65,97},{98,2}... | collective-permute-start | bytes 86024 | tf_op jit(solution)/shard_map/ppermute | solution.py:323
  104.4 3.0 %collective-permute-start.9 = (bf16[16,896]{1,0:T(8,128)(2,1)S(1)}, bf16[16,896]{1,0:T(8,128)(2,1)S(1)}, u32[]{:S(2)}, u32[]{:S(2)}) collective-permute-start(bf16[16,896]{1,0:T(8,128)(2,1)S(1)} %activate.1.a_ref), channel_id=1, source_target_pairs={{32,0},{64,32},{96,64},{0,96},{33,1},{65,33},{97,65},{1,97},{34,2}... | collective-permute-start | bytes 86024 | tf_op jit(solution)/shard_map/ppermute | solution.py:323

commit v3 on v2

--- a/solution.py
+++ b/solution.py
@@ -18,7 +18,7 @@
 ROWS = 4
 WIDE = 32
 PACKED = 40
-AT_ONCE = 4
+AT_ONCE = 2
 OWN = 16
 BLOCK = 256
 HIDDEN_UNITS = 800
@@ -32,17 +32,28 @@
 NT = (((1,), (1,)), ((), ()))
 
 
-def call(kernel, out_shape, in_specs, scratch_shapes=(), limit=24, name=None):
+def call(
+    kernel, out_shape, in_specs, scratch_shapes=(), limit=24, name=None, out_spec=VMEM, cost=None
+):
     many = isinstance(out_shape, (tuple, list))
     return pl.pallas_call(
         kernel,
         out_shape=out_shape,
         in_specs=in_specs,
-        out_specs=[VMEM] * len(out_shape) if many else VMEM,
+        out_specs=[out_spec] * len(out_shape) if many else out_spec,
         scratch_shapes=list(scratch_shapes),
         compiler_params=pltpu.CompilerParams(vmem_limit_bytes=limit << 20),
+        cost_estimate=cost,
         name=name,
     )
+
+
+def in_hbm(value):
+    return pltpu.with_memory_space_constraint(value, pltpu.HBM)
+
+
+def in_vmem(value):
+    return pltpu.with_memory_space_constraint(value, pltpu.VMEM)
 
 
 def row_block(mine, k):
@@ -112,75 +123,52 @@
     out_ref[...] = jnp.broadcast_to(out[None], out_ref.shape)
 
 
+def load_kernel(after_ref, k_hbm, v_hbm, k_out, v_out, sems):
+    del after_ref
+    moves = []
+    for at, (source, target) in enumerate(((k_hbm, k_out), (v_hbm, v_out))):
+        for b in range(OWN):
+            moves.append(pltpu.make_async_copy(source.at[b], target.at[b], sems.at[at, b]))
+    for move in moves:
+        move.start()
+    for move in moves:
+        move.wait()
+
+
 def attend_kernel(
-    length_ref,
-    block_ref,
-    g_ref,
-    k_hbm,
-    v_hbm,
-    o_ref,
-    k_scr,
-    v_scr,
-    q_scr,
-    p_scr,
-    w_scr,
-    n_scr,
-    s_scr,
-    k_sems,
-    v_sems,
+    length_ref, block_ref, g_ref, k_ref, v_ref, o_ref, q_scr, p_scr, w_scr, n_scr, s_scr
 ):
-    def k_move(b):
-        return pltpu.make_async_copy(k_hbm.at[b], k_scr.at[b], k_sems.at[b])
-
-    def v_move(b):
-        return pltpu.make_async_copy(v_hbm.at[b], v_scr.at[b], v_sems.at[b])
-
-    for b in range(OWN):
-        k_move(b).start()
-    for b in range(OWN):
-        v_move(b).start()
-
     for head in range(QUERY_HEADS):
         w, j = divmod(head, 2)
         q_scr[pl.ds(head, OWN, stride=QUERY_HEADS), :] = g_ref[
             w, j * OWN : (j + 1) * OWN, :
         ].astype(f32)
 
-    def rows_of(b, start, size):
-        return pl.ds(pl.multiple_of(b * QUERY_HEADS + start, 16), size)
-
-    def limit(b):
-        return length_ref[b] - block_ref[b] * BLOCK
-
     row = lax.broadcasted_iota(jnp.int32, (16, 256), 0)
     lane = lax.broadcasted_iota(jnp.int32, (16, 256), 1)
     own_half = (row < 8) == (lane < 128)
     slot = lax.broadcasted_iota(jnp.int32, (QUERY_HEADS, 256), 1)
     place = lax.rem(lax.broadcasted_iota(jnp.int32, (QUERY_HEADS, 128), 1), 8)
 
-    @pl.loop(0, OWN // AT_ONCE)
-    def _(step):
+    def score(group):
         for u in range(AT_ONCE):
-            k_move(step * AT_ONCE + u).wait()
-        for u in range(AT_ONCE):
-            b = step * AT_ONCE + u
+            b = group * AT_ONCE + u
             for p in range(4):
-                here = rows_of(b, 16 * p, 16)
+                here = pl.ds(pl.multiple_of(b * QUERY_HEADS + 16 * p, 16), 16)
                 pair = q_scr[here, :]
                 query = jnp.where(own_half, jnp.concatenate([pair, pair], axis=1), 0.0)
                 p_scr[here, :] = lax.dot_general(
                     query.astype(bf16),
-                    k_scr[b, :, 256 * p : 256 * p + 256],
+                    k_ref[b, :, 256 * p : 256 * p + 256],
                     NT,
                     preferred_element_type=f32,
                 )
 
-    @pl.loop(0, OWN // AT_ONCE)
-    def _(step):
+    def weigh(group):
         for u in range(AT_ONCE):
-            b = step * AT_ONCE + u
-            here = rows_of(b, 0, QUERY_HEADS)
-            visible = slot < limit(b)
+            b = group * AT_ONCE + u
+            here = pl.ds(pl.multiple_of(b * QUERY_HEADS, QUERY_HEADS), QUERY_HEADS)
+            visible = slot < length_ref[b] - block_ref[b] * BLOCK
             scores = jnp.where(visible, p_scr[here, :] * SCALE, MASKED)
             shift = jnp.max(scores, axis=1, keepdims=True).astype(bf16).astype(f32)
             weights = jnp.where(visible, jnp.exp(scores - shift), 0.0)
@@ -189,29 +177,42 @@
             stats = jnp.where(place == 0, shift, 0.0)
             for at, term in enumerate(terms(total, 2)):
                 stats = jnp.where(place == at + 1, term, stats)
-            s_scr[here, :] = stats
-
-    @pl.loop(0, OWN // AT_ONCE)
-    def _(step):
+            s_scr[pl.ds(b, QUERY_HEADS, stride=OWN), :] = stats
+
+    def add_up(group):
         for u in range(AT_ONCE):
-            v_move(step * AT_ONCE + u).wait()
-        for u in range(AT_ONCE):
-            b = step * AT_ONCE + u
+            b = group * AT_ONCE + u
             for p in range(4):
-                here = rows_of(b, 16 * p, 16)
+                here = pl.ds(pl.multiple_of(b * QUERY_HEADS + 16 * p, 16), 16)
                 both = jnp.dot(
                     w_scr[here, :],
-                    v_scr[b, :, 256 * p : 256 * p + 256],
+                    v_ref[b, :, 256 * p : 256 * p + 256],
                     preferred_element_type=f32,
                 )
-                n_scr[here, :] = jnp.concatenate([both[:8, :128], both[8:, 128:]], axis=0)
+                n_scr[pl.ds(16 * p * OWN + b, 16, stride=OWN), :] = jnp.concatenate(
+                    [both[:8, :128], both[8:, 128:]], axis=0
+                )
+
+    last = OWN // AT_ONCE - 1
+    score(0)
+    weigh(0)
+    score(1)
+
+    @pl.loop(1, last)
+    def _(group):
+        add_up(group - 1)
+        weigh(group)
+        score(group + 1)
+
+    add_up(last - 1)
+    weigh(last)
+    add_up(last)
 
     lane = lax.broadcasted_iota(jnp.int32, (OWN, 128), 1)
     first = lax.rem(lane, 64) < 8
     for w in range(WIDE):
-        rows = [pl.ds(2 * w + j, OWN, stride=QUERY_HEADS) for j in range(2)]
-        for j in range(2):
-            o_ref[w, j * OWN : (j + 1) * OWN, :] = n_scr[rows[j], :].astype(bf16)
+        rows = [slice((2 * w + j) * OWN, (2 * w + j + 1) * OWN) for j in range(2)]
+        o_ref[w, : 2 * OWN, :] = n_scr[2 * w * OWN : 2 * (w + 1) * OWN, :].astype(bf16)
         stats = jnp.where(first, s_scr[rows[0], :], s_scr[rows[1], :])
         o_ref[w, 2 * OWN :, :] = jnp.where(lane[:8] < 64, stats[:8], stats[8:]).astype(bf16)
 
@@ -375,32 +376,38 @@
             pltpu.VMEM(w_keyval.shape[::-1], bf16),
             pltpu.SemaphoreType.DMA((3,)),
         ],
-        limit=60,
+        limit=8,
         name="project",
-    )(mine, hidden, attn_gain[None], w_query, w_keyval.T)
+    )(mine, in_hbm(hidden), attn_gain[None], in_hbm(w_query), in_hbm(w_keyval.T))
     payload = call(
         heads_kernel, sds((WIDE, PACKED, 128), bf16), [VMEM] * 6, limit=8, name="heads"
     )(*to_rows(blocks), straight, swapped)
     gathered = exchange(payload)
 
+    keys, values = call(
+        load_kernel,
+        [pltpu.VMEM(keys_cache.shape, bf16)] * 2,
+        [pl.BlockSpec(memory_space=pl.ANY)] + [HBM] * 2,
+        [pltpu.SemaphoreType.DMA((2, OWN))],
+        limit=1,
+        name="load",
+        out_spec=pl.BlockSpec(memory_space=pl.ANY),
+        cost=pl.CostEstimate(flops=0, bytes_accessed=4 * keys_cache.size, transcendentals=0),
+    )(payload, in_hbm(keys_cache), in_hbm(values_cache))
     parts = call(
         attend_kernel,
         sds((WIDE, PACKED, 128), bf16),
-        [SMEM, SMEM, VMEM, HBM, HBM],
+        [SMEM, SMEM] + [VMEM] * 3,
         [
-            pltpu.VMEM(keys_cache.shape, bf16),
-            pltpu.VMEM(values_cache.shape, bf16),
             pltpu.VMEM((OWN * QUERY_HEADS, 128), f32),
             pltpu.VMEM((OWN * QUERY_HEADS, 256), f32),
             pltpu.VMEM((OWN * QUERY_HEADS, 256), bf16),
             pltpu.VMEM((OWN * QUERY_HEADS, 128), f32),
             pltpu.VMEM((OWN * QUERY_HEADS, 128), f32),
-            pltpu.SemaphoreType.DMA((OWN,)),
-            pltpu.SemaphoreType.DMA((OWN,)),
         ],
-        limit=57,
+        limit=12,
         name="attend",
-    )(lengths, block_index.reshape(OWN), gathered, keys_cache, values_cache)
+    )(lengths, block_index.reshape(OWN), gathered, in_vmem(keys), in_vmem(values))
     heads_out, heads_own = call(
         combine_kernel, [sds((OWN, 256), bf16)] * 2, [SMEM] + [VMEM] * 4, limit=8, name="combine"
     )(wide, exchange(parts), gathered, straight, swapped)

time: 135 us -> 144 us (1.067)
  blocking collectives: 58 us -> 38.9 us
  local copies, waits for them, and re-layouts: 4.8 us -> 19 us
  starting transfers between devices: 23.8 us -> 35.4 us
  waiting for transfers between devices: 25.2 us -> 26.9 us
    all_to_all x4 -> x3, blocking collectives: 58 us -> 38.9 us  [exchange(): lax.all_to_all(blocks, 'wide', split_axis=0, concat_axis=0, tiled=True)]
    unnamed x16 -> x22, local copies, waits for them, and re-layouts: 2.33 us -> 16.4 us
    all_to_all x2 -> x3, starting transfers between devices: 7.68 us -> 20.9 us  [exchange(): lax.all_to_all(blocks, 'wide', split_axis=0, concat_axis=0, tiled=True)]
    ppermute x6, waiting for transfers between devices: 5.23 us -> 7.36 us  [from_rows(): lax.ppermute(own, 'rows', [((i + k) % ROWS, i) for i in range(ROWS)])]
    all_to_all x2 -> x3, waiting for transfers between devices: 17.7 us -> 17.1 us  [exchange(): lax.all_to_all(blocks, 'wide', split_axis=0, concat_axis=0, tiled=True)]
    pallas_call x1 -> x2, Pallas kernels: 11.5 us -> 12 us  [the longest x1 6.05 us: body(): call(load_kernel, [pltpu.VMEM(keys_cache.shape, bf16)] * 2, [pl.BlockSpec...]
  transfers between devices with their start and end apart: 14 -> 15, of which waited for: 7 -> 9; matrix products, arithmetic and copies ran while one was open for 2% -> 3% of each run, Pallas kernels for 0% -> 4%
where the time goes in v3:
time: 144 us; the launch traced here: 143 us
  blocking collectives  38.9 us (27%)
  starting transfers between devices  35.4 us (25%)
  waiting for transfers between devices  26.9 us (19%)
  local copies, waits for them, and re-layouts  19 us (13%)
  Pallas kernels  18.8 us (13%)
  other arithmetic  3.26 us (2%)
    all_to_all x3, blocking collectives, exchange(): lax.all_to_all(blocks, 'wide', split_axis=0, concat_axis=0, tiled=True)  38.9 us
    all_to_all x3, starting transfers between devices, exchange(): lax.all_to_all(blocks, 'wide', split_axis=0, concat_axis=0, tiled=True)  20.9 us
    all_to_all x3, waiting for transfers between devices, exchange(): lax.all_to_all(blocks, 'wide', split_axis=0, concat_axis=0, tiled=True)  17.1 us
    unnamed x22, local copies, waits for them, and re-layouts  16.4 us
    ppermute x6, starting transfers between devices, to_rows(): lax.ppermute(blocks[k], 'rows', [(i, (i + k) % ROWS) for i in range(ROWS)])  9.2 us
    ppermute x6, waiting for transfers between devices, from_rows(): lax.ppermute(own, 'rows', [((i + k) % ROWS, i) for i in range(ROWS)])  7.36 us
    pallas_call x1, Pallas kernels, body(): call(load_kernel, [pltpu.VMEM(keys_cache.shape, bf16)] * 2, [pl.BlockSpec...  6.05 us
    pallas_call x1, Pallas kernels, body(): call(attend_kernel, sds((WIDE, PACKED, 128), bf16), [SMEM, SMEM] + [VMEM]...  5.9 us
  transfers between devices with their start and end apart: 15, of which 9 were waited for; matrix products, arithmetic and copies ran while one was open for 3% of the time, Pallas kernels for 4%

profile of v3, /device:TPU:1, one launch (start us, length us, event | category | flops | bytes accessed | tf_op | source)
XLA Modules:
  0.0 143.1 jit_solution(16170810732597115450)
XLA Ops:
  1.3 1.6 %project.1 = (f32[16,384]{1,0:T(8,128)S(1)}, f32[16,384]{1,0:T(8,128)S(1)}, f32[16,384]{1,0:T(8,128)S(1)}, f32[16,384]{1,0:T(8,128)S(1)}) custom-call(s32[1]{0:T(128)} %bitcast.mine_ref, bf16[64,1280]{1,0:T(8,128)(2,1)} %hidden_ref.1, bf16[1,1280]{1,0:T(2,128)(2,1)S(1)} %broadcast_in_dim.8.gain_ref, bf16[1280,256]{1,0:T(8,128)(2,1)} %wq_hbm.1, ...), custom_call_target="tpu_custom_call" | custom-call | tf_op jit(solution)/shard_map/project/pallas_call | solution.py:368
  2.9 2.1 %collective-permute-start = (f32[16,384]{1,0:T(8,128)S(1)}, f32[16,384]{1,0:T(8,128)S(1)}, u32[]{:S(2)}, u32[]{:S(2)}) collective-permute-start(f32[16,384]{1,0:T(8,128)S(1)} %get-tuple-element.16), channel_id=1, source_target_pairs={{0,32},{32,64},{64,96},{96,0},{1,33},{33,65},{65,97},{97,1},{2,34}... | collective-permute-start | bytes 73736 | tf_op jit(solution)/shard_map/ppermute | solution.py:317
  5.0 2.5 %collective-permute-start.1 = (f32[16,384]{1,0:T(8,128)S(1)}, f32[16,384]{1,0:T(8,128)S(1)}, u32[]{:S(2)}, u32[]{:S(2)}) collective-permute-start(f32[16,384]{1,0:T(8,128)S(1)} %get-tuple-element.17), channel_id=1, source_target_pairs={{0,64},{32,96},{64,0},{96,32},{1,65},{33,97},{65,1},{97,33},{2,66}... | collective-permute-start | bytes 73736 | tf_op jit(solution)/shard_map/ppermute | solution.py:317
  12.7 9.6 %all-to-all-start = ((bf16[32,40,128]{2,1,0:T(8,128)(2,1)}), bf16[32,40,128]{2,1,0:T(8,128)(2,1)S(1)}, u32[]{:S(2)}, u32[]{:S(2)}) async-start(bf16[32,40,128]{2,1,0:T(8,128)(2,1)} %heads.1.after_ref), calls=%async_computation | async-start | bytes 655360 | tf_op jit(solution)/shard_map/all_to_all | solution.py:329
  22.3 6.1 %load.1 = (bf16[16,256,1024]{2,1,0:T(8,128)(2,1)S(1)}, bf16[16,256,1024]{2,1,0:T(8,128)(2,1)S(1)}) custom-call(bf16[32,40,128]{2,1,0:T(8,128)(2,1)} %heads.1.after_ref, bf16[16,256,1024]{2,1,0:T(8,128)(2,1)} %k_hbm.1, bf16[16,256,1024]{2,1,0:T(8,128)(2,1)} %v_hbm.1), custom_call_target="tpu_custom_call" | custom-call | bytes 16777216 | tf_op jit(solution)/shard_map/load/pallas_call | solution.py:387
  28.4 3.3 %copy-done = bf16[16,256,1024]{2,1,0:T(8,128)(2,1)} copy-done((bf16[16,256,1024]{2,1,0:T(8,128)(2,1)}, bf16[16,256,1024]{2,1,0:T(8,128)(2,1)S(1)}, u32[]{:S(2)}) %copy-start) | copy-done | bytes 8388632
  31.7 3.2 %copy-done.2 = bf16[16,256,1024]{2,1,0:T(8,128)(2,1)} copy-done((bf16[16,256,1024]{2,1,0:T(8,128)(2,1)}, bf16[16,256,1024]{2,1,0:T(8,128)(2,1)S(1)}, u32[]{:S(2)}) %copy-start.2) | copy-done | bytes 8388632
  34.9 3.4 %copy-done.1 = bf16[16,256,1024]{2,1,0:T(8,128)(2,1)S(1)} copy-done((bf16[16,256,1024]{2,1,0:T(8,128)(2,1)S(1)}, bf16[16,256,1024]{2,1,0:T(8,128)(2,1)}, u32[]{:S(2)}) %copy-start.1) | copy-done | bytes 8388632
  38.3 3.4 %copy-done.3 = bf16[16,256,1024]{2,1,0:T(8,128)(2,1)S(1)} copy-done((bf16[16,256,1024]{2,1,0:T(8,128)(2,1)S(1)}, bf16[16,256,1024]{2,1,0:T(8,128)(2,1)}, u32[]{:S(2)}) %copy-start.3) | copy-done | bytes 8388632
  41.7 5.9 %attend.1 = bf16[32,40,128]{2,1,0:T(8,128)(2,1)} custom-call(s32[16]{0:T(128)S(1)} %copy-done.9, s32[16]{0:T(128)S(1)} %bitcast.13, bf16[32,40,128]{2,1,0:T(8,128)(2,1)S(1)} %all-to-all-done.g_ref, bf16[16,256,1024]{2,1,0:T(8,128)(2,1)S(1)} %copy-done.1, bf16[16,256,1024]{2,1,0:T(8,128)(2,1)S(1)} %copy-done.3), custom_call_target="tpu_custom_call" | custom-call | tf_op jit(solution)/shard_map/attend/pallas_call | solution.py:397
  47.6 7.4 %all-to-all-start.1 = ((bf16[32,40,128]{2,1,0:T(8,128)(2,1)}), bf16[32,40,128]{2,1,0:T(8,128)(2,1)S(1)}, u32[]{:S(2)}, u32[]{:S(2)}) async-start(bf16[32,40,128]{2,1,0:T(8,128)(2,1)} %attend.1), calls=%async_computation.1 | async-start | bytes 655360 | tf_op jit(solution)/shard_map/all_to_all | solution.py:329
  54.9 9.6 %all-to-all-done.1.r_ref = bf16[32,40,128]{2,1,0:T(8,128)(2,1)S(1)} async-done(((bf16[32,40,128]{2,1,0:T(8,128)(2,1)}), bf16[32,40,128]{2,1,0:T(8,128)(2,1)S(1)}, u32[]{:S(2)}, u32[]{:S(2)}) %all-to-all-start.1) | async-done | bytes 327712 | tf_op jit(solution)/shard_map/all_to_all | solution.py:329
  66.0 1.7 %collective-permute-start.3 = (bf16[16,256]{1,0:T(8,128)(2,1)S(1)}, bf16[16,256]{1,0:T(8,128)(2,1)S(1)}, u32[]{:S(2)}, u32[]{:S(2)}) collective-permute-start(bf16[16,256]{1,0:T(8,128)(2,1)S(1)} %get-tuple-element.21.a_ref), channel_id=1, source_target_pairs={{32,0},{64,32},{96,64},{0,96},{33,1},{65,33},{97,65},{1,97},{34,2}... | collective-permute-start | bytes 24584 | tf_op jit(solution)/shard_map/ppermute | solution.py:324
  68.5 3.2 %collective-permute-done.4.c_ref = bf16[16,256]{1,0:T(8,128)(2,1)S(1)} collective-permute-done((bf16[16,256]{1,0:T(8,128)(2,1)S(1)}, bf16[16,256]{1,0:T(8,128)(2,1)S(1)}, u32[]{:S(2)}, u32[]{:S(2)}) %collective-permute-start.4) | collective-permute-done | bytes 8224 | tf_op jit(solution)/shard_map/ppermute | solution.py:324
  72.1 13.1 %all_to_all.30 = bf16[32,2,1280]{2,1,0:T(2,128)(2,1)S(1)} all-to-all(bf16[32,2,1280]{2,1,0:T(2,128)(2,1)S(1)} %reshape.69), channel_id=1, replica_groups=mesh['rows'=4,'wide'=32] {'wide'}, dimensions={0} | all-to-all | bytes 327680 | tf_op jit(solution)/shard_map/all_to_all | solution.py:329
  86.1 3.9 %all-to-all-start.3 = ((bf16[32,2,1280]{2,1,0:T(2,128)(2,1)}), bf16[32,2,1280]{2,1,0:T(2,128)(2,1)S(1)}, u32[]{:S(2)}, u32[]{:S(2)}) async-start(bf16[32,2,1280]{2,1,0:T(2,128)(2,1)} %broadcast_in_dim.9), calls=%async_computation.3 | async-start | bytes 327680 | tf_op jit(solution)/shard_map/all_to_all | solution.py:329
  90.7 7.4 %all-to-all-done.3 = bf16[32,2,1280]{2,1,0:T(2,128)(2,1)S(1)} async-done(((bf16[32,2,1280]{2,1,0:T(2,128)(2,1)}), bf16[32,2,1280]{2,1,0:T(2,128)(2,1)S(1)}, u32[]{:S(2)}, u32[]{:S(2)}) %all-to-all-start.3) | async-done | bytes 163872 | tf_op jit(solution)/shard_map/all_to_all | solution.py:329
  101.2 1.7 %collective-permute-start.7 = (bf16[16,1792]{1,0:T(8,128)(2,1)S(1)}, bf16[16,1792]{1,0:T(8,128)(2,1)S(1)}, u32[]{:S(2)}, u32[]{:S(2)}) collective-permute-start(bf16[16,1792]{1,0:T(8,128)(2,1)S(1)} %get-tuple-element.25), channel_id=1, source_target_pairs={{0,64},{32,96},{64,0},{96,32},{1,65},{33,97},{65,1},{97,33},{2,66}... | collective-permute-start | bytes 172040 | tf_op jit(solution)/shard_map/ppermute | solution.py:317
  102.9 1.7 %collective-permute-start.8 = (bf16[16,1792]{1,0:T(8,128)(2,1)S(1)}, bf16[16,1792]{1,0:T(8,128)(2,1)S(1)}, u32[]{:S(2)}, u32[]{:S(2)}) collective-permute-start(bf16[16,1792]{1,0:T(8,128)(2,1)S(1)} %get-tuple-element.26), channel_id=1, source_target_pairs={{0,96},{32,0},{64,32},{96,64},{1,97},{33,1},{65,33},{97,65},{2,98}... | collective-permute-start | bytes 172040 | tf_op jit(solution)/shard_map/ppermute | solution.py:317
  104.6 2.5 %collective-permute-done.6.b_ref = bf16[16,1792]{1,0:T(8,128)(2,1)S(1)} collective-permute-done((bf16[16,1792]{1,0:T(8,128)(2,1)S(1)}, bf16[16,1792]{1,0:T(8,128)(2,1)S(1)}, u32[]{:S(2)}, u32[]{:S(2)}) %collective-permute-start.6) | collective-permute-done | bytes 57376 | tf_op jit(solution)/shard_map/ppermute | solution.py:317
  107.3 2.4 %collective-permute-start.9 = (bf16[16,896]{1,0:T(8,128)(2,1)S(1)}, bf16[16,896]{1,0:T(8,128)(2,1)S(1)}, u32[]{:S(2)}, u32[]{:S(2)}) collective-permute-start(bf16[16,896]{1,0:T(8,128)(2,1)S(1)} %activate.1.a_ref), channel_id=1, source_target_pairs={{32,0},{64,32},{96,64},{0,96},{33,1},{65,33},{97,65},{1,97},{34,2}... | collective-permute-start | bytes 86024 | tf_op jit(solution)/shard_map/ppermute | solution.py:324
  110.7 3.3 %collective-permute-done.10.c_ref = bf16[16,896]{1,0:T(8,128)(2,1)S(1)} collective-permute-done((bf16[16,896]{1,0:T(8,128)(2,1)S(1)}, bf16[16,896]{1,0:T(8,128)(2,1)S(1)}, u32[]{:S(2)}, u32[]{:S(2)}) %collective-permute-start.10) | collective-permute-done | bytes 28704 | tf_op jit(solution)/shard_map/ppermute | solution.py:324
  116.3 14.3 %all_to_all.31 = bf16[32,2,1280]{2,1,0:T(2,128)(2,1)S(1)} all-to-all(bf16[32,2,1280]{2,1,0:T(2,128)(2,1)S(1)} %reshape.71), channel_id=1, replica_groups=mesh['rows'=4,'wide'=32] {'wide'}, dimensions={0} | all-to-all | bytes 327680 | tf_op jit(solution)/shard_map/all_to_all | solution.py:329
  130.8 11.6 %all_to_all.32 = bf16[32,2,1280]{2,1,0:T(2,128)(2,1)S(1)} all-to-all(bf16[32,2,1280]{2,1,0:T(2,128)(2,1)S(1)} %broadcast_in_dim.11), channel_id=1, replica_groups=mesh['rows'=4,'wide'=32] {'wide'}, dimensions={0} | all-to-all | bytes 327680 | tf_op jit(solution)/shard_map/all_to_all | solution.py:329
  (60 shorter events, 17.6 us)
Async XLA Ops:
  2.9 8.8 %collective-permute-start = (f32[16,384]{1,0:T(8,128)S(1)}, f32[16,384]{1,0:T(8,128)S(1)}, u32[]{:S(2)}, u32[]{:S(2)}) collective-permute-start(f32[16,384]{1,0:T(8,128)S(1)} %get-tuple-element.16), channel_id=1, source_target_pairs={{0,32},{32,64},{64,96},{96,0},{1,33},{33,65},{65,97},{97,1},{2,34}... | collective-permute-start | bytes 73736 | tf_op jit(solution)/shard_map/ppermute | solution.py:317
  5.0 6.6 %collective-permute-start.1 = (f32[16,384]{1,0:T(8,128)S(1)}, f32[16,384]{1,0:T(8,128)S(1)}, u32[]{:S(2)}, u32[]{:S(2)}) collective-permute-start(f32[16,384]{1,0:T(8,128)S(1)} %get-tuple-element.17), channel_id=1, source_target_pairs={{0,64},{32,96},{64,0},{96,32},{1,65},{33,97},{65,1},{97,33},{2,66}... | collective-permute-start | bytes 73736 | tf_op jit(solution)/shard_map/ppermute | solution.py:317
  7.5 4.2 %collective-permute-start.2 = (f32[16,384]{1,0:T(8,128)S(1)}, f32[16,384]{1,0:T(8,128)S(1)}, u32[]{:S(2)}, u32[]{:S(2)}) collective-permute-start(f32[16,384]{1,0:T(8,128)S(1)} %get-tuple-element.18), channel_id=1, source_target_pairs={{0,96},{32,0},{64,32},{96,64},{1,97},{33,1},{65,33},{97,65},{2,98}... | collective-permute-start | bytes 73736 | tf_op jit(solution)/shard_map/ppermute | solution.py:317
  12.7 22.2 %all-to-all-start = ((bf16[32,40,128]{2,1,0:T(8,128)(2,1)}), bf16[32,40,128]{2,1,0:T(8,128)(2,1)S(1)}, u32[]{:S(2)}, u32[]{:S(2)}) async-start(bf16[32,40,128]{2,1,0:T(8,128)(2,1)} %heads.1.after_ref), calls=%async_computation | async-start | bytes 655360 | tf_op jit(solution)/shard_map/all_to_all | solution.py:329
  22.3 12.6 %copy-start.9 = (s32[16]{0:T(128)S(1)}, s32[16]{0:T(128)}, u32[]{:S(2)}) copy-start(s32[16]{0:T(128)} %length_ref.1) | copy-start | bytes 196
  22.3 12.6 %copy-start.10 = (s32[16,1]{0,1:T(1,128)S(1)}, s32[16,1]{0,1:T(1,128)}, u32[]{:S(2)}) copy-start(s32[16,1]{0,1:T(1,128)} %param.25) | copy-start | bytes 196
  28.4 3.3 %copy-start = (bf16[16,256,1024]{2,1,0:T(8,128)(2,1)}, bf16[16,256,1024]{2,1,0:T(8,128)(2,1)S(1)}, u32[]{:S(2)}) copy-start(bf16[16,256,1024]{2,1,0:T(8,128)(2,1)S(1)} %get-tuple-element.19.k_ref) | copy-start | bytes 25165828
  31.7 3.2 %copy-start.2 = (bf16[16,256,1024]{2,1,0:T(8,128)(2,1)}, bf16[16,256,1024]{2,1,0:T(8,128)(2,1)S(1)}, u32[]{:S(2)}) copy-start(bf16[16,256,1024]{2,1,0:T(8,128)(2,1)S(1)} %get-tuple-element.20.v_ref) | copy-start | bytes 25165828
  34.9 3.4 %copy-start.1 = (bf16[16,256,1024]{2,1,0:T(8,128)(2,1)S(1)}, bf16[16,256,1024]{2,1,0:T(8,128)(2,1)}, u32[]{:S(2)}) copy-start(bf16[16,256,1024]{2,1,0:T(8,128)(2,1)} %copy-done) | copy-start | bytes 25165828
  38.3 3.4 %copy-start.3 = (bf16[16,256,1024]{2,1,0:T(8,128)(2,1)S(1)}, bf16[16,256,1024]{2,1,0:T(8,128)(2,1)}, u32[]{:S(2)}) copy-start(bf16[16,256,1024]{2,1,0:T(8,128)(2,1)} %copy-done.2) | copy-start | bytes 25165828
  41.6 30.2 %copy-start.8 = (bf16[256,1280]{1,0:T(8,128)(2,1)S(1)}, bf16[256,1280]{1,0:T(8,128)(2,1)}, u32[]{:S(2)}) copy-start(bf16[256,1280]{1,0:T(8,128)(2,1)} %w_ref.2) | copy-start | bytes 1966084
  41.6 56.6 %copy-start.4 = (bf16[1280,800]{0,1:T(8,128)(2,1)S(1)}, bf16[1280,800]{0,1:T(8,128)(2,1)}, u32[]{:S(2)}) copy-start(bf16[1280,800]{0,1:T(8,128)(2,1)} %param.28) | copy-start | bytes 6144004
  41.7 56.6 %copy-start.7 = (bf16[64,1280]{1,0:T(8,128)(2,1)S(1)}, bf16[64,1280]{1,0:T(8,128)(2,1)}, u32[]{:S(2)}) copy-start(bf16[64,1280]{1,0:T(8,128)(2,1)} %hidden_ref.1) | copy-start | bytes 491524
  47.6 17.0 %all-to-all-start.1 = ((bf16[32,40,128]{2,1,0:T(8,128)(2,1)}), bf16[32,40,128]{2,1,0:T(8,128)(2,1)S(1)}, u32[]{:S(2)}, u32[]{:S(2)}) async-start(bf16[32,40,128]{2,1,0:T(8,128)(2,1)} %attend.1), calls=%async_computation.1 | async-start | bytes 655360 | tf_op jit(solution)/shard_map/all_to_all | solution.py:329
  66.0 2.5 %collective-permute-start.3 = (bf16[16,256]{1,0:T(8,128)(2,1)S(1)}, bf16[16,256]{1,0:T(8,128)(2,1)S(1)}, u32[]{:S(2)}, u32[]{:S(2)}) collective-permute-start(bf16[16,256]{1,0:T(8,128)(2,1)S(1)} %get-tuple-element.21.a_ref), channel_id=1, source_target_pairs={{32,0},{64,32},{96,64},{0,96},{33,1},{65,33},{97,65},{1,97},{34,2}... | collective-permute-start | bytes 24584 | tf_op jit(solution)/shard_map/ppermute | solution.py:324
  67.7 4.0 %collective-permute-start.4 = (bf16[16,256]{1,0:T(8,128)(2,1)S(1)}, bf16[16,256]{1,0:T(8,128)(2,1)S(1)}, u32[]{:S(2)}, u32[]{:S(2)}) collective-permute-start(bf16[16,256]{1,0:T(8,128)(2,1)S(1)} %get-tuple-element.21.a_ref), channel_id=1, source_target_pairs={{64,0},{96,32},{0,64},{32,96},{65,1},{97,33},{1,65},{33,97},{66,2}... | collective-permute-start | bytes 24584 | tf_op jit(solution)/shard_map/ppermute | solution.py:324
  68.1 3.7 %collective-permute-start.5 = (bf16[16,256]{1,0:T(8,128)(2,1)S(1)}, bf16[16,256]{1,0:T(8,128)(2,1)S(1)}, u32[]{:S(2)}, u32[]{:S(2)}) collective-permute-start(bf16[16,256]{1,0:T(8,128)(2,1)S(1)} %get-tuple-element.21.a_ref), channel_id=1, source_target_pairs={{96,0},{0,32},{32,64},{64,96},{97,1},{1,33},{33,65},{65,97},{98,2}... | collective-permute-start | bytes 24584 | tf_op jit(solution)/shard_map/ppermute | solution.py:324
  86.1 12.0 %all-to-all-start.3 = ((bf16[32,2,1280]{2,1,0:T(2,128)(2,1)}), bf16[32,2,1280]{2,1,0:T(2,128)(2,1)S(1)}, u32[]{:S(2)}, u32[]{:S(2)}) async-start(bf16[32,2,1280]{2,1,0:T(2,128)(2,1)} %broadcast_in_dim.9), calls=%async_computation.3 | async-start | bytes 327680 | tf_op jit(solution)/shard_map/all_to_all | solution.py:329
  101.1 6.0 %collective-permute-start.6 = (bf16[16,1792]{1,0:T(8,128)(2,1)S(1)}, bf16[16,1792]{1,0:T(8,128)(2,1)S(1)}, u32[]{:S(2)}, u32[]{:S(2)}) collective-permute-start(bf16[16,1792]{1,0:T(8,128)(2,1)S(1)} %get-tuple-element.24), channel_id=1, source_target_pairs={{0,32},{32,64},{64,96},{96,0},{1,33},{33,65},{65,97},{97,1},{2,34}... | collective-permute-start | bytes 172040 | tf_op jit(solution)/shard_map/ppermute | solution.py:317
  101.2 5.9 %collective-permute-start.7 = (bf16[16,1792]{1,0:T(8,128)(2,1)S(1)}, bf16[16,1792]{1,0:T(8,128)(2,1)S(1)}, u32[]{:S(2)}, u32[]{:S(2)}) collective-permute-start(bf16[16,1792]{1,0:T(8,128)(2,1)S(1)} %get-tuple-element.25), channel_id=1, source_target_pairs={{0,64},{32,96},{64,0},{96,32},{1,65},{33,97},{65,1},{97,33},{2,66}... | collective-permute-start | bytes 172040 | tf_op jit(solution)/shard_map/ppermute | solution.py:317
  102.9 4.2 %collective-permute-start.8 = (bf16[16,1792]{1,0:T(8,128)(2,1)S(1)}, bf16[16,1792]{1,0:T(8,128)(2,1)S(1)}, u32[]{:S(2)}, u32[]{:S(2)}) collective-permute-start(bf16[16,1792]{1,0:T(8,128)(2,1)S(1)} %get-tuple-element.26), channel_id=1, source_target_pairs={{0,96},{32,0},{64,32},{96,64},{1,97},{33,1},{65,33},{97,65},{2,98}... | collective-permute-start | bytes 172040 | tf_op jit(solution)/shard_map/ppermute | solution.py:317
  107.3 3.4 %collective-permute-start.9 = (bf16[16,896]{1,0:T(8,128)(2,1)S(1)}, bf16[16,896]{1,0:T(8,128)(2,1)S(1)}, u32[]{:S(2)}, u32[]{:S(2)}) collective-permute-start(bf16[16,896]{1,0:T(8,128)(2,1)S(1)} %activate.1.a_ref), channel_id=1, source_target_pairs={{32,0},{64,32},{96,64},{0,96},{33,1},{65,33},{97,65},{1,97},{34,2}... | collective-permute-start | bytes 86024 | tf_op jit(solution)/shard_map/ppermute | solution.py:324
  109.7 4.3 %collective-permute-start.10 = (bf16[16,896]{1,0:T(8,128)(2,1)S(1)}, bf16[16,896]{1,0:T(8,128)(2,1)S(1)}, u32[]{:S(2)}, u32[]{:S(2)}) collective-permute-start(bf16[16,896]{1,0:T(8,128)(2,1)S(1)} %activate.1.a_ref), channel_id=1, source_target_pairs={{64,0},{96,32},{0,64},{32,96},{65,1},{97,33},{1,65},{33,97},{66,2}... | collective-permute-start | bytes 86024 | tf_op jit(solution)/shard_map/ppermute | solution.py:324
  109.9 4.2 %collective-permute-start.11 = (bf16[16,896]{1,0:T(8,128)(2,1)S(1)}, bf16[16,896]{1,0:T(8,128)(2,1)S(1)}, u32[]{:S(2)}, u32[]{:S(2)}) collective-permute-start(bf16[16,896]{1,0:T(8,128)(2,1)S(1)} %activate.1.a_ref), channel_id=1, source_target_pairs={{96,0},{0,32},{32,64},{64,96},{97,1},{1,33},{33,65},{65,97},{98,2}... | collective-permute-start | bytes 86024 | tf_op jit(solution)/shard_map/ppermute | solution.py:324
  (2 other events, 3.2 us)

commit v4 on v3

--- a/solution.py
+++ b/solution.py
@@ -19,6 +19,7 @@
 WIDE = 32
 PACKED = 40
 AT_ONCE = 2
+GROUPS = 8
 OWN = 16
 BLOCK = 256
 HIDDEN_UNITS = 800
@@ -33,14 +34,14 @@
 
 
 def call(
-    kernel, out_shape, in_specs, scratch_shapes=(), limit=24, name=None, out_spec=VMEM, cost=None
+    kernel, out_shape, in_specs, scratch_shapes=(), limit=24, name=None, cost=None
 ):
     many = isinstance(out_shape, (tuple, list))
     return pl.pallas_call(
         kernel,
         out_shape=out_shape,
         in_specs=in_specs,
-        out_specs=[out_spec] * len(out_shape) if many else out_spec,
+        out_specs=[VMEM] * len(out_shape) if many else VMEM,
         scratch_shapes=list(scratch_shapes),
         compiler_params=pltpu.CompilerParams(vmem_limit_bytes=limit << 20),
         cost_estimate=cost,
@@ -48,12 +49,12 @@
     )
 
 
+def in_vmem(value):
+    return pltpu.with_memory_space_constraint(value, pltpu.VMEM)
+
+
 def in_hbm(value):
     return pltpu.with_memory_space_constraint(value, pltpu.HBM)
-
-
-def in_vmem(value):
-    return pltpu.with_memory_space_constraint(value, pltpu.VMEM)
 
 
 def row_block(mine, k):
@@ -86,12 +87,17 @@
     return jnp.concatenate([value[:, :64], value[:, 64:]], axis=0)
 
 
-def project_kernel(mine_ref, hidden_hbm, gain_ref, wq_hbm, wkv_hbm, *rest):
-    outs, (whole, hidden_ref, wq_ref, wkv_ref, sems) = rest[:ROWS], rest[ROWS:]
+def project_kernel(place_ref, hidden_hbm, gain_hbm, wq_hbm, wkv_hbm, *rest):
+    outs, (whole, hidden_ref, gain_ref, wq_ref, wkv_ref, sems) = rest[:ROWS], rest[ROWS:]
     moves = [
         pltpu.make_async_copy(source, target, sems.at[at])
         for at, (source, target) in enumerate(
-            ((hidden_hbm, hidden_ref), (wkv_hbm, wkv_ref), (wq_hbm, wq_ref))
+            (
+                (hidden_hbm, hidden_ref),
+                (wkv_hbm, wkv_ref),
+                (wq_hbm, wq_ref),
+                (gain_hbm, gain_ref),
+            )
         )
     ]
     for move in moves:
@@ -99,15 +105,46 @@
     moves[0].wait()
     hidden = hidden_ref[...].astype(f32)
     square = jnp.sum(hidden * hidden, axis=1, keepdims=True)
-    scaled = (hidden * gain_ref[...].astype(f32)).astype(bf16)
+    moves[3].wait()
+    scaled = (hidden * gain_ref[...].astype(f32)[None]).astype(bf16)
     moves[1].wait()
     keyval = lax.dot_general(scaled, wkv_ref[...], NT, preferred_element_type=f32)
     whole[:, 256:] = jnp.concatenate([keyval, jnp.broadcast_to(square, keyval.shape)], axis=1)
     moves[2].wait()
     whole[:, :256] = jnp.dot(scaled, wq_ref[...], preferred_element_type=f32)
-    mine = mine_ref[0]
+    mine = place_ref[0] // WIDE
     for k in range(ROWS):
         outs[k][...] = whole[row_block(mine, k), :]
+
+
+def table_kernel(
+    length_ref, query_hbm, key_hbm, straight_ref, swapped_ref, query_ref, key_ref, sems
+):
+    gains = (query_ref, key_ref)
+    moves = [
+        pltpu.make_async_copy(source, gains[at], sems.at[at])
+        for at, source in enumerate((query_hbm, key_hbm))
+    ]
+    for move in moves:
+        move.start()
+    row = lax.broadcasted_iota(jnp.int32, (OWN, 128), 0)
+    lane = lax.broadcasted_iota(jnp.int32, (OWN, 128), 1)
+    position = jnp.zeros((OWN, 128), jnp.int32)
+    for b in range(OWN):
+        position = jnp.where(row == b, length_ref[b], position)
+    half = HEAD_WIDTH // 2
+    pair = lax.rem(lax.broadcasted_iota(jnp.int32, (1, 128), 1), half)
+    frequency = jnp.zeros((1, 128), f32)
+    for at in range(half):
+        frequency = jnp.where(pair == at, np.float32(ROPE_BASE ** (-2.0 * at / HEAD_WIDTH)), frequency)
+    angle = position.astype(f32) * frequency
+    cosine, sine = jnp.cos(angle), jnp.sin(angle)
+    sine = jnp.where(lane < half, -sine, sine)
+    for at in range(2):
+        moves[at].wait()
+        gain = gains[at][...].astype(f32)[None]
+        straight_ref[at] = cosine * gain
+        swapped_ref[at] = sine * swap_halves(gain)
 
 
 def heads_kernel(a_ref, b_ref, c_ref, d_ref, straight_ref, swapped_ref, out_ref):
@@ -121,18 +158,6 @@
     parts.append(pack(scaled[:, 256:320]))
     out = jnp.concatenate(parts, axis=0).astype(bf16)
     out_ref[...] = jnp.broadcast_to(out[None], out_ref.shape)
-
-
-def load_kernel(after_ref, k_hbm, v_hbm, k_out, v_out, sems):
-    del after_ref
-    moves = []
-    for at, (source, target) in enumerate(((k_hbm, k_out), (v_hbm, v_out))):
-        for b in range(OWN):
-            moves.append(pltpu.make_async_copy(source.at[b], target.at[b], sems.at[at, b]))
-    for move in moves:
-        move.start()
-    for move in moves:
-        move.wait()
 
 
 def attend_kernel(
@@ -193,7 +218,7 @@
                     [both[:8, :128], both[8:, 128:]], axis=0
                 )
 
-    last = OWN // AT_ONCE - 1
+    last = GROUPS - 1
     score(0)
     weigh(0)
     score(1)
@@ -217,56 +242,77 @@
         o_ref[w, 2 * OWN :, :] = jnp.where(lane[:8] < 64, stats[:8], stats[8:]).astype(bf16)
 
 
-def combine_kernel(wide_ref, r_ref, g_ref, straight_ref, swapped_ref, out_ref, again_ref):
-    wide = wide_ref[0]
+def combine_kernel(place_ref, r_ref, g_ref, straight_ref, swapped_ref, out_ref, again_ref):
+    wide = lax.rem(place_ref[0], WIDE)
     group = wide // 4
 
     def half(source):
         return unpack(g_ref[source, 2 * OWN :, :].astype(f32))
+
+    def column(value, at):
+        return jnp.concatenate(
+            [value[..., at : at + 1], value[..., 64 + at : 65 + at]], axis=-2
+        )
 
     key = jnp.concatenate([half(2 * group), half(2 * group + 1)], axis=1)
     value = jnp.concatenate([half(16 + 2 * group), half(17 + 2 * group)], axis=1)
     key = norm_rope(key, straight_ref[1], swapped_ref[1]).astype(bf16).astype(f32)
+    fresh = [
+        jnp.sum(g_ref[wide, j * OWN : (j + 1) * OWN, :].astype(f32) * key, axis=1, keepdims=True)
+        * SCALE
+        for j in range(2)
+    ]
+    lane = lax.broadcasted_iota(jnp.int32, (8, 128), 1)
     stats = r_ref[:, 2 * OWN :, :].astype(f32)
-
-    def stat(at):
-        return jnp.concatenate(
-            [stats[:, :, at : at + 1], stats[:, :, 64 + at : 65 + at]], axis=1
-        )
-
+    highest = jnp.max(stats, axis=0)
+    for j in range(2):
+        packed = jnp.where(lane < 64, fresh[j][:8], fresh[j][8:])
+        highest = jnp.where(lax.rem(lane, 64) == 8 * j, jnp.maximum(highest, packed), highest)
+    shift_lane = (lax.rem(lane, 64) == 0) | (lax.rem(lane, 64) == 8)
+    factors = jnp.where(shift_lane[None], jnp.exp(jnp.where(shift_lane, stats - highest, 0.0)), 0.0)
+    spread_factors = factors
+    for shift in (1, 2):
+        spread_factors = spread_factors + jnp.roll(factors, shift, axis=2)
+    totals = jnp.sum(spread_factors * jnp.where(shift_lane, 0.0, stats), axis=0)
     for j in range(2):
         lanes = slice(j * 128, (j + 1) * 128)
         here = slice(j * OWN, (j + 1) * OWN)
-        query = g_ref[wide, here, :].astype(f32)
-        fresh = jnp.sum(query * key, axis=1, keepdims=True) * SCALE
-        shifts = stat(8 * j)
-        totals = stat(8 * j + 1) + stat(8 * j + 2)
-        highest = jnp.maximum(jnp.max(shifts, axis=0), fresh)
-        factors = jnp.exp(shifts - highest[None])
-        fresh_weight = jnp.exp(fresh - highest)
-        weight_sum = jnp.sum(factors * totals, axis=0) + fresh_weight
-        numer = jnp.sum(r_ref[:, here, :].astype(f32) * factors, axis=0)
+        fresh_weight = jnp.exp(fresh[j] - column(highest, 8 * j))
+        weight_sum = column(totals, 8 * j + 1) + column(totals, 8 * j + 2) + fresh_weight
+        numer = jnp.sum(r_ref[:, here, :].astype(f32) * column(factors, 8 * j), axis=0)
         numer = numer + fresh_weight.astype(bf16).astype(f32) * value
         heads = (numer / weight_sum).astype(bf16)
         out_ref[:, lanes] = heads
         again_ref[:, lanes] = heads
 
 
+def store_pairs(out_ref, value):
+    for block in range(WIDE):
+        out_ref[block] = value[2 * block : 2 * block + 2]
+
+
 def output_kernel(a_ref, b_ref, c_ref, d_ref, w_ref, out_ref):
     heads = jnp.concatenate([a_ref[...], b_ref[...], c_ref[...], d_ref[...]], axis=0)
-    out_ref[...] = jnp.dot(heads, w_ref[...], preferred_element_type=f32).astype(bf16)
-
-
-def gate_up_kernel(mine_ref, hidden_ref, attended_ref, gain_ref, wg_ref, wu_ref, stream_ref, *outs):
-    mine = mine_ref[0]
+    store_pairs(out_ref, jnp.dot(heads, w_ref[...], preferred_element_type=f32).astype(bf16))
+
+
+def sum_spread_kernel(got_ref, out_ref):
+    total = jnp.sum(got_ref[...].astype(f32), axis=0).astype(bf16)
+    out_ref[...] = jnp.broadcast_to(total[None], out_ref.shape)
+
+
+def gate_up_kernel(
+    place_ref, hidden_ref, attended_ref, gain_ref, wg_ref, wu_ref, stream_ref, *outs
+):
+    mine = place_ref[0] // WIDE
     for k in range(ROWS):
         at = slice(k * OWN, (k + 1) * OWN)
-        stream_ref[at, :] = hidden_ref[row_block(mine, k), :].astype(f32) + attended_ref[
-            at, :
-        ].astype(f32)
+        blocks = attended_ref[k * WIDE // ROWS : (k + 1) * WIDE // ROWS]
+        attended = blocks.astype(f32).reshape(OWN, blocks.shape[-1])
+        stream_ref[at, :] = hidden_ref[row_block(mine, k), :].astype(f32) + attended
     stream = stream_ref[...]
     square = jnp.sum(stream * stream, axis=1, keepdims=True)
-    scaled = (stream * gain_ref[...].astype(f32)).astype(bf16)
+    scaled = (stream * gain_ref[...].astype(f32)[None]).astype(bf16)
     gate = lax.dot_general(scaled, wg_ref[...], NT, preferred_element_type=f32).astype(bf16)
     up = lax.dot_general(scaled, wu_ref[...], NT, preferred_element_type=f32).astype(bf16)
     pad = HALF - HIDDEN_UNITS
@@ -297,31 +343,30 @@
 
 def down_kernel(a_ref, b_ref, c_ref, d_ref, w_ref, out_ref):
     units = jnp.concatenate([a_ref[...], b_ref[...], c_ref[...], d_ref[...]], axis=0)
-    out_ref[...] = jnp.dot(
-        units[:, :HIDDEN_UNITS], w_ref[...], preferred_element_type=f32
-    ).astype(bf16)
-
-
-def final_kernel(mine_ref, stream_ref, down_ref, out_ref):
-    mine = mine_ref[0]
+    part = jnp.dot(units[:, :HIDDEN_UNITS], w_ref[...], preferred_element_type=f32)
+    store_pairs(out_ref, part.astype(bf16))
+
+
+def final_kernel(place_ref, stream_ref, down_ref, out_ref):
+    mine = place_ref[0] // WIDE
     for k in range(ROWS):
         at = slice(k * OWN, (k + 1) * OWN)
-        out_ref[row_block(mine, k), :] = (stream_ref[at, :] + down_ref[at, :].astype(f32)).astype(
-            bf16
-        )
+        blocks = down_ref[k * WIDE // ROWS : (k + 1) * WIDE // ROWS]
+        down = blocks.astype(f32).reshape(OWN, blocks.shape[-1])
+        out_ref[row_block(mine, k), :] = (stream_ref[at, :] + down).astype(bf16)
 
 
 def to_rows(blocks):
-    got = [blocks[0]]
-    for k in range(1, ROWS):
-        got.append(lax.ppermute(blocks[k], "rows", [(i, (i + k) % ROWS) for i in range(ROWS)]))
+    got = list(blocks)
+    for k in (2, 1, 3):
+        got[k] = lax.ppermute(blocks[k], "rows", [(i, (i + k) % ROWS) for i in range(ROWS)])
     return got
 
 
 def from_rows(own):
-    got = [own]
-    for k in range(1, ROWS):
-        got.append(lax.ppermute(own, "rows", [((i + k) % ROWS, i) for i in range(ROWS)]))
+    got = [own] * ROWS
+    for k in (2, 1, 3):
+        got[k] = lax.ppermute(own, "rows", [((i + k) % ROWS, i) for i in range(ROWS)])
     return got
 
 
@@ -330,10 +375,14 @@
 
 
 def sum_wide(part):
-    height, width = part.shape
-    got = exchange(part.reshape(WIDE, height // WIDE, width))
-    total = jnp.sum(got.astype(f32), axis=0).astype(bf16)
-    return exchange(jnp.broadcast_to(total[None], got.shape)).reshape(height, width)
+    total = call(
+        sum_spread_kernel,
+        jax.ShapeDtypeStruct(part.shape, bf16),
+        [VMEM],
+        limit=4,
+        name="sum_spread",
+    )(exchange(part))
+    return exchange(total)
 
 
 def body(
@@ -353,51 +402,46 @@
     w_up,
     w_down,
 ):
-    mine = lax.axis_index("rows").astype(jnp.int32).reshape(1)
-    wide = lax.axis_index("wide").astype(jnp.int32).reshape(1)
+    place = lax.axis_index(("rows", "wide")).astype(jnp.int32).reshape(1)
     sds = jax.ShapeDtypeStruct
-
-    half = HEAD_WIDTH // 2
-    frequency = np.power(ROPE_BASE, -(np.arange(half) * 2.0 / HEAD_WIDTH)).astype(np.float32)
-    angles = lengths.astype(f32)[:, None] * jnp.asarray(frequency)[None, :]
-    cosine, sine = jnp.cos(angles), jnp.sin(angles)
-    gains = jnp.stack([query_gain, key_norm_gain]).astype(f32)[:, None, :]
-    straight = gains * jnp.concatenate([cosine, cosine], axis=1)
-    swapped = swap_halves(gains) * jnp.concatenate([-sine, sine], axis=1)
 
     blocks = call(
         project_kernel,
         [sds((OWN, 384), f32)] * ROWS,
-        [SMEM, HBM, VMEM, HBM, HBM],
+        [SMEM] + [HBM] * 4,
         [
             pltpu.VMEM((64, 384), f32),
             pltpu.VMEM(hidden.shape, bf16),
+            pltpu.VMEM(attn_gain.shape, bf16),
             pltpu.VMEM(w_query.shape, bf16),
             pltpu.VMEM(w_keyval.shape[::-1], bf16),
-            pltpu.SemaphoreType.DMA((3,)),
+            pltpu.SemaphoreType.DMA((4,)),
         ],
         limit=8,
         name="project",
-    )(mine, in_hbm(hidden), attn_gain[None], in_hbm(w_query), in_hbm(w_keyval.T))
+    )(place, *map(in_hbm, (hidden, attn_gain, w_query, w_keyval.T)))
+    straight, swapped = call(
+        table_kernel,
+        [sds((2, OWN, 128), f32)] * 2,
+        [SMEM, HBM, HBM],
+        [pltpu.VMEM((HEAD_WIDTH,), bf16)] * 2 + [pltpu.SemaphoreType.DMA((2,))],
+        limit=4,
+        name="tables",
+    )(*map(in_hbm, (lengths, query_gain, key_norm_gain)))
     payload = call(
-        heads_kernel, sds((WIDE, PACKED, 128), bf16), [VMEM] * 6, limit=8, name="heads"
+        heads_kernel,
+        sds((WIDE, PACKED, 128), bf16),
+        [VMEM] * 6,
+        limit=8,
+        name="heads",
+        cost=pl.CostEstimate(flops=20_000_000_000, bytes_accessed=1 << 20, transcendentals=0),
     )(*to_rows(blocks), straight, swapped)
     gathered = exchange(payload)
 
-    keys, values = call(
-        load_kernel,
-        [pltpu.VMEM(keys_cache.shape, bf16)] * 2,
-        [pl.BlockSpec(memory_space=pl.ANY)] + [HBM] * 2,
-        [pltpu.SemaphoreType.DMA((2, OWN))],
-        limit=1,
-        name="load",
-        out_spec=pl.BlockSpec(memory_space=pl.ANY),
-        cost=pl.CostEstimate(flops=0, bytes_accessed=4 * keys_cache.size, transcendentals=0),
-    )(payload, in_hbm(keys_cache), in_hbm(values_cache))
     parts = call(
         attend_kernel,
         sds((WIDE, PACKED, 128), bf16),
-        [SMEM, SMEM] + [VMEM] * 3,
+        [SMEM, SMEM, VMEM, VMEM, VMEM],
         [
             pltpu.VMEM((OWN * QUERY_HEADS, 128), f32),
             pltpu.VMEM((OWN * QUERY_HEADS, 256), f32),
@@ -405,14 +449,14 @@
             pltpu.VMEM((OWN * QUERY_HEADS, 128), f32),
             pltpu.VMEM((OWN * QUERY_HEADS, 128), f32),
         ],
-        limit=12,
+        limit=8,
         name="attend",
-    )(lengths, block_index.reshape(OWN), gathered, in_vmem(keys), in_vmem(values))
+    )(lengths, block_index.reshape(OWN), gathered, in_vmem(keys_cache), in_vmem(values_cache))
     heads_out, heads_own = call(
         combine_kernel, [sds((OWN, 256), bf16)] * 2, [SMEM] + [VMEM] * 4, limit=8, name="combine"
-    )(wide, exchange(parts), gathered, straight, swapped)
-
-    out_part = call(output_kernel, sds((64, 1280), bf16), [VMEM] * 5, limit=8, name="output")(
+    )(place, exchange(parts), gathered, straight, swapped)
+
+    out_part = call(output_kernel, sds((WIDE, 2, 1280), bf16), [VMEM] * 5, limit=8, name="output")(
         *from_rows(heads_own), w_out
     )
     attended = sum_wide(out_part)
@@ -421,17 +465,17 @@
         gate_up_kernel,
         [sds((64, 1280), f32)] + [sds((OWN, 2 * HALF), bf16)] * ROWS,
         [SMEM] + [VMEM] * 5,
-        limit=16,
+        limit=12,
         name="gate_up",
-    )(mine, hidden, attended, mlp_gain[None], w_gate.T, w_up.T)
+    )(place, hidden, attended, mlp_gain, w_gate.T, w_up.T)
     activated = call(
         activate_kernel, sds((OWN, HALF), bf16), [VMEM] * 4, limit=8, name="activate"
     )(*to_rows(blocks))
-    down_part = call(down_kernel, sds((64, 1280), bf16), [VMEM] * 5, limit=8, name="down")(
+    down_part = call(down_kernel, sds((WIDE, 2, 1280), bf16), [VMEM] * 5, limit=8, name="down")(
         *from_rows(activated), w_down
     )
     layer_out = call(final_kernel, sds((64, 1280), bf16), [SMEM] + [VMEM] * 2, limit=8, name="final")(
-        mine, stream, sum_wide(down_part)
+        place, stream, sum_wide(down_part)
     )
     return (layer_out, heads_out)
 

time: 144 us -> 122 us (0.85)
  blocking collectives: 38.9 us -> 83.6 us
  starting transfers between devices: 35.4 us -> 16.3 us
  local copies, waits for them, and re-layouts: 19 us -> 0.07 us
  waiting for transfers between devices: 26.9 us -> 8.05 us
  Pallas kernels: 18.8 us -> 13.3 us
  other arithmetic: 3.26 us -> 0.01 us
    all_to_all x3 -> x6, blocking collectives: 38.9 us -> 83.6 us  [exchange(): lax.all_to_all(blocks, 'wide', split_axis=0, concat_axis=0, tiled=True)]
    all_to_all x3 -> x0, starting transfers between devices: 20.9 us -> none  [exchange(): lax.all_to_all(blocks, 'wide', split_axis=0, concat_axis=0, tiled=True)]
    all_to_all x3 -> x0, waiting for transfers between devices: 17.1 us -> none  [exchange(): lax.all_to_all(blocks, 'wide', split_axis=0, concat_axis=0, tiled=True)]
    unnamed x22 -> x24, local copies, waits for them, and re-layouts: 16.4 us -> 0.07 us
    pallas_call x5 -> x7, Pallas kernels: 14.2 us -> 9.37 us  [the longest x1 5.2 us: body(): call(attend_kernel, sds((WIDE, PACKED, 128), bf16), [SMEM, SMEM, VMEM, VM...]
    broadcast_in_dim x4 -> x0, local copies, waits for them, and re-layouts: 2.23 us -> none  [the longest x2 0.84 us: sum_wide(): jnp.broadcast_to(total[None], got.shape)]
    ppermute x6, waiting for transfers between devices: 7.36 us -> 5.19 us  [from_rows(): lax.ppermute(own, 'rows', [((i + k) % ROWS, i) for i in range(ROWS)])]
    convert_element_type x3 -> x0, other arithmetic: 2.02 us -> none  [the longest x2 1.36 us: body(): gains = jnp.stack([query_gain, key_norm_gain]).astype(f32)[:, None, :]]
  transfers between devices with their start and end apart: 15 -> 12, of which waited for: 9 -> 10; matrix products, arithmetic and copies ran while one was open for 3% -> 0% of each run, Pallas kernels for 4% -> 1%
where the time goes in v4:
time: 122 us
  blocking collectives  83.6 us (69%)
  starting transfers between devices  16.3 us (13%)
  Pallas kernels  13.3 us (11%)
  waiting for transfers between devices  8.05 us (7%)
    all_to_all x6, blocking collectives, exchange(): lax.all_to_all(blocks, 'wide', split_axis=0, concat_axis=0, tiled=True)  83.6 us
    ppermute x6, starting transfers between devices, to_rows(): lax.ppermute(blocks[k], 'rows', [(i, (i + k) % ROWS) for i in range(ROWS)])  9.07 us
    ppermute x6, starting transfers between devices, from_rows(): lax.ppermute(own, 'rows', [((i + k) % ROWS, i) for i in range(ROWS)])  7.22 us
    pallas_call x1, Pallas kernels, body(): call(attend_kernel, sds((WIDE, PACKED, 128), bf16), [SMEM, SMEM, VMEM, VM...  5.2 us
    ppermute x6, waiting for transfers between devices, from_rows(): lax.ppermute(own, 'rows', [((i + k) % ROWS, i) for i in range(ROWS)])  5.19 us
    ppermute x6, waiting for transfers between devices, to_rows(): lax.ppermute(blocks[k], 'rows', [(i, (i + k) % ROWS) for i in range(ROWS)])  2.86 us
  transfers between devices with their start and end apart: 12, of which 10 were waited for; matrix products, arithmetic and copies ran while one was open for 0% of the time, Pallas kernels for 1%

profile of v4, /device:TPU:1, one launch (start us, length us, event | category | flops | bytes accessed | tf_op | source)
XLA Modules:
  0.0 122.1 jit_solution(13187325850937173001)
XLA Ops:
  0.6 1.6 %project.1 = (f32[16,384]{1,0:T(8,128)S(1)}, f32[16,384]{1,0:T(8,128)S(1)}, f32[16,384]{1,0:T(8,128)S(1)}, f32[16,384]{1,0:T(8,128)S(1)}) custom-call(s32[1]{0:T(128)} %bitcast.place_ref, bf16[64,1280]{1,0:T(8,128)(2,1)} %hidden_ref.1, bf16[1280]{0:T(1024)(128)(2,1)} %gain_hbm.1, bf16[1280,256]{1,0:T(8,128)(2,1)} %wq_hbm.1, bf16[64,1280]{1,0:T(8,128)(2,1)} %bitcast.12), custom_call_target="tpu_custom_call" | custom-call | tf_op jit(solution)/shard_map/project/pallas_call | solution.py:408
  2.3 2.1 %collective-permute-start = (f32[16,384]{1,0:T(8,128)S(1)}, f32[16,384]{1,0:T(8,128)S(1)}, u32[]{:S(2)}, u32[]{:S(2)}) collective-permute-start(f32[16,384]{1,0:T(8,128)S(1)} %get-tuple-element.16), channel_id=1, source_target_pairs={{0,32},{32,64},{64,96},{96,0},{1,33},{33,65},{65,97},{97,1},{2,34}... | collective-permute-start | bytes 73736 | tf_op jit(solution)/shard_map/ppermute | solution.py:362
  4.4 2.5 %collective-permute-start.1 = (f32[16,384]{1,0:T(8,128)S(1)}, f32[16,384]{1,0:T(8,128)S(1)}, u32[]{:S(2)}, u32[]{:S(2)}) collective-permute-start(f32[16,384]{1,0:T(8,128)S(1)} %get-tuple-element.17), channel_id=1, source_target_pairs={{0,64},{32,96},{64,0},{96,32},{1,65},{33,97},{65,1},{97,33},{2,66}... | collective-permute-start | bytes 73736 | tf_op jit(solution)/shard_map/ppermute | solution.py:362
  6.8 1.2 collective-permute-start.2
  8.0 1.5 %tables.1 = (f32[2,16,128]{2,1,0:T(8,128)S(1)}, f32[2,16,128]{2,1,0:T(8,128)S(1)}) custom-call(s32[16]{0:T(128)} %length_ref.3, bf16[128]{0:T(256)(128)(2,1)} %query_hbm.1, bf16[128]{0:T(256)(128)(2,1)} %key_hbm.1), custom_call_target="tpu_custom_call" | custom-call | tf_op jit(solution)/shard_map/tables/pallas_call | solution.py:423
  10.1 19.9 %all_to_all.30.g_ref = bf16[32,40,128]{2,1,0:T(8,128)(2,1)S(1)} all-to-all(bf16[32,40,128]{2,1,0:T(8,128)(2,1)S(1)} %heads.1), channel_id=1, replica_groups=mesh['rows'=4,'wide'=32] {'wide'}, dimensions={0} | all-to-all | bytes 655360 | tf_op jit(solution)/shard_map/all_to_all | solution.py:374
  30.1 5.2 %attend.1 = bf16[32,40,128]{2,1,0:T(8,128)(2,1)S(1)} custom-call(s32[16]{0:T(128)S(1)} %copy-done.6, s32[16]{0:T(128)S(1)} %bitcast.11, bf16[32,40,128]{2,1,0:T(8,128)(2,1)S(1)} %all_to_all.30.g_ref, bf16[16,256,1024]{2,1,0:T(8,128)(2,1)S(1)} %bitcast.6, bf16[16,256,1024]{2,1,0:T(8,128)(2,1)S(1)} %bitcast.8), custom_call_target="tpu_custom_call" | custom-call | tf_op jit(solution)/shard_map/attend/pallas_call | solution.py:441
  35.3 13.2 %all_to_all.31.r_ref = bf16[32,40,128]{2,1,0:T(8,128)(2,1)S(1)} all-to-all(bf16[32,40,128]{2,1,0:T(8,128)(2,1)S(1)} %attend.1), channel_id=1, replica_groups=mesh['rows'=4,'wide'=32] {'wide'}, dimensions={0} | all-to-all | bytes 655360 | tf_op jit(solution)/shard_map/all_to_all | solution.py:374
  48.5 1.4 %combine.1 = (bf16[16,256]{1,0:T(8,128)(2,1)}, bf16[16,256]{1,0:T(8,128)(2,1)S(1)}) custom-call(s32[1]{0:T(128)} %bitcast.place_ref, bf16[32,40,128]{2,1,0:T(8,128)(2,1)S(1)} %all_to_all.31.r_ref, bf16[32,40,128]{2,1,0:T(8,128)(2,1)S(1)} %all_to_all.30.g_ref, f32[2,16,128]{2,1,0:T(8,128)S(1)} %get-tuple-element.19.straight_ref, ...), custom_call_target="tpu_custom_call" | custom-call | tf_op jit(solution)/shard_map/combine/pallas_call | solution.py:455
  49.9 3.5 %collective-permute-start.4 = (bf16[16,256]{1,0:T(8,128)(2,1)S(1)}, bf16[16,256]{1,0:T(8,128)(2,1)S(1)}, u32[]{:S(2)}, u32[]{:S(2)}) collective-permute-start(bf16[16,256]{1,0:T(8,128)(2,1)S(1)} %get-tuple-element.21.a_ref), channel_id=1, source_target_pairs={{64,0},{96,32},{0,64},{32,96},{65,1},{97,33},{1,65},{33,97},{66,2}... | collective-permute-start | bytes 24584 | tf_op jit(solution)/shard_map/ppermute | solution.py:369
  53.6 1.0 collective-permute-done.4.c_ref
  54.5 1.4 %collective-permute-done.3.b_ref = bf16[16,256]{1,0:T(8,128)(2,1)S(1)} collective-permute-done((bf16[16,256]{1,0:T(8,128)(2,1)S(1)}, bf16[16,256]{1,0:T(8,128)(2,1)S(1)}, u32[]{:S(2)}, u32[]{:S(2)}) %collective-permute-start.3) | collective-permute-done | bytes 8224 | tf_op jit(solution)/shard_map/ppermute | solution.py:369
  56.2 13.1 %all_to_all.32.got_ref = bf16[32,2,1280]{2,1,0:T(2,128)(2,1)S(1)} all-to-all(bf16[32,2,1280]{2,1,0:T(2,128)(2,1)S(1)} %output.1), channel_id=1, replica_groups=mesh['rows'=4,'wide'=32] {'wide'}, dimensions={0} | all-to-all | bytes 327680 | tf_op jit(solution)/shard_map/all_to_all | solution.py:374
  69.5 11.6 %all_to_all.33.attended_ref = bf16[32,2,1280]{2,1,0:T(2,128)(2,1)S(1)} all-to-all(bf16[32,2,1280]{2,1,0:T(2,128)(2,1)S(1)} %sum_spread.2), channel_id=1, replica_groups=mesh['rows'=4,'wide'=32] {'wide'}, dimensions={0} | all-to-all | bytes 327680 | tf_op jit(solution)/shard_map/all_to_all | solution.py:374
  81.1 1.3 %gate_up.1 = (f32[64,1280]{1,0:T(8,128)S(1)}, bf16[16,1792]{1,0:T(8,128)(2,1)S(1)}, bf16[16,1792]{1,0:T(8,128)(2,1)S(1)}, bf16[16,1792]{1,0:T(8,128)(2,1)S(1)}, bf16[16,1792]{1,0:T(8,128)(2,1)S(1)}) custom-call(s32[1]{0:T(128)} %bitcast.place_ref, bf16[64,1280]{1,0:T(8,128)(2,1)S(1)} %copy-done.3, bf16[32,2,1280]{2,1,0:T(2,128)(2,1)S(1)} %all_to_all.33.attended_ref, ...), custom_call_target="tpu_custom_call" | custom-call | tf_op jit(solution)/shard_map/gate_up/pallas_call | solution.py:464
  82.5 2.1 %collective-permute-start.7 = (bf16[16,1792]{1,0:T(8,128)(2,1)S(1)}, bf16[16,1792]{1,0:T(8,128)(2,1)S(1)}, u32[]{:S(2)}, u32[]{:S(2)}) collective-permute-start(bf16[16,1792]{1,0:T(8,128)(2,1)S(1)} %get-tuple-element.25), channel_id=1, source_target_pairs={{0,64},{32,96},{64,0},{96,32},{1,65},{33,97},{65,1},{97,33},{2,66}... | collective-permute-start | bytes 172040 | tf_op jit(solution)/shard_map/ppermute | solution.py:362
  84.6 1.1 collective-permute-start.8
  85.8 1.5 %collective-permute-done.6.b_ref = bf16[16,1792]{1,0:T(8,128)(2,1)S(1)} collective-permute-done((bf16[16,1792]{1,0:T(8,128)(2,1)S(1)}, bf16[16,1792]{1,0:T(8,128)(2,1)S(1)}, u32[]{:S(2)}, u32[]{:S(2)}) %collective-permute-start.6) | collective-permute-done | bytes 57376 | tf_op jit(solution)/shard_map/ppermute | solution.py:362
  88.5 1.2 collective-permute-start.11
  89.7 2.5 %collective-permute-start.10 = (bf16[16,896]{1,0:T(8,128)(2,1)S(1)}, bf16[16,896]{1,0:T(8,128)(2,1)S(1)}, u32[]{:S(2)}, u32[]{:S(2)}) collective-permute-start(bf16[16,896]{1,0:T(8,128)(2,1)S(1)} %activate.1.a_ref), channel_id=1, source_target_pairs={{64,0},{96,32},{0,64},{32,96},{65,1},{97,33},{1,65},{33,97},{66,2}... | collective-permute-start | bytes 86024 | tf_op jit(solution)/shard_map/ppermute | solution.py:369
  92.5 1.4 %collective-permute-done.10.c_ref = bf16[16,896]{1,0:T(8,128)(2,1)S(1)} collective-permute-done((bf16[16,896]{1,0:T(8,128)(2,1)S(1)}, bf16[16,896]{1,0:T(8,128)(2,1)S(1)}, u32[]{:S(2)}, u32[]{:S(2)}) %collective-permute-start.10) | collective-permute-done | bytes 28704 | tf_op jit(solution)/shard_map/ppermute | solution.py:369
  93.9 1.0 collective-permute-done.9.b_ref
  95.3 14.3 %all_to_all.34.got_ref = bf16[32,2,1280]{2,1,0:T(2,128)(2,1)S(1)} all-to-all(bf16[32,2,1280]{2,1,0:T(2,128)(2,1)S(1)} %down.1), channel_id=1, replica_groups=mesh['rows'=4,'wide'=32] {'wide'}, dimensions={0} | all-to-all | bytes 327680 | tf_op jit(solution)/shard_map/all_to_all | solution.py:374
  109.8 11.6 %all_to_all.35.down_ref = bf16[32,2,1280]{2,1,0:T(2,128)(2,1)S(1)} all-to-all(bf16[32,2,1280]{2,1,0:T(2,128)(2,1)S(1)} %sum_spread.3), channel_id=1, replica_groups=mesh['rows'=4,'wide'=32] {'wide'}, dimensions={0} | all-to-all | bytes 327680 | tf_op jit(solution)/shard_map/all_to_all | solution.py:374
  (44 shorter events, 4.2 us)
Async XLA Ops:
  2.3 7.2 %collective-permute-start = (f32[16,384]{1,0:T(8,128)S(1)}, f32[16,384]{1,0:T(8,128)S(1)}, u32[]{:S(2)}, u32[]{:S(2)}) collective-permute-start(f32[16,384]{1,0:T(8,128)S(1)} %get-tuple-element.16), channel_id=1, source_target_pairs={{0,32},{32,64},{64,96},{96,0},{1,33},{33,65},{65,97},{97,1},{2,34}... | collective-permute-start | bytes 73736 | tf_op jit(solution)/shard_map/ppermute | solution.py:362
  4.4 5.1 %collective-permute-start.1 = (f32[16,384]{1,0:T(8,128)S(1)}, f32[16,384]{1,0:T(8,128)S(1)}, u32[]{:S(2)}, u32[]{:S(2)}) collective-permute-start(f32[16,384]{1,0:T(8,128)S(1)} %get-tuple-element.17), channel_id=1, source_target_pairs={{0,64},{32,96},{64,0},{96,32},{1,65},{33,97},{65,1},{97,33},{2,66}... | collective-permute-start | bytes 73736 | tf_op jit(solution)/shard_map/ppermute | solution.py:362
  6.8 3.0 %collective-permute-start.2 = (f32[16,384]{1,0:T(8,128)S(1)}, f32[16,384]{1,0:T(8,128)S(1)}, u32[]{:S(2)}, u32[]{:S(2)}) collective-permute-start(f32[16,384]{1,0:T(8,128)S(1)} %get-tuple-element.18), channel_id=1, source_target_pairs={{0,96},{32,0},{64,32},{96,64},{1,97},{33,1},{65,33},{97,65},{2,98}... | collective-permute-start | bytes 73736 | tf_op jit(solution)/shard_map/ppermute | solution.py:362
  9.8 20.2 %slice-start = ((s8[8388608]{0:T(1024)(128)(4,1)}), s8[4194304]{0:T(1024)(128)(4,1)S(1)}, s32[]{:S(2)}) async-start(s8[8388608]{0:T(1024)(128)(4,1)} %bitcast.5), calls=%async_computation.6 | async-start | bytes 8388608
  9.8 20.2 %slice-start.2 = ((s8[8388608]{0:T(1024)(128)(4,1)}), s8[4194304]{0:T(1024)(128)(4,1)S(1)}, s32[]{:S(2)}) async-start(s8[8388608]{0:T(1024)(128)(4,1)} %bitcast.7), calls=%async_computation.8 | async-start | bytes 8388608
  9.8 20.2 %slice-start.1 = ((s8[8388608]{0:T(1024)(128)(4,1)}), s8[4194304]{0:T(1024)(128)(4,1)S(1)}, s32[]{:S(2)}) async-start(s8[8388608]{0:T(1024)(128)(4,1)} %bitcast.5), calls=%async_computation.7 | async-start | bytes 8388608
  9.8 20.2 %slice-start.3 = ((s8[8388608]{0:T(1024)(128)(4,1)}), s8[4194304]{0:T(1024)(128)(4,1)S(1)}, s32[]{:S(2)}) async-start(s8[8388608]{0:T(1024)(128)(4,1)} %bitcast.7), calls=%async_computation.9 | async-start | bytes 8388608
  9.8 20.2 %copy-start.6 = (s32[16]{0:T(128)S(1)}, s32[16]{0:T(128)}, u32[]{:S(2)}) copy-start(s32[16]{0:T(128)} %length_ref.3) | copy-start | bytes 196
  9.8 20.2 %copy-start.7 = (s32[16,1]{0,1:T(1,128)S(1)}, s32[16,1]{0,1:T(1,128)}, u32[]{:S(2)}) copy-start(s32[16,1]{0,1:T(1,128)} %param.24) | copy-start | bytes 196
  30.0 25.9 %copy-start.4 = (bf16[256,1280]{1,0:T(8,128)(2,1)S(1)}, bf16[256,1280]{1,0:T(8,128)(2,1)}, u32[]{:S(2)}) copy-start(bf16[256,1280]{1,0:T(8,128)(2,1)} %w_ref.2) | copy-start | bytes 1966084
  30.1 51.0 %copy-start.1 = (bf16[1280,800]{0,1:T(8,128)(2,1)S(1)}, bf16[1280,800]{0,1:T(8,128)(2,1)}, u32[]{:S(2)}) copy-start(bf16[1280,800]{0,1:T(8,128)(2,1)} %param.28) | copy-start | bytes 6144004
  35.3 45.8 %copy-start = (bf16[1280,800]{0,1:T(8,128)(2,1)S(1)}, bf16[1280,800]{0,1:T(8,128)(2,1)}, u32[]{:S(2)}) copy-start(bf16[1280,800]{0,1:T(8,128)(2,1)} %param.27) | copy-start | bytes 6144004
  35.3 45.8 %copy-start.3 = (bf16[64,1280]{1,0:T(8,128)(2,1)S(1)}, bf16[64,1280]{1,0:T(8,128)(2,1)}, u32[]{:S(2)}) copy-start(bf16[64,1280]{1,0:T(8,128)(2,1)} %hidden_ref.1) | copy-start | bytes 491524
  35.3 45.7 %copy-start.5 = (bf16[1280]{0:T(1024)(128)(2,1)S(1)}, bf16[1280]{0:T(1024)(128)(2,1)}, u32[]{:S(2)}) copy-start(bf16[1280]{0:T(1024)(128)(2,1)} %gain_ref.1) | copy-start | bytes 7684
  49.9 3.7 %collective-permute-start.5 = (bf16[16,256]{1,0:T(8,128)(2,1)S(1)}, bf16[16,256]{1,0:T(8,128)(2,1)S(1)}, u32[]{:S(2)}, u32[]{:S(2)}) collective-permute-start(bf16[16,256]{1,0:T(8,128)(2,1)S(1)} %get-tuple-element.21.a_ref), channel_id=1, source_target_pairs={{96,0},{0,32},{32,64},{64,96},{97,1},{1,33},{33,65},{65,97},{98,2}... | collective-permute-start | bytes 24584 | tf_op jit(solution)/shard_map/ppermute | solution.py:369
  49.9 4.7 %collective-permute-start.4 = (bf16[16,256]{1,0:T(8,128)(2,1)S(1)}, bf16[16,256]{1,0:T(8,128)(2,1)S(1)}, u32[]{:S(2)}, u32[]{:S(2)}) collective-permute-start(bf16[16,256]{1,0:T(8,128)(2,1)S(1)} %get-tuple-element.21.a_ref), channel_id=1, source_target_pairs={{64,0},{96,32},{0,64},{32,96},{65,1},{97,33},{1,65},{33,97},{66,2}... | collective-permute-start | bytes 24584 | tf_op jit(solution)/shard_map/ppermute | solution.py:369
  53.4 2.5 %collective-permute-start.3 = (bf16[16,256]{1,0:T(8,128)(2,1)S(1)}, bf16[16,256]{1,0:T(8,128)(2,1)S(1)}, u32[]{:S(2)}, u32[]{:S(2)}) collective-permute-start(bf16[16,256]{1,0:T(8,128)(2,1)S(1)} %get-tuple-element.21.a_ref), channel_id=1, source_target_pairs={{32,0},{64,32},{96,64},{0,96},{33,1},{65,33},{97,65},{1,97},{34,2}... | collective-permute-start | bytes 24584 | tf_op jit(solution)/shard_map/ppermute | solution.py:369
  81.1 13.8 %copy-start.2 = (bf16[800,1280]{1,0:T(8,128)(2,1)S(1)}, bf16[800,1280]{1,0:T(8,128)(2,1)}, u32[]{:S(2)}) copy-start(bf16[800,1280]{1,0:T(8,128)(2,1)} %w_ref.3) | copy-start | bytes 6144004
  82.4 4.9 %collective-permute-start.6 = (bf16[16,1792]{1,0:T(8,128)(2,1)S(1)}, bf16[16,1792]{1,0:T(8,128)(2,1)S(1)}, u32[]{:S(2)}, u32[]{:S(2)}) collective-permute-start(bf16[16,1792]{1,0:T(8,128)(2,1)S(1)} %get-tuple-element.24), channel_id=1, source_target_pairs={{0,32},{32,64},{64,96},{96,0},{1,33},{33,65},{65,97},{97,1},{2,34}... | collective-permute-start | bytes 172040 | tf_op jit(solution)/shard_map/ppermute | solution.py:362
  82.5 5.5 %collective-permute-start.7 = (bf16[16,1792]{1,0:T(8,128)(2,1)S(1)}, bf16[16,1792]{1,0:T(8,128)(2,1)S(1)}, u32[]{:S(2)}, u32[]{:S(2)}) collective-permute-start(bf16[16,1792]{1,0:T(8,128)(2,1)S(1)} %get-tuple-element.25), channel_id=1, source_target_pairs={{0,64},{32,96},{64,0},{96,32},{1,65},{33,97},{65,1},{97,33},{2,66}... | collective-permute-start | bytes 172040 | tf_op jit(solution)/shard_map/ppermute | solution.py:362
  84.6 3.7 %collective-permute-start.8 = (bf16[16,1792]{1,0:T(8,128)(2,1)S(1)}, bf16[16,1792]{1,0:T(8,128)(2,1)S(1)}, u32[]{:S(2)}, u32[]{:S(2)}) collective-permute-start(bf16[16,1792]{1,0:T(8,128)(2,1)S(1)} %get-tuple-element.26), channel_id=1, source_target_pairs={{0,96},{32,0},{64,32},{96,64},{1,97},{33,1},{65,33},{97,65},{2,98}... | collective-permute-start | bytes 172040 | tf_op jit(solution)/shard_map/ppermute | solution.py:362
  88.5 4.0 %collective-permute-start.11 = (bf16[16,896]{1,0:T(8,128)(2,1)S(1)}, bf16[16,896]{1,0:T(8,128)(2,1)S(1)}, u32[]{:S(2)}, u32[]{:S(2)}) collective-permute-start(bf16[16,896]{1,0:T(8,128)(2,1)S(1)} %activate.1.a_ref), channel_id=1, source_target_pairs={{96,0},{0,32},{32,64},{64,96},{97,1},{1,33},{33,65},{65,97},{98,2}... | collective-permute-start | bytes 86024 | tf_op jit(solution)/shard_map/ppermute | solution.py:369
  89.7 4.2 %collective-permute-start.10 = (bf16[16,896]{1,0:T(8,128)(2,1)S(1)}, bf16[16,896]{1,0:T(8,128)(2,1)S(1)}, u32[]{:S(2)}, u32[]{:S(2)}) collective-permute-start(bf16[16,896]{1,0:T(8,128)(2,1)S(1)} %activate.1.a_ref), channel_id=1, source_target_pairs={{64,0},{96,32},{0,64},{32,96},{65,1},{97,33},{1,65},{33,97},{66,2}... | collective-permute-start | bytes 86024 | tf_op jit(solution)/shard_map/ppermute | solution.py:369
  92.1 2.7 %collective-permute-start.9 = (bf16[16,896]{1,0:T(8,128)(2,1)S(1)}, bf16[16,896]{1,0:T(8,128)(2,1)S(1)}, u32[]{:S(2)}, u32[]{:S(2)}) collective-permute-start(bf16[16,896]{1,0:T(8,128)(2,1)S(1)} %activate.1.a_ref), channel_id=1, source_target_pairs={{32,0},{64,32},{96,64},{0,96},{33,1},{65,33},{97,65},{1,97},{34,2}... | collective-permute-start | bytes 86024 | tf_op jit(solution)/shard_map/ppermute | solution.py:369

commit v5 on v4

--- a/solution.py
+++ b/solution.py
@@ -59,6 +59,10 @@
 
 def row_block(mine, k):
     return pl.ds(pl.multiple_of(lax.rem(mine + k, ROWS) * OWN, OWN), OWN)
+
+
+def height(place_ref):
+    return lax.rem(place_ref[0], WIDE) // 8
 
 
 def terms(value, count):
@@ -112,9 +116,7 @@
     whole[:, 256:] = jnp.concatenate([keyval, jnp.broadcast_to(square, keyval.shape)], axis=1)
     moves[2].wait()
     whole[:, :256] = jnp.dot(scaled, wq_ref[...], preferred_element_type=f32)
-    mine = place_ref[0] // WIDE
-    for k in range(ROWS):
-        outs[k][...] = whole[row_block(mine, k), :]
+    split_rows(outs, whole, place_ref[0] // WIDE)
 
 
 def table_kernel(
@@ -286,30 +288,31 @@
         again_ref[:, lanes] = heads
 
 
-def store_pairs(out_ref, value):
-    for block in range(WIDE):
-        out_ref[block] = value[2 * block : 2 * block + 2]
-
-
-def output_kernel(a_ref, b_ref, c_ref, d_ref, w_ref, out_ref):
+def split_rows(outs, whole, first):
+    for k in range(ROWS):
+        outs[k][...] = whole[row_block(first, k), :]
+
+
+def output_kernel(place_ref, a_ref, b_ref, c_ref, d_ref, w_ref, *rest):
+    outs, whole = rest[:ROWS], rest[ROWS]
     heads = jnp.concatenate([a_ref[...], b_ref[...], c_ref[...], d_ref[...]], axis=0)
-    store_pairs(out_ref, jnp.dot(heads, w_ref[...], preferred_element_type=f32).astype(bf16))
-
-
-def sum_spread_kernel(got_ref, out_ref):
-    total = jnp.sum(got_ref[...].astype(f32), axis=0).astype(bf16)
-    out_ref[...] = jnp.broadcast_to(total[None], out_ref.shape)
-
-
-def gate_up_kernel(
-    place_ref, hidden_ref, attended_ref, gain_ref, wg_ref, wu_ref, stream_ref, *outs
-):
-    mine = place_ref[0] // WIDE
-    for k in range(ROWS):
-        at = slice(k * OWN, (k + 1) * OWN)
-        blocks = attended_ref[k * WIDE // ROWS : (k + 1) * WIDE // ROWS]
-        attended = blocks.astype(f32).reshape(OWN, blocks.shape[-1])
-        stream_ref[at, :] = hidden_ref[row_block(mine, k), :].astype(f32) + attended
+    whole[...] = jnp.dot(heads, w_ref[...], preferred_element_type=f32).astype(bf16)
+    split_rows(outs, whole, height(place_ref))
+
+
+def add_kernel(*refs):
+    out_ref = refs[-1]
+    parts = [ref[...].astype(f32) for ref in refs[:-1]]
+    if len(parts) == ROWS:
+        parts = [parts[0] + parts[2], parts[1] + parts[3]]
+    out_ref[...] = (parts[0] + parts[1]).astype(bf16)
+
+
+def gate_up_kernel(place_ref, hidden_ref, a_ref, b_ref, c_ref, d_ref, gain_ref, wg_ref, wu_ref, stream_ref, *outs):
+    mine, first = place_ref[0] // WIDE, height(place_ref)
+    for k, ref in enumerate((a_ref, b_ref, c_ref, d_ref)):
+        hidden = hidden_ref[row_block(mine + first, k), :].astype(f32)
+        stream_ref[row_block(first, k), :] = hidden + ref[...].astype(f32)
     stream = stream_ref[...]
     square = jnp.sum(stream * stream, axis=1, keepdims=True)
     scaled = (stream * gain_ref[...].astype(f32)[None]).astype(bf16)
@@ -341,32 +344,42 @@
     out_ref[...] = (gate / (1.0 + jnp.exp(-gate)) * up).astype(bf16)
 
 
-def down_kernel(a_ref, b_ref, c_ref, d_ref, w_ref, out_ref):
+def down_kernel(place_ref, a_ref, b_ref, c_ref, d_ref, w_ref, *rest):
+    outs, whole = rest[:ROWS], rest[ROWS]
     units = jnp.concatenate([a_ref[...], b_ref[...], c_ref[...], d_ref[...]], axis=0)
     part = jnp.dot(units[:, :HIDDEN_UNITS], w_ref[...], preferred_element_type=f32)
-    store_pairs(out_ref, part.astype(bf16))
-
-
-def final_kernel(place_ref, stream_ref, down_ref, out_ref):
-    mine = place_ref[0] // WIDE
-    for k in range(ROWS):
-        at = slice(k * OWN, (k + 1) * OWN)
-        blocks = down_ref[k * WIDE // ROWS : (k + 1) * WIDE // ROWS]
-        down = blocks.astype(f32).reshape(OWN, blocks.shape[-1])
-        out_ref[row_block(mine, k), :] = (stream_ref[at, :] + down).astype(bf16)
-
-
-def to_rows(blocks):
+    whole[...] = part.astype(bf16)
+    split_rows(outs, whole, height(place_ref))
+
+
+def final_kernel(place_ref, stream_ref, a_ref, b_ref, c_ref, d_ref, out_ref):
+    mine, first = place_ref[0] // WIDE, height(place_ref)
+    for k, ref in enumerate((a_ref, b_ref, c_ref, d_ref)):
+        stream = stream_ref[row_block(first, k), :]
+        out_ref[row_block(mine + first, k), :] = (stream + ref[...].astype(f32)).astype(bf16)
+
+
+def ahead(axis, k):
+    if axis == "x":
+        return "rows", [(i, (i + k) % ROWS) for i in range(ROWS)]
+    if axis == "y":
+        return "wide", [(i, (i + 8 * k) % WIDE) for i in range(WIDE)]
+    if axis == "z":
+        return "wide", [(i, i // 8 * 8 + (i + 2 * k) % 8) for i in range(WIDE)]
+    return "wide", [(i, i ^ 1) for i in range(WIDE)]
+
+
+def to_peers(blocks, axis):
     got = list(blocks)
     for k in (2, 1, 3):
-        got[k] = lax.ppermute(blocks[k], "rows", [(i, (i + k) % ROWS) for i in range(ROWS)])
+        got[k] = lax.ppermute(blocks[k], *ahead(axis, k))
     return got
 
 
-def from_rows(own):
+def from_peers(own, axis):
     got = [own] * ROWS
     for k in (2, 1, 3):
-        got[k] = lax.ppermute(own, "rows", [((i + k) % ROWS, i) for i in range(ROWS)])
+        got[k] = lax.ppermute(own, *ahead(axis, ROWS - k))
     return got
 
 
@@ -374,15 +387,20 @@
     return lax.all_to_all(blocks, "wide", split_axis=0, concat_axis=0, tiled=True)
 
 
-def sum_wide(part):
-    total = call(
-        sum_spread_kernel,
-        jax.ShapeDtypeStruct(part.shape, bf16),
-        [VMEM],
-        limit=4,
-        name="sum_spread",
-    )(exchange(part))
-    return exchange(total)
+def sum_wide(blocks):
+    def add(parts):
+        return call(
+            add_kernel,
+            jax.ShapeDtypeStruct(parts[0].shape, bf16),
+            [VMEM] * len(parts),
+            limit=4,
+            name="add",
+        )(*parts)
+
+    own = add(to_peers(blocks, "y"))
+    own = add(from_peers(own, "z"))
+    own = add([own, lax.ppermute(own, *ahead("core", 1))])
+    return from_peers(own, "y")
 
 
 def body(
@@ -435,7 +453,7 @@
         limit=8,
         name="heads",
         cost=pl.CostEstimate(flops=20_000_000_000, bytes_accessed=1 << 20, transcendentals=0),
-    )(*to_rows(blocks), straight, swapped)
+    )(*to_peers(blocks, "x"), straight, swapped)
     gathered = exchange(payload)
 
     parts = call(
@@ -456,27 +474,27 @@
         combine_kernel, [sds((OWN, 256), bf16)] * 2, [SMEM] + [VMEM] * 4, limit=8, name="combine"
     )(place, exchange(parts), gathered, straight, swapped)
 
-    out_part = call(output_kernel, sds((WIDE, 2, 1280), bf16), [VMEM] * 5, limit=8, name="output")(
-        *from_rows(heads_own), w_out
+    part = [sds((OWN, 1280), bf16)] * ROWS
+    whole = [pltpu.VMEM((64, 1280), bf16)]
+    parts = call(output_kernel, part, [SMEM] + [VMEM] * 5, whole, limit=8, name="output")(
+        place, *from_peers(heads_own, "x"), w_out
     )
-    attended = sum_wide(out_part)
-
     stream, *blocks = call(
         gate_up_kernel,
         [sds((64, 1280), f32)] + [sds((OWN, 2 * HALF), bf16)] * ROWS,
-        [SMEM] + [VMEM] * 5,
+        [SMEM] + [VMEM] * 8,
         limit=12,
         name="gate_up",
-    )(place, hidden, attended, mlp_gain, w_gate.T, w_up.T)
+    )(place, hidden, *sum_wide(parts), mlp_gain, w_gate.T, w_up.T)
     activated = call(
         activate_kernel, sds((OWN, HALF), bf16), [VMEM] * 4, limit=8, name="activate"
-    )(*to_rows(blocks))
-    down_part = call(down_kernel, sds((WIDE, 2, 1280), bf16), [VMEM] * 5, limit=8, name="down")(
-        *from_rows(activated), w_down
+    )(*to_peers(blocks, "x"))
+    parts = call(down_kernel, part, [SMEM] + [VMEM] * 5, whole, limit=8, name="down")(
+        place, *from_peers(activated, "x"), w_down
     )
-    layer_out = call(final_kernel, sds((64, 1280), bf16), [SMEM] + [VMEM] * 2, limit=8, name="final")(
-        place, stream, sum_wide(down_part)
-    )
+    layer_out = call(
+        final_kernel, sds((64, 1280), bf16), [SMEM] + [VMEM] * 5, limit=8, name="final"
+    )(place, stream, *sum_wide(parts))
     return (layer_out, heads_out)
 
 

time: 122 us -> 122 us (level)
  blocking collectives: 83.6 us -> 33.1 us
  starting transfers between devices: 16.3 us -> 49.7 us
  waiting for transfers between devices: 8.05 us -> 24.6 us
    all_to_all x6 -> x2, blocking collectives: 83.6 us -> 33.1 us  [exchange(): lax.all_to_all(blocks, 'wide', split_axis=0, concat_axis=0, tiled=True)]
    ppermute x12 -> x32, starting transfers between devices: 16.3 us -> 49.7 us  [the longest x18 21.1 us: from_peers(): got[k] = lax.ppermute(own, *ahead(axis, ROWS - k))]
    ppermute x12 -> x32, waiting for transfers between devices: 8.05 us -> 24.6 us  [the longest x18 16.5 us: from_peers(): got[k] = lax.ppermute(own, *ahead(axis, ROWS - k))]
  transfers between devices with their start and end apart: 12 -> 32, of which waited for: 10 -> 29; matrix products, arithmetic and copies ran while one was open for 0% -> 0% of each run, Pallas kernels for 1% -> 1%
where the time goes in v5:
time: 122 us; the launch traced here: 121 us
  starting transfers between devices  49.7 us (41%)
  blocking collectives  33.1 us (27%)
  waiting for transfers between devices  24.6 us (20%)
  Pallas kernels  13 us (11%)
    all_to_all x2, blocking collectives, exchange(): lax.all_to_all(blocks, 'wide', split_axis=0, concat_axis=0, tiled=True)  33.1 us
    ppermute x18, starting transfers between devices, from_peers(): got[k] = lax.ppermute(own, *ahead(axis, ROWS - k))  21.1 us
    ppermute x18, waiting for transfers between devices, from_peers(): got[k] = lax.ppermute(own, *ahead(axis, ROWS - k))  16.5 us
    ppermute x12, starting transfers between devices, to_peers(): got[k] = lax.ppermute(blocks[k], *ahead(axis, k))  15.6 us
    ppermute x2, starting transfers between devices, sum_wide(): own = add([own, lax.ppermute(own, *ahead('core', 1))])  13 us
    ppermute x12, waiting for transfers between devices, to_peers(): got[k] = lax.ppermute(blocks[k], *ahead(axis, k))  6.38 us
    pallas_call x1, Pallas kernels, body(): call(attend_kernel, sds((WIDE, PACKED, 128), bf16), [SMEM, SMEM, VMEM, VM...  5.2 us
  transfers between devices with their start and end apart: 32, of which 29 were waited for; matrix products, arithmetic and copies ran while one was open for 0% of the time, Pallas kernels for 1%

profile of v5, /device:TPU:1, one launch (start us, length us, event | category | flops | bytes accessed | tf_op | source)
XLA Modules:
  0.0 121.3 jit_solution(6849382062837822666)
XLA Ops:
  0.6 1.6 %project.1 = (f32[16,384]{1,0:T(8,128)S(1)}, f32[16,384]{1,0:T(8,128)S(1)}, f32[16,384]{1,0:T(8,128)S(1)}, f32[16,384]{1,0:T(8,128)S(1)}) custom-call(s32[1]{0:T(128)} %bitcast.place_ref, bf16[64,1280]{1,0:T(8,128)(2,1)} %hidden_ref.1, bf16[1280]{0:T(1024)(128)(2,1)} %gain_hbm.1, bf16[1280,256]{1,0:T(8,128)(2,1)} %wq_hbm.1, bf16[64,1280]{1,0:T(8,128)(2,1)} %bitcast.12), custom_call_target="tpu_custom_call" | custom-call | tf_op jit(solution)/shard_map/project/pallas_call | solution.py:426
  2.3 2.1 %collective-permute-start = (f32[16,384]{1,0:T(8,128)S(1)}, f32[16,384]{1,0:T(8,128)S(1)}, u32[]{:S(2)}, u32[]{:S(2)}) collective-permute-start(f32[16,384]{1,0:T(8,128)S(1)} %get-tuple-element.24), channel_id=1, source_target_pairs={{0,32},{32,64},{64,96},{96,0},{1,33},{33,65},{65,97},{97,1},{2,34}... | collective-permute-start | bytes 73736 | tf_op jit(solution)/shard_map/ppermute | solution.py:375
  4.4 2.5 %collective-permute-start.1 = (f32[16,384]{1,0:T(8,128)S(1)}, f32[16,384]{1,0:T(8,128)S(1)}, u32[]{:S(2)}, u32[]{:S(2)}) collective-permute-start(f32[16,384]{1,0:T(8,128)S(1)} %get-tuple-element.25), channel_id=1, source_target_pairs={{0,64},{32,96},{64,0},{96,32},{1,65},{33,97},{65,1},{97,33},{2,66}... | collective-permute-start | bytes 73736 | tf_op jit(solution)/shard_map/ppermute | solution.py:375
  8.0 1.5 %tables.1 = (f32[2,16,128]{2,1,0:T(8,128)S(1)}, f32[2,16,128]{2,1,0:T(8,128)S(1)}) custom-call(s32[16]{0:T(128)} %length_ref.3, bf16[128]{0:T(256)(128)(2,1)} %query_hbm.1, bf16[128]{0:T(256)(128)(2,1)} %key_hbm.1), custom_call_target="tpu_custom_call" | custom-call | tf_op jit(solution)/shard_map/tables/pallas_call | solution.py:441
  10.1 19.9 %all_to_all.10.g_ref = bf16[32,40,128]{2,1,0:T(8,128)(2,1)S(1)} all-to-all(bf16[32,40,128]{2,1,0:T(8,128)(2,1)S(1)} %heads.1), channel_id=1, replica_groups=mesh['rows'=4,'wide'=32] {'wide'}, dimensions={0} | all-to-all | bytes 655360 | tf_op jit(solution)/shard_map/all_to_all | solution.py:387
  30.1 5.2 %attend.1 = bf16[32,40,128]{2,1,0:T(8,128)(2,1)S(1)} custom-call(s32[16]{0:T(128)S(1)} %copy-done.6, s32[16]{0:T(128)S(1)} %bitcast.11, bf16[32,40,128]{2,1,0:T(8,128)(2,1)S(1)} %all_to_all.10.g_ref, bf16[16,256,1024]{2,1,0:T(8,128)(2,1)S(1)} %bitcast.6, bf16[16,256,1024]{2,1,0:T(8,128)(2,1)S(1)} %bitcast.8), custom_call_target="tpu_custom_call" | custom-call | tf_op jit(solution)/shard_map/attend/pallas_call | solution.py:459
  35.3 13.2 %all_to_all.11.r_ref = bf16[32,40,128]{2,1,0:T(8,128)(2,1)S(1)} all-to-all(bf16[32,40,128]{2,1,0:T(8,128)(2,1)S(1)} %attend.1), channel_id=1, replica_groups=mesh['rows'=4,'wide'=32] {'wide'}, dimensions={0} | all-to-all | bytes 655360 | tf_op jit(solution)/shard_map/all_to_all | solution.py:387
  48.5 1.4 %combine.1 = (bf16[16,256]{1,0:T(8,128)(2,1)}, bf16[16,256]{1,0:T(8,128)(2,1)S(1)}) custom-call(s32[1]{0:T(128)} %bitcast.place_ref, bf16[32,40,128]{2,1,0:T(8,128)(2,1)S(1)} %all_to_all.11.r_ref, bf16[32,40,128]{2,1,0:T(8,128)(2,1)S(1)} %all_to_all.10.g_ref, f32[2,16,128]{2,1,0:T(8,128)S(1)} %get-tuple-element.27.straight_ref, ...), custom_call_target="tpu_custom_call" | custom-call | tf_op jit(solution)/shard_map/combine/pallas_call | solution.py:473
  49.9 3.5 %collective-permute-start.4 = (bf16[16,256]{1,0:T(8,128)(2,1)S(1)}, bf16[16,256]{1,0:T(8,128)(2,1)S(1)}, u32[]{:S(2)}, u32[]{:S(2)}) collective-permute-start(bf16[16,256]{1,0:T(8,128)(2,1)S(1)} %get-tuple-element.29.a_ref), channel_id=1, source_target_pairs={{0,64},{32,96},{64,0},{96,32},{1,65},{33,97},{65,1},{97,33},{2,66}... | collective-permute-start | bytes 24584 | tf_op jit(solution)/shard_map/ppermute | solution.py:382
  54.5 1.4 %collective-permute-done.3.b_ref = bf16[16,256]{1,0:T(8,128)(2,1)S(1)} collective-permute-done((bf16[16,256]{1,0:T(8,128)(2,1)S(1)}, bf16[16,256]{1,0:T(8,128)(2,1)S(1)}, u32[]{:S(2)}, u32[]{:S(2)}) %collective-permute-start.3) | collective-permute-done | bytes 8224 | tf_op jit(solution)/shard_map/ppermute | solution.py:382
  56.5 1.7 %collective-permute-start.7 = (bf16[16,1280]{1,0:T(8,128)(2,1)S(1)}, bf16[16,1280]{1,0:T(8,128)(2,1)S(1)}, u32[]{:S(2)}, u32[]{:S(2)}) collective-permute-start(bf16[16,1280]{1,0:T(8,128)(2,1)S(1)} %get-tuple-element.32), channel_id=1, source_target_pairs={{0,16},{1,17},{2,18},{3,19},{4,20},{5,21},{6,22},{7,23},{8,24},{9,... | collective-permute-start | bytes 122888 | tf_op jit(solution)/shard_map/ppermute | solution.py:375
  61.6 2.0 %collective-permute-start.10 = (bf16[16,1280]{1,0:T(8,128)(2,1)S(1)}, bf16[16,1280]{1,0:T(8,128)(2,1)S(1)}, u32[]{:S(2)}, u32[]{:S(2)}) collective-permute-start(bf16[16,1280]{1,0:T(8,128)(2,1)S(1)} %add.10.refs_0_), channel_id=1, source_target_pairs={{0,4},{1,5},{2,6},{3,7},{4,0},{5,1},{6,2},{7,3},{8,12},{9,13},{10,... | collective-permute-start | bytes 122888 | tf_op jit(solution)/shard_map/ppermute | solution.py:382
  64.1 1.4 %collective-permute-done.11.refs_3_ = bf16[16,1280]{1,0:T(8,128)(2,1)S(1)} collective-permute-done((bf16[16,1280]{1,0:T(8,128)(2,1)S(1)}, bf16[16,1280]{1,0:T(8,128)(2,1)S(1)}, u32[]{:S(2)}, u32[]{:S(2)}) %collective-permute-start.11) | collective-permute-done | bytes 40992 | tf_op jit(solution)/shard_map/ppermute | solution.py:382
  66.5 4.9 %collective-permute-start.12 = (bf16[16,1280]{1,0:T(8,128)(2,1)S(1)}, bf16[16,1280]{1,0:T(8,128)(2,1)S(1)}, u32[]{:S(2)}, u32[]{:S(2)}) collective-permute-start(bf16[16,1280]{1,0:T(8,128)(2,1)S(1)} %add.11.refs_0_), channel_id=1, source_target_pairs={{0,1},{1,0},{2,3},{3,2},{4,5},{5,4},{6,7},{7,6},{8,9},{9,8},{10,11... | collective-permute-start | bytes 122888 | tf_op jit(solution)/shard_map/ppermute | solution.py:402
  73.6 2.5 %collective-permute-start.14 = (bf16[16,1280]{1,0:T(8,128)(2,1)S(1)}, bf16[16,1280]{1,0:T(8,128)(2,1)S(1)}, u32[]{:S(2)}, u32[]{:S(2)}) collective-permute-start(bf16[16,1280]{1,0:T(8,128)(2,1)S(1)} %add.12.a_ref), channel_id=1, source_target_pairs={{0,16},{1,17},{2,18},{3,19},{4,20},{5,21},{6,22},{7,23},{8,24},{9,... | collective-permute-start | bytes 122888 | tf_op jit(solution)/shard_map/ppermute | solution.py:382
  76.4 1.6 %collective-permute-done.14.c_ref = bf16[16,1280]{1,0:T(8,128)(2,1)S(1)} collective-permute-done((bf16[16,1280]{1,0:T(8,128)(2,1)S(1)}, bf16[16,1280]{1,0:T(8,128)(2,1)S(1)}, u32[]{:S(2)}, u32[]{:S(2)}) %collective-permute-start.14) | collective-permute-done | bytes 40992 | tf_op jit(solution)/shard_map/ppermute | solution.py:382
  80.6 2.1 %collective-permute-start.17 = (bf16[16,1792]{1,0:T(8,128)(2,1)S(1)}, bf16[16,1792]{1,0:T(8,128)(2,1)S(1)}, u32[]{:S(2)}, u32[]{:S(2)}) collective-permute-start(bf16[16,1792]{1,0:T(8,128)(2,1)S(1)} %get-tuple-element.37), channel_id=1, source_target_pairs={{0,64},{32,96},{64,0},{96,32},{1,65},{33,97},{65,1},{97,33},{2,66}... | collective-permute-start | bytes 172040 | tf_op jit(solution)/shard_map/ppermute | solution.py:375
  83.9 1.6 %collective-permute-done.16.b_ref = bf16[16,1792]{1,0:T(8,128)(2,1)S(1)} collective-permute-done((bf16[16,1792]{1,0:T(8,128)(2,1)S(1)}, bf16[16,1792]{1,0:T(8,128)(2,1)S(1)}, u32[]{:S(2)}, u32[]{:S(2)}) %collective-permute-start.16) | collective-permute-done | bytes 57376 | tf_op jit(solution)/shard_map/ppermute | solution.py:375
  87.2 2.7 %collective-permute-start.20 = (bf16[16,896]{1,0:T(8,128)(2,1)S(1)}, bf16[16,896]{1,0:T(8,128)(2,1)S(1)}, u32[]{:S(2)}, u32[]{:S(2)}) collective-permute-start(bf16[16,896]{1,0:T(8,128)(2,1)S(1)} %activate.1.a_ref), channel_id=1, source_target_pairs={{0,64},{32,96},{64,0},{96,32},{1,65},{33,97},{65,1},{97,33},{2,66}... | collective-permute-start | bytes 86024 | tf_op jit(solution)/shard_map/ppermute | solution.py:382
  93.2 2.4 %collective-permute-start.23 = (bf16[16,1280]{1,0:T(8,128)(2,1)S(1)}, bf16[16,1280]{1,0:T(8,128)(2,1)S(1)}, u32[]{:S(2)}, u32[]{:S(2)}) collective-permute-start(bf16[16,1280]{1,0:T(8,128)(2,1)S(1)} %get-tuple-element.41), channel_id=1, source_target_pairs={{0,16},{1,17},{2,18},{3,19},{4,20},{5,21},{6,22},{7,23},{8,24},{9,... | collective-permute-start | bytes 122888 | tf_op jit(solution)/shard_map/ppermute | solution.py:375
  99.7 2.4 %collective-permute-start.26 = (bf16[16,1280]{1,0:T(8,128)(2,1)S(1)}, bf16[16,1280]{1,0:T(8,128)(2,1)S(1)}, u32[]{:S(2)}, u32[]{:S(2)}) collective-permute-start(bf16[16,1280]{1,0:T(8,128)(2,1)S(1)} %add.13.refs_0_), channel_id=1, source_target_pairs={{0,4},{1,5},{2,6},{3,7},{4,0},{5,1},{6,2},{7,3},{8,12},{9,13},{10,... | collective-permute-start | bytes 122888 | tf_op jit(solution)/shard_map/ppermute | solution.py:382
  105.0 8.1 %collective-permute-start.28 = (bf16[16,1280]{1,0:T(8,128)(2,1)S(1)}, bf16[16,1280]{1,0:T(8,128)(2,1)S(1)}, u32[]{:S(2)}, u32[]{:S(2)}) collective-permute-start(bf16[16,1280]{1,0:T(8,128)(2,1)S(1)} %add.14.refs_0_), channel_id=1, source_target_pairs={{0,1},{1,0},{2,3},{3,2},{4,5},{5,4},{6,7},{7,6},{8,9},{9,8},{10,11... | collective-permute-start | bytes 122888 | tf_op jit(solution)/shard_map/ppermute | solution.py:402
  115.0 2.4 %collective-permute-start.30 = (bf16[16,1280]{1,0:T(8,128)(2,1)S(1)}, bf16[16,1280]{1,0:T(8,128)(2,1)S(1)}, u32[]{:S(2)}, u32[]{:S(2)}) collective-permute-start(bf16[16,1280]{1,0:T(8,128)(2,1)S(1)} %add.15.a_ref), channel_id=1, source_target_pairs={{0,16},{1,17},{2,18},{3,19},{4,20},{5,21},{6,22},{7,23},{8,24},{9,... | collective-permute-start | bytes 122888 | tf_op jit(solution)/shard_map/ppermute | solution.py:382
  118.1 1.4 %collective-permute-done.30.c_ref = bf16[16,1280]{1,0:T(8,128)(2,1)S(1)} collective-permute-done((bf16[16,1280]{1,0:T(8,128)(2,1)S(1)}, bf16[16,1280]{1,0:T(8,128)(2,1)S(1)}, u32[]{:S(2)}, u32[]{:S(2)}) %collective-permute-start.30) | collective-permute-done | bytes 40992 | tf_op jit(solution)/shard_map/ppermute | solution.py:382
  (84 shorter events, 30.9 us)
Async XLA Ops:
  2.3 7.2 %collective-permute-start = (f32[16,384]{1,0:T(8,128)S(1)}, f32[16,384]{1,0:T(8,128)S(1)}, u32[]{:S(2)}, u32[]{:S(2)}) collective-permute-start(f32[16,384]{1,0:T(8,128)S(1)} %get-tuple-element.24), channel_id=1, source_target_pairs={{0,32},{32,64},{64,96},{96,0},{1,33},{33,65},{65,97},{97,1},{2,34}... | collective-permute-start | bytes 73736 | tf_op jit(solution)/shard_map/ppermute | solution.py:375
  4.4 5.1 %collective-permute-start.1 = (f32[16,384]{1,0:T(8,128)S(1)}, f32[16,384]{1,0:T(8,128)S(1)}, u32[]{:S(2)}, u32[]{:S(2)}) collective-permute-start(f32[16,384]{1,0:T(8,128)S(1)} %get-tuple-element.25), channel_id=1, source_target_pairs={{0,64},{32,96},{64,0},{96,32},{1,65},{33,97},{65,1},{97,33},{2,66}... | collective-permute-start | bytes 73736 | tf_op jit(solution)/shard_map/ppermute | solution.py:375
  49.9 3.7 %collective-permute-start.5 = (bf16[16,256]{1,0:T(8,128)(2,1)S(1)}, bf16[16,256]{1,0:T(8,128)(2,1)S(1)}, u32[]{:S(2)}, u32[]{:S(2)}) collective-permute-start(bf16[16,256]{1,0:T(8,128)(2,1)S(1)} %get-tuple-element.29.a_ref), channel_id=1, source_target_pairs={{0,32},{32,64},{64,96},{96,0},{1,33},{33,65},{65,97},{97,1},{2,34}... | collective-permute-start | bytes 24584 | tf_op jit(solution)/shard_map/ppermute | solution.py:382
  49.9 4.7 %collective-permute-start.4 = (bf16[16,256]{1,0:T(8,128)(2,1)S(1)}, bf16[16,256]{1,0:T(8,128)(2,1)S(1)}, u32[]{:S(2)}, u32[]{:S(2)}) collective-permute-start(bf16[16,256]{1,0:T(8,128)(2,1)S(1)} %get-tuple-element.29.a_ref), channel_id=1, source_target_pairs={{0,64},{32,96},{64,0},{96,32},{1,65},{33,97},{65,1},{97,33},{2,66}... | collective-permute-start | bytes 24584 | tf_op jit(solution)/shard_map/ppermute | solution.py:382
  56.2 4.1 %collective-permute-start.6 = (bf16[16,1280]{1,0:T(8,128)(2,1)S(1)}, bf16[16,1280]{1,0:T(8,128)(2,1)S(1)}, u32[]{:S(2)}, u32[]{:S(2)}) collective-permute-start(bf16[16,1280]{1,0:T(8,128)(2,1)S(1)} %get-tuple-element.31), channel_id=1, source_target_pairs={{0,8},{1,9},{2,10},{3,11},{4,12},{5,13},{6,14},{7,15},{8,16},{9,17... | collective-permute-start | bytes 122888 | tf_op jit(solution)/shard_map/ppermute | solution.py:375
  56.5 4.4 %collective-permute-start.7 = (bf16[16,1280]{1,0:T(8,128)(2,1)S(1)}, bf16[16,1280]{1,0:T(8,128)(2,1)S(1)}, u32[]{:S(2)}, u32[]{:S(2)}) collective-permute-start(bf16[16,1280]{1,0:T(8,128)(2,1)S(1)} %get-tuple-element.32), channel_id=1, source_target_pairs={{0,16},{1,17},{2,18},{3,19},{4,20},{5,21},{6,22},{7,23},{8,24},{9,... | collective-permute-start | bytes 122888 | tf_op jit(solution)/shard_map/ppermute | solution.py:375
  61.4 4.1 %collective-permute-start.11 = (bf16[16,1280]{1,0:T(8,128)(2,1)S(1)}, bf16[16,1280]{1,0:T(8,128)(2,1)S(1)}, u32[]{:S(2)}, u32[]{:S(2)}) collective-permute-start(bf16[16,1280]{1,0:T(8,128)(2,1)S(1)} %add.10.refs_0_), channel_id=1, source_target_pairs={{0,2},{1,3},{2,4},{3,5},{4,6},{5,7},{6,0},{7,1},{8,10},{9,11},{10,... | collective-permute-start | bytes 122888 | tf_op jit(solution)/shard_map/ppermute | solution.py:382
  61.6 4.4 %collective-permute-start.10 = (bf16[16,1280]{1,0:T(8,128)(2,1)S(1)}, bf16[16,1280]{1,0:T(8,128)(2,1)S(1)}, u32[]{:S(2)}, u32[]{:S(2)}) collective-permute-start(bf16[16,1280]{1,0:T(8,128)(2,1)S(1)} %add.10.refs_0_), channel_id=1, source_target_pairs={{0,4},{1,5},{2,6},{3,7},{4,0},{5,1},{6,2},{7,3},{8,12},{9,13},{10,... | collective-permute-start | bytes 122888 | tf_op jit(solution)/shard_map/ppermute | solution.py:382
  66.5 5.8 %collective-permute-start.12 = (bf16[16,1280]{1,0:T(8,128)(2,1)S(1)}, bf16[16,1280]{1,0:T(8,128)(2,1)S(1)}, u32[]{:S(2)}, u32[]{:S(2)}) collective-permute-start(bf16[16,1280]{1,0:T(8,128)(2,1)S(1)} %add.11.refs_0_), channel_id=1, source_target_pairs={{0,1},{1,0},{2,3},{3,2},{4,5},{5,4},{6,7},{7,6},{8,9},{9,8},{10,11... | collective-permute-start | bytes 122888 | tf_op jit(solution)/shard_map/ppermute | solution.py:402
  72.3 4.1 %collective-permute-start.15 = (bf16[16,1280]{1,0:T(8,128)(2,1)S(1)}, bf16[16,1280]{1,0:T(8,128)(2,1)S(1)}, u32[]{:S(2)}, u32[]{:S(2)}) collective-permute-start(bf16[16,1280]{1,0:T(8,128)(2,1)S(1)} %add.12.a_ref), channel_id=1, source_target_pairs={{0,8},{1,9},{2,10},{3,11},{4,12},{5,13},{6,14},{7,15},{8,16},{9,17... | collective-permute-start | bytes 122888 | tf_op jit(solution)/shard_map/ppermute | solution.py:382
  73.6 4.5 %collective-permute-start.14 = (bf16[16,1280]{1,0:T(8,128)(2,1)S(1)}, bf16[16,1280]{1,0:T(8,128)(2,1)S(1)}, u32[]{:S(2)}, u32[]{:S(2)}) collective-permute-start(bf16[16,1280]{1,0:T(8,128)(2,1)S(1)} %add.12.a_ref), channel_id=1, source_target_pairs={{0,16},{1,17},{2,18},{3,19},{4,20},{5,21},{6,22},{7,23},{8,24},{9,... | collective-permute-start | bytes 122888 | tf_op jit(solution)/shard_map/ppermute | solution.py:382
  76.1 3.1 %collective-permute-start.13 = (bf16[16,1280]{1,0:T(8,128)(2,1)S(1)}, bf16[16,1280]{1,0:T(8,128)(2,1)S(1)}, u32[]{:S(2)}, u32[]{:S(2)}) collective-permute-start(bf16[16,1280]{1,0:T(8,128)(2,1)S(1)} %add.12.a_ref), channel_id=1, source_target_pairs={{0,24},{1,25},{2,26},{3,27},{4,28},{5,29},{6,30},{7,31},{8,0},{9,1... | collective-permute-start | bytes 122888 | tf_op jit(solution)/shard_map/ppermute | solution.py:382
  80.6 4.9 %collective-permute-start.16 = (bf16[16,1792]{1,0:T(8,128)(2,1)S(1)}, bf16[16,1792]{1,0:T(8,128)(2,1)S(1)}, u32[]{:S(2)}, u32[]{:S(2)}) collective-permute-start(bf16[16,1792]{1,0:T(8,128)(2,1)S(1)} %get-tuple-element.36), channel_id=1, source_target_pairs={{0,32},{32,64},{64,96},{96,0},{1,33},{33,65},{65,97},{97,1},{2,34}... | collective-permute-start | bytes 172040 | tf_op jit(solution)/shard_map/ppermute | solution.py:375
  80.6 4.8 %collective-permute-start.17 = (bf16[16,1792]{1,0:T(8,128)(2,1)S(1)}, bf16[16,1792]{1,0:T(8,128)(2,1)S(1)}, u32[]{:S(2)}, u32[]{:S(2)}) collective-permute-start(bf16[16,1792]{1,0:T(8,128)(2,1)S(1)} %get-tuple-element.37), channel_id=1, source_target_pairs={{0,64},{32,96},{64,0},{96,32},{1,65},{33,97},{65,1},{97,33},{2,66}... | collective-permute-start | bytes 172040 | tf_op jit(solution)/shard_map/ppermute | solution.py:375
  82.8 3.3 %collective-permute-start.18 = (bf16[16,1792]{1,0:T(8,128)(2,1)S(1)}, bf16[16,1792]{1,0:T(8,128)(2,1)S(1)}, u32[]{:S(2)}, u32[]{:S(2)}) collective-permute-start(bf16[16,1792]{1,0:T(8,128)(2,1)S(1)} %get-tuple-element.38), channel_id=1, source_target_pairs={{0,96},{32,0},{64,32},{96,64},{1,97},{33,1},{65,33},{97,65},{2,98}... | collective-permute-start | bytes 172040 | tf_op jit(solution)/shard_map/ppermute | solution.py:375
  86.3 4.0 %collective-permute-start.21 = (bf16[16,896]{1,0:T(8,128)(2,1)S(1)}, bf16[16,896]{1,0:T(8,128)(2,1)S(1)}, u32[]{:S(2)}, u32[]{:S(2)}) collective-permute-start(bf16[16,896]{1,0:T(8,128)(2,1)S(1)} %activate.1.a_ref), channel_id=1, source_target_pairs={{0,32},{32,64},{64,96},{96,0},{1,33},{33,65},{65,97},{97,1},{2,34}... | collective-permute-start | bytes 86024 | tf_op jit(solution)/shard_map/ppermute | solution.py:382
  87.2 4.3 %collective-permute-start.20 = (bf16[16,896]{1,0:T(8,128)(2,1)S(1)}, bf16[16,896]{1,0:T(8,128)(2,1)S(1)}, u32[]{:S(2)}, u32[]{:S(2)}) collective-permute-start(bf16[16,896]{1,0:T(8,128)(2,1)S(1)} %activate.1.a_ref), channel_id=1, source_target_pairs={{0,64},{32,96},{64,0},{96,32},{1,65},{33,97},{65,1},{97,33},{2,66}... | collective-permute-start | bytes 86024 | tf_op jit(solution)/shard_map/ppermute | solution.py:382
  93.1 4.1 %collective-permute-start.22 = (bf16[16,1280]{1,0:T(8,128)(2,1)S(1)}, bf16[16,1280]{1,0:T(8,128)(2,1)S(1)}, u32[]{:S(2)}, u32[]{:S(2)}) collective-permute-start(bf16[16,1280]{1,0:T(8,128)(2,1)S(1)} %get-tuple-element.40), channel_id=1, source_target_pairs={{0,8},{1,9},{2,10},{3,11},{4,12},{5,13},{6,14},{7,15},{8,16},{9,17... | collective-permute-start | bytes 122888 | tf_op jit(solution)/shard_map/ppermute | solution.py:375
  93.2 4.5 %collective-permute-start.23 = (bf16[16,1280]{1,0:T(8,128)(2,1)S(1)}, bf16[16,1280]{1,0:T(8,128)(2,1)S(1)}, u32[]{:S(2)}, u32[]{:S(2)}) collective-permute-start(bf16[16,1280]{1,0:T(8,128)(2,1)S(1)} %get-tuple-element.41), channel_id=1, source_target_pairs={{0,16},{1,17},{2,18},{3,19},{4,20},{5,21},{6,22},{7,23},{8,24},{9,... | collective-permute-start | bytes 122888 | tf_op jit(solution)/shard_map/ppermute | solution.py:375
  98.5 4.4 %collective-permute-start.27 = (bf16[16,1280]{1,0:T(8,128)(2,1)S(1)}, bf16[16,1280]{1,0:T(8,128)(2,1)S(1)}, u32[]{:S(2)}, u32[]{:S(2)}) collective-permute-start(bf16[16,1280]{1,0:T(8,128)(2,1)S(1)} %add.13.refs_0_), channel_id=1, source_target_pairs={{0,2},{1,3},{2,4},{3,5},{4,6},{5,7},{6,0},{7,1},{8,10},{9,11},{10,... | collective-permute-start | bytes 122888 | tf_op jit(solution)/shard_map/ppermute | solution.py:382
  99.7 4.4 %collective-permute-start.26 = (bf16[16,1280]{1,0:T(8,128)(2,1)S(1)}, bf16[16,1280]{1,0:T(8,128)(2,1)S(1)}, u32[]{:S(2)}, u32[]{:S(2)}) collective-permute-start(bf16[16,1280]{1,0:T(8,128)(2,1)S(1)} %add.13.refs_0_), channel_id=1, source_target_pairs={{0,4},{1,5},{2,6},{3,7},{4,0},{5,1},{6,2},{7,3},{8,12},{9,13},{10,... | collective-permute-start | bytes 122888 | tf_op jit(solution)/shard_map/ppermute | solution.py:382
  105.0 9.0 %collective-permute-start.28 = (bf16[16,1280]{1,0:T(8,128)(2,1)S(1)}, bf16[16,1280]{1,0:T(8,128)(2,1)S(1)}, u32[]{:S(2)}, u32[]{:S(2)}) collective-permute-start(bf16[16,1280]{1,0:T(8,128)(2,1)S(1)} %add.14.refs_0_), channel_id=1, source_target_pairs={{0,1},{1,0},{2,3},{3,2},{4,5},{5,4},{6,7},{7,6},{8,9},{9,8},{10,11... | collective-permute-start | bytes 122888 | tf_op jit(solution)/shard_map/ppermute | solution.py:402
  114.0 4.1 %collective-permute-start.31 = (bf16[16,1280]{1,0:T(8,128)(2,1)S(1)}, bf16[16,1280]{1,0:T(8,128)(2,1)S(1)}, u32[]{:S(2)}, u32[]{:S(2)}) collective-permute-start(bf16[16,1280]{1,0:T(8,128)(2,1)S(1)} %add.15.a_ref), channel_id=1, source_target_pairs={{0,8},{1,9},{2,10},{3,11},{4,12},{5,13},{6,14},{7,15},{8,16},{9,17... | collective-permute-start | bytes 122888 | tf_op jit(solution)/shard_map/ppermute | solution.py:382
  115.0 4.5 %collective-permute-start.30 = (bf16[16,1280]{1,0:T(8,128)(2,1)S(1)}, bf16[16,1280]{1,0:T(8,128)(2,1)S(1)}, u32[]{:S(2)}, u32[]{:S(2)}) collective-permute-start(bf16[16,1280]{1,0:T(8,128)(2,1)S(1)} %add.15.a_ref), channel_id=1, source_target_pairs={{0,16},{1,17},{2,18},{3,19},{4,20},{5,21},{6,22},{7,23},{8,24},{9,... | collective-permute-start | bytes 122888 | tf_op jit(solution)/shard_map/ppermute | solution.py:382
  (20 other events, 364.5 us)

commit v6 on v4

--- a/solution.py
+++ b/solution.py
@@ -57,8 +57,29 @@
     return pltpu.with_memory_space_constraint(value, pltpu.HBM)
 
 
-def row_block(mine, k):
-    return pl.ds(pl.multiple_of(lax.rem(mine + k, ROWS) * OWN, OWN), OWN)
+def rows_at(block):
+    return pl.ds(pl.multiple_of(block * OWN, OWN), OWN)
+
+
+def split(mine, whole, keep_ref, send_ref):
+    for ref, pair in ((keep_ref, (0, 3)), (send_ref, (1, 2))):
+        for at, other in enumerate(pair):
+            block = whole[rows_at(mine ^ other), :]
+            ref[at * OWN : (at + 1) * OWN, :] = block.astype(ref.dtype)
+
+
+def gathered_blocks(mine, near_ref, far_ref):
+    for ref, pair in ((near_ref, (0, 3)), (far_ref, (1, 2))):
+        for at, other in enumerate(pair):
+            yield mine ^ other, ref[at * OWN : (at + 1) * OWN, :]
+
+
+def along_x(place_ref):
+    return place_ref[0] // WIDE
+
+
+def along_y(place_ref):
+    return lax.rem(place_ref[0], WIDE) // 8
 
 
 def terms(value, count):
@@ -88,7 +109,7 @@
 
 
 def project_kernel(place_ref, hidden_hbm, gain_hbm, wq_hbm, wkv_hbm, *rest):
-    outs, (whole, hidden_ref, gain_ref, wq_ref, wkv_ref, sems) = rest[:ROWS], rest[ROWS:]
+    keep_ref, send_ref, whole, hidden_ref, gain_ref, wq_ref, wkv_ref, sems = rest
     moves = [
         pltpu.make_async_copy(source, target, sems.at[at])
         for at, (source, target) in enumerate(
@@ -112,9 +133,7 @@
     whole[:, 256:] = jnp.concatenate([keyval, jnp.broadcast_to(square, keyval.shape)], axis=1)
     moves[2].wait()
     whole[:, :256] = jnp.dot(scaled, wq_ref[...], preferred_element_type=f32)
-    mine = place_ref[0] // WIDE
-    for k in range(ROWS):
-        outs[k][...] = whole[row_block(mine, k), :]
+    split(along_x(place_ref), whole, keep_ref, send_ref)
 
 
 def table_kernel(
@@ -147,8 +166,8 @@
         swapped_ref[at] = sine * swap_halves(gain)
 
 
-def heads_kernel(a_ref, b_ref, c_ref, d_ref, straight_ref, swapped_ref, out_ref):
-    total = (a_ref[...] + b_ref[...]) + (c_ref[...] + d_ref[...])
+def heads_kernel(a_ref, b_ref, straight_ref, swapped_ref, out_ref):
+    total = a_ref[...] + b_ref[...]
     inverse = lax.rsqrt(total[:, 320:321] / MODEL_WIDTH + EPSILON)
     scaled = total * inverse
     straight, swapped = straight_ref[0], swapped_ref[0]
@@ -286,103 +305,129 @@
         again_ref[:, lanes] = heads
 
 
-def store_pairs(out_ref, value):
-    for block in range(WIDE):
-        out_ref[block] = value[2 * block : 2 * block + 2]
-
-
-def output_kernel(a_ref, b_ref, c_ref, d_ref, w_ref, out_ref):
-    heads = jnp.concatenate([a_ref[...], b_ref[...], c_ref[...], d_ref[...]], axis=0)
-    store_pairs(out_ref, jnp.dot(heads, w_ref[...], preferred_element_type=f32).astype(bf16))
-
-
-def sum_spread_kernel(got_ref, out_ref):
-    total = jnp.sum(got_ref[...].astype(f32), axis=0).astype(bf16)
-    out_ref[...] = jnp.broadcast_to(total[None], out_ref.shape)
+def product_kernel(place_ref, near_ref, far_ref, w_ref, keep_ref, send_ref, left, whole):
+    for block, value in gathered_blocks(along_x(place_ref), near_ref, far_ref):
+        left[rows_at(block), :] = value
+    depth = w_ref.shape[0]
+    whole[...] = jnp.dot(left[:, :depth], w_ref[...], preferred_element_type=f32)
+    split(along_y(place_ref), whole, keep_ref, send_ref)
+
+
+def pass_on_kernel(keep_ref, got_ref, own_ref, next_ref):
+    own_ref[...] = keep_ref[:OWN, :] + got_ref[:OWN, :].astype(f32)
+    following = keep_ref[OWN:, :] + got_ref[OWN:, :].astype(f32)
+    if next_ref.shape[1] == 2 * HALF:
+        place = lax.broadcasted_iota(jnp.int32, (OWN, HALF - HIDDEN_UNITS), 1)
+        norm = norm_lanes(squared_sum(following), place)
+        following = jnp.concatenate([following[:, :HIDDEN_UNITS], norm, following[:, HALF:]], axis=1)
+    next_ref[...] = following.astype(next_ref.dtype)
+
+
+def add_kernel(a_ref, b_ref, out_ref):
+    out_ref[...] = (a_ref[...].astype(f32) + b_ref[...].astype(f32)).astype(bf16)
+
+
+def join_kernel(a_ref, b_ref, out_ref):
+    out_ref[:OWN, :] = a_ref[...]
+    out_ref[OWN:, :] = b_ref[...]
+
+
+def norm_lanes(square, place):
+    norm = jnp.zeros(place.shape, f32)
+    for at, term in enumerate(terms(square, 3)):
+        norm = jnp.where(place == at, term, norm)
+    return norm
+
+
+def squared_sum(value):
+    first = HIDDEN_UNITS
+    return value[:, first : first + 1] + value[:, first + 1 : first + 2] + value[:, first + 2 : first + 3]
 
 
 def gate_up_kernel(
-    place_ref, hidden_ref, attended_ref, gain_ref, wg_ref, wu_ref, stream_ref, *outs
+    place_ref,
+    hidden_ref,
+    near_ref,
+    far_ref,
+    gain_ref,
+    wg_ref,
+    wu_ref,
+    stream_ref,
+    keep_ref,
+    send_ref,
+    whole,
 ):
-    mine = place_ref[0] // WIDE
-    for k in range(ROWS):
-        at = slice(k * OWN, (k + 1) * OWN)
-        blocks = attended_ref[k * WIDE // ROWS : (k + 1) * WIDE // ROWS]
-        attended = blocks.astype(f32).reshape(OWN, blocks.shape[-1])
-        stream_ref[at, :] = hidden_ref[row_block(mine, k), :].astype(f32) + attended
+    for block, value in gathered_blocks(along_y(place_ref), near_ref, far_ref):
+        at = rows_at(block)
+        stream_ref[at, :] = hidden_ref[at, :].astype(f32) + value.astype(f32)
     stream = stream_ref[...]
     square = jnp.sum(stream * stream, axis=1, keepdims=True)
     scaled = (stream * gain_ref[...].astype(f32)[None]).astype(bf16)
-    gate = lax.dot_general(scaled, wg_ref[...], NT, preferred_element_type=f32).astype(bf16)
-    up = lax.dot_general(scaled, wu_ref[...], NT, preferred_element_type=f32).astype(bf16)
-    pad = HALF - HIDDEN_UNITS
-    place = lax.broadcasted_iota(jnp.int32, (stream.shape[0], pad), 1)
-    norm = jnp.zeros(place.shape, f32)
-    for at, term in enumerate(terms(square, 3)):
-        norm = jnp.where(place == at, term, norm)
-    norm = norm.astype(bf16)
-    for k in range(ROWS):
-        at = slice(k * OWN, (k + 1) * OWN)
-        outs[k][...] = jnp.concatenate([gate[at], norm[at], up[at], norm[at]], axis=1)
-
-
-def activate_kernel(a_ref, b_ref, c_ref, d_ref, out_ref):
-    total = (a_ref[...].astype(f32) + b_ref[...].astype(f32)) + (
-        c_ref[...].astype(f32) + d_ref[...].astype(f32)
-    )
-    square = (
-        total[:, HIDDEN_UNITS : HIDDEN_UNITS + 1]
-        + total[:, HIDDEN_UNITS + 1 : HIDDEN_UNITS + 2]
-        + total[:, HIDDEN_UNITS + 2 : HIDDEN_UNITS + 3]
-    )
-    inverse = lax.rsqrt(square / MODEL_WIDTH + EPSILON)
+    gate = lax.dot_general(scaled, wg_ref[...], NT, preferred_element_type=f32)
+    up = lax.dot_general(scaled, wu_ref[...], NT, preferred_element_type=f32)
+    place = lax.broadcasted_iota(jnp.int32, (stream.shape[0], HALF - HIDDEN_UNITS), 1)
+    norm = norm_lanes(square, place)
+    whole[...] = jnp.concatenate([gate, norm, up, jnp.zeros(norm.shape, f32)], axis=1)
+    split(along_x(place_ref), whole, keep_ref, send_ref)
+
+
+def activate_kernel(a_ref, b_ref, out_ref):
+    total = a_ref[...] + b_ref[...].astype(f32)
+    inverse = lax.rsqrt(squared_sum(total) / MODEL_WIDTH + EPSILON)
     gate = total[:, :HALF] * inverse
     up = total[:, HALF:] * inverse
     out_ref[...] = (gate / (1.0 + jnp.exp(-gate)) * up).astype(bf16)
 
 
-def down_kernel(a_ref, b_ref, c_ref, d_ref, w_ref, out_ref):
-    units = jnp.concatenate([a_ref[...], b_ref[...], c_ref[...], d_ref[...]], axis=0)
-    part = jnp.dot(units[:, :HIDDEN_UNITS], w_ref[...], preferred_element_type=f32)
-    store_pairs(out_ref, part.astype(bf16))
-
-
-def final_kernel(place_ref, stream_ref, down_ref, out_ref):
-    mine = place_ref[0] // WIDE
-    for k in range(ROWS):
-        at = slice(k * OWN, (k + 1) * OWN)
-        blocks = down_ref[k * WIDE // ROWS : (k + 1) * WIDE // ROWS]
-        down = blocks.astype(f32).reshape(OWN, blocks.shape[-1])
-        out_ref[row_block(mine, k), :] = (stream_ref[at, :] + down).astype(bf16)
-
-
-def to_rows(blocks):
-    got = list(blocks)
-    for k in (2, 1, 3):
-        got[k] = lax.ppermute(blocks[k], "rows", [(i, (i + k) % ROWS) for i in range(ROWS)])
-    return got
-
-
-def from_rows(own):
-    got = [own] * ROWS
-    for k in (2, 1, 3):
-        got[k] = lax.ppermute(own, "rows", [((i + k) % ROWS, i) for i in range(ROWS)])
-    return got
+def final_kernel(place_ref, stream_ref, near_ref, far_ref, out_ref):
+    for block, value in gathered_blocks(along_y(place_ref), near_ref, far_ref):
+        at = rows_at(block)
+        out_ref[at, :] = (stream_ref[at, :] + value.astype(f32)).astype(bf16)
+
+
+def swap(value, axis, other):
+    if axis == "x":
+        return lax.ppermute(value, "rows", [(i, i ^ other) for i in range(ROWS)])
+    other *= {"y": 8, "z": 2, "core": 1}[axis]
+    return lax.ppermute(value, "wide", [(i, i ^ other) for i in range(WIDE)])
+
+
+def reduce_blocks(keep, send, axis):
+    width = keep.shape[1]
+    own, following = call(
+        pass_on_kernel,
+        [
+            jax.ShapeDtypeStruct((OWN, width), f32),
+            jax.ShapeDtypeStruct((OWN, width), send.dtype),
+        ],
+        [VMEM] * 2,
+        limit=4,
+        name="pass_on",
+    )(keep, swap(send, axis, 1))
+    return own, swap(following, axis, 3)
+
+
+def add(a, b):
+    shape = jax.ShapeDtypeStruct(a.shape, bf16)
+    return call(add_kernel, shape, [VMEM] * 2, limit=4, name="add")(a, b)
+
+
+def gather(own, axis):
+    shape = jax.ShapeDtypeStruct((2 * OWN, own.shape[1]), own.dtype)
+    near = call(join_kernel, shape, [VMEM] * 2, limit=4, name="join")(own, swap(own, axis, 3))
+    return near, swap(near, axis, 1)
 
 
 def exchange(blocks):
     return lax.all_to_all(blocks, "wide", split_axis=0, concat_axis=0, tiled=True)
 
 
-def sum_wide(part):
-    total = call(
-        sum_spread_kernel,
-        jax.ShapeDtypeStruct(part.shape, bf16),
-        [VMEM],
-        limit=4,
-        name="sum_spread",
-    )(exchange(part))
-    return exchange(total)
+def sum_wide(keep, send):
+    own = add(*reduce_blocks(keep, send, "y"))
+    own = add(own, swap(own, "z", 1))
+    own = add(own, swap(own, "z", 3))
+    own = add(own, swap(own, "core", 1))
+    return gather(own, "y")
 
 
 def body(
@@ -405,9 +450,9 @@
     place = lax.axis_index(("rows", "wide")).astype(jnp.int32).reshape(1)
     sds = jax.ShapeDtypeStruct
 
-    blocks = call(
+    keep, send = call(
         project_kernel,
-        [sds((OWN, 384), f32)] * ROWS,
+        [sds((2 * OWN, 384), f32)] * 2,
         [SMEM] + [HBM] * 4,
         [
             pltpu.VMEM((64, 384), f32),
@@ -431,11 +476,11 @@
     payload = call(
         heads_kernel,
         sds((WIDE, PACKED, 128), bf16),
-        [VMEM] * 6,
+        [VMEM] * 4,
         limit=8,
         name="heads",
         cost=pl.CostEstimate(flops=20_000_000_000, bytes_accessed=1 << 20, transcendentals=0),
-    )(*to_rows(blocks), straight, swapped)
+    )(*reduce_blocks(keep, send, "x"), straight, swapped)
     gathered = exchange(payload)
 
     parts = call(
@@ -456,27 +501,34 @@
         combine_kernel, [sds((OWN, 256), bf16)] * 2, [SMEM] + [VMEM] * 4, limit=8, name="combine"
     )(place, exchange(parts), gathered, straight, swapped)
 
-    out_part = call(output_kernel, sds((WIDE, 2, 1280), bf16), [VMEM] * 5, limit=8, name="output")(
-        *from_rows(heads_own), w_out
-    )
-    attended = sum_wide(out_part)
-
-    stream, *blocks = call(
+    def product(own, weight, name):
+        return call(
+            product_kernel,
+            [sds((2 * OWN, 1280), f32), sds((2 * OWN, 1280), bf16)],
+            [SMEM] + [VMEM] * 3,
+            [pltpu.VMEM((64, own.shape[1]), bf16), pltpu.VMEM((64, 1280), f32)],
+            limit=8,
+            name=name,
+        )(place, *gather(own, "x"), weight)
+
+    stream, keep, send = call(
         gate_up_kernel,
-        [sds((64, 1280), f32)] + [sds((OWN, 2 * HALF), bf16)] * ROWS,
-        [SMEM] + [VMEM] * 5,
+        [
+            sds((64, 1280), f32),
+            sds((2 * OWN, 2 * HALF), f32),
+            sds((2 * OWN, 2 * HALF), bf16),
+        ],
+        [SMEM] + [VMEM] * 6,
+        [pltpu.VMEM((64, 2 * HALF), f32)],
         limit=12,
         name="gate_up",
-    )(place, hidden, attended, mlp_gain, w_gate.T, w_up.T)
+    )(place, hidden, *sum_wide(*product(heads_own, w_out, "output")), mlp_gain, w_gate.T, w_up.T)
     activated = call(
-        activate_kernel, sds((OWN, HALF), bf16), [VMEM] * 4, limit=8, name="activate"
-    )(*to_rows(blocks))
-    down_part = call(down_kernel, sds((WIDE, 2, 1280), bf16), [VMEM] * 5, limit=8, name="down")(
-        *from_rows(activated), w_down
-    )
-    layer_out = call(final_kernel, sds((64, 1280), bf16), [SMEM] + [VMEM] * 2, limit=8, name="final")(
-        place, stream, sum_wide(down_part)
-    )
+        activate_kernel, sds((OWN, HALF), bf16), [VMEM] * 2, limit=8, name="activate"
+    )(*reduce_blocks(keep, send, "x"))
+    layer_out = call(
+        final_kernel, sds((64, 1280), bf16), [SMEM] + [VMEM] * 3, limit=8, name="final"
+    )(place, stream, *sum_wide(*product(activated, w_down, "down")))
     return (layer_out, heads_out)
 
 

time: 122 us -> 142 us (1.16)
  blocking collectives: 83.6 us -> 33.8 us
  waiting for transfers between devices: 8.05 us -> 55.1 us
  starting transfers between devices: 16.3 us -> 37.6 us
    all_to_all x6 -> x2, blocking collectives: 83.6 us -> 33.8 us  [exchange(): lax.all_to_all(blocks, 'wide', split_axis=0, concat_axis=0, tiled=True)]
    ppermute x12 -> x22, waiting for transfers between devices: 8.05 us -> 55.1 us  [the longest x14 39.3 us: swap(): return lax.ppermute(value, 'wide', [(i, i ^ other) for i in range(WIDE)])]
    ppermute x12 -> x22, starting transfers between devices: 16.3 us -> 37.6 us  [the longest x14 25.1 us: swap(): return lax.ppermute(value, 'wide', [(i, i ^ other) for i in range(WIDE)])]
    pallas_call x9 -> x23, Pallas kernels: 5.18 us -> 5.23 us  [the longest x1 1.61 us: body(): call(project_kernel, [sds((2 * OWN, 384), f32)] * 2, [SMEM] + [HBM] * 4,...]
  transfers between devices with their start and end apart: 12 -> 22, of which waited for: 10 -> 21; matrix products, arithmetic and copies ran while one was open for 0% -> 0% of each run, Pallas kernels for 1% -> 1%
where the time goes in v6:
time: 142 us; the launch traced here: 141 us
  waiting for transfers between devices  55.1 us (39%)
  starting transfers between devices  37.6 us (26%)
  blocking collectives  33.8 us (24%)
  Pallas kernels  13.3 us (9%)
    ppermute x14, waiting for transfers between devices, swap(): return lax.ppermute(value, 'wide', [(i, i ^ other) for i in range(WIDE)])  39.3 us
    all_to_all x2, blocking collectives, exchange(): lax.all_to_all(blocks, 'wide', split_axis=0, concat_axis=0, tiled=True)  33.8 us
    ppermute x14, starting transfers between devices, swap(): return lax.ppermute(value, 'wide', [(i, i ^ other) for i in range(WIDE)])  25.1 us
    ppermute x8, waiting for transfers between devices, swap(): return lax.ppermute(value, 'rows', [(i, i ^ other) for i in range(ROWS)])  15.8 us
    ppermute x8, starting transfers between devices, swap(): return lax.ppermute(value, 'rows', [(i, i ^ other) for i in range(ROWS)])  12.5 us
    pallas_call x1, Pallas kernels, body(): call(attend_kernel, sds((WIDE, PACKED, 128), bf16), [SMEM, SMEM, VMEM, VM...  5.2 us
  transfers between devices with their start and end apart: 22, of which 21 were waited for; matrix products, arithmetic and copies ran while one was open for 0% of the time, Pallas kernels for 1%

profile of v6, /device:TPU:1, one launch (start us, length us, event | category | flops | bytes accessed | tf_op | source)
XLA Modules:
  0.0 140.8 jit_solution(6494065356197490049)
XLA Ops:
  5.9 2.8 %collective-permute-start.1 = (f32[16,384]{1,0:T(8,128)S(1)}, f32[16,384]{1,0:T(8,128)S(1)}, u32[]{:S(2)}, u32[]{:S(2)}) collective-permute-start(f32[16,384]{1,0:T(8,128)S(1)} %get-tuple-element.26), channel_id=1, source_target_pairs={{0,96},{32,64},{64,32},{96,0},{1,97},{33,65},{65,33},{97,1},{2,98}... | collective-permute-start | bytes 73736 | tf_op jit(solution)/shard_map/ppermute | solution.py:390
  10.5 20.6 %all_to_all.10.g_ref = bf16[32,40,128]{2,1,0:T(8,128)(2,1)S(1)} all-to-all(bf16[32,40,128]{2,1,0:T(8,128)(2,1)S(1)} %heads.1), channel_id=1, replica_groups=mesh['rows'=4,'wide'=32] {'wide'}, dimensions={0} | all-to-all | bytes 655360 | tf_op jit(solution)/shard_map/all_to_all | solution.py:422
  31.2 5.2 %attend.1 = bf16[32,40,128]{2,1,0:T(8,128)(2,1)S(1)} custom-call(s32[16]{0:T(128)S(1)} %copy-done.6, s32[16]{0:T(128)S(1)} %bitcast.11, bf16[32,40,128]{2,1,0:T(8,128)(2,1)S(1)} %all_to_all.10.g_ref, bf16[16,256,1024]{2,1,0:T(8,128)(2,1)S(1)} %bitcast.6, bf16[16,256,1024]{2,1,0:T(8,128)(2,1)S(1)} %bitcast.8), custom_call_target="tpu_custom_call" | custom-call | tf_op jit(solution)/shard_map/attend/pallas_call | solution.py:486
  36.5 13.2 %all_to_all.11.r_ref = bf16[32,40,128]{2,1,0:T(8,128)(2,1)S(1)} all-to-all(bf16[32,40,128]{2,1,0:T(8,128)(2,1)S(1)} %attend.1), channel_id=1, replica_groups=mesh['rows'=4,'wide'=32] {'wide'}, dimensions={0} | all-to-all | bytes 655360 | tf_op jit(solution)/shard_map/all_to_all | solution.py:422
  51.0 2.5 %collective-permute-start.2 = (bf16[16,256]{1,0:T(8,128)(2,1)S(1)}, bf16[16,256]{1,0:T(8,128)(2,1)S(1)}, u32[]{:S(2)}, u32[]{:S(2)}) collective-permute-start(bf16[16,256]{1,0:T(8,128)(2,1)S(1)} %get-tuple-element.29.a_ref), channel_id=1, source_target_pairs={{0,96},{32,64},{64,32},{96,0},{1,97},{33,65},{65,33},{97,1},{2,98}... | collective-permute-start | bytes 24584 | tf_op jit(solution)/shard_map/ppermute | solution.py:390
  54.8 2.6 %collective-permute-done.3.far_ref = bf16[32,256]{1,0:T(8,128)(2,1)S(1)} collective-permute-done((bf16[32,256]{1,0:T(8,128)(2,1)S(1)}, bf16[32,256]{1,0:T(8,128)(2,1)S(1)}, u32[]{:S(2)}, u32[]{:S(2)}) %collective-permute-start.3) | collective-permute-done | bytes 16416 | tf_op jit(solution)/shard_map/ppermute | solution.py:390
  58.0 3.0 %collective-permute-done.4.got_ref = bf16[32,1280]{1,0:T(8,128)(2,1)S(1)} collective-permute-done((bf16[32,1280]{1,0:T(8,128)(2,1)S(1)}, bf16[32,1280]{1,0:T(8,128)(2,1)S(1)}, u32[]{:S(2)}, u32[]{:S(2)}) %collective-permute-start.4) | collective-permute-done | bytes 81952 | tf_op jit(solution)/shard_map/ppermute | solution.py:392
  61.9 3.3 %collective-permute-done.5.b_ref = bf16[16,1280]{1,0:T(8,128)(2,1)S(1)} collective-permute-done((bf16[16,1280]{1,0:T(8,128)(2,1)S(1)}, bf16[16,1280]{1,0:T(8,128)(2,1)S(1)}, u32[]{:S(2)}, u32[]{:S(2)}) %collective-permute-start.5) | collective-permute-done | bytes 40992 | tf_op jit(solution)/shard_map/ppermute | solution.py:392
  65.4 2.7 %collective-permute-done.6.b_ref = bf16[16,1280]{1,0:T(8,128)(2,1)S(1)} collective-permute-done((bf16[16,1280]{1,0:T(8,128)(2,1)S(1)}, bf16[16,1280]{1,0:T(8,128)(2,1)S(1)}, u32[]{:S(2)}, u32[]{:S(2)}) %collective-permute-start.6) | collective-permute-done | bytes 40992 | tf_op jit(solution)/shard_map/ppermute | solution.py:392
  69.2 3.1 %collective-permute-done.7.b_ref = bf16[16,1280]{1,0:T(8,128)(2,1)S(1)} collective-permute-done((bf16[16,1280]{1,0:T(8,128)(2,1)S(1)}, bf16[16,1280]{1,0:T(8,128)(2,1)S(1)}, u32[]{:S(2)}, u32[]{:S(2)}) %collective-permute-start.7) | collective-permute-done | bytes 40992 | tf_op jit(solution)/shard_map/ppermute | solution.py:392
  72.3 7.0 %collective-permute-start.8 = (bf16[16,1280]{1,0:T(8,128)(2,1)S(1)}, bf16[16,1280]{1,0:T(8,128)(2,1)S(1)}, u32[]{:S(2)}, u32[]{:S(2)}) collective-permute-start(bf16[16,1280]{1,0:T(8,128)(2,1)S(1)} %add.14.a_ref), channel_id=1, source_target_pairs={{0,1},{1,0},{2,3},{3,2},{4,5},{5,4},{6,7},{7,6},{8,9},{9,8},{10,11... | collective-permute-start | bytes 122888 | tf_op jit(solution)/shard_map/ppermute | solution.py:392
  81.2 3.1 %collective-permute-done.9.b_ref = bf16[16,1280]{1,0:T(8,128)(2,1)S(1)} collective-permute-done((bf16[16,1280]{1,0:T(8,128)(2,1)S(1)}, bf16[16,1280]{1,0:T(8,128)(2,1)S(1)}, u32[]{:S(2)}, u32[]{:S(2)}) %collective-permute-start.9) | collective-permute-done | bytes 40992 | tf_op jit(solution)/shard_map/ppermute | solution.py:392
  84.3 3.3 %collective-permute-done.10.far_ref = bf16[32,1280]{1,0:T(8,128)(2,1)S(1)} collective-permute-done((bf16[32,1280]{1,0:T(8,128)(2,1)S(1)}, bf16[32,1280]{1,0:T(8,128)(2,1)S(1)}, u32[]{:S(2)}, u32[]{:S(2)}) %collective-permute-start.10) | collective-permute-done | bytes 81952 | tf_op jit(solution)/shard_map/ppermute | solution.py:392
  89.1 3.6 %collective-permute-done.11.got_ref = bf16[32,1792]{1,0:T(8,128)(2,1)S(1)} collective-permute-done((bf16[32,1792]{1,0:T(8,128)(2,1)S(1)}, bf16[32,1792]{1,0:T(8,128)(2,1)S(1)}, u32[]{:S(2)}, u32[]{:S(2)}) %collective-permute-start.11) | collective-permute-done | bytes 114720 | tf_op jit(solution)/shard_map/ppermute | solution.py:390
  92.9 2.5 %collective-permute-start.12 = (bf16[16,1792]{1,0:T(8,128)(2,1)S(1)}, bf16[16,1792]{1,0:T(8,128)(2,1)S(1)}, u32[]{:S(2)}, u32[]{:S(2)}) collective-permute-start(bf16[16,1792]{1,0:T(8,128)(2,1)S(1)} %get-tuple-element.38), channel_id=1, source_target_pairs={{0,96},{32,64},{64,32},{96,0},{1,97},{33,65},{65,33},{97,1},{2,98}... | collective-permute-start | bytes 172040 | tf_op jit(solution)/shard_map/ppermute | solution.py:390
  97.4 2.6 %collective-permute-start.13 = (bf16[16,896]{1,0:T(8,128)(2,1)S(1)}, bf16[16,896]{1,0:T(8,128)(2,1)S(1)}, u32[]{:S(2)}, u32[]{:S(2)}) collective-permute-start(bf16[16,896]{1,0:T(8,128)(2,1)S(1)} %activate.1.a_ref), channel_id=1, source_target_pairs={{0,96},{32,64},{64,32},{96,0},{1,97},{33,65},{65,33},{97,1},{2,98}... | collective-permute-start | bytes 86024 | tf_op jit(solution)/shard_map/ppermute | solution.py:390
  102.0 3.0 %collective-permute-done.14.far_ref = bf16[32,896]{1,0:T(8,128)(2,1)S(1)} collective-permute-done((bf16[32,896]{1,0:T(8,128)(2,1)S(1)}, bf16[32,896]{1,0:T(8,128)(2,1)S(1)}, u32[]{:S(2)}, u32[]{:S(2)}) %collective-permute-start.14) | collective-permute-done | bytes 57376 | tf_op jit(solution)/shard_map/ppermute | solution.py:390
  105.6 3.3 %collective-permute-done.15.got_ref = bf16[32,1280]{1,0:T(8,128)(2,1)S(1)} collective-permute-done((bf16[32,1280]{1,0:T(8,128)(2,1)S(1)}, bf16[32,1280]{1,0:T(8,128)(2,1)S(1)}, u32[]{:S(2)}, u32[]{:S(2)}) %collective-permute-start.15) | collective-permute-done | bytes 81952 | tf_op jit(solution)/shard_map/ppermute | solution.py:392
  109.9 3.1 %collective-permute-done.16.b_ref = bf16[16,1280]{1,0:T(8,128)(2,1)S(1)} collective-permute-done((bf16[16,1280]{1,0:T(8,128)(2,1)S(1)}, bf16[16,1280]{1,0:T(8,128)(2,1)S(1)}, u32[]{:S(2)}, u32[]{:S(2)}) %collective-permute-start.16) | collective-permute-done | bytes 40992 | tf_op jit(solution)/shard_map/ppermute | solution.py:392
  113.1 3.1 %collective-permute-done.17.b_ref = bf16[16,1280]{1,0:T(8,128)(2,1)S(1)} collective-permute-done((bf16[16,1280]{1,0:T(8,128)(2,1)S(1)}, bf16[16,1280]{1,0:T(8,128)(2,1)S(1)}, u32[]{:S(2)}, u32[]{:S(2)}) %collective-permute-start.17) | collective-permute-done | bytes 40992 | tf_op jit(solution)/shard_map/ppermute | solution.py:392
  117.3 3.2 %collective-permute-done.18.b_ref = bf16[16,1280]{1,0:T(8,128)(2,1)S(1)} collective-permute-done((bf16[16,1280]{1,0:T(8,128)(2,1)S(1)}, bf16[16,1280]{1,0:T(8,128)(2,1)S(1)}, u32[]{:S(2)}, u32[]{:S(2)}) %collective-permute-start.18) | collective-permute-done | bytes 40992 | tf_op jit(solution)/shard_map/ppermute | solution.py:392
  120.5 11.3 %collective-permute-start.19 = (bf16[16,1280]{1,0:T(8,128)(2,1)S(1)}, bf16[16,1280]{1,0:T(8,128)(2,1)S(1)}, u32[]{:S(2)}, u32[]{:S(2)}) collective-permute-start(bf16[16,1280]{1,0:T(8,128)(2,1)S(1)} %add.18.a_ref), channel_id=1, source_target_pairs={{0,1},{1,0},{2,3},{3,2},{4,5},{5,4},{6,7},{7,6},{8,9},{9,8},{10,11... | collective-permute-start | bytes 122888 | tf_op jit(solution)/shard_map/ppermute | solution.py:392
  133.7 3.1 %collective-permute-done.20.b_ref = bf16[16,1280]{1,0:T(8,128)(2,1)S(1)} collective-permute-done((bf16[16,1280]{1,0:T(8,128)(2,1)S(1)}, bf16[16,1280]{1,0:T(8,128)(2,1)S(1)}, u32[]{:S(2)}, u32[]{:S(2)}) %collective-permute-start.20) | collective-permute-done | bytes 40992 | tf_op jit(solution)/shard_map/ppermute | solution.py:392
  136.8 3.3 %collective-permute-done.21.far_ref = bf16[32,1280]{1,0:T(8,128)(2,1)S(1)} collective-permute-done((bf16[32,1280]{1,0:T(8,128)(2,1)S(1)}, bf16[32,1280]{1,0:T(8,128)(2,1)S(1)}, u32[]{:S(2)}, u32[]{:S(2)}) %collective-permute-start.21) | collective-permute-done | bytes 81952 | tf_op jit(solution)/shard_map/ppermute | solution.py:392
  (74 shorter events, 25.4 us)
Async XLA Ops:
  2.3 3.6 %collective-permute-start = (f32[32,384]{1,0:T(8,128)S(1)}, f32[32,384]{1,0:T(8,128)S(1)}, u32[]{:S(2)}, u32[]{:S(2)}) collective-permute-start(f32[32,384]{1,0:T(8,128)S(1)} %get-tuple-element.24), channel_id=1, source_target_pairs={{0,32},{32,0},{64,96},{96,64},{1,33},{33,1},{65,97},{97,65},{2,34}... | collective-permute-start | bytes 147464 | tf_op jit(solution)/shard_map/ppermute | solution.py:390
  5.9 4.3 %collective-permute-start.1 = (f32[16,384]{1,0:T(8,128)S(1)}, f32[16,384]{1,0:T(8,128)S(1)}, u32[]{:S(2)}, u32[]{:S(2)}) collective-permute-start(f32[16,384]{1,0:T(8,128)S(1)} %get-tuple-element.26), channel_id=1, source_target_pairs={{0,96},{32,64},{64,32},{96,0},{1,97},{33,65},{65,33},{97,1},{2,98}... | collective-permute-start | bytes 73736 | tf_op jit(solution)/shard_map/ppermute | solution.py:390
  31.2 56.4 %copy-start.1 = (bf16[1280,800]{0,1:T(8,128)(2,1)S(1)}, bf16[1280,800]{0,1:T(8,128)(2,1)}, u32[]{:S(2)}) copy-start(bf16[1280,800]{0,1:T(8,128)(2,1)} %param.28) | copy-start | bytes 6144004
  36.4 51.2 %copy-start = (bf16[1280,800]{0,1:T(8,128)(2,1)S(1)}, bf16[1280,800]{0,1:T(8,128)(2,1)}, u32[]{:S(2)}) copy-start(bf16[1280,800]{0,1:T(8,128)(2,1)} %param.27) | copy-start | bytes 6144004
  51.0 3.7 %collective-permute-start.2 = (bf16[16,256]{1,0:T(8,128)(2,1)S(1)}, bf16[16,256]{1,0:T(8,128)(2,1)S(1)}, u32[]{:S(2)}, u32[]{:S(2)}) collective-permute-start(bf16[16,256]{1,0:T(8,128)(2,1)S(1)} %get-tuple-element.29.a_ref), channel_id=1, source_target_pairs={{0,96},{32,64},{64,32},{96,0},{1,97},{33,65},{65,33},{97,1},{2,98}... | collective-permute-start | bytes 24584 | tf_op jit(solution)/shard_map/ppermute | solution.py:390
  54.8 2.6 %collective-permute-start.3 = (bf16[32,256]{1,0:T(8,128)(2,1)S(1)}, bf16[32,256]{1,0:T(8,128)(2,1)S(1)}, u32[]{:S(2)}, u32[]{:S(2)}) collective-permute-start(bf16[32,256]{1,0:T(8,128)(2,1)S(1)} %join.4.near_ref), channel_id=1, source_target_pairs={{0,32},{32,0},{64,96},{96,64},{1,33},{33,1},{65,97},{97,65},{2,34}... | collective-permute-start | bytes 49160 | tf_op jit(solution)/shard_map/ppermute | solution.py:390
  57.6 3.4 %collective-permute-start.4 = (bf16[32,1280]{1,0:T(8,128)(2,1)S(1)}, bf16[32,1280]{1,0:T(8,128)(2,1)S(1)}, u32[]{:S(2)}, u32[]{:S(2)}) collective-permute-start(bf16[32,1280]{1,0:T(8,128)(2,1)S(1)} %get-tuple-element.31), channel_id=1, source_target_pairs={{0,8},{1,9},{2,10},{3,11},{4,12},{5,13},{6,14},{7,15},{8,0},{9,1},... | collective-permute-start | bytes 245768 | tf_op jit(solution)/shard_map/ppermute | solution.py:392
  61.0 4.1 %collective-permute-start.5 = (bf16[16,1280]{1,0:T(8,128)(2,1)S(1)}, bf16[16,1280]{1,0:T(8,128)(2,1)S(1)}, u32[]{:S(2)}, u32[]{:S(2)}) collective-permute-start(bf16[16,1280]{1,0:T(8,128)(2,1)S(1)} %get-tuple-element.33), channel_id=1, source_target_pairs={{0,24},{1,25},{2,26},{3,27},{4,28},{5,29},{6,30},{7,31},{8,16},{9,... | collective-permute-start | bytes 122888 | tf_op jit(solution)/shard_map/ppermute | solution.py:392
  65.2 2.9 %collective-permute-start.6 = (bf16[16,1280]{1,0:T(8,128)(2,1)S(1)}, bf16[16,1280]{1,0:T(8,128)(2,1)S(1)}, u32[]{:S(2)}, u32[]{:S(2)}) collective-permute-start(bf16[16,1280]{1,0:T(8,128)(2,1)S(1)} %add.12.a_ref), channel_id=1, source_target_pairs={{0,2},{1,3},{2,0},{3,1},{4,6},{5,7},{6,4},{7,5},{8,10},{9,11},{10,... | collective-permute-start | bytes 122888 | tf_op jit(solution)/shard_map/ppermute | solution.py:392
  68.1 4.1 %collective-permute-start.7 = (bf16[16,1280]{1,0:T(8,128)(2,1)S(1)}, bf16[16,1280]{1,0:T(8,128)(2,1)S(1)}, u32[]{:S(2)}, u32[]{:S(2)}) collective-permute-start(bf16[16,1280]{1,0:T(8,128)(2,1)S(1)} %add.13.a_ref), channel_id=1, source_target_pairs={{0,6},{1,7},{2,4},{3,5},{4,2},{5,3},{6,0},{7,1},{8,14},{9,15},{10,... | collective-permute-start | bytes 122888 | tf_op jit(solution)/shard_map/ppermute | solution.py:392
  72.3 7.9 %collective-permute-start.8 = (bf16[16,1280]{1,0:T(8,128)(2,1)S(1)}, bf16[16,1280]{1,0:T(8,128)(2,1)S(1)}, u32[]{:S(2)}, u32[]{:S(2)}) collective-permute-start(bf16[16,1280]{1,0:T(8,128)(2,1)S(1)} %add.14.a_ref), channel_id=1, source_target_pairs={{0,1},{1,0},{2,3},{3,2},{4,5},{5,4},{6,7},{7,6},{8,9},{9,8},{10,11... | collective-permute-start | bytes 122888 | tf_op jit(solution)/shard_map/ppermute | solution.py:392
  80.2 4.1 %collective-permute-start.9 = (bf16[16,1280]{1,0:T(8,128)(2,1)S(1)}, bf16[16,1280]{1,0:T(8,128)(2,1)S(1)}, u32[]{:S(2)}, u32[]{:S(2)}) collective-permute-start(bf16[16,1280]{1,0:T(8,128)(2,1)S(1)} %add.15.a_ref), channel_id=1, source_target_pairs={{0,24},{1,25},{2,26},{3,27},{4,28},{5,29},{6,30},{7,31},{8,16},{9,... | collective-permute-start | bytes 122888 | tf_op jit(solution)/shard_map/ppermute | solution.py:392
  84.3 3.3 %collective-permute-start.10 = (bf16[32,1280]{1,0:T(8,128)(2,1)S(1)}, bf16[32,1280]{1,0:T(8,128)(2,1)S(1)}, u32[]{:S(2)}, u32[]{:S(2)}) collective-permute-start(bf16[32,1280]{1,0:T(8,128)(2,1)S(1)} %join.5.near_ref), channel_id=1, source_target_pairs={{0,8},{1,9},{2,10},{3,11},{4,12},{5,13},{6,14},{7,15},{8,0},{9,1},... | collective-permute-start | bytes 245768 | tf_op jit(solution)/shard_map/ppermute | solution.py:392
  89.0 3.7 %collective-permute-start.11 = (bf16[32,1792]{1,0:T(8,128)(2,1)S(1)}, bf16[32,1792]{1,0:T(8,128)(2,1)S(1)}, u32[]{:S(2)}, u32[]{:S(2)}) collective-permute-start(bf16[32,1792]{1,0:T(8,128)(2,1)S(1)} %get-tuple-element.36), channel_id=1, source_target_pairs={{0,32},{32,0},{64,96},{96,64},{1,33},{33,1},{65,97},{97,65},{2,34}... | collective-permute-start | bytes 344072 | tf_op jit(solution)/shard_map/ppermute | solution.py:390
  92.9 4.2 %collective-permute-start.12 = (bf16[16,1792]{1,0:T(8,128)(2,1)S(1)}, bf16[16,1792]{1,0:T(8,128)(2,1)S(1)}, u32[]{:S(2)}, u32[]{:S(2)}) collective-permute-start(bf16[16,1792]{1,0:T(8,128)(2,1)S(1)} %get-tuple-element.38), channel_id=1, source_target_pairs={{0,96},{32,64},{64,32},{96,0},{1,97},{33,65},{65,33},{97,1},{2,98}... | collective-permute-start | bytes 172040 | tf_op jit(solution)/shard_map/ppermute | solution.py:390
  97.4 4.6 %collective-permute-start.13 = (bf16[16,896]{1,0:T(8,128)(2,1)S(1)}, bf16[16,896]{1,0:T(8,128)(2,1)S(1)}, u32[]{:S(2)}, u32[]{:S(2)}) collective-permute-start(bf16[16,896]{1,0:T(8,128)(2,1)S(1)} %activate.1.a_ref), channel_id=1, source_target_pairs={{0,96},{32,64},{64,32},{96,0},{1,97},{33,65},{65,33},{97,1},{2,98}... | collective-permute-start | bytes 86024 | tf_op jit(solution)/shard_map/ppermute | solution.py:390
  102.0 3.0 %collective-permute-start.14 = (bf16[32,896]{1,0:T(8,128)(2,1)S(1)}, bf16[32,896]{1,0:T(8,128)(2,1)S(1)}, u32[]{:S(2)}, u32[]{:S(2)}) collective-permute-start(bf16[32,896]{1,0:T(8,128)(2,1)S(1)} %join.6.near_ref), channel_id=1, source_target_pairs={{0,32},{32,0},{64,96},{96,64},{1,33},{33,1},{65,97},{97,65},{2,34}... | collective-permute-start | bytes 172040 | tf_op jit(solution)/shard_map/ppermute | solution.py:390
  105.5 3.4 %collective-permute-start.15 = (bf16[32,1280]{1,0:T(8,128)(2,1)S(1)}, bf16[32,1280]{1,0:T(8,128)(2,1)S(1)}, u32[]{:S(2)}, u32[]{:S(2)}) collective-permute-start(bf16[32,1280]{1,0:T(8,128)(2,1)S(1)} %get-tuple-element.40), channel_id=1, source_target_pairs={{0,8},{1,9},{2,10},{3,11},{4,12},{5,13},{6,14},{7,15},{8,0},{9,1},... | collective-permute-start | bytes 245768 | tf_op jit(solution)/shard_map/ppermute | solution.py:392
  108.9 4.1 %collective-permute-start.16 = (bf16[16,1280]{1,0:T(8,128)(2,1)S(1)}, bf16[16,1280]{1,0:T(8,128)(2,1)S(1)}, u32[]{:S(2)}, u32[]{:S(2)}) collective-permute-start(bf16[16,1280]{1,0:T(8,128)(2,1)S(1)} %get-tuple-element.42), channel_id=1, source_target_pairs={{0,24},{1,25},{2,26},{3,27},{4,28},{5,29},{6,30},{7,31},{8,16},{9,... | collective-permute-start | bytes 122888 | tf_op jit(solution)/shard_map/ppermute | solution.py:392
  113.0 3.2 %collective-permute-start.17 = (bf16[16,1280]{1,0:T(8,128)(2,1)S(1)}, bf16[16,1280]{1,0:T(8,128)(2,1)S(1)}, u32[]{:S(2)}, u32[]{:S(2)}) collective-permute-start(bf16[16,1280]{1,0:T(8,128)(2,1)S(1)} %add.16.a_ref), channel_id=1, source_target_pairs={{0,2},{1,3},{2,0},{3,1},{4,6},{5,7},{6,4},{7,5},{8,10},{9,11},{10,... | collective-permute-start | bytes 122888 | tf_op jit(solution)/shard_map/ppermute | solution.py:392
  116.3 4.1 %collective-permute-start.18 = (bf16[16,1280]{1,0:T(8,128)(2,1)S(1)}, bf16[16,1280]{1,0:T(8,128)(2,1)S(1)}, u32[]{:S(2)}, u32[]{:S(2)}) collective-permute-start(bf16[16,1280]{1,0:T(8,128)(2,1)S(1)} %add.17.a_ref), channel_id=1, source_target_pairs={{0,6},{1,7},{2,4},{3,5},{4,2},{5,3},{6,0},{7,1},{8,14},{9,15},{10,... | collective-permute-start | bytes 122888 | tf_op jit(solution)/shard_map/ppermute | solution.py:392
  120.5 12.2 %collective-permute-start.19 = (bf16[16,1280]{1,0:T(8,128)(2,1)S(1)}, bf16[16,1280]{1,0:T(8,128)(2,1)S(1)}, u32[]{:S(2)}, u32[]{:S(2)}) collective-permute-start(bf16[16,1280]{1,0:T(8,128)(2,1)S(1)} %add.18.a_ref), channel_id=1, source_target_pairs={{0,1},{1,0},{2,3},{3,2},{4,5},{5,4},{6,7},{7,6},{8,9},{9,8},{10,11... | collective-permute-start | bytes 122888 | tf_op jit(solution)/shard_map/ppermute | solution.py:392
  132.7 4.1 %collective-permute-start.20 = (bf16[16,1280]{1,0:T(8,128)(2,1)S(1)}, bf16[16,1280]{1,0:T(8,128)(2,1)S(1)}, u32[]{:S(2)}, u32[]{:S(2)}) collective-permute-start(bf16[16,1280]{1,0:T(8,128)(2,1)S(1)} %add.19.a_ref), channel_id=1, source_target_pairs={{0,24},{1,25},{2,26},{3,27},{4,28},{5,29},{6,30},{7,31},{8,16},{9,... | collective-permute-start | bytes 122888 | tf_op jit(solution)/shard_map/ppermute | solution.py:392
  136.8 3.3 %collective-permute-start.21 = (bf16[32,1280]{1,0:T(8,128)(2,1)S(1)}, bf16[32,1280]{1,0:T(8,128)(2,1)S(1)}, u32[]{:S(2)}, u32[]{:S(2)}) collective-permute-start(bf16[32,1280]{1,0:T(8,128)(2,1)S(1)} %join.7.near_ref), channel_id=1, source_target_pairs={{0,8},{1,9},{2,10},{3,11},{4,12},{5,13},{6,14},{7,15},{8,0},{9,1},... | collective-permute-start | bytes 245768 | tf_op jit(solution)/shard_map/ppermute | solution.py:392
  (10 other events, 271.6 us)

commit v7 on v4

--- a/solution.py
+++ b/solution.py
@@ -17,6 +17,9 @@
 
 ROWS = 4
 WIDE = 32
+WIDE_AXES = ("y", "z", "core")
+CHIPS = 16
+CHIP_AXES = ("y", "z")
 PACKED = 40
 AT_ONCE = 2
 GROUPS = 8
@@ -160,14 +163,33 @@
     out_ref[...] = jnp.broadcast_to(out[None], out_ref.shape)
 
 
+def of_cores(place_ref, own_ref, other_ref):
+    core = lax.rem(place_ref[0], 2)
+    return (own_ref, core), (other_ref, 1 - core)
+
+
 def attend_kernel(
-    length_ref, block_ref, g_ref, k_ref, v_ref, o_ref, q_scr, p_scr, w_scr, n_scr, s_scr
+    place_ref,
+    length_ref,
+    block_ref,
+    own_ref,
+    other_ref,
+    k_ref,
+    v_ref,
+    o_ref,
+    q_scr,
+    p_scr,
+    w_scr,
+    n_scr,
+    s_scr,
 ):
-    for head in range(QUERY_HEADS):
-        w, j = divmod(head, 2)
-        q_scr[pl.ds(head, OWN, stride=QUERY_HEADS), :] = g_ref[
-            w, j * OWN : (j + 1) * OWN, :
-        ].astype(f32)
+    for ref, core in of_cores(place_ref, own_ref, other_ref):
+        for chip in range(CHIPS):
+            for j in range(2):
+                head = 4 * chip + 2 * core + j
+                q_scr[pl.ds(head, OWN, stride=QUERY_HEADS), :] = ref[
+                    chip, j * OWN : (j + 1) * OWN, :
+                ].astype(f32)
 
     row = lax.broadcasted_iota(jnp.int32, (16, 256), 0)
     lane = lax.broadcasted_iota(jnp.int32, (16, 256), 1)
@@ -242,23 +264,30 @@
         o_ref[w, 2 * OWN :, :] = jnp.where(lane[:8] < 64, stats[:8], stats[8:]).astype(bf16)
 
 
-def combine_kernel(place_ref, r_ref, g_ref, straight_ref, swapped_ref, out_ref, again_ref):
+def combine_kernel(
+    place_ref, r_ref, own_ref, other_ref, straight_ref, swapped_ref, out_ref, again_ref
+):
     wide = lax.rem(place_ref[0], WIDE)
     group = wide // 4
 
-    def half(source):
-        return unpack(g_ref[source, 2 * OWN :, :].astype(f32))
+    def both_halves(chip):
+        parts = [unpack(ref[chip, 2 * OWN :, :].astype(f32)) for ref in (own_ref, other_ref)]
+        return jnp.where(
+            lax.rem(wide, 2) == 0,
+            jnp.concatenate(parts, axis=1),
+            jnp.concatenate(parts[::-1], axis=1),
+        )
 
     def column(value, at):
         return jnp.concatenate(
             [value[..., at : at + 1], value[..., 64 + at : 65 + at]], axis=-2
         )
 
-    key = jnp.concatenate([half(2 * group), half(2 * group + 1)], axis=1)
-    value = jnp.concatenate([half(16 + 2 * group), half(17 + 2 * group)], axis=1)
+    key = both_halves(group)
+    value = both_halves(8 + group)
     key = norm_rope(key, straight_ref[1], swapped_ref[1]).astype(bf16).astype(f32)
     fresh = [
-        jnp.sum(g_ref[wide, j * OWN : (j + 1) * OWN, :].astype(f32) * key, axis=1, keepdims=True)
+        jnp.sum(own_ref[wide // 2, j * OWN : (j + 1) * OWN, :].astype(f32) * key, axis=1, keepdims=True)
         * SCALE
         for j in range(2)
     ]
@@ -286,14 +315,18 @@
         again_ref[:, lanes] = heads
 
 
-def store_pairs(out_ref, value):
-    for block in range(WIDE):
-        out_ref[block] = value[2 * block : 2 * block + 2]
-
-
-def output_kernel(a_ref, b_ref, c_ref, d_ref, w_ref, out_ref):
-    heads = jnp.concatenate([a_ref[...], b_ref[...], c_ref[...], d_ref[...]], axis=0)
-    store_pairs(out_ref, jnp.dot(heads, w_ref[...], preferred_element_type=f32).astype(bf16))
+def product_kernel(place_ref, a_ref, b_ref, c_ref, d_ref, w_ref, keep_ref, send_ref, whole):
+    left = jnp.concatenate([a_ref[...], b_ref[...], c_ref[...], d_ref[...]], axis=0)
+    whole[...] = jnp.dot(left[:, : w_ref.shape[0]], w_ref[...], preferred_element_type=f32)
+    half = keep_ref.shape[0]
+    for ref, core in of_cores(place_ref, keep_ref, send_ref):
+        ref[...] = whole[pl.ds(pl.multiple_of(core * half, half), half), :].astype(ref.dtype)
+
+
+def chip_sum_kernel(keep_ref, got_ref, out_ref):
+    total = (keep_ref[...] + got_ref[...].astype(f32)).astype(bf16)
+    for chip in range(CHIPS):
+        out_ref[chip] = total[2 * chip : 2 * chip + 2]
 
 
 def sum_spread_kernel(got_ref, out_ref):
@@ -301,15 +334,20 @@
     out_ref[...] = jnp.broadcast_to(total[None], out_ref.shape)
 
 
+def row_blocks(place_ref, own_ref, other_ref):
+    for ref, core in of_cores(place_ref, own_ref, other_ref):
+        for at in range(2):
+            block = ref[at * 8 : (at + 1) * 8].astype(f32)
+            yield 2 * core + at, block.reshape(OWN, block.shape[-1])
+
+
 def gate_up_kernel(
-    place_ref, hidden_ref, attended_ref, gain_ref, wg_ref, wu_ref, stream_ref, *outs
+    place_ref, hidden_ref, own_ref, other_ref, gain_ref, wg_ref, wu_ref, stream_ref, *outs
 ):
     mine = place_ref[0] // WIDE
-    for k in range(ROWS):
-        at = slice(k * OWN, (k + 1) * OWN)
-        blocks = attended_ref[k * WIDE // ROWS : (k + 1) * WIDE // ROWS]
-        attended = blocks.astype(f32).reshape(OWN, blocks.shape[-1])
-        stream_ref[at, :] = hidden_ref[row_block(mine, k), :].astype(f32) + attended
+    for block, attended in row_blocks(place_ref, own_ref, other_ref):
+        hidden = hidden_ref[row_block(mine, block), :].astype(f32)
+        stream_ref[row_block(0, block), :] = hidden + attended
     stream = stream_ref[...]
     square = jnp.sum(stream * stream, axis=1, keepdims=True)
     scaled = (stream * gain_ref[...].astype(f32)[None]).astype(bf16)
@@ -341,19 +379,11 @@
     out_ref[...] = (gate / (1.0 + jnp.exp(-gate)) * up).astype(bf16)
 
 
-def down_kernel(a_ref, b_ref, c_ref, d_ref, w_ref, out_ref):
-    units = jnp.concatenate([a_ref[...], b_ref[...], c_ref[...], d_ref[...]], axis=0)
-    part = jnp.dot(units[:, :HIDDEN_UNITS], w_ref[...], preferred_element_type=f32)
-    store_pairs(out_ref, part.astype(bf16))
-
-
-def final_kernel(place_ref, stream_ref, down_ref, out_ref):
+def final_kernel(place_ref, stream_ref, own_ref, other_ref, out_ref):
     mine = place_ref[0] // WIDE
-    for k in range(ROWS):
-        at = slice(k * OWN, (k + 1) * OWN)
-        blocks = down_ref[k * WIDE // ROWS : (k + 1) * WIDE // ROWS]
-        down = blocks.astype(f32).reshape(OWN, blocks.shape[-1])
-        out_ref[row_block(mine, k), :] = (stream_ref[at, :] + down).astype(bf16)
+    for block, down in row_blocks(place_ref, own_ref, other_ref):
+        total = stream_ref[row_block(0, block), :] + down
+        out_ref[row_block(mine, block), :] = total.astype(bf16)
 
 
 def to_rows(blocks):
@@ -370,19 +400,24 @@
     return got
 
 
-def exchange(blocks):
-    return lax.all_to_all(blocks, "wide", split_axis=0, concat_axis=0, tiled=True)
-
-
-def sum_wide(part):
-    total = call(
-        sum_spread_kernel,
-        jax.ShapeDtypeStruct(part.shape, bf16),
-        [VMEM],
-        limit=4,
-        name="sum_spread",
-    )(exchange(part))
-    return exchange(total)
+def exchange(blocks, axes):
+    return lax.all_to_all(blocks, axes, split_axis=0, concat_axis=0, tiled=True)
+
+
+def from_other_core(value):
+    return lax.ppermute(value, "core", [(0, 1), (1, 0)])
+
+
+def sum_wide(keep, send):
+    blocks = jax.ShapeDtypeStruct((CHIPS, 2, send.shape[1]), bf16)
+    part = call(chip_sum_kernel, blocks, [VMEM] * 2, limit=4, name="chip_sum")(
+        keep, from_other_core(send)
+    )
+    total = call(sum_spread_kernel, blocks, [VMEM], limit=4, name="sum_spread")(
+        exchange(part, CHIP_AXES)
+    )
+    own = exchange(total, CHIP_AXES)
+    return own, from_other_core(own)
 
 
 def body(
@@ -402,7 +437,7 @@
     w_up,
     w_down,
 ):
-    place = lax.axis_index(("rows", "wide")).astype(jnp.int32).reshape(1)
+    place = lax.axis_index(("rows", *WIDE_AXES)).astype(jnp.int32).reshape(1)
     sds = jax.ShapeDtypeStruct
 
     blocks = call(
@@ -430,18 +465,19 @@
     )(*map(in_hbm, (lengths, query_gain, key_norm_gain)))
     payload = call(
         heads_kernel,
-        sds((WIDE, PACKED, 128), bf16),
+        sds((CHIPS, PACKED, 128), bf16),
         [VMEM] * 6,
         limit=8,
         name="heads",
         cost=pl.CostEstimate(flops=20_000_000_000, bytes_accessed=1 << 20, transcendentals=0),
     )(*to_rows(blocks), straight, swapped)
-    gathered = exchange(payload)
+    gathered = exchange(payload, CHIP_AXES)
+    gathered = (gathered, from_other_core(gathered))
 
     parts = call(
         attend_kernel,
         sds((WIDE, PACKED, 128), bf16),
-        [SMEM, SMEM, VMEM, VMEM, VMEM],
+        [SMEM] * 3 + [VMEM] * 4,
         [
             pltpu.VMEM((OWN * QUERY_HEADS, 128), f32),
             pltpu.VMEM((OWN * QUERY_HEADS, 256), f32),
@@ -451,52 +487,59 @@
         ],
         limit=8,
         name="attend",
-    )(lengths, block_index.reshape(OWN), gathered, in_vmem(keys_cache), in_vmem(values_cache))
+    )(place, lengths, block_index.reshape(OWN), *gathered, in_vmem(keys_cache), in_vmem(values_cache))
     heads_out, heads_own = call(
-        combine_kernel, [sds((OWN, 256), bf16)] * 2, [SMEM] + [VMEM] * 4, limit=8, name="combine"
-    )(place, exchange(parts), gathered, straight, swapped)
-
-    out_part = call(output_kernel, sds((WIDE, 2, 1280), bf16), [VMEM] * 5, limit=8, name="output")(
-        *from_rows(heads_own), w_out
-    )
-    attended = sum_wide(out_part)
-
+        combine_kernel, [sds((OWN, 256), bf16)] * 2, [SMEM] + [VMEM] * 5, limit=8, name="combine"
+    )(place, exchange(parts, WIDE_AXES), *gathered, straight, swapped)
+
+    def product(own, weight, name):
+        return call(
+            product_kernel,
+            [sds((32, 1280), f32), sds((32, 1280), bf16)],
+            [SMEM] + [VMEM] * 5,
+            [pltpu.VMEM((64, 1280), f32)],
+            limit=8,
+            name=name,
+        )(place, *from_rows(own), weight)
+
+    attended = sum_wide(*product(heads_own, w_out, "output"))
     stream, *blocks = call(
         gate_up_kernel,
         [sds((64, 1280), f32)] + [sds((OWN, 2 * HALF), bf16)] * ROWS,
-        [SMEM] + [VMEM] * 5,
+        [SMEM] + [VMEM] * 6,
         limit=12,
         name="gate_up",
-    )(place, hidden, attended, mlp_gain, w_gate.T, w_up.T)
+    )(place, hidden, *attended, mlp_gain, w_gate.T, w_up.T)
     activated = call(
         activate_kernel, sds((OWN, HALF), bf16), [VMEM] * 4, limit=8, name="activate"
     )(*to_rows(blocks))
-    down_part = call(down_kernel, sds((WIDE, 2, 1280), bf16), [VMEM] * 5, limit=8, name="down")(
-        *from_rows(activated), w_down
-    )
-    layer_out = call(final_kernel, sds((64, 1280), bf16), [SMEM] + [VMEM] * 2, limit=8, name="final")(
-        place, stream, sum_wide(down_part)
-    )
+    down = sum_wide(*product(activated, w_down, "down"))
+    layer_out = call(
+        final_kernel, sds((64, 1280), bf16), [SMEM] + [VMEM] * 3, limit=8, name="final"
+    )(place, stream, *down)
     return (layer_out, heads_out)
 
 
 def solution(mesh):
+    mesh = jax.sharding.Mesh(
+        mesh.devices.reshape(4, 4, 4, 2), ("rows", "y", "z", "core")
+    )
     in_specs = (
         P(None, "rows"),
         P("rows"),
-        P("rows", "wide"),
-        P("rows", "wide"),
+        P("rows", WIDE_AXES),
+        P("rows", WIDE_AXES),
         P(),
         P(),
-        P("rows", "wide", None),
-        P("rows", "wide", None),
+        P("rows", WIDE_AXES, None),
+        P("rows", WIDE_AXES, None),
         P("rows"),
-        P("rows", "wide"),
-        P("wide", "rows"),
+        P("rows", WIDE_AXES),
+        P(WIDE_AXES, "rows"),
         P("rows"),
-        P("rows", "wide"),
-        P("rows", "wide"),
-        P("wide", "rows"),
-    )
-    out_specs = (P(None, "rows"), P("rows", "wide"))
+        P("rows", WIDE_AXES),
+        P("rows", WIDE_AXES),
+        P(WIDE_AXES, "rows"),
+    )
+    out_specs = (P(None, "rows"), P("rows", WIDE_AXES))
     return jax.shard_map(body, mesh=mesh, in_specs=in_specs, out_specs=out_specs, check_vma=False)

time: 122 us -> 125 us (1.025)
  blocking collectives: 83.6 us -> 67.1 us
  starting transfers between devices: 16.3 us -> 30.7 us
  waiting for transfers between devices: 8.05 us -> 12.8 us
    all_to_all x6, blocking collectives: 83.6 us -> 67.1 us  [exchange(): return lax.all_to_all(blocks, axes, split_axis=0, concat_axis=0, tiled=True)]
    ppermute x0 -> x5, starting transfers between devices: none -> 14.4 us  [from_other_core(): return lax.ppermute(value, 'core', [(0, 1), (1, 0)])]
    ppermute x0 -> x5, waiting for transfers between devices: none -> 4.72 us  [from_other_core(): return lax.ppermute(value, 'core', [(0, 1), (1, 0)])]
    pallas_call x8 -> x10, Pallas kernels: 8.67 us -> 8.59 us  [the longest x1 5.23 us: body(): call(attend_kernel, sds((WIDE, PACKED, 128), bf16), [SMEM] * 3 + [VMEM] *...]
  transfers between devices with their start and end apart: 12 -> 17, of which waited for: 10 -> 15; matrix products, arithmetic and copies ran while one was open for 0% -> 0% of each run, Pallas kernels for 1% -> 1%
where the time goes in v7:
time: 125 us
  blocking collectives  67.1 us (54%)
  starting transfers between devices  30.7 us (25%)
  Pallas kernels  13.2 us (11%)
  waiting for transfers between devices  12.8 us (10%)
    all_to_all x6, blocking collectives, exchange(): return lax.all_to_all(blocks, axes, split_axis=0, concat_axis=0, tiled=True)  67.1 us
    ppermute x5, starting transfers between devices, from_other_core(): return lax.ppermute(value, 'core', [(0, 1), (1, 0)])  14.4 us
    ppermute x6, starting transfers between devices, to_rows(): lax.ppermute(blocks[k], 'rows', [(i, (i + k) % ROWS) for i in range(ROWS)])  9.08 us
    ppermute x6, starting transfers between devices, from_rows(): lax.ppermute(own, 'rows', [((i + k) % ROWS, i) for i in range(ROWS)])  7.23 us
    pallas_call x1, Pallas kernels, body(): call(attend_kernel, sds((WIDE, PACKED, 128), bf16), [SMEM] * 3 + [VMEM] *...  5.23 us
    ppermute x6, waiting for transfers between devices, from_rows(): lax.ppermute(own, 'rows', [((i + k) % ROWS, i) for i in range(ROWS)])  5.18 us
    ppermute x5, waiting for transfers between devices, from_other_core(): return lax.ppermute(value, 'core', [(0, 1), (1, 0)])  4.72 us
    ppermute x6, waiting for transfers between devices, to_rows(): lax.ppermute(blocks[k], 'rows', [(i, (i + k) % ROWS) for i in range(ROWS)])  2.85 us
  transfers between devices with their start and end apart: 17, of which 15 were waited for; matrix products, arithmetic and copies ran while one was open for 0% of the time, Pallas kernels for 1%

profile of v7, /device:TPU:1, one launch (start us, length us, event | category | flops | bytes accessed | tf_op | source)
XLA Modules:
  0.0 124.8 jit_solution(16827053482145314266)
XLA Ops:
  0.6 1.6 %project.1 = (f32[16,384]{1,0:T(8,128)S(1)}, f32[16,384]{1,0:T(8,128)S(1)}, f32[16,384]{1,0:T(8,128)S(1)}, f32[16,384]{1,0:T(8,128)S(1)}) custom-call(s32[1]{0:T(128)} %bitcast.place_ref, bf16[64,1280]{1,0:T(8,128)(2,1)} %hidden_ref.1, bf16[1280]{0:T(1024)(128)(2,1)} %gain_hbm.1, bf16[1280,256]{1,0:T(8,128)(2,1)} %wq_hbm.1, bf16[64,1280]{1,0:T(8,128)(2,1)} %bitcast.12), custom_call_target="tpu_custom_call" | custom-call | tf_op jit(solution)/shard_map/project/pallas_call | solution.py:443
  2.3 2.1 %collective-permute-start = (f32[16,384]{1,0:T(8,128)S(1)}, f32[16,384]{1,0:T(8,128)S(1)}, u32[]{:S(2)}, u32[]{:S(2)}) collective-permute-start(f32[16,384]{1,0:T(8,128)S(1)} %get-tuple-element.20), channel_id=1, source_target_pairs={{0,32},{32,64},{64,96},{96,0},{1,33},{33,65},{65,97},{97,1},{2,34}... | collective-permute-start | bytes 73736 | tf_op jit(solution)/shard_map/ppermute | solution.py:392
  4.4 2.5 %collective-permute-start.1 = (f32[16,384]{1,0:T(8,128)S(1)}, f32[16,384]{1,0:T(8,128)S(1)}, u32[]{:S(2)}, u32[]{:S(2)}) collective-permute-start(f32[16,384]{1,0:T(8,128)S(1)} %get-tuple-element.21), channel_id=1, source_target_pairs={{0,64},{32,96},{64,0},{96,32},{1,65},{33,97},{65,1},{97,33},{2,66}... | collective-permute-start | bytes 73736 | tf_op jit(solution)/shard_map/ppermute | solution.py:392
  8.0 1.5 %tables.1 = (f32[2,16,128]{2,1,0:T(8,128)S(1)}, f32[2,16,128]{2,1,0:T(8,128)S(1)}) custom-call(s32[16]{0:T(128)} %length_ref.3, bf16[128]{0:T(256)(128)(2,1)} %query_hbm.1, bf16[128]{0:T(256)(128)(2,1)} %key_hbm.1), custom_call_target="tpu_custom_call" | custom-call | tf_op jit(solution)/shard_map/tables/pallas_call | solution.py:458
  10.1 14.6 %all_to_all.30.own_ref = bf16[16,40,128]{2,1,0:T(8,128)(2,1)S(1)} all-to-all(bf16[16,40,128]{2,1,0:T(8,128)(2,1)S(1)} %heads.1), channel_id=1, replica_groups=mesh['rows'=4,'y'=4,'z'=4,'core'=2] {'y','z'}, dimensions={0} | all-to-all | bytes 327680 | tf_op jit(solution)/shard_map/all_to_all | solution.py:404
  24.7 3.5 %collective-permute-start.3 = (bf16[16,40,128]{2,1,0:T(8,128)(2,1)S(1)}, bf16[16,40,128]{2,1,0:T(8,128)(2,1)S(1)}, u32[]{:S(2)}, u32[]{:S(2)}) collective-permute-start(bf16[16,40,128]{2,1,0:T(8,128)(2,1)S(1)} %all_to_all.30.own_ref), channel_id=1, source_target_pairs={{0,1},{1,0},{2,3},{3,2},{4,5},{5,4},{6,7},{7,6},{8,9},{9,8},{10,11... | collective-permute-start | bytes 491528 | tf_op jit(solution)/shard_map/ppermute | solution.py:408
  29.3 5.2 %attend.1 = bf16[32,40,128]{2,1,0:T(8,128)(2,1)S(1)} custom-call(s32[1]{0:T(128)} %bitcast.place_ref, s32[16]{0:T(128)S(1)} %copy-done.6, s32[16]{0:T(128)S(1)} %bitcast.11, bf16[16,40,128]{2,1,0:T(8,128)(2,1)S(1)} %all_to_all.30.own_ref, bf16[16,40,128]{2,1,0:T(8,128)(2,1)S(1)} %collective-permute-done.3.other_ref, bf16[16,256,1024]{2,1,0:T(8,128)(2,1)S(1)} %bitcast.6, ...), custom_call_target="tpu_custom_call" | custom-call | tf_op jit(solution)/shard_map/attend/pallas_call | solution.py:477
  34.6 13.7 %all_to_all.31.r_ref = bf16[32,40,128]{2,1,0:T(8,128)(2,1)S(1)} all-to-all(bf16[32,40,128]{2,1,0:T(8,128)(2,1)S(1)} %attend.1), channel_id=1, replica_groups=mesh['rows'=4,'y'=4,'z'=4,'core'=2] {'y','z','core'}, dimensions={0} | all-to-all | bytes 655360 | tf_op jit(solution)/shard_map/all_to_all | solution.py:404
  48.3 1.4 %combine.1 = (bf16[16,256]{1,0:T(8,128)(2,1)}, bf16[16,256]{1,0:T(8,128)(2,1)S(1)}) custom-call(s32[1]{0:T(128)} %bitcast.place_ref, bf16[32,40,128]{2,1,0:T(8,128)(2,1)S(1)} %all_to_all.31.r_ref, bf16[16,40,128]{2,1,0:T(8,128)(2,1)S(1)} %all_to_all.30.own_ref, bf16[16,40,128]{2,1,0:T(8,128)(2,1)S(1)} %collective-permute-done.3.other_ref, ...), custom_call_target="tpu_custom_call" | custom-call | tf_op jit(solution)/shard_map/combine/pallas_call | solution.py:491
  49.7 3.5 %collective-permute-start.5 = (bf16[16,256]{1,0:T(8,128)(2,1)S(1)}, bf16[16,256]{1,0:T(8,128)(2,1)S(1)}, u32[]{:S(2)}, u32[]{:S(2)}) collective-permute-start(bf16[16,256]{1,0:T(8,128)(2,1)S(1)} %get-tuple-element.25.a_ref), channel_id=1, source_target_pairs={{64,0},{96,32},{0,64},{32,96},{65,1},{97,33},{1,65},{33,97},{66,2}... | collective-permute-start | bytes 24584 | tf_op jit(solution)/shard_map/ppermute | solution.py:399
  54.3 1.4 %collective-permute-done.4.b_ref = bf16[16,256]{1,0:T(8,128)(2,1)S(1)} collective-permute-done((bf16[16,256]{1,0:T(8,128)(2,1)S(1)}, bf16[16,256]{1,0:T(8,128)(2,1)S(1)}, u32[]{:S(2)}, u32[]{:S(2)}) %collective-permute-start.4) | collective-permute-done | bytes 8224 | tf_op jit(solution)/shard_map/ppermute | solution.py:399
  56.0 1.8 %collective-permute-start.7 = (bf16[32,1280]{1,0:T(8,128)(2,1)S(1)}, bf16[32,1280]{1,0:T(8,128)(2,1)S(1)}, u32[]{:S(2)}, u32[]{:S(2)}) collective-permute-start(bf16[32,1280]{1,0:T(8,128)(2,1)S(1)} %get-tuple-element.27), channel_id=1, source_target_pairs={{0,1},{1,0},{2,3},{3,2},{4,5},{5,4},{6,7},{7,6},{8,9},{9,8},{10,11... | collective-permute-start | bytes 245768 | tf_op jit(solution)/shard_map/ppermute | solution.py:408
  58.7 9.6 %all_to_all.32.got_ref = bf16[16,2,1280]{2,1,0:T(2,128)(2,1)S(1)} all-to-all(bf16[16,2,1280]{2,1,0:T(2,128)(2,1)S(1)} %chip_sum.2), channel_id=1, replica_groups=mesh['rows'=4,'y'=4,'z'=4,'core'=2] {'y','z'}, dimensions={0} | all-to-all | bytes 163840 | tf_op jit(solution)/shard_map/all_to_all | solution.py:404
  68.4 9.8 %all_to_all.33.own_ref = bf16[16,2,1280]{2,1,0:T(2,128)(2,1)S(1)} all-to-all(bf16[16,2,1280]{2,1,0:T(2,128)(2,1)S(1)} %sum_spread.2), channel_id=1, replica_groups=mesh['rows'=4,'y'=4,'z'=4,'core'=2] {'y','z'}, dimensions={0} | all-to-all | bytes 163840 | tf_op jit(solution)/shard_map/all_to_all | solution.py:404
  78.3 2.9 %collective-permute-start.8 = (bf16[16,2,1280]{2,1,0:T(2,128)(2,1)S(1)}, bf16[16,2,1280]{2,1,0:T(2,128)(2,1)S(1)}, u32[]{:S(2)}, u32[]{:S(2)}) collective-permute-start(bf16[16,2,1280]{2,1,0:T(2,128)(2,1)S(1)} %all_to_all.33.own_ref), channel_id=1, source_target_pairs={{0,1},{1,0},{2,3},{3,2},{4,5},{5,4},{6,7},{7,6},{8,9},{9,8},{10,11... | collective-permute-start | bytes 245768 | tf_op jit(solution)/shard_map/ppermute | solution.py:408
  82.1 1.3 %gate_up.1 = (f32[64,1280]{1,0:T(8,128)S(1)}, bf16[16,1792]{1,0:T(8,128)(2,1)S(1)}, bf16[16,1792]{1,0:T(8,128)(2,1)S(1)}, bf16[16,1792]{1,0:T(8,128)(2,1)S(1)}, bf16[16,1792]{1,0:T(8,128)(2,1)S(1)}) custom-call(s32[1]{0:T(128)} %bitcast.place_ref, bf16[64,1280]{1,0:T(8,128)(2,1)S(1)} %copy-done.3, bf16[16,2,1280]{2,1,0:T(2,128)(2,1)S(1)} %all_to_all.33.own_ref, ...), custom_call_target="tpu_custom_call" | custom-call | tf_op jit(solution)/shard_map/gate_up/pallas_call | solution.py:506
  83.6 2.1 %collective-permute-start.10 = (bf16[16,1792]{1,0:T(8,128)(2,1)S(1)}, bf16[16,1792]{1,0:T(8,128)(2,1)S(1)}, u32[]{:S(2)}, u32[]{:S(2)}) collective-permute-start(bf16[16,1792]{1,0:T(8,128)(2,1)S(1)} %get-tuple-element.31), channel_id=1, source_target_pairs={{0,64},{32,96},{64,0},{96,32},{1,65},{33,97},{65,1},{97,33},{2,66}... | collective-permute-start | bytes 172040 | tf_op jit(solution)/shard_map/ppermute | solution.py:392
  86.9 1.5 %collective-permute-done.9.b_ref = bf16[16,1792]{1,0:T(8,128)(2,1)S(1)} collective-permute-done((bf16[16,1792]{1,0:T(8,128)(2,1)S(1)}, bf16[16,1792]{1,0:T(8,128)(2,1)S(1)}, u32[]{:S(2)}, u32[]{:S(2)}) %collective-permute-start.9) | collective-permute-done | bytes 57376 | tf_op jit(solution)/shard_map/ppermute | solution.py:392
  90.8 2.5 %collective-permute-start.13 = (bf16[16,896]{1,0:T(8,128)(2,1)S(1)}, bf16[16,896]{1,0:T(8,128)(2,1)S(1)}, u32[]{:S(2)}, u32[]{:S(2)}) collective-permute-start(bf16[16,896]{1,0:T(8,128)(2,1)S(1)} %activate.1.a_ref), channel_id=1, source_target_pairs={{64,0},{96,32},{0,64},{32,96},{65,1},{97,33},{1,65},{33,97},{66,2}... | collective-permute-start | bytes 86024 | tf_op jit(solution)/shard_map/ppermute | solution.py:399
  93.6 1.4 %collective-permute-done.13.c_ref = bf16[16,896]{1,0:T(8,128)(2,1)S(1)} collective-permute-done((bf16[16,896]{1,0:T(8,128)(2,1)S(1)}, bf16[16,896]{1,0:T(8,128)(2,1)S(1)}, u32[]{:S(2)}, u32[]{:S(2)}) %collective-permute-start.13) | collective-permute-done | bytes 28704 | tf_op jit(solution)/shard_map/ppermute | solution.py:399
  96.4 3.3 %collective-permute-start.15 = (bf16[32,1280]{1,0:T(8,128)(2,1)S(1)}, bf16[32,1280]{1,0:T(8,128)(2,1)S(1)}, u32[]{:S(2)}, u32[]{:S(2)}) collective-permute-start(bf16[32,1280]{1,0:T(8,128)(2,1)S(1)} %get-tuple-element.34), channel_id=1, source_target_pairs={{0,1},{1,0},{2,3},{3,2},{4,5},{5,4},{6,7},{7,6},{8,9},{9,8},{10,11... | collective-permute-start | bytes 245768 | tf_op jit(solution)/shard_map/ppermute | solution.py:408
  100.7 9.5 %all_to_all.34.got_ref = bf16[16,2,1280]{2,1,0:T(2,128)(2,1)S(1)} all-to-all(bf16[16,2,1280]{2,1,0:T(2,128)(2,1)S(1)} %chip_sum.3), channel_id=1, replica_groups=mesh['rows'=4,'y'=4,'z'=4,'core'=2] {'y','z'}, dimensions={0} | all-to-all | bytes 163840 | tf_op jit(solution)/shard_map/all_to_all | solution.py:404
  110.3 9.8 %all_to_all.35.own_ref = bf16[16,2,1280]{2,1,0:T(2,128)(2,1)S(1)} all-to-all(bf16[16,2,1280]{2,1,0:T(2,128)(2,1)S(1)} %sum_spread.3), channel_id=1, replica_groups=mesh['rows'=4,'y'=4,'z'=4,'core'=2] {'y','z'}, dimensions={0} | all-to-all | bytes 163840 | tf_op jit(solution)/shard_map/all_to_all | solution.py:404
  120.2 2.9 %collective-permute-start.16 = (bf16[16,2,1280]{2,1,0:T(2,128)(2,1)S(1)}, bf16[16,2,1280]{2,1,0:T(2,128)(2,1)S(1)}, u32[]{:S(2)}, u32[]{:S(2)}) collective-permute-start(bf16[16,2,1280]{2,1,0:T(2,128)(2,1)S(1)} %all_to_all.35.own_ref), channel_id=1, source_target_pairs={{0,1},{1,0},{2,3},{3,2},{4,5},{5,4},{6,7},{7,6},{8,9},{9,8},{10,11... | collective-permute-start | bytes 245768 | tf_op jit(solution)/shard_map/ppermute | solution.py:408
  (56 shorter events, 14.3 us)
Async XLA Ops:
  2.3 7.2 %collective-permute-start = (f32[16,384]{1,0:T(8,128)S(1)}, f32[16,384]{1,0:T(8,128)S(1)}, u32[]{:S(2)}, u32[]{:S(2)}) collective-permute-start(f32[16,384]{1,0:T(8,128)S(1)} %get-tuple-element.20), channel_id=1, source_target_pairs={{0,32},{32,64},{64,96},{96,0},{1,33},{33,65},{65,97},{97,1},{2,34}... | collective-permute-start | bytes 73736 | tf_op jit(solution)/shard_map/ppermute | solution.py:392
  4.4 5.1 %collective-permute-start.1 = (f32[16,384]{1,0:T(8,128)S(1)}, f32[16,384]{1,0:T(8,128)S(1)}, u32[]{:S(2)}, u32[]{:S(2)}) collective-permute-start(f32[16,384]{1,0:T(8,128)S(1)} %get-tuple-element.21), channel_id=1, source_target_pairs={{0,64},{32,96},{64,0},{96,32},{1,65},{33,97},{65,1},{97,33},{2,66}... | collective-permute-start | bytes 73736 | tf_op jit(solution)/shard_map/ppermute | solution.py:392
  6.8 3.0 %collective-permute-start.2 = (f32[16,384]{1,0:T(8,128)S(1)}, f32[16,384]{1,0:T(8,128)S(1)}, u32[]{:S(2)}, u32[]{:S(2)}) collective-permute-start(f32[16,384]{1,0:T(8,128)S(1)} %get-tuple-element.22), channel_id=1, source_target_pairs={{0,96},{32,0},{64,32},{96,64},{1,97},{33,1},{65,33},{97,65},{2,98}... | collective-permute-start | bytes 73736 | tf_op jit(solution)/shard_map/ppermute | solution.py:392
  9.8 19.5 %slice-start.3 = ((s8[8388608]{0:T(1024)(128)(4,1)}), s8[4194304]{0:T(1024)(128)(4,1)S(1)}, s32[]{:S(2)}) async-start(s8[8388608]{0:T(1024)(128)(4,1)} %bitcast.7), calls=%async_computation.9 | async-start | bytes 8388608
  9.8 19.5 %copy-start.6 = (s32[16]{0:T(128)S(1)}, s32[16]{0:T(128)}, u32[]{:S(2)}) copy-start(s32[16]{0:T(128)} %length_ref.3) | copy-start | bytes 196
  24.7 4.5 %collective-permute-start.3 = (bf16[16,40,128]{2,1,0:T(8,128)(2,1)S(1)}, bf16[16,40,128]{2,1,0:T(8,128)(2,1)S(1)}, u32[]{:S(2)}, u32[]{:S(2)}) collective-permute-start(bf16[16,40,128]{2,1,0:T(8,128)(2,1)S(1)} %all_to_all.30.own_ref), channel_id=1, source_target_pairs={{0,1},{1,0},{2,3},{3,2},{4,5},{5,4},{6,7},{7,6},{8,9},{9,8},{10,11... | collective-permute-start | bytes 491528 | tf_op jit(solution)/shard_map/ppermute | solution.py:408
  29.3 26.4 %copy-start.4 = (bf16[256,1280]{1,0:T(8,128)(2,1)S(1)}, bf16[256,1280]{1,0:T(8,128)(2,1)}, u32[]{:S(2)}) copy-start(bf16[256,1280]{1,0:T(8,128)(2,1)} %w_ref.2) | copy-start | bytes 1966084
  29.3 52.8 %copy-start.1 = (bf16[1280,800]{0,1:T(8,128)(2,1)S(1)}, bf16[1280,800]{0,1:T(8,128)(2,1)}, u32[]{:S(2)}) copy-start(bf16[1280,800]{0,1:T(8,128)(2,1)} %param.28) | copy-start | bytes 6144004
  34.6 47.6 %copy-start = (bf16[1280,800]{0,1:T(8,128)(2,1)S(1)}, bf16[1280,800]{0,1:T(8,128)(2,1)}, u32[]{:S(2)}) copy-start(bf16[1280,800]{0,1:T(8,128)(2,1)} %param.27) | copy-start | bytes 6144004
  34.6 47.5 %copy-start.3 = (bf16[64,1280]{1,0:T(8,128)(2,1)S(1)}, bf16[64,1280]{1,0:T(8,128)(2,1)}, u32[]{:S(2)}) copy-start(bf16[64,1280]{1,0:T(8,128)(2,1)} %hidden_ref.1) | copy-start | bytes 491524
  34.6 47.5 %copy-start.5 = (bf16[1280]{0:T(1024)(128)(2,1)S(1)}, bf16[1280]{0:T(1024)(128)(2,1)}, u32[]{:S(2)}) copy-start(bf16[1280]{0:T(1024)(128)(2,1)} %gain_ref.1) | copy-start | bytes 7684
  49.7 3.7 %collective-permute-start.6 = (bf16[16,256]{1,0:T(8,128)(2,1)S(1)}, bf16[16,256]{1,0:T(8,128)(2,1)S(1)}, u32[]{:S(2)}, u32[]{:S(2)}) collective-permute-start(bf16[16,256]{1,0:T(8,128)(2,1)S(1)} %get-tuple-element.25.a_ref), channel_id=1, source_target_pairs={{96,0},{0,32},{32,64},{64,96},{97,1},{1,33},{33,65},{65,97},{98,2}... | collective-permute-start | bytes 24584 | tf_op jit(solution)/shard_map/ppermute | solution.py:399
  49.7 4.7 %collective-permute-start.5 = (bf16[16,256]{1,0:T(8,128)(2,1)S(1)}, bf16[16,256]{1,0:T(8,128)(2,1)S(1)}, u32[]{:S(2)}, u32[]{:S(2)}) collective-permute-start(bf16[16,256]{1,0:T(8,128)(2,1)S(1)} %get-tuple-element.25.a_ref), channel_id=1, source_target_pairs={{64,0},{96,32},{0,64},{32,96},{65,1},{97,33},{1,65},{33,97},{66,2}... | collective-permute-start | bytes 24584 | tf_op jit(solution)/shard_map/ppermute | solution.py:399
  53.2 2.5 %collective-permute-start.4 = (bf16[16,256]{1,0:T(8,128)(2,1)S(1)}, bf16[16,256]{1,0:T(8,128)(2,1)S(1)}, u32[]{:S(2)}, u32[]{:S(2)}) collective-permute-start(bf16[16,256]{1,0:T(8,128)(2,1)S(1)} %get-tuple-element.25.a_ref), channel_id=1, source_target_pairs={{32,0},{64,32},{96,64},{0,96},{33,1},{65,33},{97,65},{1,97},{34,2}... | collective-permute-start | bytes 24584 | tf_op jit(solution)/shard_map/ppermute | solution.py:399
  56.0 2.7 %collective-permute-start.7 = (bf16[32,1280]{1,0:T(8,128)(2,1)S(1)}, bf16[32,1280]{1,0:T(8,128)(2,1)S(1)}, u32[]{:S(2)}, u32[]{:S(2)}) collective-permute-start(bf16[32,1280]{1,0:T(8,128)(2,1)S(1)} %get-tuple-element.27), channel_id=1, source_target_pairs={{0,1},{1,0},{2,3},{3,2},{4,5},{5,4},{6,7},{7,6},{8,9},{9,8},{10,11... | collective-permute-start | bytes 245768 | tf_op jit(solution)/shard_map/ppermute | solution.py:408
  78.3 3.8 %collective-permute-start.8 = (bf16[16,2,1280]{2,1,0:T(2,128)(2,1)S(1)}, bf16[16,2,1280]{2,1,0:T(2,128)(2,1)S(1)}, u32[]{:S(2)}, u32[]{:S(2)}) collective-permute-start(bf16[16,2,1280]{2,1,0:T(2,128)(2,1)S(1)} %all_to_all.33.own_ref), channel_id=1, source_target_pairs={{0,1},{1,0},{2,3},{3,2},{4,5},{5,4},{6,7},{7,6},{8,9},{9,8},{10,11... | collective-permute-start | bytes 245768 | tf_op jit(solution)/shard_map/ppermute | solution.py:408
  83.5 4.9 %collective-permute-start.9 = (bf16[16,1792]{1,0:T(8,128)(2,1)S(1)}, bf16[16,1792]{1,0:T(8,128)(2,1)S(1)}, u32[]{:S(2)}, u32[]{:S(2)}) collective-permute-start(bf16[16,1792]{1,0:T(8,128)(2,1)S(1)} %get-tuple-element.30), channel_id=1, source_target_pairs={{0,32},{32,64},{64,96},{96,0},{1,33},{33,65},{65,97},{97,1},{2,34}... | collective-permute-start | bytes 172040 | tf_op jit(solution)/shard_map/ppermute | solution.py:392
  83.6 5.5 %collective-permute-start.10 = (bf16[16,1792]{1,0:T(8,128)(2,1)S(1)}, bf16[16,1792]{1,0:T(8,128)(2,1)S(1)}, u32[]{:S(2)}, u32[]{:S(2)}) collective-permute-start(bf16[16,1792]{1,0:T(8,128)(2,1)S(1)} %get-tuple-element.31), channel_id=1, source_target_pairs={{0,64},{32,96},{64,0},{96,32},{1,65},{33,97},{65,1},{97,33},{2,66}... | collective-permute-start | bytes 172040 | tf_op jit(solution)/shard_map/ppermute | solution.py:392
  85.7 3.7 %collective-permute-start.11 = (bf16[16,1792]{1,0:T(8,128)(2,1)S(1)}, bf16[16,1792]{1,0:T(8,128)(2,1)S(1)}, u32[]{:S(2)}, u32[]{:S(2)}) collective-permute-start(bf16[16,1792]{1,0:T(8,128)(2,1)S(1)} %get-tuple-element.32), channel_id=1, source_target_pairs={{0,96},{32,0},{64,32},{96,64},{1,97},{33,1},{65,33},{97,65},{2,98}... | collective-permute-start | bytes 172040 | tf_op jit(solution)/shard_map/ppermute | solution.py:392
  89.6 4.0 %collective-permute-start.14 = (bf16[16,896]{1,0:T(8,128)(2,1)S(1)}, bf16[16,896]{1,0:T(8,128)(2,1)S(1)}, u32[]{:S(2)}, u32[]{:S(2)}) collective-permute-start(bf16[16,896]{1,0:T(8,128)(2,1)S(1)} %activate.1.a_ref), channel_id=1, source_target_pairs={{96,0},{0,32},{32,64},{64,96},{97,1},{1,33},{33,65},{65,97},{98,2}... | collective-permute-start | bytes 86024 | tf_op jit(solution)/shard_map/ppermute | solution.py:399
  90.8 4.2 %collective-permute-start.13 = (bf16[16,896]{1,0:T(8,128)(2,1)S(1)}, bf16[16,896]{1,0:T(8,128)(2,1)S(1)}, u32[]{:S(2)}, u32[]{:S(2)}) collective-permute-start(bf16[16,896]{1,0:T(8,128)(2,1)S(1)} %activate.1.a_ref), channel_id=1, source_target_pairs={{64,0},{96,32},{0,64},{32,96},{65,1},{97,33},{1,65},{33,97},{66,2}... | collective-permute-start | bytes 86024 | tf_op jit(solution)/shard_map/ppermute | solution.py:399
  93.2 2.7 %collective-permute-start.12 = (bf16[16,896]{1,0:T(8,128)(2,1)S(1)}, bf16[16,896]{1,0:T(8,128)(2,1)S(1)}, u32[]{:S(2)}, u32[]{:S(2)}) collective-permute-start(bf16[16,896]{1,0:T(8,128)(2,1)S(1)} %activate.1.a_ref), channel_id=1, source_target_pairs={{32,0},{64,32},{96,64},{0,96},{33,1},{65,33},{97,65},{1,97},{34,2}... | collective-permute-start | bytes 86024 | tf_op jit(solution)/shard_map/ppermute | solution.py:399
  96.4 4.2 %collective-permute-start.15 = (bf16[32,1280]{1,0:T(8,128)(2,1)S(1)}, bf16[32,1280]{1,0:T(8,128)(2,1)S(1)}, u32[]{:S(2)}, u32[]{:S(2)}) collective-permute-start(bf16[32,1280]{1,0:T(8,128)(2,1)S(1)} %get-tuple-element.34), channel_id=1, source_target_pairs={{0,1},{1,0},{2,3},{3,2},{4,5},{5,4},{6,7},{7,6},{8,9},{9,8},{10,11... | collective-permute-start | bytes 245768 | tf_op jit(solution)/shard_map/ppermute | solution.py:408
  120.2 3.8 %collective-permute-start.16 = (bf16[16,2,1280]{2,1,0:T(2,128)(2,1)S(1)}, bf16[16,2,1280]{2,1,0:T(2,128)(2,1)S(1)}, u32[]{:S(2)}, u32[]{:S(2)}) collective-permute-start(bf16[16,2,1280]{2,1,0:T(2,128)(2,1)S(1)} %all_to_all.35.own_ref), channel_id=1, source_target_pairs={{0,1},{1,0},{2,3},{3,2},{4,5},{5,4},{6,7},{7,6},{8,9},{9,8},{10,11... | collective-permute-start | bytes 245768 | tf_op jit(solution)/shard_map/ppermute | solution.py:408
  (5 other events, 91.7 us)

commit v8 on v7

--- a/solution.py
+++ b/solution.py
@@ -323,22 +323,18 @@
         ref[...] = whole[pl.ds(pl.multiple_of(core * half, half), half), :].astype(ref.dtype)
 
 
-def chip_sum_kernel(keep_ref, got_ref, out_ref):
-    total = (keep_ref[...] + got_ref[...].astype(f32)).astype(bf16)
-    for chip in range(CHIPS):
-        out_ref[chip] = total[2 * chip : 2 * chip + 2]
-
-
-def sum_spread_kernel(got_ref, out_ref):
-    total = jnp.sum(got_ref[...].astype(f32), axis=0).astype(bf16)
-    out_ref[...] = jnp.broadcast_to(total[None], out_ref.shape)
+def add_kernel(*refs):
+    out_ref = refs[-1]
+    parts = [ref[...].astype(f32) for ref in refs[:-1]]
+    if len(parts) == ROWS:
+        parts = [parts[0] + parts[2], parts[1] + parts[3]]
+    out_ref[...] = (parts[0] + parts[1]).astype(bf16)
 
 
 def row_blocks(place_ref, own_ref, other_ref):
     for ref, core in of_cores(place_ref, own_ref, other_ref):
         for at in range(2):
-            block = ref[at * 8 : (at + 1) * 8].astype(f32)
-            yield 2 * core + at, block.reshape(OWN, block.shape[-1])
+            yield 2 * core + at, ref[at * OWN : (at + 1) * OWN, :].astype(f32)
 
 
 def gate_up_kernel(
@@ -393,10 +389,10 @@
     return got
 
 
-def from_rows(own):
+def from_peers(own, axis):
     got = [own] * ROWS
     for k in (2, 1, 3):
-        got[k] = lax.ppermute(own, "rows", [((i + k) % ROWS, i) for i in range(ROWS)])
+        got[k] = lax.ppermute(own, axis, [((i + k) % ROWS, i) for i in range(ROWS)])
     return got
 
 
@@ -409,14 +405,13 @@
 
 
 def sum_wide(keep, send):
-    blocks = jax.ShapeDtypeStruct((CHIPS, 2, send.shape[1]), bf16)
-    part = call(chip_sum_kernel, blocks, [VMEM] * 2, limit=4, name="chip_sum")(
-        keep, from_other_core(send)
-    )
-    total = call(sum_spread_kernel, blocks, [VMEM], limit=4, name="sum_spread")(
-        exchange(part, CHIP_AXES)
-    )
-    own = exchange(total, CHIP_AXES)
+    def add(*parts):
+        shape = jax.ShapeDtypeStruct(send.shape, bf16)
+        return call(add_kernel, shape, [VMEM] * len(parts), limit=4, name="add")(*parts)
+
+    own = add(keep, from_other_core(send))
+    own = add(*from_peers(own, "y"))
+    own = add(*from_peers(own, "z"))
     return own, from_other_core(own)
 
 
@@ -500,7 +495,7 @@
             [pltpu.VMEM((64, 1280), f32)],
             limit=8,
             name=name,
-        )(place, *from_rows(own), weight)
+        )(place, *from_peers(own, "rows"), weight)
 
     attended = sum_wide(*product(heads_own, w_out, "output"))
     stream, *blocks = call(

time: 125 us -> 114 us (0.912)
  blocking collectives: 67.1 us -> 28.3 us
  waiting for transfers between devices: 12.8 us -> 27.5 us
  starting transfers between devices: 30.7 us -> 44.1 us
    all_to_all x6 -> x2, blocking collectives: 67.1 us -> 28.3 us  [exchange(): return lax.all_to_all(blocks, axes, split_axis=0, concat_axis=0, tiled=True)]
    ppermute x6 -> x18, waiting for transfers between devices: 5.18 us -> 19.9 us  [from_peers(): got[k] = lax.ppermute(own, axis, [((i + k) % ROWS, i) for i in range(ROWS)])]
    ppermute x6 -> x18, starting transfers between devices: 7.23 us -> 21.3 us  [from_peers(): got[k] = lax.ppermute(own, axis, [((i + k) % ROWS, i) for i in range(ROWS)])]
  transfers between devices with their start and end apart: 17 -> 29, of which waited for: 15 -> 25; matrix products, arithmetic and copies ran while one was open for 0% -> 0% of each run, Pallas kernels for 1% -> 1%
where the time goes in v8:
time: 114 us
  starting transfers between devices  44.1 us (39%)
  blocking collectives  28.3 us (25%)
  waiting for transfers between devices  27.5 us (24%)
  Pallas kernels  13.1 us (11%)
    all_to_all x2, blocking collectives, exchange(): return lax.all_to_all(blocks, axes, split_axis=0, concat_axis=0, tiled=True)  28.3 us
    ppermute x18, starting transfers between devices, from_peers(): got[k] = lax.ppermute(own, axis, [((i + k) % ROWS, i) for i in range(ROWS)])  21.3 us
    ppermute x18, waiting for transfers between devices, from_peers(): got[k] = lax.ppermute(own, axis, [((i + k) % ROWS, i) for i in range(ROWS)])  19.9 us
    ppermute x5, starting transfers between devices, from_other_core(): return lax.ppermute(value, 'core', [(0, 1), (1, 0)])  13.8 us
    ppermute x6, starting transfers between devices, to_rows(): lax.ppermute(blocks[k], 'rows', [(i, (i + k) % ROWS) for i in range(ROWS)])  9.08 us
    pallas_call x1, Pallas kernels, body(): call(attend_kernel, sds((WIDE, PACKED, 128), bf16), [SMEM] * 3 + [VMEM] *...  5.23 us
    ppermute x5, waiting for transfers between devices, from_other_core(): return lax.ppermute(value, 'core', [(0, 1), (1, 0)])  4.72 us
    ppermute x6, waiting for transfers between devices, to_rows(): lax.ppermute(blocks[k], 'rows', [(i, (i + k) % ROWS) for i in range(ROWS)])  2.84 us
  transfers between devices with their start and end apart: 29, of which 25 were waited for; matrix products, arithmetic and copies ran while one was open for 0% of the time, Pallas kernels for 1%

profile of v8, /device:TPU:1, one launch (start us, length us, event | category | flops | bytes accessed | tf_op | source)
XLA Modules:
  0.0 114.0 jit_solution(2475330857653732018)
XLA Ops:
  0.6 1.6 %project.1 = (f32[16,384]{1,0:T(8,128)S(1)}, f32[16,384]{1,0:T(8,128)S(1)}, f32[16,384]{1,0:T(8,128)S(1)}, f32[16,384]{1,0:T(8,128)S(1)}) custom-call(s32[1]{0:T(128)} %bitcast.place_ref, bf16[64,1280]{1,0:T(8,128)(2,1)} %hidden_ref.1, bf16[1280]{0:T(1024)(128)(2,1)} %gain_hbm.1, bf16[1280,256]{1,0:T(8,128)(2,1)} %wq_hbm.1, bf16[64,1280]{1,0:T(8,128)(2,1)} %bitcast.12), custom_call_target="tpu_custom_call" | custom-call | tf_op jit(solution)/shard_map/project/pallas_call | solution.py:438
  2.3 2.1 %collective-permute-start = (f32[16,384]{1,0:T(8,128)S(1)}, f32[16,384]{1,0:T(8,128)S(1)}, u32[]{:S(2)}, u32[]{:S(2)}) collective-permute-start(f32[16,384]{1,0:T(8,128)S(1)} %get-tuple-element.20), channel_id=1, source_target_pairs={{0,32},{32,64},{64,96},{96,0},{1,33},{33,65},{65,97},{97,1},{2,34}... | collective-permute-start | bytes 73736 | tf_op jit(solution)/shard_map/ppermute | solution.py:388
  4.4 2.5 %collective-permute-start.1 = (f32[16,384]{1,0:T(8,128)S(1)}, f32[16,384]{1,0:T(8,128)S(1)}, u32[]{:S(2)}, u32[]{:S(2)}) collective-permute-start(f32[16,384]{1,0:T(8,128)S(1)} %get-tuple-element.21), channel_id=1, source_target_pairs={{0,64},{32,96},{64,0},{96,32},{1,65},{33,97},{65,1},{97,33},{2,66}... | collective-permute-start | bytes 73736 | tf_op jit(solution)/shard_map/ppermute | solution.py:388
  8.0 1.5 %tables.1 = (f32[2,16,128]{2,1,0:T(8,128)S(1)}, f32[2,16,128]{2,1,0:T(8,128)S(1)}) custom-call(s32[16]{0:T(128)} %length_ref.3, bf16[128]{0:T(256)(128)(2,1)} %query_hbm.1, bf16[128]{0:T(256)(128)(2,1)} %key_hbm.1), custom_call_target="tpu_custom_call" | custom-call | tf_op jit(solution)/shard_map/tables/pallas_call | solution.py:453
  10.1 14.6 %all_to_all.10.own_ref = bf16[16,40,128]{2,1,0:T(8,128)(2,1)S(1)} all-to-all(bf16[16,40,128]{2,1,0:T(8,128)(2,1)S(1)} %heads.1), channel_id=1, replica_groups=mesh['rows'=4,'y'=4,'z'=4,'core'=2] {'y','z'}, dimensions={0} | all-to-all | bytes 327680 | tf_op jit(solution)/shard_map/all_to_all | solution.py:400
  24.7 3.5 %collective-permute-start.3 = (bf16[16,40,128]{2,1,0:T(8,128)(2,1)S(1)}, bf16[16,40,128]{2,1,0:T(8,128)(2,1)S(1)}, u32[]{:S(2)}, u32[]{:S(2)}) collective-permute-start(bf16[16,40,128]{2,1,0:T(8,128)(2,1)S(1)} %all_to_all.10.own_ref), channel_id=1, source_target_pairs={{0,1},{1,0},{2,3},{3,2},{4,5},{5,4},{6,7},{7,6},{8,9},{9,8},{10,11... | collective-permute-start | bytes 491528 | tf_op jit(solution)/shard_map/ppermute | solution.py:404
  29.3 5.2 %attend.1 = bf16[32,40,128]{2,1,0:T(8,128)(2,1)S(1)} custom-call(s32[1]{0:T(128)} %bitcast.place_ref, s32[16]{0:T(128)S(1)} %copy-done.6, s32[16]{0:T(128)S(1)} %bitcast.11, bf16[16,40,128]{2,1,0:T(8,128)(2,1)S(1)} %all_to_all.10.own_ref, bf16[16,40,128]{2,1,0:T(8,128)(2,1)S(1)} %collective-permute-done.3.other_ref, bf16[16,256,1024]{2,1,0:T(8,128)(2,1)S(1)} %bitcast.6, ...), custom_call_target="tpu_custom_call" | custom-call | tf_op jit(solution)/shard_map/attend/pallas_call | solution.py:472
  34.6 13.7 %all_to_all.11.r_ref = bf16[32,40,128]{2,1,0:T(8,128)(2,1)S(1)} all-to-all(bf16[32,40,128]{2,1,0:T(8,128)(2,1)S(1)} %attend.1), channel_id=1, replica_groups=mesh['rows'=4,'y'=4,'z'=4,'core'=2] {'y','z','core'}, dimensions={0} | all-to-all | bytes 655360 | tf_op jit(solution)/shard_map/all_to_all | solution.py:400
  49.7 3.5 %collective-permute-start.5 = (bf16[16,256]{1,0:T(8,128)(2,1)S(1)}, bf16[16,256]{1,0:T(8,128)(2,1)S(1)}, u32[]{:S(2)}, u32[]{:S(2)}) collective-permute-start(bf16[16,256]{1,0:T(8,128)(2,1)S(1)} %get-tuple-element.25.a_ref), channel_id=1, source_target_pairs={{64,0},{96,32},{0,64},{32,96},{65,1},{97,33},{1,65},{33,97},{66,2}... | collective-permute-start | bytes 24584 | tf_op jit(solution)/shard_map/ppermute | solution.py:395
  56.0 1.8 %collective-permute-start.7 = (bf16[32,1280]{1,0:T(8,128)(2,1)S(1)}, bf16[32,1280]{1,0:T(8,128)(2,1)S(1)}, u32[]{:S(2)}, u32[]{:S(2)}) collective-permute-start(bf16[32,1280]{1,0:T(8,128)(2,1)S(1)} %get-tuple-element.27), channel_id=1, source_target_pairs={{0,1},{1,0},{2,3},{3,2},{4,5},{5,4},{6,7},{7,6},{8,9},{9,8},{10,11... | collective-permute-start | bytes 245768 | tf_op jit(solution)/shard_map/ppermute | solution.py:404
  59.1 1.8 %collective-permute-start.9 = (bf16[32,1280]{1,0:T(8,128)(2,1)S(1)}, bf16[32,1280]{1,0:T(8,128)(2,1)S(1)}, u32[]{:S(2)}, u32[]{:S(2)}) collective-permute-start(bf16[32,1280]{1,0:T(8,128)(2,1)S(1)} %add.18.refs_0_), channel_id=1, source_target_pairs={{16,0},{24,8},{0,16},{8,24},{17,1},{25,9},{1,17},{9,25},{18,2},{26... | collective-permute-start | bytes 245768 | tf_op jit(solution)/shard_map/ppermute | solution.py:395
  62.1 2.1 %collective-permute-done.10.refs_3_ = bf16[32,1280]{1,0:T(8,128)(2,1)S(1)} collective-permute-done((bf16[32,1280]{1,0:T(8,128)(2,1)S(1)}, bf16[32,1280]{1,0:T(8,128)(2,1)S(1)}, u32[]{:S(2)}, u32[]{:S(2)}) %collective-permute-start.10) | collective-permute-done | bytes 81952 | tf_op jit(solution)/shard_map/ppermute | solution.py:395
  65.9 2.0 %collective-permute-start.12 = (bf16[32,1280]{1,0:T(8,128)(2,1)S(1)}, bf16[32,1280]{1,0:T(8,128)(2,1)S(1)}, u32[]{:S(2)}, u32[]{:S(2)}) collective-permute-start(bf16[32,1280]{1,0:T(8,128)(2,1)S(1)} %add.19.refs_0_), channel_id=1, source_target_pairs={{4,0},{6,2},{0,4},{2,6},{5,1},{7,3},{1,5},{3,7},{12,8},{14,10},{8,... | collective-permute-start | bytes 245768 | tf_op jit(solution)/shard_map/ppermute | solution.py:395
  69.1 2.1 %collective-permute-done.13.refs_3_ = bf16[32,1280]{1,0:T(8,128)(2,1)S(1)} collective-permute-done((bf16[32,1280]{1,0:T(8,128)(2,1)S(1)}, bf16[32,1280]{1,0:T(8,128)(2,1)S(1)}, u32[]{:S(2)}, u32[]{:S(2)}) %collective-permute-start.13) | collective-permute-done | bytes 81952 | tf_op jit(solution)/shard_map/ppermute | solution.py:395
  72.1 2.7 %collective-permute-start.14 = (bf16[32,1280]{1,0:T(8,128)(2,1)S(1)}, bf16[32,1280]{1,0:T(8,128)(2,1)S(1)}, u32[]{:S(2)}, u32[]{:S(2)}) collective-permute-start(bf16[32,1280]{1,0:T(8,128)(2,1)S(1)} %add.20.own_ref), channel_id=1, source_target_pairs={{0,1},{1,0},{2,3},{3,2},{4,5},{5,4},{6,7},{7,6},{8,9},{9,8},{10,11... | collective-permute-start | bytes 245768 | tf_op jit(solution)/shard_map/ppermute | solution.py:404
  77.2 2.1 %collective-permute-start.16 = (bf16[16,1792]{1,0:T(8,128)(2,1)S(1)}, bf16[16,1792]{1,0:T(8,128)(2,1)S(1)}, u32[]{:S(2)}, u32[]{:S(2)}) collective-permute-start(bf16[16,1792]{1,0:T(8,128)(2,1)S(1)} %get-tuple-element.31), channel_id=1, source_target_pairs={{0,64},{32,96},{64,0},{96,32},{1,65},{33,97},{65,1},{97,33},{2,66}... | collective-permute-start | bytes 172040 | tf_op jit(solution)/shard_map/ppermute | solution.py:388
  80.5 1.5 %collective-permute-done.15.b_ref = bf16[16,1792]{1,0:T(8,128)(2,1)S(1)} collective-permute-done((bf16[16,1792]{1,0:T(8,128)(2,1)S(1)}, bf16[16,1792]{1,0:T(8,128)(2,1)S(1)}, u32[]{:S(2)}, u32[]{:S(2)}) %collective-permute-start.15) | collective-permute-done | bytes 57376 | tf_op jit(solution)/shard_map/ppermute | solution.py:388
  84.4 2.4 %collective-permute-start.19 = (bf16[16,896]{1,0:T(8,128)(2,1)S(1)}, bf16[16,896]{1,0:T(8,128)(2,1)S(1)}, u32[]{:S(2)}, u32[]{:S(2)}) collective-permute-start(bf16[16,896]{1,0:T(8,128)(2,1)S(1)} %activate.1.a_ref), channel_id=1, source_target_pairs={{64,0},{96,32},{0,64},{32,96},{65,1},{97,33},{1,65},{33,97},{66,2}... | collective-permute-start | bytes 86024 | tf_op jit(solution)/shard_map/ppermute | solution.py:395
  90.1 3.5 %collective-permute-start.21 = (bf16[32,1280]{1,0:T(8,128)(2,1)S(1)}, bf16[32,1280]{1,0:T(8,128)(2,1)S(1)}, u32[]{:S(2)}, u32[]{:S(2)}) collective-permute-start(bf16[32,1280]{1,0:T(8,128)(2,1)S(1)} %get-tuple-element.34), channel_id=1, source_target_pairs={{0,1},{1,0},{2,3},{3,2},{4,5},{5,4},{6,7},{7,6},{8,9},{9,8},{10,11... | collective-permute-start | bytes 245768 | tf_op jit(solution)/shard_map/ppermute | solution.py:404
  95.2 3.0 %collective-permute-start.23 = (bf16[32,1280]{1,0:T(8,128)(2,1)S(1)}, bf16[32,1280]{1,0:T(8,128)(2,1)S(1)}, u32[]{:S(2)}, u32[]{:S(2)}) collective-permute-start(bf16[32,1280]{1,0:T(8,128)(2,1)S(1)} %add.21.refs_0_), channel_id=1, source_target_pairs={{16,0},{24,8},{0,16},{8,24},{17,1},{25,9},{1,17},{9,25},{18,2},{26... | collective-permute-start | bytes 245768 | tf_op jit(solution)/shard_map/ppermute | solution.py:395
  99.4 2.7 %collective-permute-done.23.refs_2_ = bf16[32,1280]{1,0:T(8,128)(2,1)S(1)} collective-permute-done((bf16[32,1280]{1,0:T(8,128)(2,1)S(1)}, bf16[32,1280]{1,0:T(8,128)(2,1)S(1)}, u32[]{:S(2)}, u32[]{:S(2)}) %collective-permute-start.23) | collective-permute-done | bytes 81952 | tf_op jit(solution)/shard_map/ppermute | solution.py:395
  103.1 2.7 %collective-permute-start.26 = (bf16[32,1280]{1,0:T(8,128)(2,1)S(1)}, bf16[32,1280]{1,0:T(8,128)(2,1)S(1)}, u32[]{:S(2)}, u32[]{:S(2)}) collective-permute-start(bf16[32,1280]{1,0:T(8,128)(2,1)S(1)} %add.22.refs_0_), channel_id=1, source_target_pairs={{4,0},{6,2},{0,4},{2,6},{5,1},{7,3},{1,5},{3,7},{12,8},{14,10},{8,... | collective-permute-start | bytes 245768 | tf_op jit(solution)/shard_map/ppermute | solution.py:395
  106.8 1.9 %collective-permute-done.26.refs_2_ = bf16[32,1280]{1,0:T(8,128)(2,1)S(1)} collective-permute-done((bf16[32,1280]{1,0:T(8,128)(2,1)S(1)}, bf16[32,1280]{1,0:T(8,128)(2,1)S(1)}, u32[]{:S(2)}, u32[]{:S(2)}) %collective-permute-start.26) | collective-permute-done | bytes 81952 | tf_op jit(solution)/shard_map/ppermute | solution.py:395
  110.1 2.3 %collective-permute-start.28 = (bf16[32,1280]{1,0:T(8,128)(2,1)S(1)}, bf16[32,1280]{1,0:T(8,128)(2,1)S(1)}, u32[]{:S(2)}, u32[]{:S(2)}) collective-permute-start(bf16[32,1280]{1,0:T(8,128)(2,1)S(1)} %add.23.own_ref), channel_id=1, source_target_pairs={{0,1},{1,0},{2,3},{3,2},{4,5},{5,4},{6,7},{7,6},{8,9},{9,8},{10,11... | collective-permute-start | bytes 245768 | tf_op jit(solution)/shard_map/ppermute | solution.py:404
  (78 shorter events, 30.2 us)
Async XLA Ops:
  2.3 7.2 %collective-permute-start = (f32[16,384]{1,0:T(8,128)S(1)}, f32[16,384]{1,0:T(8,128)S(1)}, u32[]{:S(2)}, u32[]{:S(2)}) collective-permute-start(f32[16,384]{1,0:T(8,128)S(1)} %get-tuple-element.20), channel_id=1, source_target_pairs={{0,32},{32,64},{64,96},{96,0},{1,33},{33,65},{65,97},{97,1},{2,34}... | collective-permute-start | bytes 73736 | tf_op jit(solution)/shard_map/ppermute | solution.py:388
  4.4 5.1 %collective-permute-start.1 = (f32[16,384]{1,0:T(8,128)S(1)}, f32[16,384]{1,0:T(8,128)S(1)}, u32[]{:S(2)}, u32[]{:S(2)}) collective-permute-start(f32[16,384]{1,0:T(8,128)S(1)} %get-tuple-element.21), channel_id=1, source_target_pairs={{0,64},{32,96},{64,0},{96,32},{1,65},{33,97},{65,1},{97,33},{2,66}... | collective-permute-start | bytes 73736 | tf_op jit(solution)/shard_map/ppermute | solution.py:388
  24.7 4.5 %collective-permute-start.3 = (bf16[16,40,128]{2,1,0:T(8,128)(2,1)S(1)}, bf16[16,40,128]{2,1,0:T(8,128)(2,1)S(1)}, u32[]{:S(2)}, u32[]{:S(2)}) collective-permute-start(bf16[16,40,128]{2,1,0:T(8,128)(2,1)S(1)} %all_to_all.10.own_ref), channel_id=1, source_target_pairs={{0,1},{1,0},{2,3},{3,2},{4,5},{5,4},{6,7},{7,6},{8,9},{9,8},{10,11... | collective-permute-start | bytes 491528 | tf_op jit(solution)/shard_map/ppermute | solution.py:404
  49.7 3.7 %collective-permute-start.6 = (bf16[16,256]{1,0:T(8,128)(2,1)S(1)}, bf16[16,256]{1,0:T(8,128)(2,1)S(1)}, u32[]{:S(2)}, u32[]{:S(2)}) collective-permute-start(bf16[16,256]{1,0:T(8,128)(2,1)S(1)} %get-tuple-element.25.a_ref), channel_id=1, source_target_pairs={{96,0},{0,32},{32,64},{64,96},{97,1},{1,33},{33,65},{65,97},{98,2}... | collective-permute-start | bytes 24584 | tf_op jit(solution)/shard_map/ppermute | solution.py:395
  49.7 4.7 %collective-permute-start.5 = (bf16[16,256]{1,0:T(8,128)(2,1)S(1)}, bf16[16,256]{1,0:T(8,128)(2,1)S(1)}, u32[]{:S(2)}, u32[]{:S(2)}) collective-permute-start(bf16[16,256]{1,0:T(8,128)(2,1)S(1)} %get-tuple-element.25.a_ref), channel_id=1, source_target_pairs={{64,0},{96,32},{0,64},{32,96},{65,1},{97,33},{1,65},{33,97},{66,2}... | collective-permute-start | bytes 24584 | tf_op jit(solution)/shard_map/ppermute | solution.py:395
  58.7 5.5 %collective-permute-start.10 = (bf16[32,1280]{1,0:T(8,128)(2,1)S(1)}, bf16[32,1280]{1,0:T(8,128)(2,1)S(1)}, u32[]{:S(2)}, u32[]{:S(2)}) collective-permute-start(bf16[32,1280]{1,0:T(8,128)(2,1)S(1)} %add.18.refs_0_), channel_id=1, source_target_pairs={{24,0},{0,8},{8,16},{16,24},{25,1},{1,9},{9,17},{17,25},{26,2},{2,... | collective-permute-start | bytes 245768 | tf_op jit(solution)/shard_map/ppermute | solution.py:395
  59.1 6.0 %collective-permute-start.9 = (bf16[32,1280]{1,0:T(8,128)(2,1)S(1)}, bf16[32,1280]{1,0:T(8,128)(2,1)S(1)}, u32[]{:S(2)}, u32[]{:S(2)}) collective-permute-start(bf16[32,1280]{1,0:T(8,128)(2,1)S(1)} %add.18.refs_0_), channel_id=1, source_target_pairs={{16,0},{24,8},{0,16},{8,24},{17,1},{25,9},{1,17},{9,25},{18,2},{26... | collective-permute-start | bytes 245768 | tf_op jit(solution)/shard_map/ppermute | solution.py:395
  60.9 4.8 %collective-permute-start.8 = (bf16[32,1280]{1,0:T(8,128)(2,1)S(1)}, bf16[32,1280]{1,0:T(8,128)(2,1)S(1)}, u32[]{:S(2)}, u32[]{:S(2)}) collective-permute-start(bf16[32,1280]{1,0:T(8,128)(2,1)S(1)} %add.18.refs_0_), channel_id=1, source_target_pairs={{8,0},{16,8},{24,16},{0,24},{9,1},{17,9},{25,17},{1,25},{10,2},{18... | collective-permute-start | bytes 245768 | tf_op jit(solution)/shard_map/ppermute | solution.py:395
  65.7 5.4 %collective-permute-start.13 = (bf16[32,1280]{1,0:T(8,128)(2,1)S(1)}, bf16[32,1280]{1,0:T(8,128)(2,1)S(1)}, u32[]{:S(2)}, u32[]{:S(2)}) collective-permute-start(bf16[32,1280]{1,0:T(8,128)(2,1)S(1)} %add.19.refs_0_), channel_id=1, source_target_pairs={{6,0},{0,2},{2,4},{4,6},{7,1},{1,3},{3,5},{5,7},{14,8},{8,10},{10,... | collective-permute-start | bytes 245768 | tf_op jit(solution)/shard_map/ppermute | solution.py:395
  65.9 5.3 %collective-permute-start.12 = (bf16[32,1280]{1,0:T(8,128)(2,1)S(1)}, bf16[32,1280]{1,0:T(8,128)(2,1)S(1)}, u32[]{:S(2)}, u32[]{:S(2)}) collective-permute-start(bf16[32,1280]{1,0:T(8,128)(2,1)S(1)} %add.19.refs_0_), channel_id=1, source_target_pairs={{4,0},{6,2},{0,4},{2,6},{5,1},{7,3},{1,5},{3,7},{12,8},{14,10},{8,... | collective-permute-start | bytes 245768 | tf_op jit(solution)/shard_map/ppermute | solution.py:395
  67.9 4.2 %collective-permute-start.11 = (bf16[32,1280]{1,0:T(8,128)(2,1)S(1)}, bf16[32,1280]{1,0:T(8,128)(2,1)S(1)}, u32[]{:S(2)}, u32[]{:S(2)}) collective-permute-start(bf16[32,1280]{1,0:T(8,128)(2,1)S(1)} %add.19.refs_0_), channel_id=1, source_target_pairs={{2,0},{4,2},{6,4},{0,6},{3,1},{5,3},{7,5},{1,7},{10,8},{12,10},{14... | collective-permute-start | bytes 245768 | tf_op jit(solution)/shard_map/ppermute | solution.py:395
  72.1 3.6 %collective-permute-start.14 = (bf16[32,1280]{1,0:T(8,128)(2,1)S(1)}, bf16[32,1280]{1,0:T(8,128)(2,1)S(1)}, u32[]{:S(2)}, u32[]{:S(2)}) collective-permute-start(bf16[32,1280]{1,0:T(8,128)(2,1)S(1)} %add.20.own_ref), channel_id=1, source_target_pairs={{0,1},{1,0},{2,3},{3,2},{4,5},{5,4},{6,7},{7,6},{8,9},{9,8},{10,11... | collective-permute-start | bytes 245768 | tf_op jit(solution)/shard_map/ppermute | solution.py:404
  77.1 4.9 %collective-permute-start.15 = (bf16[16,1792]{1,0:T(8,128)(2,1)S(1)}, bf16[16,1792]{1,0:T(8,128)(2,1)S(1)}, u32[]{:S(2)}, u32[]{:S(2)}) collective-permute-start(bf16[16,1792]{1,0:T(8,128)(2,1)S(1)} %get-tuple-element.30), channel_id=1, source_target_pairs={{0,32},{32,64},{64,96},{96,0},{1,33},{33,65},{65,97},{97,1},{2,34}... | collective-permute-start | bytes 172040 | tf_op jit(solution)/shard_map/ppermute | solution.py:388
  77.2 5.5 %collective-permute-start.16 = (bf16[16,1792]{1,0:T(8,128)(2,1)S(1)}, bf16[16,1792]{1,0:T(8,128)(2,1)S(1)}, u32[]{:S(2)}, u32[]{:S(2)}) collective-permute-start(bf16[16,1792]{1,0:T(8,128)(2,1)S(1)} %get-tuple-element.31), channel_id=1, source_target_pairs={{0,64},{32,96},{64,0},{96,32},{1,65},{33,97},{65,1},{97,33},{2,66}... | collective-permute-start | bytes 172040 | tf_op jit(solution)/shard_map/ppermute | solution.py:388
  79.3 3.7 %collective-permute-start.17 = (bf16[16,1792]{1,0:T(8,128)(2,1)S(1)}, bf16[16,1792]{1,0:T(8,128)(2,1)S(1)}, u32[]{:S(2)}, u32[]{:S(2)}) collective-permute-start(bf16[16,1792]{1,0:T(8,128)(2,1)S(1)} %get-tuple-element.32), channel_id=1, source_target_pairs={{0,96},{32,0},{64,32},{96,64},{1,97},{33,1},{65,33},{97,65},{2,98}... | collective-permute-start | bytes 172040 | tf_op jit(solution)/shard_map/ppermute | solution.py:388
  83.2 4.0 %collective-permute-start.20 = (bf16[16,896]{1,0:T(8,128)(2,1)S(1)}, bf16[16,896]{1,0:T(8,128)(2,1)S(1)}, u32[]{:S(2)}, u32[]{:S(2)}) collective-permute-start(bf16[16,896]{1,0:T(8,128)(2,1)S(1)} %activate.1.a_ref), channel_id=1, source_target_pairs={{96,0},{0,32},{32,64},{64,96},{97,1},{1,33},{33,65},{65,97},{98,2}... | collective-permute-start | bytes 86024 | tf_op jit(solution)/shard_map/ppermute | solution.py:395
  84.4 4.2 %collective-permute-start.19 = (bf16[16,896]{1,0:T(8,128)(2,1)S(1)}, bf16[16,896]{1,0:T(8,128)(2,1)S(1)}, u32[]{:S(2)}, u32[]{:S(2)}) collective-permute-start(bf16[16,896]{1,0:T(8,128)(2,1)S(1)} %activate.1.a_ref), channel_id=1, source_target_pairs={{64,0},{96,32},{0,64},{32,96},{65,1},{97,33},{1,65},{33,97},{66,2}... | collective-permute-start | bytes 86024 | tf_op jit(solution)/shard_map/ppermute | solution.py:395
  90.1 4.4 %collective-permute-start.21 = (bf16[32,1280]{1,0:T(8,128)(2,1)S(1)}, bf16[32,1280]{1,0:T(8,128)(2,1)S(1)}, u32[]{:S(2)}, u32[]{:S(2)}) collective-permute-start(bf16[32,1280]{1,0:T(8,128)(2,1)S(1)} %get-tuple-element.34), channel_id=1, source_target_pairs={{0,1},{1,0},{2,3},{3,2},{4,5},{5,4},{6,7},{7,6},{8,9},{9,8},{10,11... | collective-permute-start | bytes 245768 | tf_op jit(solution)/shard_map/ppermute | solution.py:404
  94.5 5.0 %collective-permute-start.24 = (bf16[32,1280]{1,0:T(8,128)(2,1)S(1)}, bf16[32,1280]{1,0:T(8,128)(2,1)S(1)}, u32[]{:S(2)}, u32[]{:S(2)}) collective-permute-start(bf16[32,1280]{1,0:T(8,128)(2,1)S(1)} %add.21.refs_0_), channel_id=1, source_target_pairs={{24,0},{0,8},{8,16},{16,24},{25,1},{1,9},{9,17},{17,25},{26,2},{2,... | collective-permute-start | bytes 245768 | tf_op jit(solution)/shard_map/ppermute | solution.py:395
  95.2 6.9 %collective-permute-start.23 = (bf16[32,1280]{1,0:T(8,128)(2,1)S(1)}, bf16[32,1280]{1,0:T(8,128)(2,1)S(1)}, u32[]{:S(2)}, u32[]{:S(2)}) collective-permute-start(bf16[32,1280]{1,0:T(8,128)(2,1)S(1)} %add.21.refs_0_), channel_id=1, source_target_pairs={{16,0},{24,8},{0,16},{8,24},{17,1},{25,9},{1,17},{9,25},{18,2},{26... | collective-permute-start | bytes 245768 | tf_op jit(solution)/shard_map/ppermute | solution.py:395
  98.2 4.0 %collective-permute-start.22 = (bf16[32,1280]{1,0:T(8,128)(2,1)S(1)}, bf16[32,1280]{1,0:T(8,128)(2,1)S(1)}, u32[]{:S(2)}, u32[]{:S(2)}) collective-permute-start(bf16[32,1280]{1,0:T(8,128)(2,1)S(1)} %add.21.refs_0_), channel_id=1, source_target_pairs={{8,0},{16,8},{24,16},{0,24},{9,1},{17,9},{25,17},{1,25},{10,2},{18... | collective-permute-start | bytes 245768 | tf_op jit(solution)/shard_map/ppermute | solution.py:395
  102.2 4.6 %collective-permute-start.27 = (bf16[32,1280]{1,0:T(8,128)(2,1)S(1)}, bf16[32,1280]{1,0:T(8,128)(2,1)S(1)}, u32[]{:S(2)}, u32[]{:S(2)}) collective-permute-start(bf16[32,1280]{1,0:T(8,128)(2,1)S(1)} %add.22.refs_0_), channel_id=1, source_target_pairs={{6,0},{0,2},{2,4},{4,6},{7,1},{1,3},{3,5},{5,7},{14,8},{8,10},{10,... | collective-permute-start | bytes 245768 | tf_op jit(solution)/shard_map/ppermute | solution.py:395
  103.1 5.5 %collective-permute-start.26 = (bf16[32,1280]{1,0:T(8,128)(2,1)S(1)}, bf16[32,1280]{1,0:T(8,128)(2,1)S(1)}, u32[]{:S(2)}, u32[]{:S(2)}) collective-permute-start(bf16[32,1280]{1,0:T(8,128)(2,1)S(1)} %add.22.refs_0_), channel_id=1, source_target_pairs={{4,0},{6,2},{0,4},{2,6},{5,1},{7,3},{1,5},{3,7},{12,8},{14,10},{8,... | collective-permute-start | bytes 245768 | tf_op jit(solution)/shard_map/ppermute | solution.py:395
  105.8 4.2 %collective-permute-start.25 = (bf16[32,1280]{1,0:T(8,128)(2,1)S(1)}, bf16[32,1280]{1,0:T(8,128)(2,1)S(1)}, u32[]{:S(2)}, u32[]{:S(2)}) collective-permute-start(bf16[32,1280]{1,0:T(8,128)(2,1)S(1)} %add.22.refs_0_), channel_id=1, source_target_pairs={{2,0},{4,2},{6,4},{0,6},{3,1},{5,3},{7,5},{1,7},{10,8},{12,10},{14... | collective-permute-start | bytes 245768 | tf_op jit(solution)/shard_map/ppermute | solution.py:395
  (17 other events, 341.1 us)

commit v9 on v8

--- a/solution.py
+++ b/solution.py
@@ -315,7 +315,7 @@
         again_ref[:, lanes] = heads
 
 
-def product_kernel(place_ref, a_ref, b_ref, c_ref, d_ref, w_ref, keep_ref, send_ref, whole):
+def product_kernel(place_ref, a_ref, b_ref, d_ref, c_ref, w_ref, keep_ref, send_ref, whole):
     left = jnp.concatenate([a_ref[...], b_ref[...], c_ref[...], d_ref[...]], axis=0)
     whole[...] = jnp.dot(left[:, : w_ref.shape[0]], w_ref[...], preferred_element_type=f32)
     half = keep_ref.shape[0]
@@ -327,7 +327,7 @@
     out_ref = refs[-1]
     parts = [ref[...].astype(f32) for ref in refs[:-1]]
     if len(parts) == ROWS:
-        parts = [parts[0] + parts[2], parts[1] + parts[3]]
+        parts = [parts[0] + parts[3], parts[1] + parts[2]]
     out_ref[...] = (parts[0] + parts[1]).astype(bf16)
 
 
@@ -383,17 +383,16 @@
 
 
 def to_rows(blocks):
-    got = list(blocks)
-    for k in (2, 1, 3):
-        got[k] = lax.ppermute(blocks[k], "rows", [(i, (i + k) % ROWS) for i in range(ROWS)])
-    return got
+    return [blocks[0]] + [
+        lax.ppermute(blocks[k], "rows", [(i, (i + k) % ROWS) for i in range(ROWS)])
+        for k in (2, 1, 3)
+    ]
 
 
 def from_peers(own, axis):
-    got = [own] * ROWS
-    for k in (2, 1, 3):
-        got[k] = lax.ppermute(own, axis, [((i + k) % ROWS, i) for i in range(ROWS)])
-    return got
+    return [own] + [
+        lax.ppermute(own, axis, [((i + k) % ROWS, i) for i in range(ROWS)]) for k in (1, 3, 2)
+    ]
 
 
 def exchange(blocks, axes):

time: 114 us -> 112 us (0.982)
  waiting for transfers between devices: 27.5 us -> 25.1 us
    ppermute x18, waiting for transfers between devices: 19.9 us -> 17.1 us  [from_peers(): lax.ppermute(own, axis, [((i + k) % ROWS, i) for i in range(ROWS)])]
    ppermute x5, starting transfers between devices: 13.8 us -> 11.6 us  [from_other_core(): return lax.ppermute(value, 'core', [(0, 1), (1, 0)])]
    ppermute x18, starting transfers between devices: 21.3 us -> 22.9 us  [from_peers(): lax.ppermute(own, axis, [((i + k) % ROWS, i) for i in range(ROWS)])]
  transfers between devices with their start and end apart: 29 -> 29, of which waited for: 25 -> 21; matrix products, arithmetic and copies ran while one was open for 0% -> 0% of each run, Pallas kernels for 1% -> 1%
where the time goes in v9:
time: 112 us
  starting transfers between devices  44 us (39%)
  blocking collectives  28.4 us (25%)
  waiting for transfers between devices  25.1 us (22%)
  Pallas kernels  13.1 us (12%)
    all_to_all x2, blocking collectives, exchange(): return lax.all_to_all(blocks, axes, split_axis=0, concat_axis=0, tiled=True)  28.4 us
    ppermute x18, starting transfers between devices, from_peers(): lax.ppermute(own, axis, [((i + k) % ROWS, i) for i in range(ROWS)])  22.9 us
    ppermute x18, waiting for transfers between devices, from_peers(): lax.ppermute(own, axis, [((i + k) % ROWS, i) for i in range(ROWS)])  17.1 us
    ppermute x5, starting transfers between devices, from_other_core(): return lax.ppermute(value, 'core', [(0, 1), (1, 0)])  11.6 us
    ppermute x6, starting transfers between devices, to_rows(): lax.ppermute(blocks[k], 'rows', [(i, (i + k) % ROWS) for i in range(ROWS)])  9.42 us
    pallas_call x1, Pallas kernels, body(): call(attend_kernel, sds((WIDE, PACKED, 128), bf16), [SMEM] * 3 + [VMEM] *...  5.23 us
    ppermute x5, waiting for transfers between devices, from_other_core(): return lax.ppermute(value, 'core', [(0, 1), (1, 0)])  4.72 us
    ppermute x6, waiting for transfers between devices, to_rows(): lax.ppermute(blocks[k], 'rows', [(i, (i + k) % ROWS) for i in range(ROWS)])  3.31 us
  transfers between devices with their start and end apart: 29, of which 21 were waited for; matrix products, arithmetic and copies ran while one was open for 0% of the time, Pallas kernels for 1%

profile of v9, /device:TPU:1, one launch (start us, length us, event | category | flops | bytes accessed | tf_op | source)
XLA Modules:
  0.0 111.6 jit_solution(16698942010508055525)
XLA Ops:
  0.6 1.6 %project.1 = (f32[16,384]{1,0:T(8,128)S(1)}, f32[16,384]{1,0:T(8,128)S(1)}, f32[16,384]{1,0:T(8,128)S(1)}, f32[16,384]{1,0:T(8,128)S(1)}) custom-call(s32[1]{0:T(128)} %bitcast.place_ref, bf16[64,1280]{1,0:T(8,128)(2,1)} %hidden_ref.1, bf16[1280]{0:T(1024)(128)(2,1)} %gain_hbm.1, bf16[1280,256]{1,0:T(8,128)(2,1)} %wq_hbm.1, bf16[64,1280]{1,0:T(8,128)(2,1)} %bitcast.12), custom_call_target="tpu_custom_call" | custom-call | tf_op jit(solution)/shard_map/project/pallas_call | solution.py:437
  2.3 3.7 %collective-permute-start = (f32[16,384]{1,0:T(8,128)S(1)}, f32[16,384]{1,0:T(8,128)S(1)}, u32[]{:S(2)}, u32[]{:S(2)}) collective-permute-start(f32[16,384]{1,0:T(8,128)S(1)} %get-tuple-element.20), channel_id=1, source_target_pairs={{0,64},{32,96},{64,0},{96,32},{1,65},{33,97},{65,1},{97,33},{2,66}... | collective-permute-start | bytes 73736 | tf_op jit(solution)/shard_map/ppermute | solution.py:387
  6.2 2.4 %collective-permute-start.2 = (f32[16,384]{1,0:T(8,128)S(1)}, f32[16,384]{1,0:T(8,128)S(1)}, u32[]{:S(2)}, u32[]{:S(2)}) collective-permute-start(f32[16,384]{1,0:T(8,128)S(1)} %get-tuple-element.22), channel_id=1, source_target_pairs={{0,96},{32,0},{64,32},{96,64},{1,97},{33,1},{65,33},{97,65},{2,98}... | collective-permute-start | bytes 73736 | tf_op jit(solution)/shard_map/ppermute | solution.py:387
  10.4 14.7 %all_to_all.10.own_ref = bf16[16,40,128]{2,1,0:T(8,128)(2,1)S(1)} all-to-all(bf16[16,40,128]{2,1,0:T(8,128)(2,1)S(1)} %heads.1), channel_id=1, replica_groups=mesh['rows'=4,'y'=4,'z'=4,'core'=2] {'y','z'}, dimensions={0} | all-to-all | bytes 327680 | tf_op jit(solution)/shard_map/all_to_all | solution.py:399
  25.2 3.1 %collective-permute-start.3 = (bf16[16,40,128]{2,1,0:T(8,128)(2,1)S(1)}, bf16[16,40,128]{2,1,0:T(8,128)(2,1)S(1)}, u32[]{:S(2)}, u32[]{:S(2)}) collective-permute-start(bf16[16,40,128]{2,1,0:T(8,128)(2,1)S(1)} %all_to_all.10.own_ref), channel_id=1, source_target_pairs={{0,1},{1,0},{2,3},{3,2},{4,5},{5,4},{6,7},{7,6},{8,9},{9,8},{10,11... | collective-permute-start | bytes 491528 | tf_op jit(solution)/shard_map/ppermute | solution.py:403
  29.4 5.2 %attend.1 = bf16[32,40,128]{2,1,0:T(8,128)(2,1)S(1)} custom-call(s32[1]{0:T(128)} %bitcast.place_ref, s32[16]{0:T(128)S(1)} %copy-done.6, s32[16]{0:T(128)S(1)} %bitcast.11, bf16[16,40,128]{2,1,0:T(8,128)(2,1)S(1)} %all_to_all.10.own_ref, bf16[16,40,128]{2,1,0:T(8,128)(2,1)S(1)} %collective-permute-done.3.other_ref, bf16[16,256,1024]{2,1,0:T(8,128)(2,1)S(1)} %bitcast.6, ...), custom_call_target="tpu_custom_call" | custom-call | tf_op jit(solution)/shard_map/attend/pallas_call | solution.py:471
  34.6 13.7 %all_to_all.11.r_ref = bf16[32,40,128]{2,1,0:T(8,128)(2,1)S(1)} all-to-all(bf16[32,40,128]{2,1,0:T(8,128)(2,1)S(1)} %attend.1), channel_id=1, replica_groups=mesh['rows'=4,'y'=4,'z'=4,'core'=2] {'y','z','core'}, dimensions={0} | all-to-all | bytes 655360 | tf_op jit(solution)/shard_map/all_to_all | solution.py:399
  50.9 2.3 %collective-permute-start.5 = (bf16[16,256]{1,0:T(8,128)(2,1)S(1)}, bf16[16,256]{1,0:T(8,128)(2,1)S(1)}, u32[]{:S(2)}, u32[]{:S(2)}) collective-permute-start(bf16[16,256]{1,0:T(8,128)(2,1)S(1)} %get-tuple-element.25.a_ref), channel_id=1, source_target_pairs={{96,0},{0,32},{32,64},{64,96},{97,1},{1,33},{33,65},{65,97},{98,2}... | collective-permute-start | bytes 24584 | tf_op jit(solution)/shard_map/ppermute | solution.py:394
  56.0 1.8 %collective-permute-start.7 = (bf16[32,1280]{1,0:T(8,128)(2,1)S(1)}, bf16[32,1280]{1,0:T(8,128)(2,1)S(1)}, u32[]{:S(2)}, u32[]{:S(2)}) collective-permute-start(bf16[32,1280]{1,0:T(8,128)(2,1)S(1)} %get-tuple-element.27), channel_id=1, source_target_pairs={{0,1},{1,0},{2,3},{3,2},{4,5},{5,4},{6,7},{7,6},{8,9},{9,8},{10,11... | collective-permute-start | bytes 245768 | tf_op jit(solution)/shard_map/ppermute | solution.py:403
  60.3 2.4 %collective-permute-start.8 = (bf16[32,1280]{1,0:T(8,128)(2,1)S(1)}, bf16[32,1280]{1,0:T(8,128)(2,1)S(1)}, u32[]{:S(2)}, u32[]{:S(2)}) collective-permute-start(bf16[32,1280]{1,0:T(8,128)(2,1)S(1)} %add.18.refs_0_), channel_id=1, source_target_pairs={{8,0},{16,8},{24,16},{0,24},{9,1},{17,9},{25,17},{1,25},{10,2},{18... | collective-permute-start | bytes 245768 | tf_op jit(solution)/shard_map/ppermute | solution.py:394
  64.0 2.0 %collective-permute-done.9.refs_2_ = bf16[32,1280]{1,0:T(8,128)(2,1)S(1)} collective-permute-done((bf16[32,1280]{1,0:T(8,128)(2,1)S(1)}, bf16[32,1280]{1,0:T(8,128)(2,1)S(1)}, u32[]{:S(2)}, u32[]{:S(2)}) %collective-permute-start.9) | collective-permute-done | bytes 81952 | tf_op jit(solution)/shard_map/ppermute | solution.py:394
  67.6 2.6 %collective-permute-start.11 = (bf16[32,1280]{1,0:T(8,128)(2,1)S(1)}, bf16[32,1280]{1,0:T(8,128)(2,1)S(1)}, u32[]{:S(2)}, u32[]{:S(2)}) collective-permute-start(bf16[32,1280]{1,0:T(8,128)(2,1)S(1)} %add.19.refs_0_), channel_id=1, source_target_pairs={{2,0},{4,2},{6,4},{0,6},{3,1},{5,3},{7,5},{1,7},{10,8},{12,10},{14... | collective-permute-start | bytes 245768 | tf_op jit(solution)/shard_map/ppermute | solution.py:394
  70.9 2.3 %collective-permute-done.12.refs_2_ = bf16[32,1280]{1,0:T(8,128)(2,1)S(1)} collective-permute-done((bf16[32,1280]{1,0:T(8,128)(2,1)S(1)}, bf16[32,1280]{1,0:T(8,128)(2,1)S(1)}, u32[]{:S(2)}, u32[]{:S(2)}) %collective-permute-start.12) | collective-permute-done | bytes 81952 | tf_op jit(solution)/shard_map/ppermute | solution.py:394
  77.3 1.8 %collective-permute-start.16 = (bf16[16,1792]{1,0:T(8,128)(2,1)S(1)}, bf16[16,1792]{1,0:T(8,128)(2,1)S(1)}, u32[]{:S(2)}, u32[]{:S(2)}) collective-permute-start(bf16[16,1792]{1,0:T(8,128)(2,1)S(1)} %get-tuple-element.31), channel_id=1, source_target_pairs={{0,32},{32,64},{64,96},{96,0},{1,33},{33,65},{65,97},{97,1},{2,34}... | collective-permute-start | bytes 172040 | tf_op jit(solution)/shard_map/ppermute | solution.py:387
  79.9 1.6 %collective-permute-done.15.b_ref = bf16[16,1792]{1,0:T(8,128)(2,1)S(1)} collective-permute-done((bf16[16,1792]{1,0:T(8,128)(2,1)S(1)}, bf16[16,1792]{1,0:T(8,128)(2,1)S(1)}, u32[]{:S(2)}, u32[]{:S(2)}) %collective-permute-start.15) | collective-permute-done | bytes 57376 | tf_op jit(solution)/shard_map/ppermute | solution.py:387
  81.5 1.7 %collective-permute-done.16.c_ref = bf16[16,1792]{1,0:T(8,128)(2,1)S(1)} collective-permute-done((bf16[16,1792]{1,0:T(8,128)(2,1)S(1)}, bf16[16,1792]{1,0:T(8,128)(2,1)S(1)}, u32[]{:S(2)}, u32[]{:S(2)}) %collective-permute-start.16) | collective-permute-done | bytes 57376 | tf_op jit(solution)/shard_map/ppermute | solution.py:387
  83.5 1.8 %collective-permute-start.19 = (bf16[16,896]{1,0:T(8,128)(2,1)S(1)}, bf16[16,896]{1,0:T(8,128)(2,1)S(1)}, u32[]{:S(2)}, u32[]{:S(2)}) collective-permute-start(bf16[16,896]{1,0:T(8,128)(2,1)S(1)} %activate.1.a_ref), channel_id=1, source_target_pairs={{96,0},{0,32},{32,64},{64,96},{97,1},{1,33},{33,65},{65,97},{98,2}... | collective-permute-start | bytes 86024 | tf_op jit(solution)/shard_map/ppermute | solution.py:394
  86.3 1.6 %collective-permute-done.20.c_ref = bf16[16,896]{1,0:T(8,128)(2,1)S(1)} collective-permute-done((bf16[16,896]{1,0:T(8,128)(2,1)S(1)}, bf16[16,896]{1,0:T(8,128)(2,1)S(1)}, u32[]{:S(2)}, u32[]{:S(2)}) %collective-permute-start.20) | collective-permute-done | bytes 28704 | tf_op jit(solution)/shard_map/ppermute | solution.py:394
  88.5 3.8 %collective-permute-start.21 = (bf16[32,1280]{1,0:T(8,128)(2,1)S(1)}, bf16[32,1280]{1,0:T(8,128)(2,1)S(1)}, u32[]{:S(2)}, u32[]{:S(2)}) collective-permute-start(bf16[32,1280]{1,0:T(8,128)(2,1)S(1)} %get-tuple-element.34), channel_id=1, source_target_pairs={{0,1},{1,0},{2,3},{3,2},{4,5},{5,4},{6,7},{7,6},{8,9},{9,8},{10,11... | collective-permute-start | bytes 245768 | tf_op jit(solution)/shard_map/ppermute | solution.py:403
  95.7 1.7 %collective-permute-start.22 = (bf16[32,1280]{1,0:T(8,128)(2,1)S(1)}, bf16[32,1280]{1,0:T(8,128)(2,1)S(1)}, u32[]{:S(2)}, u32[]{:S(2)}) collective-permute-start(bf16[32,1280]{1,0:T(8,128)(2,1)S(1)} %add.21.refs_0_), channel_id=1, source_target_pairs={{8,0},{16,8},{24,16},{0,24},{9,1},{17,9},{25,17},{1,25},{10,2},{18... | collective-permute-start | bytes 245768 | tf_op jit(solution)/shard_map/ppermute | solution.py:394
  98.5 2.1 %collective-permute-done.23.refs_2_ = bf16[32,1280]{1,0:T(8,128)(2,1)S(1)} collective-permute-done((bf16[32,1280]{1,0:T(8,128)(2,1)S(1)}, bf16[32,1280]{1,0:T(8,128)(2,1)S(1)}, u32[]{:S(2)}, u32[]{:S(2)}) %collective-permute-start.23) | collective-permute-done | bytes 81952 | tf_op jit(solution)/shard_map/ppermute | solution.py:394
  101.9 2.0 %collective-permute-start.26 = (bf16[32,1280]{1,0:T(8,128)(2,1)S(1)}, bf16[32,1280]{1,0:T(8,128)(2,1)S(1)}, u32[]{:S(2)}, u32[]{:S(2)}) collective-permute-start(bf16[32,1280]{1,0:T(8,128)(2,1)S(1)} %add.22.refs_0_), channel_id=1, source_target_pairs={{6,0},{0,2},{2,4},{4,6},{7,1},{1,3},{3,5},{5,7},{14,8},{8,10},{10,... | collective-permute-start | bytes 245768 | tf_op jit(solution)/shard_map/ppermute | solution.py:394
  105.5 1.7 %collective-permute-done.26.refs_2_ = bf16[32,1280]{1,0:T(8,128)(2,1)S(1)} collective-permute-done((bf16[32,1280]{1,0:T(8,128)(2,1)S(1)}, bf16[32,1280]{1,0:T(8,128)(2,1)S(1)}, u32[]{:S(2)}, u32[]{:S(2)}) %collective-permute-start.26) | collective-permute-done | bytes 81952 | tf_op jit(solution)/shard_map/ppermute | solution.py:394
  108.3 1.6 %collective-permute-start.28 = (bf16[32,1280]{1,0:T(8,128)(2,1)S(1)}, bf16[32,1280]{1,0:T(8,128)(2,1)S(1)}, u32[]{:S(2)}, u32[]{:S(2)}) collective-permute-start(bf16[32,1280]{1,0:T(8,128)(2,1)S(1)} %add.23.own_ref), channel_id=1, source_target_pairs={{0,1},{1,0},{2,3},{3,2},{4,5},{5,4},{6,7},{7,6},{8,9},{9,8},{10,11... | collective-permute-start | bytes 245768 | tf_op jit(solution)/shard_map/ppermute | solution.py:403
  (78 shorter events, 31.7 us)
Async XLA Ops:
  2.3 7.8 %collective-permute-start = (f32[16,384]{1,0:T(8,128)S(1)}, f32[16,384]{1,0:T(8,128)S(1)}, u32[]{:S(2)}, u32[]{:S(2)}) collective-permute-start(f32[16,384]{1,0:T(8,128)S(1)} %get-tuple-element.20), channel_id=1, source_target_pairs={{0,64},{32,96},{64,0},{96,32},{1,65},{33,97},{65,1},{97,33},{2,66}... | collective-permute-start | bytes 73736 | tf_op jit(solution)/shard_map/ppermute | solution.py:387
  5.9 4.2 %collective-permute-start.1 = (f32[16,384]{1,0:T(8,128)S(1)}, f32[16,384]{1,0:T(8,128)S(1)}, u32[]{:S(2)}, u32[]{:S(2)}) collective-permute-start(f32[16,384]{1,0:T(8,128)S(1)} %get-tuple-element.21), channel_id=1, source_target_pairs={{0,32},{32,64},{64,96},{96,0},{1,33},{33,65},{65,97},{97,1},{2,34}... | collective-permute-start | bytes 73736 | tf_op jit(solution)/shard_map/ppermute | solution.py:387
  6.2 3.9 %collective-permute-start.2 = (f32[16,384]{1,0:T(8,128)S(1)}, f32[16,384]{1,0:T(8,128)S(1)}, u32[]{:S(2)}, u32[]{:S(2)}) collective-permute-start(f32[16,384]{1,0:T(8,128)S(1)} %get-tuple-element.22), channel_id=1, source_target_pairs={{0,96},{32,0},{64,32},{96,64},{1,97},{33,1},{65,33},{97,65},{2,98}... | collective-permute-start | bytes 73736 | tf_op jit(solution)/shard_map/ppermute | solution.py:387
  25.2 4.1 %collective-permute-start.3 = (bf16[16,40,128]{2,1,0:T(8,128)(2,1)S(1)}, bf16[16,40,128]{2,1,0:T(8,128)(2,1)S(1)}, u32[]{:S(2)}, u32[]{:S(2)}) collective-permute-start(bf16[16,40,128]{2,1,0:T(8,128)(2,1)S(1)} %all_to_all.10.own_ref), channel_id=1, source_target_pairs={{0,1},{1,0},{2,3},{3,2},{4,5},{5,4},{6,7},{7,6},{8,9},{9,8},{10,11... | collective-permute-start | bytes 491528 | tf_op jit(solution)/shard_map/ppermute | solution.py:403
  49.7 4.0 %collective-permute-start.6 = (bf16[16,256]{1,0:T(8,128)(2,1)S(1)}, bf16[16,256]{1,0:T(8,128)(2,1)S(1)}, u32[]{:S(2)}, u32[]{:S(2)}) collective-permute-start(bf16[16,256]{1,0:T(8,128)(2,1)S(1)} %get-tuple-element.25.a_ref), channel_id=1, source_target_pairs={{64,0},{96,32},{0,64},{32,96},{65,1},{97,33},{1,65},{33,97},{66,2}... | collective-permute-start | bytes 24584 | tf_op jit(solution)/shard_map/ppermute | solution.py:394
  50.9 3.7 %collective-permute-start.5 = (bf16[16,256]{1,0:T(8,128)(2,1)S(1)}, bf16[16,256]{1,0:T(8,128)(2,1)S(1)}, u32[]{:S(2)}, u32[]{:S(2)}) collective-permute-start(bf16[16,256]{1,0:T(8,128)(2,1)S(1)} %get-tuple-element.25.a_ref), channel_id=1, source_target_pairs={{96,0},{0,32},{32,64},{64,96},{97,1},{1,33},{33,65},{65,97},{98,2}... | collective-permute-start | bytes 24584 | tf_op jit(solution)/shard_map/ppermute | solution.py:394
  58.7 5.3 %collective-permute-start.10 = (bf16[32,1280]{1,0:T(8,128)(2,1)S(1)}, bf16[32,1280]{1,0:T(8,128)(2,1)S(1)}, u32[]{:S(2)}, u32[]{:S(2)}) collective-permute-start(bf16[32,1280]{1,0:T(8,128)(2,1)S(1)} %add.18.refs_0_), channel_id=1, source_target_pairs={{16,0},{24,8},{0,16},{8,24},{17,1},{25,9},{1,17},{9,25},{18,2},{26... | collective-permute-start | bytes 245768 | tf_op jit(solution)/shard_map/ppermute | solution.py:394
  60.1 5.9 %collective-permute-start.9 = (bf16[32,1280]{1,0:T(8,128)(2,1)S(1)}, bf16[32,1280]{1,0:T(8,128)(2,1)S(1)}, u32[]{:S(2)}, u32[]{:S(2)}) collective-permute-start(bf16[32,1280]{1,0:T(8,128)(2,1)S(1)} %add.18.refs_0_), channel_id=1, source_target_pairs={{24,0},{0,8},{8,16},{16,24},{25,1},{1,9},{9,17},{17,25},{26,2},{2,... | collective-permute-start | bytes 245768 | tf_op jit(solution)/shard_map/ppermute | solution.py:394
  60.3 5.7 %collective-permute-start.8 = (bf16[32,1280]{1,0:T(8,128)(2,1)S(1)}, bf16[32,1280]{1,0:T(8,128)(2,1)S(1)}, u32[]{:S(2)}, u32[]{:S(2)}) collective-permute-start(bf16[32,1280]{1,0:T(8,128)(2,1)S(1)} %add.18.refs_0_), channel_id=1, source_target_pairs={{8,0},{16,8},{24,16},{0,24},{9,1},{17,9},{25,17},{1,25},{10,2},{18... | collective-permute-start | bytes 245768 | tf_op jit(solution)/shard_map/ppermute | solution.py:394
  66.1 4.9 %collective-permute-start.13 = (bf16[32,1280]{1,0:T(8,128)(2,1)S(1)}, bf16[32,1280]{1,0:T(8,128)(2,1)S(1)}, u32[]{:S(2)}, u32[]{:S(2)}) collective-permute-start(bf16[32,1280]{1,0:T(8,128)(2,1)S(1)} %add.19.refs_0_), channel_id=1, source_target_pairs={{4,0},{6,2},{0,4},{2,6},{5,1},{7,3},{1,5},{3,7},{12,8},{14,10},{8,... | collective-permute-start | bytes 245768 | tf_op jit(solution)/shard_map/ppermute | solution.py:394
  67.5 5.7 %collective-permute-start.12 = (bf16[32,1280]{1,0:T(8,128)(2,1)S(1)}, bf16[32,1280]{1,0:T(8,128)(2,1)S(1)}, u32[]{:S(2)}, u32[]{:S(2)}) collective-permute-start(bf16[32,1280]{1,0:T(8,128)(2,1)S(1)} %add.19.refs_0_), channel_id=1, source_target_pairs={{6,0},{0,2},{2,4},{4,6},{7,1},{1,3},{3,5},{5,7},{14,8},{8,10},{10,... | collective-permute-start | bytes 245768 | tf_op jit(solution)/shard_map/ppermute | solution.py:394
  67.6 5.6 %collective-permute-start.11 = (bf16[32,1280]{1,0:T(8,128)(2,1)S(1)}, bf16[32,1280]{1,0:T(8,128)(2,1)S(1)}, u32[]{:S(2)}, u32[]{:S(2)}) collective-permute-start(bf16[32,1280]{1,0:T(8,128)(2,1)S(1)} %add.19.refs_0_), channel_id=1, source_target_pairs={{2,0},{4,2},{6,4},{0,6},{3,1},{5,3},{7,5},{1,7},{10,8},{12,10},{14... | collective-permute-start | bytes 245768 | tf_op jit(solution)/shard_map/ppermute | solution.py:394
  76.9 4.7 %collective-permute-start.15 = (bf16[16,1792]{1,0:T(8,128)(2,1)S(1)}, bf16[16,1792]{1,0:T(8,128)(2,1)S(1)}, u32[]{:S(2)}, u32[]{:S(2)}) collective-permute-start(bf16[16,1792]{1,0:T(8,128)(2,1)S(1)} %get-tuple-element.30), channel_id=1, source_target_pairs={{0,64},{32,96},{64,0},{96,32},{1,65},{33,97},{65,1},{97,33},{2,66}... | collective-permute-start | bytes 172040 | tf_op jit(solution)/shard_map/ppermute | solution.py:387
  77.3 6.0 %collective-permute-start.16 = (bf16[16,1792]{1,0:T(8,128)(2,1)S(1)}, bf16[16,1792]{1,0:T(8,128)(2,1)S(1)}, u32[]{:S(2)}, u32[]{:S(2)}) collective-permute-start(bf16[16,1792]{1,0:T(8,128)(2,1)S(1)} %get-tuple-element.31), channel_id=1, source_target_pairs={{0,32},{32,64},{64,96},{96,0},{1,33},{33,65},{65,97},{97,1},{2,34}... | collective-permute-start | bytes 172040 | tf_op jit(solution)/shard_map/ppermute | solution.py:387
  79.1 4.2 %collective-permute-start.17 = (bf16[16,1792]{1,0:T(8,128)(2,1)S(1)}, bf16[16,1792]{1,0:T(8,128)(2,1)S(1)}, u32[]{:S(2)}, u32[]{:S(2)}) collective-permute-start(bf16[16,1792]{1,0:T(8,128)(2,1)S(1)} %get-tuple-element.32), channel_id=1, source_target_pairs={{0,96},{32,0},{64,32},{96,64},{1,97},{33,1},{65,33},{97,65},{2,98}... | collective-permute-start | bytes 172040 | tf_op jit(solution)/shard_map/ppermute | solution.py:387
  83.4 4.4 %collective-permute-start.20 = (bf16[16,896]{1,0:T(8,128)(2,1)S(1)}, bf16[16,896]{1,0:T(8,128)(2,1)S(1)}, u32[]{:S(2)}, u32[]{:S(2)}) collective-permute-start(bf16[16,896]{1,0:T(8,128)(2,1)S(1)} %activate.1.a_ref), channel_id=1, source_target_pairs={{64,0},{96,32},{0,64},{32,96},{65,1},{97,33},{1,65},{33,97},{66,2}... | collective-permute-start | bytes 86024 | tf_op jit(solution)/shard_map/ppermute | solution.py:394
  83.5 4.3 %collective-permute-start.19 = (bf16[16,896]{1,0:T(8,128)(2,1)S(1)}, bf16[16,896]{1,0:T(8,128)(2,1)S(1)}, u32[]{:S(2)}, u32[]{:S(2)}) collective-permute-start(bf16[16,896]{1,0:T(8,128)(2,1)S(1)} %activate.1.a_ref), channel_id=1, source_target_pairs={{96,0},{0,32},{32,64},{64,96},{97,1},{1,33},{33,65},{65,97},{98,2}... | collective-permute-start | bytes 86024 | tf_op jit(solution)/shard_map/ppermute | solution.py:394
  88.5 4.7 %collective-permute-start.21 = (bf16[32,1280]{1,0:T(8,128)(2,1)S(1)}, bf16[32,1280]{1,0:T(8,128)(2,1)S(1)}, u32[]{:S(2)}, u32[]{:S(2)}) collective-permute-start(bf16[32,1280]{1,0:T(8,128)(2,1)S(1)} %get-tuple-element.34), channel_id=1, source_target_pairs={{0,1},{1,0},{2,3},{3,2},{4,5},{5,4},{6,7},{7,6},{8,9},{9,8},{10,11... | collective-permute-start | bytes 245768 | tf_op jit(solution)/shard_map/ppermute | solution.py:403
  93.2 5.3 %collective-permute-start.24 = (bf16[32,1280]{1,0:T(8,128)(2,1)S(1)}, bf16[32,1280]{1,0:T(8,128)(2,1)S(1)}, u32[]{:S(2)}, u32[]{:S(2)}) collective-permute-start(bf16[32,1280]{1,0:T(8,128)(2,1)S(1)} %add.21.refs_0_), channel_id=1, source_target_pairs={{16,0},{24,8},{0,16},{8,24},{17,1},{25,9},{1,17},{9,25},{18,2},{26... | collective-permute-start | bytes 245768 | tf_op jit(solution)/shard_map/ppermute | solution.py:394
  94.7 5.8 %collective-permute-start.23 = (bf16[32,1280]{1,0:T(8,128)(2,1)S(1)}, bf16[32,1280]{1,0:T(8,128)(2,1)S(1)}, u32[]{:S(2)}, u32[]{:S(2)}) collective-permute-start(bf16[32,1280]{1,0:T(8,128)(2,1)S(1)} %add.21.refs_0_), channel_id=1, source_target_pairs={{24,0},{0,8},{8,16},{16,24},{25,1},{1,9},{9,17},{17,25},{26,2},{2,... | collective-permute-start | bytes 245768 | tf_op jit(solution)/shard_map/ppermute | solution.py:394
  95.7 4.9 %collective-permute-start.22 = (bf16[32,1280]{1,0:T(8,128)(2,1)S(1)}, bf16[32,1280]{1,0:T(8,128)(2,1)S(1)}, u32[]{:S(2)}, u32[]{:S(2)}) collective-permute-start(bf16[32,1280]{1,0:T(8,128)(2,1)S(1)} %add.21.refs_0_), channel_id=1, source_target_pairs={{8,0},{16,8},{24,16},{0,24},{9,1},{17,9},{25,17},{1,25},{10,2},{18... | collective-permute-start | bytes 245768 | tf_op jit(solution)/shard_map/ppermute | solution.py:394
  100.6 4.9 %collective-permute-start.27 = (bf16[32,1280]{1,0:T(8,128)(2,1)S(1)}, bf16[32,1280]{1,0:T(8,128)(2,1)S(1)}, u32[]{:S(2)}, u32[]{:S(2)}) collective-permute-start(bf16[32,1280]{1,0:T(8,128)(2,1)S(1)} %add.22.refs_0_), channel_id=1, source_target_pairs={{4,0},{6,2},{0,4},{2,6},{5,1},{7,3},{1,5},{3,7},{12,8},{14,10},{8,... | collective-permute-start | bytes 245768 | tf_op jit(solution)/shard_map/ppermute | solution.py:394
  101.9 5.3 %collective-permute-start.26 = (bf16[32,1280]{1,0:T(8,128)(2,1)S(1)}, bf16[32,1280]{1,0:T(8,128)(2,1)S(1)}, u32[]{:S(2)}, u32[]{:S(2)}) collective-permute-start(bf16[32,1280]{1,0:T(8,128)(2,1)S(1)} %add.22.refs_0_), channel_id=1, source_target_pairs={{6,0},{0,2},{2,4},{4,6},{7,1},{1,3},{3,5},{5,7},{14,8},{8,10},{10,... | collective-permute-start | bytes 245768 | tf_op jit(solution)/shard_map/ppermute | solution.py:394
  103.9 4.4 %collective-permute-start.25 = (bf16[32,1280]{1,0:T(8,128)(2,1)S(1)}, bf16[32,1280]{1,0:T(8,128)(2,1)S(1)}, u32[]{:S(2)}, u32[]{:S(2)}) collective-permute-start(bf16[32,1280]{1,0:T(8,128)(2,1)S(1)} %add.22.refs_0_), channel_id=1, source_target_pairs={{2,0},{4,2},{6,4},{0,6},{3,1},{5,3},{7,5},{1,7},{10,8},{12,10},{14... | collective-permute-start | bytes 245768 | tf_op jit(solution)/shard_map/ppermute | solution.py:394
  (17 other events, 335.4 us)

commit v10 on v9

--- a/solution.py
+++ b/solution.py
@@ -96,24 +96,24 @@
         pltpu.make_async_copy(source, target, sems.at[at])
         for at, (source, target) in enumerate(
             (
+                (gain_hbm, gain_ref),
                 (hidden_hbm, hidden_ref),
                 (wkv_hbm, wkv_ref),
                 (wq_hbm, wq_ref),
-                (gain_hbm, gain_ref),
             )
         )
     ]
     for move in moves:
         move.start()
-    moves[0].wait()
+    moves[1].wait()
     hidden = hidden_ref[...].astype(f32)
     square = jnp.sum(hidden * hidden, axis=1, keepdims=True)
-    moves[3].wait()
+    moves[0].wait()
     scaled = (hidden * gain_ref[...].astype(f32)[None]).astype(bf16)
-    moves[1].wait()
+    moves[2].wait()
     keyval = lax.dot_general(scaled, wkv_ref[...], NT, preferred_element_type=f32)
     whole[:, 256:] = jnp.concatenate([keyval, jnp.broadcast_to(square, keyval.shape)], axis=1)
-    moves[2].wait()
+    moves[3].wait()
     whole[:, :256] = jnp.dot(scaled, wq_ref[...], preferred_element_type=f32)
     mine = place_ref[0] // WIDE
     for k in range(ROWS):
@@ -168,15 +168,40 @@
     return (own_ref, core), (other_ref, 1 - core)
 
 
+def fresh_parts(place_ref, own_ref, other_ref, straight_ref, swapped_ref, fresh_ref, value_ref):
+    wide = lax.rem(place_ref[0], WIDE)
+    group = wide // 4
+
+    def both_halves(chip):
+        parts = [unpack(ref[chip, 2 * OWN :, :].astype(f32)) for ref in (own_ref, other_ref)]
+        return jnp.where(
+            lax.rem(wide, 2) == 0,
+            jnp.concatenate(parts, axis=1),
+            jnp.concatenate(parts[::-1], axis=1),
+        )
+
+    key = norm_rope(both_halves(group), straight_ref[1], swapped_ref[1])
+    key = key.astype(bf16).astype(f32)
+    for j in range(2):
+        query = own_ref[wide // 2, j * OWN : (j + 1) * OWN, :].astype(f32)
+        scores = jnp.sum(query * key, axis=1, keepdims=True) * SCALE
+        fresh_ref[j] = jnp.broadcast_to(scores, key.shape)
+    value_ref[...] = both_halves(8 + group)
+
+
 def attend_kernel(
     place_ref,
     length_ref,
     block_ref,
     own_ref,
     other_ref,
+    straight_ref,
+    swapped_ref,
     k_ref,
     v_ref,
     o_ref,
+    fresh_ref,
+    value_ref,
     q_scr,
     p_scr,
     w_scr,
@@ -190,6 +215,7 @@
                 q_scr[pl.ds(head, OWN, stride=QUERY_HEADS), :] = ref[
                     chip, j * OWN : (j + 1) * OWN, :
                 ].astype(f32)
+    fresh_parts(place_ref, own_ref, other_ref, straight_ref, swapped_ref, fresh_ref, value_ref)
 
     row = lax.broadcasted_iota(jnp.int32, (16, 256), 0)
     lane = lax.broadcasted_iota(jnp.int32, (16, 256), 1)
@@ -264,38 +290,17 @@
         o_ref[w, 2 * OWN :, :] = jnp.where(lane[:8] < 64, stats[:8], stats[8:]).astype(bf16)
 
 
-def combine_kernel(
-    place_ref, r_ref, own_ref, other_ref, straight_ref, swapped_ref, out_ref, again_ref
-):
-    wide = lax.rem(place_ref[0], WIDE)
-    group = wide // 4
-
-    def both_halves(chip):
-        parts = [unpack(ref[chip, 2 * OWN :, :].astype(f32)) for ref in (own_ref, other_ref)]
-        return jnp.where(
-            lax.rem(wide, 2) == 0,
-            jnp.concatenate(parts, axis=1),
-            jnp.concatenate(parts[::-1], axis=1),
-        )
-
+def combine_kernel(r_ref, fresh_ref, value_ref, out_ref, again_ref):
     def column(value, at):
         return jnp.concatenate(
             [value[..., at : at + 1], value[..., 64 + at : 65 + at]], axis=-2
         )
 
-    key = both_halves(group)
-    value = both_halves(8 + group)
-    key = norm_rope(key, straight_ref[1], swapped_ref[1]).astype(bf16).astype(f32)
-    fresh = [
-        jnp.sum(own_ref[wide // 2, j * OWN : (j + 1) * OWN, :].astype(f32) * key, axis=1, keepdims=True)
-        * SCALE
-        for j in range(2)
-    ]
     lane = lax.broadcasted_iota(jnp.int32, (8, 128), 1)
     stats = r_ref[:, 2 * OWN :, :].astype(f32)
     highest = jnp.max(stats, axis=0)
     for j in range(2):
-        packed = jnp.where(lane < 64, fresh[j][:8], fresh[j][8:])
+        packed = jnp.where(lane < 64, fresh_ref[j, :8, :], fresh_ref[j, 8:, :])
         highest = jnp.where(lax.rem(lane, 64) == 8 * j, jnp.maximum(highest, packed), highest)
     shift_lane = (lax.rem(lane, 64) == 0) | (lax.rem(lane, 64) == 8)
     factors = jnp.where(shift_lane[None], jnp.exp(jnp.where(shift_lane, stats - highest, 0.0)), 0.0)
@@ -306,10 +311,10 @@
     for j in range(2):
         lanes = slice(j * 128, (j + 1) * 128)
         here = slice(j * OWN, (j + 1) * OWN)
-        fresh_weight = jnp.exp(fresh[j] - column(highest, 8 * j))
+        fresh_weight = jnp.exp(fresh_ref[j] - column(highest, 8 * j))
         weight_sum = column(totals, 8 * j + 1) + column(totals, 8 * j + 2) + fresh_weight
         numer = jnp.sum(r_ref[:, here, :].astype(f32) * column(factors, 8 * j), axis=0)
-        numer = numer + fresh_weight.astype(bf16).astype(f32) * value
+        numer = numer + fresh_weight.astype(bf16).astype(f32) * value_ref[...]
         heads = (numer / weight_sum).astype(bf16)
         out_ref[:, lanes] = heads
         again_ref[:, lanes] = heads
@@ -468,10 +473,10 @@
     gathered = exchange(payload, CHIP_AXES)
     gathered = (gathered, from_other_core(gathered))
 
-    parts = call(
+    parts, fresh, value = call(
         attend_kernel,
-        sds((WIDE, PACKED, 128), bf16),
-        [SMEM] * 3 + [VMEM] * 4,
+        [sds((WIDE, PACKED, 128), bf16), sds((2, OWN, 128), f32), sds((OWN, 128), f32)],
+        [SMEM] * 3 + [VMEM] * 6,
         [
             pltpu.VMEM((OWN * QUERY_HEADS, 128), f32),
             pltpu.VMEM((OWN * QUERY_HEADS, 256), f32),
@@ -481,10 +486,10 @@
         ],
         limit=8,
         name="attend",
-    )(place, lengths, block_index.reshape(OWN), *gathered, in_vmem(keys_cache), in_vmem(values_cache))
+    )(place, lengths, block_index.reshape(OWN), *gathered, straight, swapped, in_vmem(keys_cache), in_vmem(values_cache))
     heads_out, heads_own = call(
-        combine_kernel, [sds((OWN, 256), bf16)] * 2, [SMEM] + [VMEM] * 5, limit=8, name="combine"
-    )(place, exchange(parts, WIDE_AXES), *gathered, straight, swapped)
+        combine_kernel, [sds((OWN, 256), bf16)] * 2, [VMEM] * 3, limit=8, name="combine"
+    )(exchange(parts, WIDE_AXES), fresh, value)
 
     def product(own, weight, name):
         return call(

time: 112 us -> 111 us (level)
  no operation moved by 1% of the time
where the time goes in v10:
time: 111 us
  starting transfers between devices  44 us (40%)
  blocking collectives  28.4 us (26%)
  waiting for transfers between devices  25.1 us (23%)
  Pallas kernels  12.8 us (12%)
    all_to_all x2, blocking collectives, exchange(): return lax.all_to_all(blocks, axes, split_axis=0, concat_axis=0, tiled=True)  28.4 us
    ppermute x18, starting transfers between devices, from_peers(): lax.ppermute(own, axis, [((i + k) % ROWS, i) for i in range(ROWS)])  23.1 us
    ppermute x18, waiting for transfers between devices, from_peers(): lax.ppermute(own, axis, [((i + k) % ROWS, i) for i in range(ROWS)])  17.1 us
    ppermute x5, starting transfers between devices, from_other_core(): return lax.ppermute(value, 'core', [(0, 1), (1, 0)])  11.4 us
    ppermute x6, starting transfers between devices, to_rows(): lax.ppermute(blocks[k], 'rows', [(i, (i + k) % ROWS) for i in range(ROWS)])  9.42 us
    pallas_call x1, Pallas kernels, body(): call(attend_kernel, [sds((WIDE, PACKED, 128), bf16), sds((2, OWN, 128), f...  5.23 us
    ppermute x5, waiting for transfers between devices, from_other_core(): return lax.ppermute(value, 'core', [(0, 1), (1, 0)])  4.72 us
    ppermute x6, waiting for transfers between devices, to_rows(): lax.ppermute(blocks[k], 'rows', [(i, (i + k) % ROWS) for i in range(ROWS)])  3.31 us
  transfers between devices with their start and end apart: 29, of which 21 were waited for; matrix products, arithmetic and copies ran while one was open for 0% of the time, Pallas kernels for 1%

profile of v10, /device:TPU:1, one launch (start us, length us, event | category | flops | bytes accessed | tf_op | source)
XLA Modules:
  0.0 111.2 jit_solution(11978461044529692545)
XLA Ops:
  0.6 1.6 %project.1 = (f32[16,384]{1,0:T(8,128)S(1)}, f32[16,384]{1,0:T(8,128)S(1)}, f32[16,384]{1,0:T(8,128)S(1)}, f32[16,384]{1,0:T(8,128)S(1)}) custom-call(s32[1]{0:T(128)} %bitcast.place_ref, bf16[64,1280]{1,0:T(8,128)(2,1)} %hidden_ref.1, bf16[1280]{0:T(1024)(128)(2,1)} %gain_hbm.1, bf16[1280,256]{1,0:T(8,128)(2,1)} %wq_hbm.1, bf16[64,1280]{1,0:T(8,128)(2,1)} %bitcast.12), custom_call_target="tpu_custom_call" | custom-call | tf_op jit(solution)/shard_map/project/pallas_call | solution.py:442
  2.3 3.7 %collective-permute-start = (f32[16,384]{1,0:T(8,128)S(1)}, f32[16,384]{1,0:T(8,128)S(1)}, u32[]{:S(2)}, u32[]{:S(2)}) collective-permute-start(f32[16,384]{1,0:T(8,128)S(1)} %get-tuple-element.23), channel_id=1, source_target_pairs={{0,64},{32,96},{64,0},{96,32},{1,65},{33,97},{65,1},{97,33},{2,66}... | collective-permute-start | bytes 73736 | tf_op jit(solution)/shard_map/ppermute | solution.py:392
  6.2 2.4 %collective-permute-start.2 = (f32[16,384]{1,0:T(8,128)S(1)}, f32[16,384]{1,0:T(8,128)S(1)}, u32[]{:S(2)}, u32[]{:S(2)}) collective-permute-start(f32[16,384]{1,0:T(8,128)S(1)} %get-tuple-element.25), channel_id=1, source_target_pairs={{0,96},{32,0},{64,32},{96,64},{1,97},{33,1},{65,33},{97,65},{2,98}... | collective-permute-start | bytes 73736 | tf_op jit(solution)/shard_map/ppermute | solution.py:392
  10.4 14.7 %all_to_all.10.own_ref = bf16[16,40,128]{2,1,0:T(8,128)(2,1)S(1)} all-to-all(bf16[16,40,128]{2,1,0:T(8,128)(2,1)S(1)} %heads.1), channel_id=1, replica_groups=mesh['rows'=4,'y'=4,'z'=4,'core'=2] {'y','z'}, dimensions={0} | all-to-all | bytes 327680 | tf_op jit(solution)/shard_map/all_to_all | solution.py:404
  25.2 3.1 %collective-permute-start.3 = (bf16[16,40,128]{2,1,0:T(8,128)(2,1)S(1)}, bf16[16,40,128]{2,1,0:T(8,128)(2,1)S(1)}, u32[]{:S(2)}, u32[]{:S(2)}) collective-permute-start(bf16[16,40,128]{2,1,0:T(8,128)(2,1)S(1)} %all_to_all.10.own_ref), channel_id=1, source_target_pairs={{0,1},{1,0},{2,3},{3,2},{4,5},{5,4},{6,7},{7,6},{8,9},{9,8},{10,11... | collective-permute-start | bytes 491528 | tf_op jit(solution)/shard_map/ppermute | solution.py:408
  29.4 5.2 %attend.1 = (bf16[32,40,128]{2,1,0:T(8,128)(2,1)S(1)}, f32[2,16,128]{2,1,0:T(8,128)S(1)}, f32[16,128]{1,0:T(8,128)S(1)}) custom-call(s32[1]{0:T(128)} %bitcast.place_ref, s32[16]{0:T(128)S(1)} %copy-done.6, s32[16]{0:T(128)S(1)} %bitcast.11, bf16[16,40,128]{2,1,0:T(8,128)(2,1)S(1)} %all_to_all.10.own_ref, ...), custom_call_target="tpu_custom_call" | custom-call | tf_op jit(solution)/shard_map/attend/pallas_call | solution.py:476
  34.6 13.7 %all_to_all.11.r_ref = bf16[32,40,128]{2,1,0:T(8,128)(2,1)S(1)} all-to-all(bf16[32,40,128]{2,1,0:T(8,128)(2,1)S(1)} %get-tuple-element.28), channel_id=1, replica_groups=mesh['rows'=4,'y'=4,'z'=4,'core'=2] {'y','z','core'}, dimensions={0} | all-to-all | bytes 655360 | tf_op jit(solution)/shard_map/all_to_all | solution.py:404
  50.5 2.3 %collective-permute-start.5 = (bf16[16,256]{1,0:T(8,128)(2,1)S(1)}, bf16[16,256]{1,0:T(8,128)(2,1)S(1)}, u32[]{:S(2)}, u32[]{:S(2)}) collective-permute-start(bf16[16,256]{1,0:T(8,128)(2,1)S(1)} %get-tuple-element.31.a_ref), channel_id=1, source_target_pairs={{96,0},{0,32},{32,64},{64,96},{97,1},{1,33},{33,65},{65,97},{98,2}... | collective-permute-start | bytes 24584 | tf_op jit(solution)/shard_map/ppermute | solution.py:399
  55.7 1.8 %collective-permute-start.7 = (bf16[32,1280]{1,0:T(8,128)(2,1)S(1)}, bf16[32,1280]{1,0:T(8,128)(2,1)S(1)}, u32[]{:S(2)}, u32[]{:S(2)}) collective-permute-start(bf16[32,1280]{1,0:T(8,128)(2,1)S(1)} %get-tuple-element.33), channel_id=1, source_target_pairs={{0,1},{1,0},{2,3},{3,2},{4,5},{5,4},{6,7},{7,6},{8,9},{9,8},{10,11... | collective-permute-start | bytes 245768 | tf_op jit(solution)/shard_map/ppermute | solution.py:408
  60.0 2.4 %collective-permute-start.8 = (bf16[32,1280]{1,0:T(8,128)(2,1)S(1)}, bf16[32,1280]{1,0:T(8,128)(2,1)S(1)}, u32[]{:S(2)}, u32[]{:S(2)}) collective-permute-start(bf16[32,1280]{1,0:T(8,128)(2,1)S(1)} %add.18.refs_0_), channel_id=1, source_target_pairs={{8,0},{16,8},{24,16},{0,24},{9,1},{17,9},{25,17},{1,25},{10,2},{18... | collective-permute-start | bytes 245768 | tf_op jit(solution)/shard_map/ppermute | solution.py:399
  63.6 2.0 %collective-permute-done.9.refs_2_ = bf16[32,1280]{1,0:T(8,128)(2,1)S(1)} collective-permute-done((bf16[32,1280]{1,0:T(8,128)(2,1)S(1)}, bf16[32,1280]{1,0:T(8,128)(2,1)S(1)}, u32[]{:S(2)}, u32[]{:S(2)}) %collective-permute-start.9) | collective-permute-done | bytes 81952 | tf_op jit(solution)/shard_map/ppermute | solution.py:399
  67.3 2.6 %collective-permute-start.11 = (bf16[32,1280]{1,0:T(8,128)(2,1)S(1)}, bf16[32,1280]{1,0:T(8,128)(2,1)S(1)}, u32[]{:S(2)}, u32[]{:S(2)}) collective-permute-start(bf16[32,1280]{1,0:T(8,128)(2,1)S(1)} %add.19.refs_0_), channel_id=1, source_target_pairs={{2,0},{4,2},{6,4},{0,6},{3,1},{5,3},{7,5},{1,7},{10,8},{12,10},{14... | collective-permute-start | bytes 245768 | tf_op jit(solution)/shard_map/ppermute | solution.py:399
  70.6 2.3 %collective-permute-done.12.refs_2_ = bf16[32,1280]{1,0:T(8,128)(2,1)S(1)} collective-permute-done((bf16[32,1280]{1,0:T(8,128)(2,1)S(1)}, bf16[32,1280]{1,0:T(8,128)(2,1)S(1)}, u32[]{:S(2)}, u32[]{:S(2)}) %collective-permute-start.12) | collective-permute-done | bytes 81952 | tf_op jit(solution)/shard_map/ppermute | solution.py:399
  76.9 1.8 %collective-permute-start.16 = (bf16[16,1792]{1,0:T(8,128)(2,1)S(1)}, bf16[16,1792]{1,0:T(8,128)(2,1)S(1)}, u32[]{:S(2)}, u32[]{:S(2)}) collective-permute-start(bf16[16,1792]{1,0:T(8,128)(2,1)S(1)} %get-tuple-element.37), channel_id=1, source_target_pairs={{0,32},{32,64},{64,96},{96,0},{1,33},{33,65},{65,97},{97,1},{2,34}... | collective-permute-start | bytes 172040 | tf_op jit(solution)/shard_map/ppermute | solution.py:392
  79.6 1.6 %collective-permute-done.15.b_ref = bf16[16,1792]{1,0:T(8,128)(2,1)S(1)} collective-permute-done((bf16[16,1792]{1,0:T(8,128)(2,1)S(1)}, bf16[16,1792]{1,0:T(8,128)(2,1)S(1)}, u32[]{:S(2)}, u32[]{:S(2)}) %collective-permute-start.15) | collective-permute-done | bytes 57376 | tf_op jit(solution)/shard_map/ppermute | solution.py:392
  81.2 1.7 %collective-permute-done.16.c_ref = bf16[16,1792]{1,0:T(8,128)(2,1)S(1)} collective-permute-done((bf16[16,1792]{1,0:T(8,128)(2,1)S(1)}, bf16[16,1792]{1,0:T(8,128)(2,1)S(1)}, u32[]{:S(2)}, u32[]{:S(2)}) %collective-permute-start.16) | collective-permute-done | bytes 57376 | tf_op jit(solution)/shard_map/ppermute | solution.py:392
  83.2 1.8 %collective-permute-start.19 = (bf16[16,896]{1,0:T(8,128)(2,1)S(1)}, bf16[16,896]{1,0:T(8,128)(2,1)S(1)}, u32[]{:S(2)}, u32[]{:S(2)}) collective-permute-start(bf16[16,896]{1,0:T(8,128)(2,1)S(1)} %activate.1.a_ref), channel_id=1, source_target_pairs={{96,0},{0,32},{32,64},{64,96},{97,1},{1,33},{33,65},{65,97},{98,2}... | collective-permute-start | bytes 86024 | tf_op jit(solution)/shard_map/ppermute | solution.py:399
  88.1 3.6 %collective-permute-start.21 = (bf16[32,1280]{1,0:T(8,128)(2,1)S(1)}, bf16[32,1280]{1,0:T(8,128)(2,1)S(1)}, u32[]{:S(2)}, u32[]{:S(2)}) collective-permute-start(bf16[32,1280]{1,0:T(8,128)(2,1)S(1)} %get-tuple-element.40), channel_id=1, source_target_pairs={{0,1},{1,0},{2,3},{3,2},{4,5},{5,4},{6,7},{7,6},{8,9},{9,8},{10,11... | collective-permute-start | bytes 245768 | tf_op jit(solution)/shard_map/ppermute | solution.py:408
  92.7 1.7 %collective-permute-start.24 = (bf16[32,1280]{1,0:T(8,128)(2,1)S(1)}, bf16[32,1280]{1,0:T(8,128)(2,1)S(1)}, u32[]{:S(2)}, u32[]{:S(2)}) collective-permute-start(bf16[32,1280]{1,0:T(8,128)(2,1)S(1)} %add.21.refs_0_), channel_id=1, source_target_pairs={{16,0},{24,8},{0,16},{8,24},{17,1},{25,9},{1,17},{9,25},{18,2},{26... | collective-permute-start | bytes 245768 | tf_op jit(solution)/shard_map/ppermute | solution.py:399
  95.3 1.7 %collective-permute-start.22 = (bf16[32,1280]{1,0:T(8,128)(2,1)S(1)}, bf16[32,1280]{1,0:T(8,128)(2,1)S(1)}, u32[]{:S(2)}, u32[]{:S(2)}) collective-permute-start(bf16[32,1280]{1,0:T(8,128)(2,1)S(1)} %add.21.refs_0_), channel_id=1, source_target_pairs={{8,0},{16,8},{24,16},{0,24},{9,1},{17,9},{25,17},{1,25},{10,2},{18... | collective-permute-start | bytes 245768 | tf_op jit(solution)/shard_map/ppermute | solution.py:399
  98.1 2.1 %collective-permute-done.23.refs_2_ = bf16[32,1280]{1,0:T(8,128)(2,1)S(1)} collective-permute-done((bf16[32,1280]{1,0:T(8,128)(2,1)S(1)}, bf16[32,1280]{1,0:T(8,128)(2,1)S(1)}, u32[]{:S(2)}, u32[]{:S(2)}) %collective-permute-start.23) | collective-permute-done | bytes 81952 | tf_op jit(solution)/shard_map/ppermute | solution.py:399
  101.5 2.0 %collective-permute-start.26 = (bf16[32,1280]{1,0:T(8,128)(2,1)S(1)}, bf16[32,1280]{1,0:T(8,128)(2,1)S(1)}, u32[]{:S(2)}, u32[]{:S(2)}) collective-permute-start(bf16[32,1280]{1,0:T(8,128)(2,1)S(1)} %add.22.refs_0_), channel_id=1, source_target_pairs={{6,0},{0,2},{2,4},{4,6},{7,1},{1,3},{3,5},{5,7},{14,8},{8,10},{10,... | collective-permute-start | bytes 245768 | tf_op jit(solution)/shard_map/ppermute | solution.py:399
  105.1 1.7 %collective-permute-done.26.refs_2_ = bf16[32,1280]{1,0:T(8,128)(2,1)S(1)} collective-permute-done((bf16[32,1280]{1,0:T(8,128)(2,1)S(1)}, bf16[32,1280]{1,0:T(8,128)(2,1)S(1)}, u32[]{:S(2)}, u32[]{:S(2)}) %collective-permute-start.26) | collective-permute-done | bytes 81952 | tf_op jit(solution)/shard_map/ppermute | solution.py:399
  108.0 1.6 %collective-permute-start.28 = (bf16[32,1280]{1,0:T(8,128)(2,1)S(1)}, bf16[32,1280]{1,0:T(8,128)(2,1)S(1)}, u32[]{:S(2)}, u32[]{:S(2)}) collective-permute-start(bf16[32,1280]{1,0:T(8,128)(2,1)S(1)} %add.23.own_ref), channel_id=1, source_target_pairs={{0,1},{1,0},{2,3},{3,2},{4,5},{5,4},{6,7},{7,6},{8,9},{9,8},{10,11... | collective-permute-start | bytes 245768 | tf_op jit(solution)/shard_map/ppermute | solution.py:408
  (78 shorter events, 31.4 us)
Async XLA Ops:
  2.3 7.8 %collective-permute-start = (f32[16,384]{1,0:T(8,128)S(1)}, f32[16,384]{1,0:T(8,128)S(1)}, u32[]{:S(2)}, u32[]{:S(2)}) collective-permute-start(f32[16,384]{1,0:T(8,128)S(1)} %get-tuple-element.23), channel_id=1, source_target_pairs={{0,64},{32,96},{64,0},{96,32},{1,65},{33,97},{65,1},{97,33},{2,66}... | collective-permute-start | bytes 73736 | tf_op jit(solution)/shard_map/ppermute | solution.py:392
  5.9 4.2 %collective-permute-start.1 = (f32[16,384]{1,0:T(8,128)S(1)}, f32[16,384]{1,0:T(8,128)S(1)}, u32[]{:S(2)}, u32[]{:S(2)}) collective-permute-start(f32[16,384]{1,0:T(8,128)S(1)} %get-tuple-element.24), channel_id=1, source_target_pairs={{0,32},{32,64},{64,96},{96,0},{1,33},{33,65},{65,97},{97,1},{2,34}... | collective-permute-start | bytes 73736 | tf_op jit(solution)/shard_map/ppermute | solution.py:392
  6.2 3.9 %collective-permute-start.2 = (f32[16,384]{1,0:T(8,128)S(1)}, f32[16,384]{1,0:T(8,128)S(1)}, u32[]{:S(2)}, u32[]{:S(2)}) collective-permute-start(f32[16,384]{1,0:T(8,128)S(1)} %get-tuple-element.25), channel_id=1, source_target_pairs={{0,96},{32,0},{64,32},{96,64},{1,97},{33,1},{65,33},{97,65},{2,98}... | collective-permute-start | bytes 73736 | tf_op jit(solution)/shard_map/ppermute | solution.py:392
  25.2 4.1 %collective-permute-start.3 = (bf16[16,40,128]{2,1,0:T(8,128)(2,1)S(1)}, bf16[16,40,128]{2,1,0:T(8,128)(2,1)S(1)}, u32[]{:S(2)}, u32[]{:S(2)}) collective-permute-start(bf16[16,40,128]{2,1,0:T(8,128)(2,1)S(1)} %all_to_all.10.own_ref), channel_id=1, source_target_pairs={{0,1},{1,0},{2,3},{3,2},{4,5},{5,4},{6,7},{7,6},{8,9},{9,8},{10,11... | collective-permute-start | bytes 491528 | tf_op jit(solution)/shard_map/ppermute | solution.py:408
  49.4 4.0 %collective-permute-start.6 = (bf16[16,256]{1,0:T(8,128)(2,1)S(1)}, bf16[16,256]{1,0:T(8,128)(2,1)S(1)}, u32[]{:S(2)}, u32[]{:S(2)}) collective-permute-start(bf16[16,256]{1,0:T(8,128)(2,1)S(1)} %get-tuple-element.31.a_ref), channel_id=1, source_target_pairs={{64,0},{96,32},{0,64},{32,96},{65,1},{97,33},{1,65},{33,97},{66,2}... | collective-permute-start | bytes 24584 | tf_op jit(solution)/shard_map/ppermute | solution.py:399
  50.5 3.7 %collective-permute-start.5 = (bf16[16,256]{1,0:T(8,128)(2,1)S(1)}, bf16[16,256]{1,0:T(8,128)(2,1)S(1)}, u32[]{:S(2)}, u32[]{:S(2)}) collective-permute-start(bf16[16,256]{1,0:T(8,128)(2,1)S(1)} %get-tuple-element.31.a_ref), channel_id=1, source_target_pairs={{96,0},{0,32},{32,64},{64,96},{97,1},{1,33},{33,65},{65,97},{98,2}... | collective-permute-start | bytes 24584 | tf_op jit(solution)/shard_map/ppermute | solution.py:399
  58.4 5.3 %collective-permute-start.10 = (bf16[32,1280]{1,0:T(8,128)(2,1)S(1)}, bf16[32,1280]{1,0:T(8,128)(2,1)S(1)}, u32[]{:S(2)}, u32[]{:S(2)}) collective-permute-start(bf16[32,1280]{1,0:T(8,128)(2,1)S(1)} %add.18.refs_0_), channel_id=1, source_target_pairs={{16,0},{24,8},{0,16},{8,24},{17,1},{25,9},{1,17},{9,25},{18,2},{26... | collective-permute-start | bytes 245768 | tf_op jit(solution)/shard_map/ppermute | solution.py:399
  59.7 5.9 %collective-permute-start.9 = (bf16[32,1280]{1,0:T(8,128)(2,1)S(1)}, bf16[32,1280]{1,0:T(8,128)(2,1)S(1)}, u32[]{:S(2)}, u32[]{:S(2)}) collective-permute-start(bf16[32,1280]{1,0:T(8,128)(2,1)S(1)} %add.18.refs_0_), channel_id=1, source_target_pairs={{24,0},{0,8},{8,16},{16,24},{25,1},{1,9},{9,17},{17,25},{26,2},{2,... | collective-permute-start | bytes 245768 | tf_op jit(solution)/shard_map/ppermute | solution.py:399
  60.0 5.7 %collective-permute-start.8 = (bf16[32,1280]{1,0:T(8,128)(2,1)S(1)}, bf16[32,1280]{1,0:T(8,128)(2,1)S(1)}, u32[]{:S(2)}, u32[]{:S(2)}) collective-permute-start(bf16[32,1280]{1,0:T(8,128)(2,1)S(1)} %add.18.refs_0_), channel_id=1, source_target_pairs={{8,0},{16,8},{24,16},{0,24},{9,1},{17,9},{25,17},{1,25},{10,2},{18... | collective-permute-start | bytes 245768 | tf_op jit(solution)/shard_map/ppermute | solution.py:399
  65.7 4.9 %collective-permute-start.13 = (bf16[32,1280]{1,0:T(8,128)(2,1)S(1)}, bf16[32,1280]{1,0:T(8,128)(2,1)S(1)}, u32[]{:S(2)}, u32[]{:S(2)}) collective-permute-start(bf16[32,1280]{1,0:T(8,128)(2,1)S(1)} %add.19.refs_0_), channel_id=1, source_target_pairs={{4,0},{6,2},{0,4},{2,6},{5,1},{7,3},{1,5},{3,7},{12,8},{14,10},{8,... | collective-permute-start | bytes 245768 | tf_op jit(solution)/shard_map/ppermute | solution.py:399
  67.2 5.7 %collective-permute-start.12 = (bf16[32,1280]{1,0:T(8,128)(2,1)S(1)}, bf16[32,1280]{1,0:T(8,128)(2,1)S(1)}, u32[]{:S(2)}, u32[]{:S(2)}) collective-permute-start(bf16[32,1280]{1,0:T(8,128)(2,1)S(1)} %add.19.refs_0_), channel_id=1, source_target_pairs={{6,0},{0,2},{2,4},{4,6},{7,1},{1,3},{3,5},{5,7},{14,8},{8,10},{10,... | collective-permute-start | bytes 245768 | tf_op jit(solution)/shard_map/ppermute | solution.py:399
  67.3 5.6 %collective-permute-start.11 = (bf16[32,1280]{1,0:T(8,128)(2,1)S(1)}, bf16[32,1280]{1,0:T(8,128)(2,1)S(1)}, u32[]{:S(2)}, u32[]{:S(2)}) collective-permute-start(bf16[32,1280]{1,0:T(8,128)(2,1)S(1)} %add.19.refs_0_), channel_id=1, source_target_pairs={{2,0},{4,2},{6,4},{0,6},{3,1},{5,3},{7,5},{1,7},{10,8},{12,10},{14... | collective-permute-start | bytes 245768 | tf_op jit(solution)/shard_map/ppermute | solution.py:399
  76.5 4.7 %collective-permute-start.15 = (bf16[16,1792]{1,0:T(8,128)(2,1)S(1)}, bf16[16,1792]{1,0:T(8,128)(2,1)S(1)}, u32[]{:S(2)}, u32[]{:S(2)}) collective-permute-start(bf16[16,1792]{1,0:T(8,128)(2,1)S(1)} %get-tuple-element.36), channel_id=1, source_target_pairs={{0,64},{32,96},{64,0},{96,32},{1,65},{33,97},{65,1},{97,33},{2,66}... | collective-permute-start | bytes 172040 | tf_op jit(solution)/shard_map/ppermute | solution.py:392
  76.9 6.0 %collective-permute-start.16 = (bf16[16,1792]{1,0:T(8,128)(2,1)S(1)}, bf16[16,1792]{1,0:T(8,128)(2,1)S(1)}, u32[]{:S(2)}, u32[]{:S(2)}) collective-permute-start(bf16[16,1792]{1,0:T(8,128)(2,1)S(1)} %get-tuple-element.37), channel_id=1, source_target_pairs={{0,32},{32,64},{64,96},{96,0},{1,33},{33,65},{65,97},{97,1},{2,34}... | collective-permute-start | bytes 172040 | tf_op jit(solution)/shard_map/ppermute | solution.py:392
  78.7 4.2 %collective-permute-start.17 = (bf16[16,1792]{1,0:T(8,128)(2,1)S(1)}, bf16[16,1792]{1,0:T(8,128)(2,1)S(1)}, u32[]{:S(2)}, u32[]{:S(2)}) collective-permute-start(bf16[16,1792]{1,0:T(8,128)(2,1)S(1)} %get-tuple-element.38), channel_id=1, source_target_pairs={{0,96},{32,0},{64,32},{96,64},{1,97},{33,1},{65,33},{97,65},{2,98}... | collective-permute-start | bytes 172040 | tf_op jit(solution)/shard_map/ppermute | solution.py:392
  83.1 4.4 %collective-permute-start.20 = (bf16[16,896]{1,0:T(8,128)(2,1)S(1)}, bf16[16,896]{1,0:T(8,128)(2,1)S(1)}, u32[]{:S(2)}, u32[]{:S(2)}) collective-permute-start(bf16[16,896]{1,0:T(8,128)(2,1)S(1)} %activate.1.a_ref), channel_id=1, source_target_pairs={{64,0},{96,32},{0,64},{32,96},{65,1},{97,33},{1,65},{33,97},{66,2}... | collective-permute-start | bytes 86024 | tf_op jit(solution)/shard_map/ppermute | solution.py:399
  83.2 4.3 %collective-permute-start.19 = (bf16[16,896]{1,0:T(8,128)(2,1)S(1)}, bf16[16,896]{1,0:T(8,128)(2,1)S(1)}, u32[]{:S(2)}, u32[]{:S(2)}) collective-permute-start(bf16[16,896]{1,0:T(8,128)(2,1)S(1)} %activate.1.a_ref), channel_id=1, source_target_pairs={{96,0},{0,32},{32,64},{64,96},{97,1},{1,33},{33,65},{65,97},{98,2}... | collective-permute-start | bytes 86024 | tf_op jit(solution)/shard_map/ppermute | solution.py:399
  88.1 4.5 %collective-permute-start.21 = (bf16[32,1280]{1,0:T(8,128)(2,1)S(1)}, bf16[32,1280]{1,0:T(8,128)(2,1)S(1)}, u32[]{:S(2)}, u32[]{:S(2)}) collective-permute-start(bf16[32,1280]{1,0:T(8,128)(2,1)S(1)} %get-tuple-element.40), channel_id=1, source_target_pairs={{0,1},{1,0},{2,3},{3,2},{4,5},{5,4},{6,7},{7,6},{8,9},{9,8},{10,11... | collective-permute-start | bytes 245768 | tf_op jit(solution)/shard_map/ppermute | solution.py:408
  92.7 5.4 %collective-permute-start.24 = (bf16[32,1280]{1,0:T(8,128)(2,1)S(1)}, bf16[32,1280]{1,0:T(8,128)(2,1)S(1)}, u32[]{:S(2)}, u32[]{:S(2)}) collective-permute-start(bf16[32,1280]{1,0:T(8,128)(2,1)S(1)} %add.21.refs_0_), channel_id=1, source_target_pairs={{16,0},{24,8},{0,16},{8,24},{17,1},{25,9},{1,17},{9,25},{18,2},{26... | collective-permute-start | bytes 245768 | tf_op jit(solution)/shard_map/ppermute | solution.py:399
  94.4 5.8 %collective-permute-start.23 = (bf16[32,1280]{1,0:T(8,128)(2,1)S(1)}, bf16[32,1280]{1,0:T(8,128)(2,1)S(1)}, u32[]{:S(2)}, u32[]{:S(2)}) collective-permute-start(bf16[32,1280]{1,0:T(8,128)(2,1)S(1)} %add.21.refs_0_), channel_id=1, source_target_pairs={{24,0},{0,8},{8,16},{16,24},{25,1},{1,9},{9,17},{17,25},{26,2},{2,... | collective-permute-start | bytes 245768 | tf_op jit(solution)/shard_map/ppermute | solution.py:399
  95.3 4.9 %collective-permute-start.22 = (bf16[32,1280]{1,0:T(8,128)(2,1)S(1)}, bf16[32,1280]{1,0:T(8,128)(2,1)S(1)}, u32[]{:S(2)}, u32[]{:S(2)}) collective-permute-start(bf16[32,1280]{1,0:T(8,128)(2,1)S(1)} %add.21.refs_0_), channel_id=1, source_target_pairs={{8,0},{16,8},{24,16},{0,24},{9,1},{17,9},{25,17},{1,25},{10,2},{18... | collective-permute-start | bytes 245768 | tf_op jit(solution)/shard_map/ppermute | solution.py:399
  100.2 4.9 %collective-permute-start.27 = (bf16[32,1280]{1,0:T(8,128)(2,1)S(1)}, bf16[32,1280]{1,0:T(8,128)(2,1)S(1)}, u32[]{:S(2)}, u32[]{:S(2)}) collective-permute-start(bf16[32,1280]{1,0:T(8,128)(2,1)S(1)} %add.22.refs_0_), channel_id=1, source_target_pairs={{4,0},{6,2},{0,4},{2,6},{5,1},{7,3},{1,5},{3,7},{12,8},{14,10},{8,... | collective-permute-start | bytes 245768 | tf_op jit(solution)/shard_map/ppermute | solution.py:399
  101.5 5.3 %collective-permute-start.26 = (bf16[32,1280]{1,0:T(8,128)(2,1)S(1)}, bf16[32,1280]{1,0:T(8,128)(2,1)S(1)}, u32[]{:S(2)}, u32[]{:S(2)}) collective-permute-start(bf16[32,1280]{1,0:T(8,128)(2,1)S(1)} %add.22.refs_0_), channel_id=1, source_target_pairs={{6,0},{0,2},{2,4},{4,6},{7,1},{1,3},{3,5},{5,7},{14,8},{8,10},{10,... | collective-permute-start | bytes 245768 | tf_op jit(solution)/shard_map/ppermute | solution.py:399
  103.6 4.4 %collective-permute-start.25 = (bf16[32,1280]{1,0:T(8,128)(2,1)S(1)}, bf16[32,1280]{1,0:T(8,128)(2,1)S(1)}, u32[]{:S(2)}, u32[]{:S(2)}) collective-permute-start(bf16[32,1280]{1,0:T(8,128)(2,1)S(1)} %add.22.refs_0_), channel_id=1, source_target_pairs={{2,0},{4,2},{6,4},{0,6},{3,1},{5,3},{7,5},{1,7},{10,8},{12,10},{14... | collective-permute-start | bytes 245768 | tf_op jit(solution)/shard_map/ppermute | solution.py:399
  (17 other events, 333.6 us)

commit v11 on v10

--- a/solution.py
+++ b/solution.py
@@ -20,7 +20,7 @@
 WIDE_AXES = ("y", "z", "core")
 CHIPS = 16
 CHIP_AXES = ("y", "z")
-PACKED = 40
+PACKED = 48
 AT_ONCE = 2
 GROUPS = 8
 OWN = 16
@@ -80,14 +80,6 @@
 def norm_rope(value, straight, swapped):
     value = value * lax.rsqrt(jnp.mean(value * value, axis=-1, keepdims=True) + EPSILON)
     return value * straight + swap_halves(value) * swapped
-
-
-def pack(value):
-    return jnp.concatenate([value[:8], value[8:]], axis=1)
-
-
-def unpack(value):
-    return jnp.concatenate([value[:, :64], value[:, 64:]], axis=0)
 
 
 def project_kernel(place_ref, hidden_hbm, gain_hbm, wq_hbm, wkv_hbm, *rest):
@@ -158,7 +150,7 @@
     parts = [
         norm_rope(scaled[:, j * 128 : (j + 1) * 128], straight, swapped) for j in range(2)
     ]
-    parts.append(pack(scaled[:, 256:320]))
+    parts.append(scaled[:, 256:])
     out = jnp.concatenate(parts, axis=0).astype(bf16)
     out_ref[...] = jnp.broadcast_to(out[None], out_ref.shape)
 
@@ -173,7 +165,7 @@
     group = wide // 4
 
     def both_halves(chip):
-        parts = [unpack(ref[chip, 2 * OWN :, :].astype(f32)) for ref in (own_ref, other_ref)]
+        parts = [ref[chip, 2 * OWN :, :].astype(f32)[:, :64] for ref in (own_ref, other_ref)]
         return jnp.where(
             lax.rem(wide, 2) == 0,
             jnp.concatenate(parts, axis=1),
@@ -282,27 +274,24 @@
     add_up(last)
 
     lane = lax.broadcasted_iota(jnp.int32, (OWN, 128), 1)
-    first = lax.rem(lane, 64) < 8
+    first = lane < 8
     for w in range(WIDE):
         rows = [slice((2 * w + j) * OWN, (2 * w + j + 1) * OWN) for j in range(2)]
         o_ref[w, : 2 * OWN, :] = n_scr[2 * w * OWN : 2 * (w + 1) * OWN, :].astype(bf16)
         stats = jnp.where(first, s_scr[rows[0], :], s_scr[rows[1], :])
-        o_ref[w, 2 * OWN :, :] = jnp.where(lane[:8] < 64, stats[:8], stats[8:]).astype(bf16)
+        o_ref[w, 2 * OWN :, :] = stats.astype(bf16)
 
 
 def combine_kernel(r_ref, fresh_ref, value_ref, out_ref, again_ref):
     def column(value, at):
-        return jnp.concatenate(
-            [value[..., at : at + 1], value[..., 64 + at : 65 + at]], axis=-2
-        )
-
-    lane = lax.broadcasted_iota(jnp.int32, (8, 128), 1)
+        return value[..., at : at + 1]
+
+    lane = lax.broadcasted_iota(jnp.int32, (OWN, 128), 1)
     stats = r_ref[:, 2 * OWN :, :].astype(f32)
     highest = jnp.max(stats, axis=0)
     for j in range(2):
-        packed = jnp.where(lane < 64, fresh_ref[j, :8, :], fresh_ref[j, 8:, :])
-        highest = jnp.where(lax.rem(lane, 64) == 8 * j, jnp.maximum(highest, packed), highest)
-    shift_lane = (lax.rem(lane, 64) == 0) | (lax.rem(lane, 64) == 8)
+        highest = jnp.where(lane == 8 * j, jnp.maximum(highest, fresh_ref[j]), highest)
+    shift_lane = (lane == 0) | (lane == 8)
     factors = jnp.where(shift_lane[None], jnp.exp(jnp.where(shift_lane, stats - highest, 0.0)), 0.0)
     spread_factors = factors
     for shift in (1, 2):

time: 111 us -> 112 us (level)
  no operation moved by 1% of the time
where the time goes in v11:
time: 112 us
  starting transfers between devices  44 us (39%)
  blocking collectives  29.3 us (26%)
  waiting for transfers between devices  25.1 us (22%)
  Pallas kernels  12.8 us (11%)
    all_to_all x2, blocking collectives, exchange(): return lax.all_to_all(blocks, axes, split_axis=0, concat_axis=0, tiled=True)  29.3 us
    ppermute x18, starting transfers between devices, from_peers(): lax.ppermute(own, axis, [((i + k) % ROWS, i) for i in range(ROWS)])  23.3 us
    ppermute x18, waiting for transfers between devices, from_peers(): lax.ppermute(own, axis, [((i + k) % ROWS, i) for i in range(ROWS)])  17.1 us
    ppermute x5, starting transfers between devices, from_other_core(): return lax.ppermute(value, 'core', [(0, 1), (1, 0)])  11.3 us
    ppermute x6, starting transfers between devices, to_rows(): lax.ppermute(blocks[k], 'rows', [(i, (i + k) % ROWS) for i in range(ROWS)])  9.42 us
    pallas_call x1, Pallas kernels, body(): call(attend_kernel, [sds((WIDE, PACKED, 128), bf16), sds((2, OWN, 128), f...  5.23 us
    ppermute x5, waiting for transfers between devices, from_other_core(): return lax.ppermute(value, 'core', [(0, 1), (1, 0)])  4.76 us
    ppermute x6, waiting for transfers between devices, to_rows(): lax.ppermute(blocks[k], 'rows', [(i, (i + k) % ROWS) for i in range(ROWS)])  3.31 us
  transfers between devices with their start and end apart: 29, of which 21 were waited for; matrix products, arithmetic and copies ran while one was open for 0% of the time, Pallas kernels for 1%

profile of v11, /device:TPU:1, one launch (start us, length us, event | category | flops | bytes accessed | tf_op | source)
XLA Modules:
  0.0 112.2 jit_solution(4364138842190385973)
XLA Ops:
  0.6 1.6 %project.1 = (f32[16,384]{1,0:T(8,128)S(1)}, f32[16,384]{1,0:T(8,128)S(1)}, f32[16,384]{1,0:T(8,128)S(1)}, f32[16,384]{1,0:T(8,128)S(1)}) custom-call(s32[1]{0:T(128)} %bitcast.place_ref, bf16[64,1280]{1,0:T(8,128)(2,1)} %hidden_ref.1, bf16[1280]{0:T(1024)(128)(2,1)} %gain_hbm.1, bf16[1280,256]{1,0:T(8,128)(2,1)} %wq_hbm.1, bf16[64,1280]{1,0:T(8,128)(2,1)} %bitcast.12), custom_call_target="tpu_custom_call" | custom-call | tf_op jit(solution)/shard_map/project/pallas_call | solution.py:431
  2.3 3.7 %collective-permute-start = (f32[16,384]{1,0:T(8,128)S(1)}, f32[16,384]{1,0:T(8,128)S(1)}, u32[]{:S(2)}, u32[]{:S(2)}) collective-permute-start(f32[16,384]{1,0:T(8,128)S(1)} %get-tuple-element.23), channel_id=1, source_target_pairs={{0,64},{32,96},{64,0},{96,32},{1,65},{33,97},{65,1},{97,33},{2,66}... | collective-permute-start | bytes 73736 | tf_op jit(solution)/shard_map/ppermute | solution.py:381
  6.2 2.4 %collective-permute-start.2 = (f32[16,384]{1,0:T(8,128)S(1)}, f32[16,384]{1,0:T(8,128)S(1)}, u32[]{:S(2)}, u32[]{:S(2)}) collective-permute-start(f32[16,384]{1,0:T(8,128)S(1)} %get-tuple-element.25), channel_id=1, source_target_pairs={{0,96},{32,0},{64,32},{96,64},{1,97},{33,1},{65,33},{97,65},{2,98}... | collective-permute-start | bytes 73736 | tf_op jit(solution)/shard_map/ppermute | solution.py:381
  10.4 14.9 %all_to_all.10.own_ref = bf16[16,48,128]{2,1,0:T(8,128)(2,1)S(1)} all-to-all(bf16[16,48,128]{2,1,0:T(8,128)(2,1)S(1)} %heads.1), channel_id=1, replica_groups=mesh['rows'=4,'y'=4,'z'=4,'core'=2] {'y','z'}, dimensions={0} | all-to-all | bytes 393216 | tf_op jit(solution)/shard_map/all_to_all | solution.py:393
  25.3 3.1 %collective-permute-start.3 = (bf16[16,48,128]{2,1,0:T(8,128)(2,1)S(1)}, bf16[16,48,128]{2,1,0:T(8,128)(2,1)S(1)}, u32[]{:S(2)}, u32[]{:S(2)}) collective-permute-start(bf16[16,48,128]{2,1,0:T(8,128)(2,1)S(1)} %all_to_all.10.own_ref), channel_id=1, source_target_pairs={{0,1},{1,0},{2,3},{3,2},{4,5},{5,4},{6,7},{7,6},{8,9},{9,8},{10,11... | collective-permute-start | bytes 589832 | tf_op jit(solution)/shard_map/ppermute | solution.py:397
  29.5 5.2 %attend.1 = (bf16[32,48,128]{2,1,0:T(8,128)(2,1)S(1)}, f32[2,16,128]{2,1,0:T(8,128)S(1)}, f32[16,128]{1,0:T(8,128)S(1)}) custom-call(s32[1]{0:T(128)} %bitcast.place_ref, s32[16]{0:T(128)S(1)} %copy-done.6, s32[16]{0:T(128)S(1)} %bitcast.11, bf16[16,48,128]{2,1,0:T(8,128)(2,1)S(1)} %all_to_all.10.own_ref, ...), custom_call_target="tpu_custom_call" | custom-call | tf_op jit(solution)/shard_map/attend/pallas_call | solution.py:465
  34.8 14.4 %all_to_all.11.r_ref = bf16[32,48,128]{2,1,0:T(8,128)(2,1)S(1)} all-to-all(bf16[32,48,128]{2,1,0:T(8,128)(2,1)S(1)} %get-tuple-element.28), channel_id=1, replica_groups=mesh['rows'=4,'y'=4,'z'=4,'core'=2] {'y','z','core'}, dimensions={0} | all-to-all | bytes 786432 | tf_op jit(solution)/shard_map/all_to_all | solution.py:393
  51.5 2.3 %collective-permute-start.5 = (bf16[16,256]{1,0:T(8,128)(2,1)S(1)}, bf16[16,256]{1,0:T(8,128)(2,1)S(1)}, u32[]{:S(2)}, u32[]{:S(2)}) collective-permute-start(bf16[16,256]{1,0:T(8,128)(2,1)S(1)} %get-tuple-element.31.a_ref), channel_id=1, source_target_pairs={{96,0},{0,32},{32,64},{64,96},{97,1},{1,33},{33,65},{65,97},{98,2}... | collective-permute-start | bytes 24584 | tf_op jit(solution)/shard_map/ppermute | solution.py:388
  56.6 1.7 %collective-permute-start.7 = (bf16[32,1280]{1,0:T(8,128)(2,1)S(1)}, bf16[32,1280]{1,0:T(8,128)(2,1)S(1)}, u32[]{:S(2)}, u32[]{:S(2)}) collective-permute-start(bf16[32,1280]{1,0:T(8,128)(2,1)S(1)} %get-tuple-element.33), channel_id=1, source_target_pairs={{0,1},{1,0},{2,3},{3,2},{4,5},{5,4},{6,7},{7,6},{8,9},{9,8},{10,11... | collective-permute-start | bytes 245768 | tf_op jit(solution)/shard_map/ppermute | solution.py:397
  60.7 2.6 %collective-permute-start.8 = (bf16[32,1280]{1,0:T(8,128)(2,1)S(1)}, bf16[32,1280]{1,0:T(8,128)(2,1)S(1)}, u32[]{:S(2)}, u32[]{:S(2)}) collective-permute-start(bf16[32,1280]{1,0:T(8,128)(2,1)S(1)} %add.18.refs_0_), channel_id=1, source_target_pairs={{8,0},{16,8},{24,16},{0,24},{9,1},{17,9},{25,17},{1,25},{10,2},{18... | collective-permute-start | bytes 245768 | tf_op jit(solution)/shard_map/ppermute | solution.py:388
  64.4 2.0 %collective-permute-done.9.refs_2_ = bf16[32,1280]{1,0:T(8,128)(2,1)S(1)} collective-permute-done((bf16[32,1280]{1,0:T(8,128)(2,1)S(1)}, bf16[32,1280]{1,0:T(8,128)(2,1)S(1)}, u32[]{:S(2)}, u32[]{:S(2)}) %collective-permute-start.9) | collective-permute-done | bytes 81952 | tf_op jit(solution)/shard_map/ppermute | solution.py:388
  66.5 1.6 %collective-permute-start.13 = (bf16[32,1280]{1,0:T(8,128)(2,1)S(1)}, bf16[32,1280]{1,0:T(8,128)(2,1)S(1)}, u32[]{:S(2)}, u32[]{:S(2)}) collective-permute-start(bf16[32,1280]{1,0:T(8,128)(2,1)S(1)} %add.19.refs_0_), channel_id=1, source_target_pairs={{4,0},{6,2},{0,4},{2,6},{5,1},{7,3},{1,5},{3,7},{12,8},{14,10},{8,... | collective-permute-start | bytes 245768 | tf_op jit(solution)/shard_map/ppermute | solution.py:388
  68.3 2.5 %collective-permute-start.11 = (bf16[32,1280]{1,0:T(8,128)(2,1)S(1)}, bf16[32,1280]{1,0:T(8,128)(2,1)S(1)}, u32[]{:S(2)}, u32[]{:S(2)}) collective-permute-start(bf16[32,1280]{1,0:T(8,128)(2,1)S(1)} %add.19.refs_0_), channel_id=1, source_target_pairs={{2,0},{4,2},{6,4},{0,6},{3,1},{5,3},{7,5},{1,7},{10,8},{12,10},{14... | collective-permute-start | bytes 245768 | tf_op jit(solution)/shard_map/ppermute | solution.py:388
  71.4 2.6 %collective-permute-done.12.refs_2_ = bf16[32,1280]{1,0:T(8,128)(2,1)S(1)} collective-permute-done((bf16[32,1280]{1,0:T(8,128)(2,1)S(1)}, bf16[32,1280]{1,0:T(8,128)(2,1)S(1)}, u32[]{:S(2)}, u32[]{:S(2)}) %collective-permute-start.12) | collective-permute-done | bytes 81952 | tf_op jit(solution)/shard_map/ppermute | solution.py:388
  77.9 1.8 %collective-permute-start.16 = (bf16[16,1792]{1,0:T(8,128)(2,1)S(1)}, bf16[16,1792]{1,0:T(8,128)(2,1)S(1)}, u32[]{:S(2)}, u32[]{:S(2)}) collective-permute-start(bf16[16,1792]{1,0:T(8,128)(2,1)S(1)} %get-tuple-element.37), channel_id=1, source_target_pairs={{0,32},{32,64},{64,96},{96,0},{1,33},{33,65},{65,97},{97,1},{2,34}... | collective-permute-start | bytes 172040 | tf_op jit(solution)/shard_map/ppermute | solution.py:381
  80.6 1.6 %collective-permute-done.15.b_ref = bf16[16,1792]{1,0:T(8,128)(2,1)S(1)} collective-permute-done((bf16[16,1792]{1,0:T(8,128)(2,1)S(1)}, bf16[16,1792]{1,0:T(8,128)(2,1)S(1)}, u32[]{:S(2)}, u32[]{:S(2)}) %collective-permute-start.15) | collective-permute-done | bytes 57376 | tf_op jit(solution)/shard_map/ppermute | solution.py:381
  82.2 1.7 %collective-permute-done.16.c_ref = bf16[16,1792]{1,0:T(8,128)(2,1)S(1)} collective-permute-done((bf16[16,1792]{1,0:T(8,128)(2,1)S(1)}, bf16[16,1792]{1,0:T(8,128)(2,1)S(1)}, u32[]{:S(2)}, u32[]{:S(2)}) %collective-permute-start.16) | collective-permute-done | bytes 57376 | tf_op jit(solution)/shard_map/ppermute | solution.py:381
  84.2 1.8 %collective-permute-start.19 = (bf16[16,896]{1,0:T(8,128)(2,1)S(1)}, bf16[16,896]{1,0:T(8,128)(2,1)S(1)}, u32[]{:S(2)}, u32[]{:S(2)}) collective-permute-start(bf16[16,896]{1,0:T(8,128)(2,1)S(1)} %activate.1.a_ref), channel_id=1, source_target_pairs={{96,0},{0,32},{32,64},{64,96},{97,1},{1,33},{33,65},{65,97},{98,2}... | collective-permute-start | bytes 86024 | tf_op jit(solution)/shard_map/ppermute | solution.py:388
  89.1 3.8 %collective-permute-start.21 = (bf16[32,1280]{1,0:T(8,128)(2,1)S(1)}, bf16[32,1280]{1,0:T(8,128)(2,1)S(1)}, u32[]{:S(2)}, u32[]{:S(2)}) collective-permute-start(bf16[32,1280]{1,0:T(8,128)(2,1)S(1)} %get-tuple-element.40), channel_id=1, source_target_pairs={{0,1},{1,0},{2,3},{3,2},{4,5},{5,4},{6,7},{7,6},{8,9},{9,8},{10,11... | collective-permute-start | bytes 245768 | tf_op jit(solution)/shard_map/ppermute | solution.py:397
  96.2 1.8 %collective-permute-start.22 = (bf16[32,1280]{1,0:T(8,128)(2,1)S(1)}, bf16[32,1280]{1,0:T(8,128)(2,1)S(1)}, u32[]{:S(2)}, u32[]{:S(2)}) collective-permute-start(bf16[32,1280]{1,0:T(8,128)(2,1)S(1)} %add.21.refs_0_), channel_id=1, source_target_pairs={{8,0},{16,8},{24,16},{0,24},{9,1},{17,9},{25,17},{1,25},{10,2},{18... | collective-permute-start | bytes 245768 | tf_op jit(solution)/shard_map/ppermute | solution.py:388
  99.1 2.0 %collective-permute-done.23.refs_2_ = bf16[32,1280]{1,0:T(8,128)(2,1)S(1)} collective-permute-done((bf16[32,1280]{1,0:T(8,128)(2,1)S(1)}, bf16[32,1280]{1,0:T(8,128)(2,1)S(1)}, u32[]{:S(2)}, u32[]{:S(2)}) %collective-permute-start.23) | collective-permute-done | bytes 81952 | tf_op jit(solution)/shard_map/ppermute | solution.py:388
  102.6 1.9 %collective-permute-start.26 = (bf16[32,1280]{1,0:T(8,128)(2,1)S(1)}, bf16[32,1280]{1,0:T(8,128)(2,1)S(1)}, u32[]{:S(2)}, u32[]{:S(2)}) collective-permute-start(bf16[32,1280]{1,0:T(8,128)(2,1)S(1)} %add.22.refs_0_), channel_id=1, source_target_pairs={{6,0},{0,2},{2,4},{4,6},{7,1},{1,3},{3,5},{5,7},{14,8},{8,10},{10,... | collective-permute-start | bytes 245768 | tf_op jit(solution)/shard_map/ppermute | solution.py:388
  106.1 2.1 %collective-permute-done.26.refs_2_ = bf16[32,1280]{1,0:T(8,128)(2,1)S(1)} collective-permute-done((bf16[32,1280]{1,0:T(8,128)(2,1)S(1)}, bf16[32,1280]{1,0:T(8,128)(2,1)S(1)}, u32[]{:S(2)}, u32[]{:S(2)}) %collective-permute-start.26) | collective-permute-done | bytes 81952 | tf_op jit(solution)/shard_map/ppermute | solution.py:388
  108.9 1.6 %collective-permute-start.28 = (bf16[32,1280]{1,0:T(8,128)(2,1)S(1)}, bf16[32,1280]{1,0:T(8,128)(2,1)S(1)}, u32[]{:S(2)}, u32[]{:S(2)}) collective-permute-start(bf16[32,1280]{1,0:T(8,128)(2,1)S(1)} %add.23.own_ref), channel_id=1, source_target_pairs={{0,1},{1,0},{2,3},{3,2},{4,5},{5,4},{6,7},{7,6},{8,9},{9,8},{10,11... | collective-permute-start | bytes 245768 | tf_op jit(solution)/shard_map/ppermute | solution.py:397
  (78 shorter events, 30.6 us)
Async XLA Ops:
  2.3 7.8 %collective-permute-start = (f32[16,384]{1,0:T(8,128)S(1)}, f32[16,384]{1,0:T(8,128)S(1)}, u32[]{:S(2)}, u32[]{:S(2)}) collective-permute-start(f32[16,384]{1,0:T(8,128)S(1)} %get-tuple-element.23), channel_id=1, source_target_pairs={{0,64},{32,96},{64,0},{96,32},{1,65},{33,97},{65,1},{97,33},{2,66}... | collective-permute-start | bytes 73736 | tf_op jit(solution)/shard_map/ppermute | solution.py:381
  5.9 4.2 %collective-permute-start.1 = (f32[16,384]{1,0:T(8,128)S(1)}, f32[16,384]{1,0:T(8,128)S(1)}, u32[]{:S(2)}, u32[]{:S(2)}) collective-permute-start(f32[16,384]{1,0:T(8,128)S(1)} %get-tuple-element.24), channel_id=1, source_target_pairs={{0,32},{32,64},{64,96},{96,0},{1,33},{33,65},{65,97},{97,1},{2,34}... | collective-permute-start | bytes 73736 | tf_op jit(solution)/shard_map/ppermute | solution.py:381
  6.2 3.9 %collective-permute-start.2 = (f32[16,384]{1,0:T(8,128)S(1)}, f32[16,384]{1,0:T(8,128)S(1)}, u32[]{:S(2)}, u32[]{:S(2)}) collective-permute-start(f32[16,384]{1,0:T(8,128)S(1)} %get-tuple-element.25), channel_id=1, source_target_pairs={{0,96},{32,0},{64,32},{96,64},{1,97},{33,1},{65,33},{97,65},{2,98}... | collective-permute-start | bytes 73736 | tf_op jit(solution)/shard_map/ppermute | solution.py:381
  25.3 4.1 %collective-permute-start.3 = (bf16[16,48,128]{2,1,0:T(8,128)(2,1)S(1)}, bf16[16,48,128]{2,1,0:T(8,128)(2,1)S(1)}, u32[]{:S(2)}, u32[]{:S(2)}) collective-permute-start(bf16[16,48,128]{2,1,0:T(8,128)(2,1)S(1)} %all_to_all.10.own_ref), channel_id=1, source_target_pairs={{0,1},{1,0},{2,3},{3,2},{4,5},{5,4},{6,7},{7,6},{8,9},{9,8},{10,11... | collective-permute-start | bytes 589832 | tf_op jit(solution)/shard_map/ppermute | solution.py:397
  50.3 4.0 %collective-permute-start.6 = (bf16[16,256]{1,0:T(8,128)(2,1)S(1)}, bf16[16,256]{1,0:T(8,128)(2,1)S(1)}, u32[]{:S(2)}, u32[]{:S(2)}) collective-permute-start(bf16[16,256]{1,0:T(8,128)(2,1)S(1)} %get-tuple-element.31.a_ref), channel_id=1, source_target_pairs={{64,0},{96,32},{0,64},{32,96},{65,1},{97,33},{1,65},{33,97},{66,2}... | collective-permute-start | bytes 24584 | tf_op jit(solution)/shard_map/ppermute | solution.py:388
  51.5 3.7 %collective-permute-start.5 = (bf16[16,256]{1,0:T(8,128)(2,1)S(1)}, bf16[16,256]{1,0:T(8,128)(2,1)S(1)}, u32[]{:S(2)}, u32[]{:S(2)}) collective-permute-start(bf16[16,256]{1,0:T(8,128)(2,1)S(1)} %get-tuple-element.31.a_ref), channel_id=1, source_target_pairs={{96,0},{0,32},{32,64},{64,96},{97,1},{1,33},{33,65},{65,97},{98,2}... | collective-permute-start | bytes 24584 | tf_op jit(solution)/shard_map/ppermute | solution.py:388
  59.2 5.3 %collective-permute-start.10 = (bf16[32,1280]{1,0:T(8,128)(2,1)S(1)}, bf16[32,1280]{1,0:T(8,128)(2,1)S(1)}, u32[]{:S(2)}, u32[]{:S(2)}) collective-permute-start(bf16[32,1280]{1,0:T(8,128)(2,1)S(1)} %add.18.refs_0_), channel_id=1, source_target_pairs={{16,0},{24,8},{0,16},{8,24},{17,1},{25,9},{1,17},{9,25},{18,2},{26... | collective-permute-start | bytes 245768 | tf_op jit(solution)/shard_map/ppermute | solution.py:388
  60.6 5.9 %collective-permute-start.9 = (bf16[32,1280]{1,0:T(8,128)(2,1)S(1)}, bf16[32,1280]{1,0:T(8,128)(2,1)S(1)}, u32[]{:S(2)}, u32[]{:S(2)}) collective-permute-start(bf16[32,1280]{1,0:T(8,128)(2,1)S(1)} %add.18.refs_0_), channel_id=1, source_target_pairs={{24,0},{0,8},{8,16},{16,24},{25,1},{1,9},{9,17},{17,25},{26,2},{2,... | collective-permute-start | bytes 245768 | tf_op jit(solution)/shard_map/ppermute | solution.py:388
  60.7 5.8 %collective-permute-start.8 = (bf16[32,1280]{1,0:T(8,128)(2,1)S(1)}, bf16[32,1280]{1,0:T(8,128)(2,1)S(1)}, u32[]{:S(2)}, u32[]{:S(2)}) collective-permute-start(bf16[32,1280]{1,0:T(8,128)(2,1)S(1)} %add.18.refs_0_), channel_id=1, source_target_pairs={{8,0},{16,8},{24,16},{0,24},{9,1},{17,9},{25,17},{1,25},{10,2},{18... | collective-permute-start | bytes 245768 | tf_op jit(solution)/shard_map/ppermute | solution.py:388
  66.5 4.9 %collective-permute-start.13 = (bf16[32,1280]{1,0:T(8,128)(2,1)S(1)}, bf16[32,1280]{1,0:T(8,128)(2,1)S(1)}, u32[]{:S(2)}, u32[]{:S(2)}) collective-permute-start(bf16[32,1280]{1,0:T(8,128)(2,1)S(1)} %add.19.refs_0_), channel_id=1, source_target_pairs={{4,0},{6,2},{0,4},{2,6},{5,1},{7,3},{1,5},{3,7},{12,8},{14,10},{8,... | collective-permute-start | bytes 245768 | tf_op jit(solution)/shard_map/ppermute | solution.py:388
  68.1 5.9 %collective-permute-start.12 = (bf16[32,1280]{1,0:T(8,128)(2,1)S(1)}, bf16[32,1280]{1,0:T(8,128)(2,1)S(1)}, u32[]{:S(2)}, u32[]{:S(2)}) collective-permute-start(bf16[32,1280]{1,0:T(8,128)(2,1)S(1)} %add.19.refs_0_), channel_id=1, source_target_pairs={{6,0},{0,2},{2,4},{4,6},{7,1},{1,3},{3,5},{5,7},{14,8},{8,10},{10,... | collective-permute-start | bytes 245768 | tf_op jit(solution)/shard_map/ppermute | solution.py:388
  68.3 5.7 %collective-permute-start.11 = (bf16[32,1280]{1,0:T(8,128)(2,1)S(1)}, bf16[32,1280]{1,0:T(8,128)(2,1)S(1)}, u32[]{:S(2)}, u32[]{:S(2)}) collective-permute-start(bf16[32,1280]{1,0:T(8,128)(2,1)S(1)} %add.19.refs_0_), channel_id=1, source_target_pairs={{2,0},{4,2},{6,4},{0,6},{3,1},{5,3},{7,5},{1,7},{10,8},{12,10},{14... | collective-permute-start | bytes 245768 | tf_op jit(solution)/shard_map/ppermute | solution.py:388
  77.5 4.7 %collective-permute-start.15 = (bf16[16,1792]{1,0:T(8,128)(2,1)S(1)}, bf16[16,1792]{1,0:T(8,128)(2,1)S(1)}, u32[]{:S(2)}, u32[]{:S(2)}) collective-permute-start(bf16[16,1792]{1,0:T(8,128)(2,1)S(1)} %get-tuple-element.36), channel_id=1, source_target_pairs={{0,64},{32,96},{64,0},{96,32},{1,65},{33,97},{65,1},{97,33},{2,66}... | collective-permute-start | bytes 172040 | tf_op jit(solution)/shard_map/ppermute | solution.py:381
  77.9 6.0 %collective-permute-start.16 = (bf16[16,1792]{1,0:T(8,128)(2,1)S(1)}, bf16[16,1792]{1,0:T(8,128)(2,1)S(1)}, u32[]{:S(2)}, u32[]{:S(2)}) collective-permute-start(bf16[16,1792]{1,0:T(8,128)(2,1)S(1)} %get-tuple-element.37), channel_id=1, source_target_pairs={{0,32},{32,64},{64,96},{96,0},{1,33},{33,65},{65,97},{97,1},{2,34}... | collective-permute-start | bytes 172040 | tf_op jit(solution)/shard_map/ppermute | solution.py:381
  79.7 4.2 %collective-permute-start.17 = (bf16[16,1792]{1,0:T(8,128)(2,1)S(1)}, bf16[16,1792]{1,0:T(8,128)(2,1)S(1)}, u32[]{:S(2)}, u32[]{:S(2)}) collective-permute-start(bf16[16,1792]{1,0:T(8,128)(2,1)S(1)} %get-tuple-element.38), channel_id=1, source_target_pairs={{0,96},{32,0},{64,32},{96,64},{1,97},{33,1},{65,33},{97,65},{2,98}... | collective-permute-start | bytes 172040 | tf_op jit(solution)/shard_map/ppermute | solution.py:381
  84.1 4.4 %collective-permute-start.20 = (bf16[16,896]{1,0:T(8,128)(2,1)S(1)}, bf16[16,896]{1,0:T(8,128)(2,1)S(1)}, u32[]{:S(2)}, u32[]{:S(2)}) collective-permute-start(bf16[16,896]{1,0:T(8,128)(2,1)S(1)} %activate.1.a_ref), channel_id=1, source_target_pairs={{64,0},{96,32},{0,64},{32,96},{65,1},{97,33},{1,65},{33,97},{66,2}... | collective-permute-start | bytes 86024 | tf_op jit(solution)/shard_map/ppermute | solution.py:388
  84.2 4.3 %collective-permute-start.19 = (bf16[16,896]{1,0:T(8,128)(2,1)S(1)}, bf16[16,896]{1,0:T(8,128)(2,1)S(1)}, u32[]{:S(2)}, u32[]{:S(2)}) collective-permute-start(bf16[16,896]{1,0:T(8,128)(2,1)S(1)} %activate.1.a_ref), channel_id=1, source_target_pairs={{96,0},{0,32},{32,64},{64,96},{97,1},{1,33},{33,65},{65,97},{98,2}... | collective-permute-start | bytes 86024 | tf_op jit(solution)/shard_map/ppermute | solution.py:388
  89.1 4.7 %collective-permute-start.21 = (bf16[32,1280]{1,0:T(8,128)(2,1)S(1)}, bf16[32,1280]{1,0:T(8,128)(2,1)S(1)}, u32[]{:S(2)}, u32[]{:S(2)}) collective-permute-start(bf16[32,1280]{1,0:T(8,128)(2,1)S(1)} %get-tuple-element.40), channel_id=1, source_target_pairs={{0,1},{1,0},{2,3},{3,2},{4,5},{5,4},{6,7},{7,6},{8,9},{9,8},{10,11... | collective-permute-start | bytes 245768 | tf_op jit(solution)/shard_map/ppermute | solution.py:397
  93.9 5.3 %collective-permute-start.24 = (bf16[32,1280]{1,0:T(8,128)(2,1)S(1)}, bf16[32,1280]{1,0:T(8,128)(2,1)S(1)}, u32[]{:S(2)}, u32[]{:S(2)}) collective-permute-start(bf16[32,1280]{1,0:T(8,128)(2,1)S(1)} %add.21.refs_0_), channel_id=1, source_target_pairs={{16,0},{24,8},{0,16},{8,24},{17,1},{25,9},{1,17},{9,25},{18,2},{26... | collective-permute-start | bytes 245768 | tf_op jit(solution)/shard_map/ppermute | solution.py:388
  95.3 5.8 %collective-permute-start.23 = (bf16[32,1280]{1,0:T(8,128)(2,1)S(1)}, bf16[32,1280]{1,0:T(8,128)(2,1)S(1)}, u32[]{:S(2)}, u32[]{:S(2)}) collective-permute-start(bf16[32,1280]{1,0:T(8,128)(2,1)S(1)} %add.21.refs_0_), channel_id=1, source_target_pairs={{24,0},{0,8},{8,16},{16,24},{25,1},{1,9},{9,17},{17,25},{26,2},{2,... | collective-permute-start | bytes 245768 | tf_op jit(solution)/shard_map/ppermute | solution.py:388
  96.2 4.9 %collective-permute-start.22 = (bf16[32,1280]{1,0:T(8,128)(2,1)S(1)}, bf16[32,1280]{1,0:T(8,128)(2,1)S(1)}, u32[]{:S(2)}, u32[]{:S(2)}) collective-permute-start(bf16[32,1280]{1,0:T(8,128)(2,1)S(1)} %add.21.refs_0_), channel_id=1, source_target_pairs={{8,0},{16,8},{24,16},{0,24},{9,1},{17,9},{25,17},{1,25},{10,2},{18... | collective-permute-start | bytes 245768 | tf_op jit(solution)/shard_map/ppermute | solution.py:388
  101.2 4.9 %collective-permute-start.27 = (bf16[32,1280]{1,0:T(8,128)(2,1)S(1)}, bf16[32,1280]{1,0:T(8,128)(2,1)S(1)}, u32[]{:S(2)}, u32[]{:S(2)}) collective-permute-start(bf16[32,1280]{1,0:T(8,128)(2,1)S(1)} %add.22.refs_0_), channel_id=1, source_target_pairs={{4,0},{6,2},{0,4},{2,6},{5,1},{7,3},{1,5},{3,7},{12,8},{14,10},{8,... | collective-permute-start | bytes 245768 | tf_op jit(solution)/shard_map/ppermute | solution.py:388
  102.6 5.6 %collective-permute-start.26 = (bf16[32,1280]{1,0:T(8,128)(2,1)S(1)}, bf16[32,1280]{1,0:T(8,128)(2,1)S(1)}, u32[]{:S(2)}, u32[]{:S(2)}) collective-permute-start(bf16[32,1280]{1,0:T(8,128)(2,1)S(1)} %add.22.refs_0_), channel_id=1, source_target_pairs={{6,0},{0,2},{2,4},{4,6},{7,1},{1,3},{3,5},{5,7},{14,8},{8,10},{10,... | collective-permute-start | bytes 245768 | tf_op jit(solution)/shard_map/ppermute | solution.py:388
  104.5 4.4 %collective-permute-start.25 = (bf16[32,1280]{1,0:T(8,128)(2,1)S(1)}, bf16[32,1280]{1,0:T(8,128)(2,1)S(1)}, u32[]{:S(2)}, u32[]{:S(2)}) collective-permute-start(bf16[32,1280]{1,0:T(8,128)(2,1)S(1)} %add.22.refs_0_), channel_id=1, source_target_pairs={{2,0},{4,2},{6,4},{0,6},{3,1},{5,3},{7,5},{1,7},{10,8},{12,10},{14... | collective-permute-start | bytes 245768 | tf_op jit(solution)/shard_map/ppermute | solution.py:388
  (17 other events, 338.4 us)
